TPU v7x, 32 devices: a whole 2x2x4 slice. The times are simulated.
32 devices in a mesh: row: 8 (over z, x), col: 4 (over y, core).
Axes of the slice: x: 2, y: 2, z: 4, core: 2. Of those that a mesh axis runs over, the one named last changes fastest.
Arguments:
- matrix: float32 [2048, 2048], P('row', 'col'), as said below
Outputs:
- factored: float32 [2048, 2048], P('row', 'col')
Inputs may be any that keep to these rules, and one draw needn't show every extreme that they name: `matrix`: each diagonal entry lies between 3 and 6 times the square root of 256; every other entry has magnitude 6 or less.
All inputs are finite; a program needn't handle non-finite values.
Results may differ from a plain program's by a relative error of at most 0.00085.
Values may be sent and summed in bfloat16 or wider, within the bound.
No kernel may reach another device: no remote copies, remote signals or barrier semaphores. Data moves between devices by JAX's collectives and lax.ppermute only.
A program may use at most 64 MiB of HBM per device.

v0:
```python
import jax
import jax.numpy as jnp
from jax import lax
from jax.sharding import PartitionSpec as P

NB = 256
HIGH = lax.Precision.HIGH
APART = 2


def strides(size):
    out, stride = [], size // 2
    while stride:
        out.append(stride)
        stride //= 2
    return out


def multipliers(square, columns):
    identity = jnp.eye(NB, dtype=jnp.float32)
    diagonal = square * identity
    across = 1.0 / jnp.sum(diagonal, axis=0, keepdims=True)
    down = 1.0 / jnp.sum(diagonal, axis=1, keepdims=True)
    approx = down * (2.0 * identity - square * across)
    product = jnp.dot(jnp.concatenate([square, columns], axis=0), approx, precision=HIGH)
    return jnp.dot(product[NB:], 2.0 * identity - product[:NB], precision=HIGH)


def shards(matrix):
    rows_dev, cols_dev = matrix.shape
    assert rows_dev == NB
    n_row, n_col = lax.axis_size("row"), lax.axis_size("col")
    row_here, col_here = lax.axis_index("row"), lax.axis_index("col")

    def send(value, pairs):
        flat = [(r0 * n_col + c0, r1 * n_col + c1) for (r0, c0), (r1, c1) in pairs]
        return lax.ppermute(value, ("row", "col"), flat)

    upper = matrix.astype(jnp.bfloat16)
    pivot_columns, column_upper = matrix[:, :NB], upper[:, NB:]

    down = strides(n_row)
    orders = [down, [down[-1]] + down[:-1]]
    held = [[0], [0]]

    def upper_step(value, step):
        pairs = []
        takes = []
        for kind in range(2):
            stride = orders[kind][step]
            missing = sum(orders[kind][step + 1 :])
            takes.append((row_here & (stride | missing)) == stride)
            pairs += [
                ((h, c), (h + stride, c)) for h in held[kind] for c in range(1, n_col) if c % 2 == kind
            ]
            held[kind] = held[kind] + [h + stride for h in held[kind]]
        got = send(value, pairs)
        return jnp.where(jnp.where(col_here % 2 == 0, takes[0], takes[1]), got, value)

    workers = [r for r in range(n_row) if r & APART == 0]
    targets = workers[2:] + workers[1:2]
    square, partner = pivot_columns, pivot_columns
    near_upper = column_upper
    upper, column_upper = lax.optimization_barrier((upper_step(upper, 0), column_upper))
    for index, target in enumerate(targets):
        served = [0, targets[-1]] if index == 0 else [targets[index - 1]]
        pairs = [((0, 0), (target, 0))] + [((r + APART, 0), (r, 0)) for r in served]
        got = send(pivot_columns, pairs)
        square = jnp.where(row_here == target, got, square)
        for r in served:
            partner = jnp.where(row_here == r, got, partner)
    for target in reversed(workers[1:]):
        got = send(column_upper, [((0, 0), (target, 0))])
        near_upper = jnp.where(row_here == target, got, near_upper)
    upper = upper_step(upper, 1)

    def compute(square, partner):
        both = multipliers(square, jnp.concatenate([pivot_columns, partner], axis=0))
        both = both.astype(jnp.bfloat16)
        return both[:NB], both[NB:]

    def none(square, partner):
        zero = jnp.zeros((NB, NB), jnp.bfloat16)
        return zero, zero

    working = (row_here & APART == 0) & (col_here == 0)
    lower, lower_far = lax.cond(working, compute, none, square, partner)
    received = lower
    for c in range(2, n_col, 2):
        got = send(lower_far, [((r, 0), (r + APART, c)) for r in workers])
        received = jnp.where((row_here & APART != 0) & (col_here == c), got, received)
    got = send(lower_far, [((r, 0), (r + APART, 0)) for r in workers])
    received = jnp.where((row_here & APART != 0) & (col_here == 0), got, received)
    for c in range(2, n_col, 2):
        got = send(lower, [((r, 0), (r, c)) for r in targets])
        received = jnp.where((row_here & APART == 0) & (col_here == c), got, received)
    near_sent, _ = lax.optimization_barrier((near_upper, lower))
    got = send(near_sent, [((r, 0), (r + APART, 0)) for r in workers])
    near_upper = jnp.where(row_here & APART == 0, near_upper, got)
    for step in range(2, len(down)):
        upper = upper_step(upper, step)
    got = send(
        received, [((r, c), (r, c + 1)) for r in range(1, n_row) for c in range(0, n_col, 2)]
    )
    received = jnp.where(col_here % 2 == 0, received, got)
    received = jnp.where(row_here == 0, jnp.zeros_like(received), received)

    column_upper = jnp.concatenate([jnp.zeros((NB, NB), jnp.bfloat16), near_upper], axis=1)
    upper = jnp.where(col_here == 0, column_upper, upper)
    return matrix - jnp.dot(received, upper, preferred_element_type=jnp.float32)


def solution(mesh):
    return jax.shard_map(
        shards,
        mesh=mesh,
        in_specs=(P("row", "col"),),
        out_specs=P("row", "col"),
        check_vma=False,
    )
```

profile of v0, /device:TPU:13, one launch (start us, length us, event | category | flops | bytes accessed | tf_op | source)
XLA Modules:
  0.0 29.0 jit_solution(6280867341129428132)
XLA Ops:
  0.0 0.0 copy-start
  0.0 1.1 %convert_element_type.12 = bf16[256,512]{1,0:T(8,128)(2,1)S(1)} convert(f32[256,512]{1,0:T(8,128)} %param.3) | non-fusion elementwise | flops 131072 | bytes 786432 | tf_op jit(solution)/shard_map/convert_element_type | solution.py:39
  1.2 0.7 %collective-permute-start.7 = (bf16[256,512]{1,0:T(8,128)(2,1)S(1)}, bf16[256,512]{1,0:T(8,128)(2,1)S(1)}, u32[]{:S(2)}, u32[]{:S(2)}) collective-permute-start(bf16[256,512]{1,0:T(8,128)(2,1)S(1)} %convert_element_type.12), channel_id=1, source_target_pairs={{2,18},{1,5},{3,7}} | collective-permute-start | bytes 786440 | tf_op jit(solution)/shard_map/ppermute | solution.py:37
  1.8 0.0 copy-done
  1.9 0.7 %collective-permute-start = (f32[256,256]{1,0:T(8,128)S(1)}, f32[256,256]{1,0:T(8,128)S(1)}, u32[]{:S(2)}, u32[]{:S(2)}) collective-permute-start(f32[256,256]{1,0:T(8,128)S(1)} %slice.22), channel_id=1, source_target_pairs={{0,16},{8,0},{12,4}} | collective-permute-start | bytes 786440 | tf_op jit(solution)/shard_map/ppermute | solution.py:37
  2.6 0.7 %collective-permute-start.1 = (f32[256,256]{1,0:T(8,128)S(1)}, f32[256,256]{1,0:T(8,128)S(1)}, u32[]{:S(2)}, u32[]{:S(2)}) collective-permute-start(f32[256,256]{1,0:T(8,128)S(1)} %slice.22), channel_id=1, source_target_pairs={{0,20},{24,16}} | collective-permute-start | bytes 786440 | tf_op jit(solution)/shard_map/ppermute | solution.py:37
  3.2 0.7 %collective-permute-start.2 = (f32[256,256]{1,0:T(8,128)S(1)}, f32[256,256]{1,0:T(8,128)S(1)}, u32[]{:S(2)}, u32[]{:S(2)}) collective-permute-start(f32[256,256]{1,0:T(8,128)S(1)} %slice.22), channel_id=1, source_target_pairs={{0,4},{28,20}} | collective-permute-start | bytes 786440 | tf_op jit(solution)/shard_map/ppermute | solution.py:37
  4.0 0.0 collective-permute-done.7
  4.0 0.7 %collective-permute-start.10 = (bf16[256,256]{1,0:T(8,128)(2,1)S(1)}, bf16[256,256]{1,0:T(8,128)(2,1)S(1)}, u32[]{:S(2)}, u32[]{:S(2)}) collective-permute-start(bf16[256,256]{1,0:T(8,128)(2,1)S(1)} %slice.28), channel_id=1, source_target_pairs={{0,20}} | collective-permute-start | bytes 393224 | tf_op jit(solution)/shard_map/ppermute | solution.py:37
  4.7 0.7 %collective-permute-start.8 = (bf16[256,256]{1,0:T(8,128)(2,1)S(1)}, bf16[256,256]{1,0:T(8,128)(2,1)S(1)}, u32[]{:S(2)}, u32[]{:S(2)}) collective-permute-start(bf16[256,256]{1,0:T(8,128)(2,1)S(1)} %slice.28), channel_id=1, source_target_pairs={{0,4}} | collective-permute-start | bytes 393224 | tf_op jit(solution)/shard_map/ppermute | solution.py:37
  5.4 0.0 collective-permute-done
  5.4 0.7 %collective-permute-start.9 = (bf16[256,256]{1,0:T(8,128)(2,1)S(1)}, bf16[256,256]{1,0:T(8,128)(2,1)S(1)}, u32[]{:S(2)}, u32[]{:S(2)}) collective-permute-start(bf16[256,256]{1,0:T(8,128)(2,1)S(1)} %slice.28), channel_id=1, source_target_pairs={{0,16}} | collective-permute-start | bytes 393224 | tf_op jit(solution)/shard_map/ppermute | solution.py:37
  6.1 0.0 collective-permute-done.1
  6.1 0.7 %collective-permute-start.12 = (bf16[256,512]{1,0:T(8,128)(2,1)S(1)}, bf16[256,512]{1,0:T(8,128)(2,1)S(1)}, u32[]{:S(2)}, u32[]{:S(2)}) collective-permute-start(bf16[256,512]{1,0:T(8,128)(2,1)S(1)} %broadcast_select_fusion.1), channel_id=1, source_target_pairs={{2,10},{18,26},{1,17},{3,19},{5,21},{7,23}} | collective-permute-start | bytes 786440 | tf_op jit(solution)/shard_map/ppermute | solution.py:37
  6.8 0.0 collective-permute-done.2
  6.9 0.1 conditional.1
  6.9 0.7 %collective-permute-start.4 = (bf16[256,256]{1,0:T(8,128)(2,1)S(1)}, bf16[256,256]{1,0:T(8,128)(2,1)S(1)}, u32[]{:S(2)}, u32[]{:S(2)}) collective-permute-start(bf16[256,256]{1,0:T(8,128)(2,1)S(1)} %get-tuple-element.78), channel_id=1, source_target_pairs={{0,8},{4,12},{16,24},{20,28}} | collective-permute-start | bytes 393224 | tf_op jit(solution)/shard_map/ppermute | solution.py:37
  7.6 0.0 collective-permute-done.10
  7.6 0.7 %collective-permute-start.5 = (bf16[256,256]{1,0:T(8,128)(2,1)S(1)}, bf16[256,256]{1,0:T(8,128)(2,1)S(1)}, u32[]{:S(2)}, u32[]{:S(2)}) collective-permute-start(bf16[256,256]{1,0:T(8,128)(2,1)S(1)} %get-tuple-element.78), channel_id=1, source_target_pairs={{0,10},{4,14},{16,26},{20,30}} | collective-permute-start | bytes 393224 | tf_op jit(solution)/shard_map/ppermute | solution.py:37
  8.3 0.0 collective-permute-done.8
  8.3 0.7 %collective-permute-start.3 = (bf16[256,256]{1,0:T(8,128)(2,1)S(1)}, bf16[256,256]{1,0:T(8,128)(2,1)S(1)}, u32[]{:S(2)}, u32[]{:S(2)}) collective-permute-start(bf16[256,256]{1,0:T(8,128)(2,1)S(1)} %get-tuple-element.77), channel_id=1, source_target_pairs={{16,18},{20,22},{4,6}} | collective-permute-start | bytes 393224 | tf_op jit(solution)/shard_map/ppermute | solution.py:37
  9.0 0.0 collective-permute-done.9
  9.0 0.7 %collective-permute-start.11 = (bf16[256,256]{1,0:T(8,128)(2,1)S(1)}, bf16[256,256]{1,0:T(8,128)(2,1)S(1)}, u32[]{:S(2)}, u32[]{:S(2)}) collective-permute-start(bf16[256,256]{1,0:T(8,128)(2,1)S(1)} %select_select_fusion.2), channel_id=1, source_target_pairs={{0,8},{4,12},{16,24},{20,28}} | collective-permute-start | bytes 393224 | tf_op jit(solution)/shard_map/ppermute | solution.py:37
  9.7 0.0 collective-permute-done.12
  9.7 1.3 %collective-permute-start.13 = (bf16[256,512]{1,0:T(8,128)(2,1)S(1)}, bf16[256,512]{1,0:T(8,128)(2,1)S(1)}, u32[]{:S(2)}, u32[]{:S(2)}) collective-permute-start(bf16[256,512]{1,0:T(8,128)(2,1)S(1)} %broadcast_select_fusion), channel_id=1, source_target_pairs={{2,6},{18,22},{10,14},{26,30},{1,9},{3,11},{5,13},{7,15},{17,25},{... | collective-permute-start | bytes 786440 | tf_op jit(solution)/shard_map/ppermute | solution.py:37
  11.0 0.0 collective-permute-done.3
  11.1 0.0 collective-permute-done.4
  11.1 0.0 collective-permute-done.5
  11.1 1.3 %collective-permute-start.6 = (bf16[256,256]{1,0:T(8,128)(2,1)S(1)}, bf16[256,256]{1,0:T(8,128)(2,1)S(1)}, u32[]{:S(2)}, u32[]{:S(2)}) collective-permute-start(bf16[256,256]{1,0:T(8,128)(2,1)S(1)} %select_select_fusion.3), channel_id=1, source_target_pairs={{4,5},{6,7},{8,9},{10,11},{12,13},{14,15},{16,17},{18,19},{20,21},... | collective-permute-start | bytes 393224 | tf_op jit(solution)/shard_map/ppermute | solution.py:37
  12.4 0.0 collective-permute-done.11
  12.5 15.5 %collective-permute-done.6 = bf16[256,256]{1,0:T(8,128)(2,1)S(1)} collective-permute-done((bf16[256,256]{1,0:T(8,128)(2,1)S(1)}, bf16[256,256]{1,0:T(8,128)(2,1)S(1)}, u32[]{:S(2)}, u32[]{:S(2)}) %collective-permute-start.6) | collective-permute-done | bytes 131104 | tf_op jit(solution)/shard_map/ppermute | solution.py:37
  28.0 0.0 collective-permute-done.13
  28.0 1.1 %convolution_subtract_fusion = f32[256,512]{1,0:T(8,128)} fusion(f32[256,512]{1,0:T(8,128)S(1)} %copy-done, bf16[256,512]{1,0:T(8,128)(2,1)S(1)} %collective-permute-done.13, bf16[256,512]{1,0:T(8,128)(2,1)S(1)} %broadcast_select_fusion, bf16[256,256]{1,0:T(8,128)(2,1)S(1)} %broadcast_select_fusion.2, pred[]{:T(512)S(6)} %select_n.184, pred[]{:T(512)S(6)} %eq.74, ...), kind=kOutput, calls=%fused_computation.34 | convolution fusion | flops 67633152 | bytes 1966084 | tf_op jit(solution)/shard_map/dot_general | solution.py:110
  (10 shorter events, 0.2 us)
Async XLA Ops:
  0.0 1.8 %copy-start = (f32[256,512]{1,0:T(8,128)S(1)}, f32[256,512]{1,0:T(8,128)}, u32[]{:S(2)}) copy-start(f32[256,512]{1,0:T(8,128)} %param.3) | copy-start | bytes 1572868
  1.2 2.8 %collective-permute-start.7 = (bf16[256,512]{1,0:T(8,128)(2,1)S(1)}, bf16[256,512]{1,0:T(8,128)(2,1)S(1)}, u32[]{:S(2)}, u32[]{:S(2)}) collective-permute-start(bf16[256,512]{1,0:T(8,128)(2,1)S(1)} %convert_element_type.12), channel_id=1, source_target_pairs={{2,18},{1,5},{3,7}} | collective-permute-start | bytes 786440 | tf_op jit(solution)/shard_map/ppermute | solution.py:37
  1.9 3.5 %collective-permute-start = (f32[256,256]{1,0:T(8,128)S(1)}, f32[256,256]{1,0:T(8,128)S(1)}, u32[]{:S(2)}, u32[]{:S(2)}) collective-permute-start(f32[256,256]{1,0:T(8,128)S(1)} %slice.22), channel_id=1, source_target_pairs={{0,16},{8,0},{12,4}} | collective-permute-start | bytes 786440 | tf_op jit(solution)/shard_map/ppermute | solution.py:37
  2.6 3.5 %collective-permute-start.1 = (f32[256,256]{1,0:T(8,128)S(1)}, f32[256,256]{1,0:T(8,128)S(1)}, u32[]{:S(2)}, u32[]{:S(2)}) collective-permute-start(f32[256,256]{1,0:T(8,128)S(1)} %slice.22), channel_id=1, source_target_pairs={{0,20},{24,16}} | collective-permute-start | bytes 786440 | tf_op jit(solution)/shard_map/ppermute | solution.py:37
  3.2 3.6 %collective-permute-start.2 = (f32[256,256]{1,0:T(8,128)S(1)}, f32[256,256]{1,0:T(8,128)S(1)}, u32[]{:S(2)}, u32[]{:S(2)}) collective-permute-start(f32[256,256]{1,0:T(8,128)S(1)} %slice.22), channel_id=1, source_target_pairs={{0,4},{28,20}} | collective-permute-start | bytes 786440 | tf_op jit(solution)/shard_map/ppermute | solution.py:37
  4.0 3.6 %collective-permute-start.10 = (bf16[256,256]{1,0:T(8,128)(2,1)S(1)}, bf16[256,256]{1,0:T(8,128)(2,1)S(1)}, u32[]{:S(2)}, u32[]{:S(2)}) collective-permute-start(bf16[256,256]{1,0:T(8,128)(2,1)S(1)} %slice.28), channel_id=1, source_target_pairs={{0,20}} | collective-permute-start | bytes 393224 | tf_op jit(solution)/shard_map/ppermute | solution.py:37
  4.7 3.6 %collective-permute-start.8 = (bf16[256,256]{1,0:T(8,128)(2,1)S(1)}, bf16[256,256]{1,0:T(8,128)(2,1)S(1)}, u32[]{:S(2)}, u32[]{:S(2)}) collective-permute-start(bf16[256,256]{1,0:T(8,128)(2,1)S(1)} %slice.28), channel_id=1, source_target_pairs={{0,4}} | collective-permute-start | bytes 393224 | tf_op jit(solution)/shard_map/ppermute | solution.py:37
  5.4 3.6 %collective-permute-start.9 = (bf16[256,256]{1,0:T(8,128)(2,1)S(1)}, bf16[256,256]{1,0:T(8,128)(2,1)S(1)}, u32[]{:S(2)}, u32[]{:S(2)}) collective-permute-start(bf16[256,256]{1,0:T(8,128)(2,1)S(1)} %slice.28), channel_id=1, source_target_pairs={{0,16}} | collective-permute-start | bytes 393224 | tf_op jit(solution)/shard_map/ppermute | solution.py:37
  6.1 3.6 %collective-permute-start.12 = (bf16[256,512]{1,0:T(8,128)(2,1)S(1)}, bf16[256,512]{1,0:T(8,128)(2,1)S(1)}, u32[]{:S(2)}, u32[]{:S(2)}) collective-permute-start(bf16[256,512]{1,0:T(8,128)(2,1)S(1)} %broadcast_select_fusion.1), channel_id=1, source_target_pairs={{2,10},{18,26},{1,17},{3,19},{5,21},{7,23}} | collective-permute-start | bytes 786440 | tf_op jit(solution)/shard_map/ppermute | solution.py:37
  6.9 4.1 %collective-permute-start.4 = (bf16[256,256]{1,0:T(8,128)(2,1)S(1)}, bf16[256,256]{1,0:T(8,128)(2,1)S(1)}, u32[]{:S(2)}, u32[]{:S(2)}) collective-permute-start(bf16[256,256]{1,0:T(8,128)(2,1)S(1)} %get-tuple-element.78), channel_id=1, source_target_pairs={{0,8},{4,12},{16,24},{20,28}} | collective-permute-start | bytes 393224 | tf_op jit(solution)/shard_map/ppermute | solution.py:37
  7.6 3.5 %collective-permute-start.5 = (bf16[256,256]{1,0:T(8,128)(2,1)S(1)}, bf16[256,256]{1,0:T(8,128)(2,1)S(1)}, u32[]{:S(2)}, u32[]{:S(2)}) collective-permute-start(bf16[256,256]{1,0:T(8,128)(2,1)S(1)} %get-tuple-element.78), channel_id=1, source_target_pairs={{0,10},{4,14},{16,26},{20,30}} | collective-permute-start | bytes 393224 | tf_op jit(solution)/shard_map/ppermute | solution.py:37
  8.3 2.8 %collective-permute-start.3 = (bf16[256,256]{1,0:T(8,128)(2,1)S(1)}, bf16[256,256]{1,0:T(8,128)(2,1)S(1)}, u32[]{:S(2)}, u32[]{:S(2)}) collective-permute-start(bf16[256,256]{1,0:T(8,128)(2,1)S(1)} %get-tuple-element.77), channel_id=1, source_target_pairs={{16,18},{20,22},{4,6}} | collective-permute-start | bytes 393224 | tf_op jit(solution)/shard_map/ppermute | solution.py:37
  9.0 3.4 %collective-permute-start.11 = (bf16[256,256]{1,0:T(8,128)(2,1)S(1)}, bf16[256,256]{1,0:T(8,128)(2,1)S(1)}, u32[]{:S(2)}, u32[]{:S(2)}) collective-permute-start(bf16[256,256]{1,0:T(8,128)(2,1)S(1)} %select_select_fusion.2), channel_id=1, source_target_pairs={{0,8},{4,12},{16,24},{20,28}} | collective-permute-start | bytes 393224 | tf_op jit(solution)/shard_map/ppermute | solution.py:37
  9.7 18.2 %collective-permute-start.13 = (bf16[256,512]{1,0:T(8,128)(2,1)S(1)}, bf16[256,512]{1,0:T(8,128)(2,1)S(1)}, u32[]{:S(2)}, u32[]{:S(2)}) collective-permute-start(bf16[256,512]{1,0:T(8,128)(2,1)S(1)} %broadcast_select_fusion), channel_id=1, source_target_pairs={{2,6},{18,22},{10,14},{26,30},{1,9},{3,11},{5,13},{7,15},{17,25},{... | collective-permute-start | bytes 786440 | tf_op jit(solution)/shard_map/ppermute | solution.py:37
  11.1 16.8 %collective-permute-start.6 = (bf16[256,256]{1,0:T(8,128)(2,1)S(1)}, bf16[256,256]{1,0:T(8,128)(2,1)S(1)}, u32[]{:S(2)}, u32[]{:S(2)}) collective-permute-start(bf16[256,256]{1,0:T(8,128)(2,1)S(1)} %select_select_fusion.3), channel_id=1, source_target_pairs={{4,5},{6,7},{8,9},{10,11},{12,13},{14,15},{16,17},{18,19},{20,21},... | collective-permute-start | bytes 393224 | tf_op jit(solution)/shard_map/ppermute | solution.py:37
where the time goes:
time: 29.4 us; the launch traced here: 29 us
  waiting for transfers between devices  15.5 us (53%)
  starting transfers between devices  10.7 us (36%)
  other arithmetic  1.3 us (4%)
  matrix products  1.07 us (4%)
  between operations  0.36 us (1%)
    ppermute x14, waiting for transfers between devices, send(): return lax.ppermute(value, ('row', 'col'), flat)  15.5 us
    ppermute x14, starting transfers between devices, send(): return lax.ppermute(value, ('row', 'col'), flat)  10.7 us
    convert_element_type x1, other arithmetic, shards(): upper = matrix.astype(jnp.bfloat16)  1.15 us
    dot_general x1, matrix products, shards(): return matrix - jnp.dot(received, upper, preferred_element_type=jnp.float32)  1.07 us
  transfers between devices with their start and end apart: 14, of which 1 were waited for; matrix products, arithmetic and copies ran while one was open for 1% of the time, Pallas kernels for 0%

commit v1 on v0

--- a/solution.py
+++ b/solution.py
@@ -69,10 +69,9 @@
         square = jnp.where(row_here == target, got, square)
         for r in served:
             partner = jnp.where(row_here == r, got, partner)
-    for target in reversed(workers[1:]):
+    for target in workers[1:]:
         got = send(column_upper, [((0, 0), (target, 0))])
         near_upper = jnp.where(row_here == target, got, near_upper)
-    upper = upper_step(upper, 1)
 
     def compute(square, partner):
         both = multipliers(square, jnp.concatenate([pivot_columns, partner], axis=0))
@@ -97,7 +96,8 @@
     near_sent, _ = lax.optimization_barrier((near_upper, lower))
     got = send(near_sent, [((r, 0), (r + APART, 0)) for r in workers])
     near_upper = jnp.where(row_here & APART == 0, near_upper, got)
-    for step in range(2, len(down)):
+    upper, _ = lax.optimization_barrier((upper, lower))
+    for step in range(1, len(down)):
         upper = upper_step(upper, step)
     got = send(
         received, [((r, c), (r, c + 1)) for r in range(1, n_row) for c in range(0, n_col, 2)]

time: 29.4 us -> 30 us (1.020)
  the two profiles are of different devices: /device:TPU:13 before, /device:TPU:29 now
where the time goes in v1:
time: 30 us; the launch traced here: 29.7 us
  waiting for transfers between devices  16.2 us (54%)
  starting transfers between devices  10.7 us (36%)
  other arithmetic  1.31 us (4%)
  matrix products  1.08 us (4%)
  between operations  0.38 us (1%)
    ppermute x14, waiting for transfers between devices, send(): return lax.ppermute(value, ('row', 'col'), flat)  16.2 us
    ppermute x14, starting transfers between devices, send(): return lax.ppermute(value, ('row', 'col'), flat)  10.7 us
    convert_element_type x1, other arithmetic, shards(): upper = matrix.astype(jnp.bfloat16)  1.15 us
    dot_general x1, matrix products, shards(): return matrix - jnp.dot(received, upper, preferred_element_type=jnp.float32)  1.08 us
  transfers between devices with their start and end apart: 14, of which 1 were waited for; matrix products, arithmetic and copies ran while one was open for 1% of the time, Pallas kernels for 0%

profile of v1, /device:TPU:29, one launch (start us, length us, event | category | flops | bytes accessed | tf_op | source)
XLA Modules:
  0.0 29.7 jit_solution(18193021633036570615)
XLA Ops:
  0.0 0.0 copy-start
  0.0 1.1 %convert_element_type.12 = bf16[256,512]{1,0:T(8,128)(2,1)S(1)} convert(f32[256,512]{1,0:T(8,128)} %param.3) | non-fusion elementwise | flops 131072 | bytes 786432 | tf_op jit(solution)/shard_map/convert_element_type | solution.py:39
  1.2 0.7 %collective-permute-start.7 = (bf16[256,512]{1,0:T(8,128)(2,1)S(1)}, bf16[256,512]{1,0:T(8,128)(2,1)S(1)}, u32[]{:S(2)}, u32[]{:S(2)}) collective-permute-start(bf16[256,512]{1,0:T(8,128)(2,1)S(1)} %convert_element_type.12), channel_id=1, source_target_pairs={{2,18},{1,5},{3,7}} | collective-permute-start | bytes 786440 | tf_op jit(solution)/shard_map/ppermute | solution.py:37
  1.8 0.0 copy-done
  1.9 0.7 %collective-permute-start = (f32[256,256]{1,0:T(8,128)S(1)}, f32[256,256]{1,0:T(8,128)S(1)}, u32[]{:S(2)}, u32[]{:S(2)}) collective-permute-start(f32[256,256]{1,0:T(8,128)S(1)} %slice.22), channel_id=1, source_target_pairs={{0,16},{8,0},{12,4}} | collective-permute-start | bytes 786440 | tf_op jit(solution)/shard_map/ppermute | solution.py:37
  2.6 0.7 %collective-permute-start.1 = (f32[256,256]{1,0:T(8,128)S(1)}, f32[256,256]{1,0:T(8,128)S(1)}, u32[]{:S(2)}, u32[]{:S(2)}) collective-permute-start(f32[256,256]{1,0:T(8,128)S(1)} %slice.22), channel_id=1, source_target_pairs={{0,20},{24,16}} | collective-permute-start | bytes 786440 | tf_op jit(solution)/shard_map/ppermute | solution.py:37
  3.2 0.7 %collective-permute-start.2 = (f32[256,256]{1,0:T(8,128)S(1)}, f32[256,256]{1,0:T(8,128)S(1)}, u32[]{:S(2)}, u32[]{:S(2)}) collective-permute-start(f32[256,256]{1,0:T(8,128)S(1)} %slice.22), channel_id=1, source_target_pairs={{0,4},{28,20}} | collective-permute-start | bytes 786440 | tf_op jit(solution)/shard_map/ppermute | solution.py:37
  4.0 0.0 collective-permute-done.7
  4.0 0.7 %collective-permute-start.10 = (bf16[256,256]{1,0:T(8,128)(2,1)S(1)}, bf16[256,256]{1,0:T(8,128)(2,1)S(1)}, u32[]{:S(2)}, u32[]{:S(2)}) collective-permute-start(bf16[256,256]{1,0:T(8,128)(2,1)S(1)} %slice.28), channel_id=1, source_target_pairs={{0,4}} | collective-permute-start | bytes 393224 | tf_op jit(solution)/shard_map/ppermute | solution.py:37
  4.7 0.7 %collective-permute-start.8 = (bf16[256,256]{1,0:T(8,128)(2,1)S(1)}, bf16[256,256]{1,0:T(8,128)(2,1)S(1)}, u32[]{:S(2)}, u32[]{:S(2)}) collective-permute-start(bf16[256,256]{1,0:T(8,128)(2,1)S(1)} %slice.28), channel_id=1, source_target_pairs={{0,20}} | collective-permute-start | bytes 393224 | tf_op jit(solution)/shard_map/ppermute | solution.py:37
  5.4 0.0 collective-permute-done
  5.4 0.7 %collective-permute-start.9 = (bf16[256,256]{1,0:T(8,128)(2,1)S(1)}, bf16[256,256]{1,0:T(8,128)(2,1)S(1)}, u32[]{:S(2)}, u32[]{:S(2)}) collective-permute-start(bf16[256,256]{1,0:T(8,128)(2,1)S(1)} %slice.28), channel_id=1, source_target_pairs={{0,16}} | collective-permute-start | bytes 393224 | tf_op jit(solution)/shard_map/ppermute | solution.py:37
  6.1 0.0 collective-permute-done.1
  6.1 0.0 collective-permute-done.2
  6.2 0.1 conditional.1
  6.2 0.7 %collective-permute-start.12 = (bf16[256,512]{1,0:T(8,128)(2,1)S(1)}, bf16[256,512]{1,0:T(8,128)(2,1)S(1)}, u32[]{:S(2)}, u32[]{:S(2)}) collective-permute-start(bf16[256,512]{1,0:T(8,128)(2,1)S(1)} %broadcast_select_fusion.1), channel_id=1, source_target_pairs={{2,10},{18,26},{1,17},{3,19},{5,21},{7,23}} | collective-permute-start | bytes 786440 | tf_op jit(solution)/shard_map/ppermute | solution.py:37
  6.9 0.7 %collective-permute-start.3 = (bf16[256,256]{1,0:T(8,128)(2,1)S(1)}, bf16[256,256]{1,0:T(8,128)(2,1)S(1)}, u32[]{:S(2)}, u32[]{:S(2)}) collective-permute-start(bf16[256,256]{1,0:T(8,128)(2,1)S(1)} %get-tuple-element.78), channel_id=1, source_target_pairs={{16,18},{20,22},{4,6}} | collective-permute-start | bytes 393224 | tf_op jit(solution)/shard_map/ppermute | solution.py:37
  7.6 0.0 collective-permute-done.10
  7.6 0.7 %collective-permute-start.4 = (bf16[256,256]{1,0:T(8,128)(2,1)S(1)}, bf16[256,256]{1,0:T(8,128)(2,1)S(1)}, u32[]{:S(2)}, u32[]{:S(2)}) collective-permute-start(bf16[256,256]{1,0:T(8,128)(2,1)S(1)} %get-tuple-element.79), channel_id=1, source_target_pairs={{0,8},{4,12},{16,24},{20,28}} | collective-permute-start | bytes 393224 | tf_op jit(solution)/shard_map/ppermute | solution.py:37
  8.3 0.0 collective-permute-done.8
  8.3 0.7 %collective-permute-start.5 = (bf16[256,256]{1,0:T(8,128)(2,1)S(1)}, bf16[256,256]{1,0:T(8,128)(2,1)S(1)}, u32[]{:S(2)}, u32[]{:S(2)}) collective-permute-start(bf16[256,256]{1,0:T(8,128)(2,1)S(1)} %get-tuple-element.79), channel_id=1, source_target_pairs={{0,10},{4,14},{16,26},{20,30}} | collective-permute-start | bytes 393224 | tf_op jit(solution)/shard_map/ppermute | solution.py:37
  9.0 0.0 collective-permute-done.9
  9.0 0.7 %collective-permute-start.11 = (bf16[256,256]{1,0:T(8,128)(2,1)S(1)}, bf16[256,256]{1,0:T(8,128)(2,1)S(1)}, u32[]{:S(2)}, u32[]{:S(2)}) collective-permute-start(bf16[256,256]{1,0:T(8,128)(2,1)S(1)} %select_select_fusion.2), channel_id=1, source_target_pairs={{0,8},{4,12},{16,24},{20,28}} | collective-permute-start | bytes 393224 | tf_op jit(solution)/shard_map/ppermute | solution.py:37
  9.7 0.0 collective-permute-done.12
  9.8 1.3 %collective-permute-start.13 = (bf16[256,512]{1,0:T(8,128)(2,1)S(1)}, bf16[256,512]{1,0:T(8,128)(2,1)S(1)}, u32[]{:S(2)}, u32[]{:S(2)}) collective-permute-start(bf16[256,512]{1,0:T(8,128)(2,1)S(1)} %broadcast_select_fusion), channel_id=1, source_target_pairs={{2,6},{18,22},{10,14},{26,30},{1,9},{3,11},{5,13},{7,15},{17,25},{... | collective-permute-start | bytes 786440 | tf_op jit(solution)/shard_map/ppermute | solution.py:37
  11.1 0.0 collective-permute-done.3
  11.1 0.0 collective-permute-done.4
  11.1 0.0 collective-permute-done.5
  11.1 1.3 %collective-permute-start.6 = (bf16[256,256]{1,0:T(8,128)(2,1)S(1)}, bf16[256,256]{1,0:T(8,128)(2,1)S(1)}, u32[]{:S(2)}, u32[]{:S(2)}) collective-permute-start(bf16[256,256]{1,0:T(8,128)(2,1)S(1)} %select_select_fusion.3), channel_id=1, source_target_pairs={{4,5},{6,7},{8,9},{10,11},{12,13},{14,15},{16,17},{18,19},{20,21},... | collective-permute-start | bytes 393224 | tf_op jit(solution)/shard_map/ppermute | solution.py:37
  12.4 0.0 collective-permute-done.11
  12.5 16.1 %collective-permute-done.6 = bf16[256,256]{1,0:T(8,128)(2,1)S(1)} collective-permute-done((bf16[256,256]{1,0:T(8,128)(2,1)S(1)}, bf16[256,256]{1,0:T(8,128)(2,1)S(1)}, u32[]{:S(2)}, u32[]{:S(2)}) %collective-permute-start.6) | collective-permute-done | bytes 131104 | tf_op jit(solution)/shard_map/ppermute | solution.py:37
  28.6 0.0 collective-permute-done.13
  28.6 1.1 %convolution_subtract_fusion = f32[256,512]{1,0:T(8,128)} fusion(f32[256,512]{1,0:T(8,128)S(1)} %copy-done, bf16[256,512]{1,0:T(8,128)(2,1)S(1)} %collective-permute-done.13, bf16[256,512]{1,0:T(8,128)(2,1)S(1)} %broadcast_select_fusion, bf16[256,256]{1,0:T(8,128)(2,1)S(1)} %broadcast_select_fusion.2, pred[]{:T(512)S(6)} %select_n.184, pred[]{:T(512)S(6)} %eq.74, ...), kind=kOutput, calls=%fused_computation.34 | convolution fusion | flops 67633152 | bytes 1966084 | tf_op jit(solution)/shard_map/dot_general | solution.py:110
  (10 shorter events, 0.2 us)
Async XLA Ops:
  0.0 1.8 %copy-start = (f32[256,512]{1,0:T(8,128)S(1)}, f32[256,512]{1,0:T(8,128)}, u32[]{:S(2)}) copy-start(f32[256,512]{1,0:T(8,128)} %param.3) | copy-start | bytes 1572868
  1.2 2.8 %collective-permute-start.7 = (bf16[256,512]{1,0:T(8,128)(2,1)S(1)}, bf16[256,512]{1,0:T(8,128)(2,1)S(1)}, u32[]{:S(2)}, u32[]{:S(2)}) collective-permute-start(bf16[256,512]{1,0:T(8,128)(2,1)S(1)} %convert_element_type.12), channel_id=1, source_target_pairs={{2,18},{1,5},{3,7}} | collective-permute-start | bytes 786440 | tf_op jit(solution)/shard_map/ppermute | solution.py:37
  1.9 3.5 %collective-permute-start = (f32[256,256]{1,0:T(8,128)S(1)}, f32[256,256]{1,0:T(8,128)S(1)}, u32[]{:S(2)}, u32[]{:S(2)}) collective-permute-start(f32[256,256]{1,0:T(8,128)S(1)} %slice.22), channel_id=1, source_target_pairs={{0,16},{8,0},{12,4}} | collective-permute-start | bytes 786440 | tf_op jit(solution)/shard_map/ppermute | solution.py:37
  2.6 3.5 %collective-permute-start.1 = (f32[256,256]{1,0:T(8,128)S(1)}, f32[256,256]{1,0:T(8,128)S(1)}, u32[]{:S(2)}, u32[]{:S(2)}) collective-permute-start(f32[256,256]{1,0:T(8,128)S(1)} %slice.22), channel_id=1, source_target_pairs={{0,20},{24,16}} | collective-permute-start | bytes 786440 | tf_op jit(solution)/shard_map/ppermute | solution.py:37
  3.2 2.9 %collective-permute-start.2 = (f32[256,256]{1,0:T(8,128)S(1)}, f32[256,256]{1,0:T(8,128)S(1)}, u32[]{:S(2)}, u32[]{:S(2)}) collective-permute-start(f32[256,256]{1,0:T(8,128)S(1)} %slice.22), channel_id=1, source_target_pairs={{0,4},{28,20}} | collective-permute-start | bytes 786440 | tf_op jit(solution)/shard_map/ppermute | solution.py:37
  4.0 3.6 %collective-permute-start.10 = (bf16[256,256]{1,0:T(8,128)(2,1)S(1)}, bf16[256,256]{1,0:T(8,128)(2,1)S(1)}, u32[]{:S(2)}, u32[]{:S(2)}) collective-permute-start(bf16[256,256]{1,0:T(8,128)(2,1)S(1)} %slice.28), channel_id=1, source_target_pairs={{0,4}} | collective-permute-start | bytes 393224 | tf_op jit(solution)/shard_map/ppermute | solution.py:37
  4.7 3.6 %collective-permute-start.8 = (bf16[256,256]{1,0:T(8,128)(2,1)S(1)}, bf16[256,256]{1,0:T(8,128)(2,1)S(1)}, u32[]{:S(2)}, u32[]{:S(2)}) collective-permute-start(bf16[256,256]{1,0:T(8,128)(2,1)S(1)} %slice.28), channel_id=1, source_target_pairs={{0,20}} | collective-permute-start | bytes 393224 | tf_op jit(solution)/shard_map/ppermute | solution.py:37
  5.4 3.6 %collective-permute-start.9 = (bf16[256,256]{1,0:T(8,128)(2,1)S(1)}, bf16[256,256]{1,0:T(8,128)(2,1)S(1)}, u32[]{:S(2)}, u32[]{:S(2)}) collective-permute-start(bf16[256,256]{1,0:T(8,128)(2,1)S(1)} %slice.28), channel_id=1, source_target_pairs={{0,16}} | collective-permute-start | bytes 393224 | tf_op jit(solution)/shard_map/ppermute | solution.py:37
  6.2 3.5 %collective-permute-start.12 = (bf16[256,512]{1,0:T(8,128)(2,1)S(1)}, bf16[256,512]{1,0:T(8,128)(2,1)S(1)}, u32[]{:S(2)}, u32[]{:S(2)}) collective-permute-start(bf16[256,512]{1,0:T(8,128)(2,1)S(1)} %broadcast_select_fusion.1), channel_id=1, source_target_pairs={{2,10},{18,26},{1,17},{3,19},{5,21},{7,23}} | collective-permute-start | bytes 786440 | tf_op jit(solution)/shard_map/ppermute | solution.py:37
  6.9 4.1 %collective-permute-start.3 = (bf16[256,256]{1,0:T(8,128)(2,1)S(1)}, bf16[256,256]{1,0:T(8,128)(2,1)S(1)}, u32[]{:S(2)}, u32[]{:S(2)}) collective-permute-start(bf16[256,256]{1,0:T(8,128)(2,1)S(1)} %get-tuple-element.78), channel_id=1, source_target_pairs={{16,18},{20,22},{4,6}} | collective-permute-start | bytes 393224 | tf_op jit(solution)/shard_map/ppermute | solution.py:37
  7.6 3.5 %collective-permute-start.4 = (bf16[256,256]{1,0:T(8,128)(2,1)S(1)}, bf16[256,256]{1,0:T(8,128)(2,1)S(1)}, u32[]{:S(2)}, u32[]{:S(2)}) collective-permute-start(bf16[256,256]{1,0:T(8,128)(2,1)S(1)} %get-tuple-element.79), channel_id=1, source_target_pairs={{0,8},{4,12},{16,24},{20,28}} | collective-permute-start | bytes 393224 | tf_op jit(solution)/shard_map/ppermute | solution.py:37
  8.3 2.8 %collective-permute-start.5 = (bf16[256,256]{1,0:T(8,128)(2,1)S(1)}, bf16[256,256]{1,0:T(8,128)(2,1)S(1)}, u32[]{:S(2)}, u32[]{:S(2)}) collective-permute-start(bf16[256,256]{1,0:T(8,128)(2,1)S(1)} %get-tuple-element.79), channel_id=1, source_target_pairs={{0,10},{4,14},{16,26},{20,30}} | collective-permute-start | bytes 393224 | tf_op jit(solution)/shard_map/ppermute | solution.py:37
  9.0 3.4 %collective-permute-start.11 = (bf16[256,256]{1,0:T(8,128)(2,1)S(1)}, bf16[256,256]{1,0:T(8,128)(2,1)S(1)}, u32[]{:S(2)}, u32[]{:S(2)}) collective-permute-start(bf16[256,256]{1,0:T(8,128)(2,1)S(1)} %select_select_fusion.2), channel_id=1, source_target_pairs={{0,8},{4,12},{16,24},{20,28}} | collective-permute-start | bytes 393224 | tf_op jit(solution)/shard_map/ppermute | solution.py:37
  9.8 18.8 %collective-permute-start.13 = (bf16[256,512]{1,0:T(8,128)(2,1)S(1)}, bf16[256,512]{1,0:T(8,128)(2,1)S(1)}, u32[]{:S(2)}, u32[]{:S(2)}) collective-permute-start(bf16[256,512]{1,0:T(8,128)(2,1)S(1)} %broadcast_select_fusion), channel_id=1, source_target_pairs={{2,6},{18,22},{10,14},{26,30},{1,9},{3,11},{5,13},{7,15},{17,25},{... | collective-permute-start | bytes 786440 | tf_op jit(solution)/shard_map/ppermute | solution.py:37
  11.1 17.4 %collective-permute-start.6 = (bf16[256,256]{1,0:T(8,128)(2,1)S(1)}, bf16[256,256]{1,0:T(8,128)(2,1)S(1)}, u32[]{:S(2)}, u32[]{:S(2)}) collective-permute-start(bf16[256,256]{1,0:T(8,128)(2,1)S(1)} %select_select_fusion.3), channel_id=1, source_target_pairs={{4,5},{6,7},{8,9},{10,11},{12,13},{14,15},{16,17},{18,19},{20,21},... | collective-permute-start | bytes 393224 | tf_op jit(solution)/shard_map/ppermute | solution.py:37

commit v2 on v0

--- a/solution.py
+++ b/solution.py
@@ -36,8 +36,17 @@
         flat = [(r0 * n_col + c0, r1 * n_col + c1) for (r0, c0), (r1, c1) in pairs]
         return lax.ppermute(value, ("row", "col"), flat)
 
-    upper = matrix.astype(jnp.bfloat16)
-    pivot_columns, column_upper = matrix[:, :NB], upper[:, NB:]
+    def blocks(matrix):
+        return matrix[:, :NB], matrix.astype(jnp.bfloat16)
+
+    def no_blocks(matrix):
+        return jnp.zeros((NB, NB), matrix.dtype), jnp.zeros(matrix.shape, jnp.bfloat16)
+
+    sends_columns = (col_here == 0) & (row_here & APART != 0)
+    pivot_columns, upper = lax.cond(
+        sends_columns | (row_here == 0), blocks, no_blocks, matrix
+    )
+    column_upper = upper[:, NB:]
 
     down = strides(n_row)
     orders = [down, [down[-1]] + down[:-1]]
@@ -58,11 +67,11 @@
         return jnp.where(jnp.where(col_here % 2 == 0, takes[0], takes[1]), got, value)
 
     workers = [r for r in range(n_row) if r & APART == 0]
-    targets = workers[2:] + workers[1:2]
+    targets = workers[1:]
     square, partner = pivot_columns, pivot_columns
     near_upper = column_upper
     upper, column_upper = lax.optimization_barrier((upper_step(upper, 0), column_upper))
-    for index, target in enumerate(targets):
+    for index, target in reversed(list(enumerate(targets))):
         served = [0, targets[-1]] if index == 0 else [targets[index - 1]]
         pairs = [((0, 0), (target, 0))] + [((r + APART, 0), (r, 0)) for r in served]
         got = send(pivot_columns, pairs)
@@ -75,7 +84,7 @@
     upper = upper_step(upper, 1)
 
     def compute(square, partner):
-        both = multipliers(square, jnp.concatenate([pivot_columns, partner], axis=0))
+        both = multipliers(square, jnp.concatenate([matrix[:, :NB], partner], axis=0))
         both = both.astype(jnp.bfloat16)
         return both[:NB], both[NB:]
 

time: 29.4 us -> 28.6 us (0.973)
  the two profiles are of different devices: /device:TPU:13 before, /device:TPU:1 now
where the time goes in v2:
time: 28.6 us; the launch traced here: 28.2 us
  starting transfers between devices  12.6 us (44%)
  waiting for transfers between devices  10.2 us (36%)
  other arithmetic  2.95 us (10%)
  matrix products  1.07 us (4%)
  local copies, waits for them, and re-layouts  1.06 us (4%)
  between operations  0.33 us (1%)
    ppermute x14, starting transfers between devices, send(): return lax.ppermute(value, ('row', 'col'), flat)  12.6 us
    ppermute x14, waiting for transfers between devices, send(): return lax.ppermute(value, ('row', 'col'), flat)  10.2 us
    convert_element_type x1, other arithmetic, blocks(): return (matrix[:, :NB], matrix.astype(jnp.bfloat16))  1.85 us
    dot_general x1, matrix products, shards(): return matrix - jnp.dot(received, upper, preferred_element_type=jnp.float32)  1.07 us
    select_n x2, other arithmetic, upper_step(): jnp.where(jnp.where(col_here % 2 == 0, takes[0], takes[1]), got, value)  1.01 us
    slice x1, local copies, waits for them, and re-layouts, shards(): column_upper = upper[:, NB:]  0.91 us
  transfers between devices with their start and end apart: 14, of which 3 were waited for; matrix products, arithmetic and copies ran while one was open for 4% of the time, Pallas kernels for 0%

profile of v2, /device:TPU:1, one launch (start us, length us, event | category | flops | bytes accessed | tf_op | source)
XLA Modules:
  0.0 28.2 jit_solution(13773625299538875612)
XLA Ops:
  0.0 2.8 %conditional.2 = (f32[256,256]{1,0:T(8,128)S(1)}, bf16[256,512]{1,0:T(8,128)(2,1)}, bf16[256,256]{1,0:T(8,128)(2,1)S(1)}) conditional(s32[]{:T(128)} %convert_element_type.14, () %tuple.26, f32[256,512]{1,0:T(8,128)} %param.5), branch_computations={%region_0.0_spmd, %region_1.0_spmd} | conditional | flops 131072 | bytes 3670068 | solution.py:46
  0.0 0.0 copy-start.1
  0.0 1.8 %convert_element_type.4 = bf16[256,512]{1,0:T(8,128)(2,1)} convert(f32[256,512]{1,0:T(8,128)} %param.1) | non-fusion elementwise | flops 131072 | bytes 786432 | tf_op jit(solution)/shard_map/cond/branch_1_fun/convert_element_type | solution.py:40
  1.9 0.9 %slice.30 = bf16[256,256]{1,0:T(8,128)(2,1)S(1)} slice(bf16[256,512]{1,0:T(8,128)(2,1)} %convert_element_type.4), slice={[0:256], [256:512]} | slice | bytes 262144 | tf_op jit(solution)/shard_map/slice | solution.py:49
  2.8 0.0 copy-done.1
  2.8 1.9 %collective-permute-start.7 = (bf16[256,512]{1,0:T(8,128)(2,1)}, bf16[256,512]{1,0:T(8,128)(2,1)S(1)}, u32[]{:S(2)}, u32[]{:S(2)}) collective-permute-start(bf16[256,512]{1,0:T(8,128)(2,1)} %get-tuple-element.27), channel_id=1, source_target_pairs={{2,18},{1,5},{3,7}} | collective-permute-start | bytes 786440 | tf_op jit(solution)/shard_map/ppermute | solution.py:37
  4.7 0.7 %collective-permute-start = (f32[256,256]{1,0:T(8,128)S(1)}, f32[256,256]{1,0:T(8,128)S(1)}, u32[]{:S(2)}, u32[]{:S(2)}) collective-permute-start(f32[256,256]{1,0:T(8,128)S(1)} %get-tuple-element.80), channel_id=1, source_target_pairs={{0,4},{8,0},{28,20}} | collective-permute-start | bytes 786440 | tf_op jit(solution)/shard_map/ppermute | solution.py:37
  5.4 0.7 %collective-permute-start.1 = (f32[256,256]{1,0:T(8,128)S(1)}, f32[256,256]{1,0:T(8,128)S(1)}, u32[]{:S(2)}, u32[]{:S(2)}) collective-permute-start(f32[256,256]{1,0:T(8,128)S(1)} %get-tuple-element.80), channel_id=1, source_target_pairs={{0,16},{12,4}} | collective-permute-start | bytes 786440 | tf_op jit(solution)/shard_map/ppermute | solution.py:37
  6.1 0.7 %collective-permute-start.2 = (f32[256,256]{1,0:T(8,128)S(1)}, f32[256,256]{1,0:T(8,128)S(1)}, u32[]{:S(2)}, u32[]{:S(2)}) collective-permute-start(f32[256,256]{1,0:T(8,128)S(1)} %get-tuple-element.80), channel_id=1, source_target_pairs={{0,20},{24,16}} | collective-permute-start | bytes 786440 | tf_op jit(solution)/shard_map/ppermute | solution.py:37
  6.8 0.0 copy-start
  6.8 2.6 %collective-permute-done.7 = bf16[256,512]{1,0:T(8,128)(2,1)S(1)} collective-permute-done((bf16[256,512]{1,0:T(8,128)(2,1)}, bf16[256,512]{1,0:T(8,128)(2,1)S(1)}, u32[]{:S(2)}, u32[]{:S(2)}) %collective-permute-start.7) | collective-permute-done | bytes 262176 | tf_op jit(solution)/shard_map/ppermute | solution.py:37
  9.5 1.0 %broadcast_select_fusion.1 = bf16[256,512]{1,0:T(8,128)(2,1)S(1)} fusion(bf16[256,512]{1,0:T(8,128)(2,1)S(1)} %collective-permute-done.7, bf16[256,512]{1,0:T(8,128)(2,1)} %get-tuple-element.27, pred[]{:T(512)S(6)} %select_n.158), kind=kLoop, calls=%fused_computation.40 | loop fusion | flops 131072 | bytes 786433 | tf_op jit(solution)/shard_map/jit(_where)/select_n | solution.py:67
  10.4 0.7 %collective-permute-start.10 = (bf16[256,256]{1,0:T(8,128)(2,1)S(1)}, bf16[256,256]{1,0:T(8,128)(2,1)S(1)}, u32[]{:S(2)}, u32[]{:S(2)}) collective-permute-start(bf16[256,256]{1,0:T(8,128)(2,1)S(1)} %get-tuple-element.29), channel_id=1, source_target_pairs={{0,20}} | collective-permute-start | bytes 393224 | tf_op jit(solution)/shard_map/ppermute | solution.py:37
  11.1 0.7 %collective-permute-start.8 = (bf16[256,256]{1,0:T(8,128)(2,1)S(1)}, bf16[256,256]{1,0:T(8,128)(2,1)S(1)}, u32[]{:S(2)}, u32[]{:S(2)}) collective-permute-start(bf16[256,256]{1,0:T(8,128)(2,1)S(1)} %get-tuple-element.29), channel_id=1, source_target_pairs={{0,4}} | collective-permute-start | bytes 393224 | tf_op jit(solution)/shard_map/ppermute | solution.py:37
  11.8 0.0 collective-permute-done
  11.8 1.3 %collective-permute-start.9 = (bf16[256,256]{1,0:T(8,128)(2,1)S(1)}, bf16[256,256]{1,0:T(8,128)(2,1)}, u32[]{:S(2)}, u32[]{:S(2)}) collective-permute-start(bf16[256,256]{1,0:T(8,128)(2,1)S(1)} %get-tuple-element.29), channel_id=1, source_target_pairs={{0,16}} | collective-permute-start | bytes 393224 | tf_op jit(solution)/shard_map/ppermute | solution.py:37
  13.1 0.0 collective-permute-done.1
  13.1 1.3 %collective-permute-start.12 = (bf16[256,512]{1,0:T(8,128)(2,1)S(1)}, bf16[256,512]{1,0:T(8,128)(2,1)S(1)}, u32[]{:S(2)}, u32[]{:S(2)}) collective-permute-start(bf16[256,512]{1,0:T(8,128)(2,1)S(1)} %broadcast_select_fusion.1), channel_id=1, source_target_pairs={{2,10},{18,26},{1,17},{3,19},{5,21},{7,23}} | collective-permute-start | bytes 786440 | tf_op jit(solution)/shard_map/ppermute | solution.py:37
  14.5 0.0 collective-permute-done.2
  14.6 0.0 copy-done
  14.6 0.1 conditional.3
  14.7 0.7 %collective-permute-start.4 = (bf16[256,256]{1,0:T(8,128)(2,1)S(1)}, bf16[256,256]{1,0:T(8,128)(2,1)S(1)}, u32[]{:S(2)}, u32[]{:S(2)}) collective-permute-start(bf16[256,256]{1,0:T(8,128)(2,1)S(1)} %get-tuple-element.26), channel_id=1, source_target_pairs={{0,8},{4,12},{16,24},{20,28}} | collective-permute-start | bytes 393224 | tf_op jit(solution)/shard_map/ppermute | solution.py:37
  15.4 0.0 collective-permute-done.10
  15.4 0.7 %collective-permute-start.5 = (bf16[256,256]{1,0:T(8,128)(2,1)S(1)}, bf16[256,256]{1,0:T(8,128)(2,1)S(1)}, u32[]{:S(2)}, u32[]{:S(2)}) collective-permute-start(bf16[256,256]{1,0:T(8,128)(2,1)S(1)} %get-tuple-element.26), channel_id=1, source_target_pairs={{0,10},{4,14},{16,26},{20,30}} | collective-permute-start | bytes 393224 | tf_op jit(solution)/shard_map/ppermute | solution.py:37
  16.0 0.0 collective-permute-done.8
  16.1 0.7 %collective-permute-start.3 = (bf16[256,256]{1,0:T(8,128)(2,1)S(1)}, bf16[256,256]{1,0:T(8,128)(2,1)S(1)}, u32[]{:S(2)}, u32[]{:S(2)}) collective-permute-start(bf16[256,256]{1,0:T(8,128)(2,1)S(1)} %get-tuple-element.25), channel_id=1, source_target_pairs={{4,6},{16,18},{20,22}} | collective-permute-start | bytes 393224 | tf_op jit(solution)/shard_map/ppermute | solution.py:37
  16.7 0.0 collective-permute-done.9
  16.8 0.7 %collective-permute-start.11 = (bf16[256,256]{1,0:T(8,128)(2,1)S(1)}, bf16[256,256]{1,0:T(8,128)(2,1)S(1)}, u32[]{:S(2)}, u32[]{:S(2)}) collective-permute-start(bf16[256,256]{1,0:T(8,128)(2,1)S(1)} %select_select_fusion.3), channel_id=1, source_target_pairs={{0,8},{4,12},{16,24},{20,28}} | collective-permute-start | bytes 393224 | tf_op jit(solution)/shard_map/ppermute | solution.py:37
  17.5 2.6 %collective-permute-done.12 = bf16[256,512]{1,0:T(8,128)(2,1)S(1)} collective-permute-done((bf16[256,512]{1,0:T(8,128)(2,1)S(1)}, bf16[256,512]{1,0:T(8,128)(2,1)S(1)}, u32[]{:S(2)}, u32[]{:S(2)}) %collective-permute-start.12) | collective-permute-done | bytes 262176 | tf_op jit(solution)/shard_map/ppermute | solution.py:37
  20.1 1.3 %collective-permute-start.13 = (bf16[256,512]{1,0:T(8,128)(2,1)S(1)}, bf16[256,512]{1,0:T(8,128)(2,1)S(1)}, u32[]{:S(2)}, u32[]{:S(2)}) collective-permute-start(bf16[256,512]{1,0:T(8,128)(2,1)S(1)} %broadcast_select_fusion), channel_id=1, source_target_pairs={{2,6},{18,22},{10,14},{26,30},{1,9},{3,11},{5,13},{7,15},{17,25},{... | collective-permute-start | bytes 786440 | tf_op jit(solution)/shard_map/ppermute | solution.py:37
  21.4 0.0 collective-permute-done.3
  21.4 0.0 collective-permute-done.4
  21.4 0.0 collective-permute-done.5
  21.5 0.7 %collective-permute-start.6 = (bf16[256,256]{1,0:T(8,128)(2,1)S(1)}, bf16[256,256]{1,0:T(8,128)(2,1)S(1)}, u32[]{:S(2)}, u32[]{:S(2)}) collective-permute-start(bf16[256,256]{1,0:T(8,128)(2,1)S(1)} %select_select_fusion.4), channel_id=1, source_target_pairs={{4,5},{6,7},{8,9},{10,11},{12,13},{14,15},{16,17},{18,19},{20,21},... | collective-permute-start | bytes 393224 | tf_op jit(solution)/shard_map/ppermute | solution.py:37
  22.1 0.0 collective-permute-done.11
  22.2 0.0 collective-permute-done.6
  22.2 5.0 %collective-permute-done.13 = bf16[256,512]{1,0:T(8,128)(2,1)S(1)} collective-permute-done((bf16[256,512]{1,0:T(8,128)(2,1)S(1)}, bf16[256,512]{1,0:T(8,128)(2,1)S(1)}, u32[]{:S(2)}, u32[]{:S(2)}) %collective-permute-start.13) | collective-permute-done | bytes 262176 | tf_op jit(solution)/shard_map/ppermute | solution.py:37
  27.2 1.1 %convolution_subtract_fusion = f32[256,512]{1,0:T(8,128)} fusion(f32[256,512]{1,0:T(8,128)S(1)} %copy-done, bf16[256,512]{1,0:T(8,128)(2,1)S(1)} %collective-permute-done.13, bf16[256,512]{1,0:T(8,128)(2,1)S(1)} %broadcast_select_fusion, bf16[256,256]{1,0:T(8,128)(2,1)S(1)} %broadcast_select_fusion.2, pred[]{:T(512)S(6)} %select_n.165, pred[]{:T(512)S(6)} %eq.75, ...), kind=kOutput, calls=%fused_computation.34 | convolution fusion | flops 67633152 | bytes 1966084 | tf_op jit(solution)/shard_map/dot_general | solution.py:119
  (11 shorter events, 0.3 us)
Async XLA Ops:
  0.0 2.8 %copy-start.1 = (f32[256,512]{1,0:T(8,128)S(1)}, f32[256,512]{1,0:T(8,128)}, u32[]{:S(2)}) copy-start(f32[256,512]{1,0:T(8,128)} %param.1) | copy-start | bytes 1572868 | tf_op jit(solution)/shard_map/cond
  2.8 6.7 %collective-permute-start.7 = (bf16[256,512]{1,0:T(8,128)(2,1)}, bf16[256,512]{1,0:T(8,128)(2,1)S(1)}, u32[]{:S(2)}, u32[]{:S(2)}) collective-permute-start(bf16[256,512]{1,0:T(8,128)(2,1)} %get-tuple-element.27), channel_id=1, source_target_pairs={{2,18},{1,5},{3,7}} | collective-permute-start | bytes 786440 | tf_op jit(solution)/shard_map/ppermute | solution.py:37
  4.7 7.1 %collective-permute-start = (f32[256,256]{1,0:T(8,128)S(1)}, f32[256,256]{1,0:T(8,128)S(1)}, u32[]{:S(2)}, u32[]{:S(2)}) collective-permute-start(f32[256,256]{1,0:T(8,128)S(1)} %get-tuple-element.80), channel_id=1, source_target_pairs={{0,4},{8,0},{28,20}} | collective-permute-start | bytes 786440 | tf_op jit(solution)/shard_map/ppermute | solution.py:37
  5.4 7.7 %collective-permute-start.1 = (f32[256,256]{1,0:T(8,128)S(1)}, f32[256,256]{1,0:T(8,128)S(1)}, u32[]{:S(2)}, u32[]{:S(2)}) collective-permute-start(f32[256,256]{1,0:T(8,128)S(1)} %get-tuple-element.80), channel_id=1, source_target_pairs={{0,16},{12,4}} | collective-permute-start | bytes 786440 | tf_op jit(solution)/shard_map/ppermute | solution.py:37
  6.1 8.4 %collective-permute-start.2 = (f32[256,256]{1,0:T(8,128)S(1)}, f32[256,256]{1,0:T(8,128)S(1)}, u32[]{:S(2)}, u32[]{:S(2)}) collective-permute-start(f32[256,256]{1,0:T(8,128)S(1)} %get-tuple-element.80), channel_id=1, source_target_pairs={{0,20},{24,16}} | collective-permute-start | bytes 786440 | tf_op jit(solution)/shard_map/ppermute | solution.py:37
  6.8 7.8 %copy-start = (f32[256,512]{1,0:T(8,128)S(1)}, f32[256,512]{1,0:T(8,128)}, u32[]{:S(2)}) copy-start(f32[256,512]{1,0:T(8,128)} %param.5) | copy-start | bytes 1572868
  10.4 4.9 %collective-permute-start.10 = (bf16[256,256]{1,0:T(8,128)(2,1)S(1)}, bf16[256,256]{1,0:T(8,128)(2,1)S(1)}, u32[]{:S(2)}, u32[]{:S(2)}) collective-permute-start(bf16[256,256]{1,0:T(8,128)(2,1)S(1)} %get-tuple-element.29), channel_id=1, source_target_pairs={{0,20}} | collective-permute-start | bytes 393224 | tf_op jit(solution)/shard_map/ppermute | solution.py:37
  11.1 4.9 %collective-permute-start.8 = (bf16[256,256]{1,0:T(8,128)(2,1)S(1)}, bf16[256,256]{1,0:T(8,128)(2,1)S(1)}, u32[]{:S(2)}, u32[]{:S(2)}) collective-permute-start(bf16[256,256]{1,0:T(8,128)(2,1)S(1)} %get-tuple-element.29), channel_id=1, source_target_pairs={{0,4}} | collective-permute-start | bytes 393224 | tf_op jit(solution)/shard_map/ppermute | solution.py:37
  11.8 4.9 %collective-permute-start.9 = (bf16[256,256]{1,0:T(8,128)(2,1)S(1)}, bf16[256,256]{1,0:T(8,128)(2,1)}, u32[]{:S(2)}, u32[]{:S(2)}) collective-permute-start(bf16[256,256]{1,0:T(8,128)(2,1)S(1)} %get-tuple-element.29), channel_id=1, source_target_pairs={{0,16}} | collective-permute-start | bytes 393224 | tf_op jit(solution)/shard_map/ppermute | solution.py:37
  13.1 6.9 %collective-permute-start.12 = (bf16[256,512]{1,0:T(8,128)(2,1)S(1)}, bf16[256,512]{1,0:T(8,128)(2,1)S(1)}, u32[]{:S(2)}, u32[]{:S(2)}) collective-permute-start(bf16[256,512]{1,0:T(8,128)(2,1)S(1)} %broadcast_select_fusion.1), channel_id=1, source_target_pairs={{2,10},{18,26},{1,17},{3,19},{5,21},{7,23}} | collective-permute-start | bytes 786440 | tf_op jit(solution)/shard_map/ppermute | solution.py:37
  14.7 6.7 %collective-permute-start.4 = (bf16[256,256]{1,0:T(8,128)(2,1)S(1)}, bf16[256,256]{1,0:T(8,128)(2,1)S(1)}, u32[]{:S(2)}, u32[]{:S(2)}) collective-permute-start(bf16[256,256]{1,0:T(8,128)(2,1)S(1)} %get-tuple-element.26), channel_id=1, source_target_pairs={{0,8},{4,12},{16,24},{20,28}} | collective-permute-start | bytes 393224 | tf_op jit(solution)/shard_map/ppermute | solution.py:37
  15.4 6.0 %collective-permute-start.5 = (bf16[256,256]{1,0:T(8,128)(2,1)S(1)}, bf16[256,256]{1,0:T(8,128)(2,1)S(1)}, u32[]{:S(2)}, u32[]{:S(2)}) collective-permute-start(bf16[256,256]{1,0:T(8,128)(2,1)S(1)} %get-tuple-element.26), channel_id=1, source_target_pairs={{0,10},{4,14},{16,26},{20,30}} | collective-permute-start | bytes 393224 | tf_op jit(solution)/shard_map/ppermute | solution.py:37
  16.1 5.3 %collective-permute-start.3 = (bf16[256,256]{1,0:T(8,128)(2,1)S(1)}, bf16[256,256]{1,0:T(8,128)(2,1)S(1)}, u32[]{:S(2)}, u32[]{:S(2)}) collective-permute-start(bf16[256,256]{1,0:T(8,128)(2,1)S(1)} %get-tuple-element.25), channel_id=1, source_target_pairs={{4,6},{16,18},{20,22}} | collective-permute-start | bytes 393224 | tf_op jit(solution)/shard_map/ppermute | solution.py:37
  16.8 5.4 %collective-permute-start.11 = (bf16[256,256]{1,0:T(8,128)(2,1)S(1)}, bf16[256,256]{1,0:T(8,128)(2,1)S(1)}, u32[]{:S(2)}, u32[]{:S(2)}) collective-permute-start(bf16[256,256]{1,0:T(8,128)(2,1)S(1)} %select_select_fusion.3), channel_id=1, source_target_pairs={{0,8},{4,12},{16,24},{20,28}} | collective-permute-start | bytes 393224 | tf_op jit(solution)/shard_map/ppermute | solution.py:37
  20.1 7.1 %collective-permute-start.13 = (bf16[256,512]{1,0:T(8,128)(2,1)S(1)}, bf16[256,512]{1,0:T(8,128)(2,1)S(1)}, u32[]{:S(2)}, u32[]{:S(2)}) collective-permute-start(bf16[256,512]{1,0:T(8,128)(2,1)S(1)} %broadcast_select_fusion), channel_id=1, source_target_pairs={{2,6},{18,22},{10,14},{26,30},{1,9},{3,11},{5,13},{7,15},{17,25},{... | collective-permute-start | bytes 786440 | tf_op jit(solution)/shard_map/ppermute | solution.py:37
  21.5 0.7 %collective-permute-start.6 = (bf16[256,256]{1,0:T(8,128)(2,1)S(1)}, bf16[256,256]{1,0:T(8,128)(2,1)S(1)}, u32[]{:S(2)}, u32[]{:S(2)}) collective-permute-start(bf16[256,256]{1,0:T(8,128)(2,1)S(1)} %select_select_fusion.4), channel_id=1, source_target_pairs={{4,5},{6,7},{8,9},{10,11},{12,13},{14,15},{16,17},{18,19},{20,21},... | collective-permute-start | bytes 393224 | tf_op jit(solution)/shard_map/ppermute | solution.py:37

commit v3 on v2

--- a/solution.py
+++ b/solution.py
@@ -43,16 +43,17 @@
         return jnp.zeros((NB, NB), matrix.dtype), jnp.zeros(matrix.shape, jnp.bfloat16)
 
     sends_columns = (col_here == 0) & (row_here & APART != 0)
-    pivot_columns, upper = lax.cond(
+    pivot_columns, first_upper = lax.cond(
         sends_columns | (row_here == 0), blocks, no_blocks, matrix
     )
+    upper = matrix.astype(jnp.bfloat16)
     column_upper = upper[:, NB:]
 
     down = strides(n_row)
     orders = [down, [down[-1]] + down[:-1]]
     held = [[0], [0]]
 
-    def upper_step(value, step):
+    def upper_step(value, step, sent):
         pairs = []
         takes = []
         for kind in range(2):
@@ -63,14 +64,14 @@
                 ((h, c), (h + stride, c)) for h in held[kind] for c in range(1, n_col) if c % 2 == kind
             ]
             held[kind] = held[kind] + [h + stride for h in held[kind]]
-        got = send(value, pairs)
+        got = send(sent, pairs)
         return jnp.where(jnp.where(col_here % 2 == 0, takes[0], takes[1]), got, value)
 
     workers = [r for r in range(n_row) if r & APART == 0]
     targets = workers[1:]
-    square, partner = pivot_columns, pivot_columns
+    square, partner = matrix[:, :NB], matrix[:, :NB]
     near_upper = column_upper
-    upper, column_upper = lax.optimization_barrier((upper_step(upper, 0), column_upper))
+    upper, column_upper = lax.optimization_barrier((upper_step(upper, 0, first_upper), column_upper))
     for index, target in reversed(list(enumerate(targets))):
         served = [0, targets[-1]] if index == 0 else [targets[index - 1]]
         pairs = [((0, 0), (target, 0))] + [((r + APART, 0), (r, 0)) for r in served]
@@ -81,7 +82,7 @@
     for target in reversed(workers[1:]):
         got = send(column_upper, [((0, 0), (target, 0))])
         near_upper = jnp.where(row_here == target, got, near_upper)
-    upper = upper_step(upper, 1)
+    upper = upper_step(upper, 1, upper)
 
     def compute(square, partner):
         both = multipliers(square, jnp.concatenate([matrix[:, :NB], partner], axis=0))
@@ -107,7 +108,7 @@
     got = send(near_sent, [((r, 0), (r + APART, 0)) for r in workers])
     near_upper = jnp.where(row_here & APART == 0, near_upper, got)
     for step in range(2, len(down)):
-        upper = upper_step(upper, step)
+        upper = upper_step(upper, step, upper)
     got = send(
         received, [((r, c), (r, c + 1)) for r in range(1, n_row) for c in range(0, n_col, 2)]
     )

time: 28.6 us -> 28.2 us (0.986)
  the two profiles are of different devices: /device:TPU:1 before, /device:TPU:0 now
where the time goes in v3:
time: 28.2 us; the launch traced here: 27.8 us
  starting transfers between devices  18.8 us (67%)
  waiting for transfers between devices  3.66 us (13%)
  other arithmetic  2.62 us (9%)
  matrix products  2.04 us (7%)
  between operations  0.37 us (1%)
    ppermute x14, starting transfers between devices, send(): return lax.ppermute(value, ('row', 'col'), flat)  18.8 us
    ppermute x14, waiting for transfers between devices, send(): return lax.ppermute(value, ('row', 'col'), flat)  3.66 us
    select_n x2, other arithmetic, upper_step(): jnp.where(jnp.where(col_here % 2 == 0, takes[0], takes[1]), got, value)  1.17 us
    convert_element_type x1, other arithmetic, blocks(): return (matrix[:, :NB], matrix.astype(jnp.bfloat16))  1.15 us
    dot_general x1, matrix products, shards(): return matrix - jnp.dot(received, upper, preferred_element_type=jnp.float32)  1.08 us
  transfers between devices with their start and end apart: 14, of which 2 were waited for; matrix products, arithmetic and copies ran while one was open for 9% of the time, Pallas kernels for 0%

profile of v3, /device:TPU:0, one launch (start us, length us, event | category | flops | bytes accessed | tf_op | source)
XLA Modules:
  0.0 27.8 jit_solution(13469049817164537022)
XLA Ops:
  0.0 1.2 %conditional.2 = (f32[256,256]{1,0:T(8,128)S(1)}, bf16[256,512]{1,0:T(8,128)(2,1)S(1)}) conditional(s32[]{:T(128)} %convert_element_type.17, () %tuple.24, f32[256,512]{1,0:T(8,128)} %param.5), branch_computations={%region_0.0_spmd, %region_1.0_spmd} | conditional | flops 131072 | bytes 3407916 | solution.py:46
  0.0 0.0 copy-start.1
  0.0 1.1 %convert_element_type.6 = bf16[256,512]{1,0:T(8,128)(2,1)S(1)} convert(f32[256,512]{1,0:T(8,128)} %param.1) | non-fusion elementwise | flops 131072 | bytes 786432 | tf_op jit(solution)/shard_map/cond/branch_1_fun/convert_element_type | solution.py:40
  1.2 0.0 copy-done.1
  1.2 0.7 %collective-permute-start.7 = (bf16[256,512]{1,0:T(8,128)(2,1)S(1)}, bf16[256,512]{1,0:T(8,128)(2,1)S(1)}, u32[]{:S(2)}, u32[]{:S(2)}) collective-permute-start(bf16[256,512]{1,0:T(8,128)(2,1)S(1)} %get-tuple-element.25), channel_id=1, source_target_pairs={{2,18},{1,5},{3,7}} | collective-permute-start | bytes 786440 | tf_op jit(solution)/shard_map/ppermute | solution.py:37
  1.9 3.7 %collective-permute-start = (f32[256,256]{1,0:T(8,128)S(1)}, f32[256,256]{1,0:T(8,128)S(1)}, u32[]{:S(2)}, u32[]{:S(2)}) collective-permute-start(f32[256,256]{1,0:T(8,128)S(1)} %get-tuple-element.22), channel_id=1, source_target_pairs={{0,4},{8,0},{28,20}} | collective-permute-start | bytes 786440 | tf_op jit(solution)/shard_map/ppermute | solution.py:37
  5.6 1.8 %collective-permute-start.1 = (f32[256,256]{1,0:T(8,128)S(1)}, f32[256,256]{1,0:T(8,128)S(1)}, u32[]{:S(2)}, u32[]{:S(2)}) collective-permute-start(f32[256,256]{1,0:T(8,128)S(1)} %get-tuple-element.22), channel_id=1, source_target_pairs={{0,16},{12,4}} | collective-permute-start | bytes 786440 | tf_op jit(solution)/shard_map/ppermute | solution.py:37
  7.4 2.2 %collective-permute-start.2 = (f32[256,256]{1,0:T(8,128)S(1)}, f32[256,256]{1,0:T(8,128)S(1)}, u32[]{:S(2)}, u32[]{:S(2)}) collective-permute-start(f32[256,256]{1,0:T(8,128)S(1)} %get-tuple-element.22), channel_id=1, source_target_pairs={{0,20},{24,16}} | collective-permute-start | bytes 786440 | tf_op jit(solution)/shard_map/ppermute | solution.py:37
  9.6 0.0 copy-start
  9.7 0.0 collective-permute-done.7
  9.7 1.1 %broadcast_select_fusion.1 = (bf16[256,512]{1,0:T(8,128)(2,1)S(1)}, bf16[256,512]{1,0:T(8,128)(2,1)S(1)}) fusion(bf16[256,512]{1,0:T(8,128)(2,1)S(1)} %collective-permute-done.7, pred[]{:T(512)S(6)} %select_n.158, f32[256,512]{1,0:T(8,128)} %param.5), kind=kLoop, calls=%fused_computation.40 | loop fusion | flops 262144 | bytes 1310721 | tf_op jit(solution)/shard_map/jit(_where)/select_n | solution.py:68
  10.8 1.3 %collective-permute-start.10 = (bf16[256,256]{1,0:T(8,128)(2,1)S(1)}, bf16[256,256]{1,0:T(8,128)(2,1)S(1)}, u32[]{:S(2)}, u32[]{:S(2)}) collective-permute-start(bf16[256,256]{1,0:T(8,128)(2,1)S(1)} %slice.36), channel_id=1, source_target_pairs={{0,20}} | collective-permute-start | bytes 393224 | tf_op jit(solution)/shard_map/ppermute | solution.py:37
  12.1 1.3 %collective-permute-start.8 = (bf16[256,256]{1,0:T(8,128)(2,1)S(1)}, bf16[256,256]{1,0:T(8,128)(2,1)S(1)}, u32[]{:S(2)}, u32[]{:S(2)}) collective-permute-start(bf16[256,256]{1,0:T(8,128)(2,1)S(1)} %slice.36), channel_id=1, source_target_pairs={{0,4}} | collective-permute-start | bytes 393224 | tf_op jit(solution)/shard_map/ppermute | solution.py:37
  13.4 0.0 collective-permute-done
  13.5 1.3 %collective-permute-start.9 = (bf16[256,256]{1,0:T(8,128)(2,1)S(1)}, bf16[256,256]{1,0:T(8,128)(2,1)S(1)}, u32[]{:S(2)}, u32[]{:S(2)}) collective-permute-start(bf16[256,256]{1,0:T(8,128)(2,1)S(1)} %slice.36), channel_id=1, source_target_pairs={{0,16}} | collective-permute-start | bytes 393224 | tf_op jit(solution)/shard_map/ppermute | solution.py:37
  14.8 0.0 collective-permute-done.1
  14.8 0.7 %collective-permute-start.12 = (bf16[256,512]{1,0:T(8,128)(2,1)S(1)}, bf16[256,512]{1,0:T(8,128)(2,1)S(1)}, u32[]{:S(2)}, u32[]{:S(2)}) collective-permute-start(bf16[256,512]{1,0:T(8,128)(2,1)S(1)} %get-tuple-element.28), channel_id=1, source_target_pairs={{2,10},{18,26},{1,17},{3,19},{5,21},{7,23}} | collective-permute-start | bytes 786440 | tf_op jit(solution)/shard_map/ppermute | solution.py:37
  15.5 0.0 copy-done
  15.5 0.0 collective-permute-done.2
  15.7 1.3 %conditional.3 = (bf16[256,256]{1,0:T(8,128)(2,1)S(1)}, bf16[256,256]{1,0:T(8,128)(2,1)S(1)}) conditional(s32[]{:T(128)} %convert_element_type.16, () %tuple.23, (f32[256,512]{1,0:T(8,128)S(1)}, pred[256,256]{1,0:T(8,128)(4,1)S(1)}, pred[256,256]{1,0:T(8,128)(4,1)S(1)}, f32[256,256]{1,0:T(8,128)S(1)}, pred[256,256]{1,0:T(8,128)(4,1)S(1)}, ...), branch_computations={%region_2.3_spmd, %region_3.6_spmd.clone} | conditional | flops 505085952 | bytes 5709840 | solution.py:97
  15.7 0.2 fusion.14
  15.9 0.6 %fusion = f32[768,256]{1,0:T(8,128)S(1)} fusion(f32[256,256]{1,0:T(8,128)S(1)} %get-tuple-element.84, f32[256,256]{1,0:T(8,128)S(1)} %slice.27, f32[256,256]{1,0:T(8,128)S(1)} %get-tuple-element.81, f32[256]{0:T(256)S(1)} %get-tuple-element.87, f32[256]{0:T(256)S(1)} %get-tuple-element.88), kind=kOutput, calls=%fused_computation.1 | convolution fusion | flops 302710784 | bytes 1574912 | tf_op jit(solution)/shard_map/cond/branch_1_fun/dot_general | solution.py:25
  16.5 0.4 %convolution_convert_fusion = bf16[512,256]{1,0:T(8,128)(2,1)S(1)} fusion(f32[768,256]{1,0:T(8,128)S(1)} %fusion), kind=kOutput, calls=%fused_computation | convolution fusion | flops 201654272 | bytes 1048576 | tf_op jit(solution)/shard_map/cond/branch_1_fun/dot_general | solution.py:26
  16.9 1.3 %collective-permute-start.4 = (bf16[256,256]{1,0:T(8,128)(2,1)S(1)}, bf16[256,256]{1,0:T(8,128)(2,1)S(1)}, u32[]{:S(2)}, u32[]{:S(2)}) collective-permute-start(bf16[256,256]{1,0:T(8,128)(2,1)S(1)} %get-tuple-element.24), channel_id=1, source_target_pairs={{0,8},{4,12},{16,24},{20,28}} | collective-permute-start | bytes 393224 | tf_op jit(solution)/shard_map/ppermute | solution.py:37
  18.2 0.0 collective-permute-done.10
  18.3 1.3 %collective-permute-start.5 = (bf16[256,256]{1,0:T(8,128)(2,1)S(1)}, bf16[256,256]{1,0:T(8,128)(2,1)S(1)}, u32[]{:S(2)}, u32[]{:S(2)}) collective-permute-start(bf16[256,256]{1,0:T(8,128)(2,1)S(1)} %get-tuple-element.24), channel_id=1, source_target_pairs={{0,10},{4,14},{16,26},{20,30}} | collective-permute-start | bytes 393224 | tf_op jit(solution)/shard_map/ppermute | solution.py:37
  19.6 0.0 collective-permute-done.8
  19.6 0.7 %collective-permute-start.3 = (bf16[256,256]{1,0:T(8,128)(2,1)S(1)}, bf16[256,256]{1,0:T(8,128)(2,1)S(1)}, u32[]{:S(2)}, u32[]{:S(2)}) collective-permute-start(bf16[256,256]{1,0:T(8,128)(2,1)S(1)} %get-tuple-element.23), channel_id=1, source_target_pairs={{4,6},{16,18},{20,22}} | collective-permute-start | bytes 393224 | tf_op jit(solution)/shard_map/ppermute | solution.py:37
  20.2 0.0 collective-permute-done.9
  20.3 1.3 %collective-permute-start.11 = (bf16[256,256]{1,0:T(8,128)(2,1)S(1)}, bf16[256,256]{1,0:T(8,128)(2,1)S(1)}, u32[]{:S(2)}, u32[]{:S(2)}) collective-permute-start(bf16[256,256]{1,0:T(8,128)(2,1)S(1)} %select_select_fusion.3), channel_id=1, source_target_pairs={{0,8},{4,12},{16,24},{20,28}} | collective-permute-start | bytes 393224 | tf_op jit(solution)/shard_map/ppermute | solution.py:37
  21.6 0.0 collective-permute-done.12
  21.6 0.7 %collective-permute-start.13 = (bf16[256,512]{1,0:T(8,128)(2,1)S(1)}, bf16[256,512]{1,0:T(8,128)(2,1)S(1)}, u32[]{:S(2)}, u32[]{:S(2)}) collective-permute-start(bf16[256,512]{1,0:T(8,128)(2,1)S(1)} %broadcast_select_fusion), channel_id=1, source_target_pairs={{2,6},{18,22},{10,14},{26,30},{1,9},{3,11},{5,13},{7,15},{17,25},{... | collective-permute-start | bytes 786440 | tf_op jit(solution)/shard_map/ppermute | solution.py:37
  22.3 0.0 collective-permute-done.3
  22.3 0.0 collective-permute-done.4
  22.4 1.5 %collective-permute-done.5 = bf16[256,256]{1,0:T(8,128)(2,1)S(1)} collective-permute-done((bf16[256,256]{1,0:T(8,128)(2,1)S(1)}, bf16[256,256]{1,0:T(8,128)(2,1)S(1)}, u32[]{:S(2)}, u32[]{:S(2)}) %collective-permute-start.5) | collective-permute-done | bytes 131104 | tf_op jit(solution)/shard_map/ppermute | solution.py:37
  23.9 0.7 %collective-permute-start.6 = (bf16[256,256]{1,0:T(8,128)(2,1)S(1)}, bf16[256,256]{1,0:T(8,128)(2,1)S(1)}, u32[]{:S(2)}, u32[]{:S(2)}) collective-permute-start(bf16[256,256]{1,0:T(8,128)(2,1)S(1)} %select_select_fusion.4), channel_id=1, source_target_pairs={{4,5},{6,7},{8,9},{10,11},{12,13},{14,15},{16,17},{18,19},{20,21},... | collective-permute-start | bytes 393224 | tf_op jit(solution)/shard_map/ppermute | solution.py:37
  24.6 2.1 %collective-permute-done.11 = bf16[256,256]{1,0:T(8,128)(2,1)S(1)} collective-permute-done((bf16[256,256]{1,0:T(8,128)(2,1)S(1)}, bf16[256,256]{1,0:T(8,128)(2,1)S(1)}, u32[]{:S(2)}, u32[]{:S(2)}) %collective-permute-start.11) | collective-permute-done | bytes 131104 | tf_op jit(solution)/shard_map/ppermute | solution.py:37
  26.7 0.0 collective-permute-done.6
  26.7 0.0 collective-permute-done.13
  26.7 1.1 %convolution_subtract_fusion = f32[256,512]{1,0:T(8,128)} fusion(f32[256,512]{1,0:T(8,128)S(1)} %copy-done, bf16[256,512]{1,0:T(8,128)(2,1)S(1)} %collective-permute-done.13, bf16[256,512]{1,0:T(8,128)(2,1)S(1)} %broadcast_select_fusion, bf16[256,256]{1,0:T(8,128)(2,1)S(1)} %broadcast_select_fusion.2, pred[]{:T(512)S(6)} %select_n.165, pred[]{:T(512)S(6)} %eq.75, ...), kind=kOutput, calls=%fused_computation.34 | convolution fusion | flops 67633152 | bytes 1966084 | tf_op jit(solution)/shard_map/dot_general | solution.py:120
  (14 shorter events, 0.3 us)
Async XLA Ops:
  0.0 1.2 %copy-start.1 = (f32[256,512]{1,0:T(8,128)S(1)}, f32[256,512]{1,0:T(8,128)}, u32[]{:S(2)}) copy-start(f32[256,512]{1,0:T(8,128)} %param.1) | copy-start | bytes 1572868 | tf_op jit(solution)/shard_map/cond
  1.2 8.4 %collective-permute-start.7 = (bf16[256,512]{1,0:T(8,128)(2,1)S(1)}, bf16[256,512]{1,0:T(8,128)(2,1)S(1)}, u32[]{:S(2)}, u32[]{:S(2)}) collective-permute-start(bf16[256,512]{1,0:T(8,128)(2,1)S(1)} %get-tuple-element.25), channel_id=1, source_target_pairs={{2,18},{1,5},{3,7}} | collective-permute-start | bytes 786440 | tf_op jit(solution)/shard_map/ppermute | solution.py:37
  1.9 11.5 %collective-permute-start = (f32[256,256]{1,0:T(8,128)S(1)}, f32[256,256]{1,0:T(8,128)S(1)}, u32[]{:S(2)}, u32[]{:S(2)}) collective-permute-start(f32[256,256]{1,0:T(8,128)S(1)} %get-tuple-element.22), channel_id=1, source_target_pairs={{0,4},{8,0},{28,20}} | collective-permute-start | bytes 786440 | tf_op jit(solution)/shard_map/ppermute | solution.py:37
  5.6 9.2 %collective-permute-start.1 = (f32[256,256]{1,0:T(8,128)S(1)}, f32[256,256]{1,0:T(8,128)S(1)}, u32[]{:S(2)}, u32[]{:S(2)}) collective-permute-start(f32[256,256]{1,0:T(8,128)S(1)} %get-tuple-element.22), channel_id=1, source_target_pairs={{0,16},{12,4}} | collective-permute-start | bytes 786440 | tf_op jit(solution)/shard_map/ppermute | solution.py:37
  7.4 8.1 %collective-permute-start.2 = (f32[256,256]{1,0:T(8,128)S(1)}, f32[256,256]{1,0:T(8,128)S(1)}, u32[]{:S(2)}, u32[]{:S(2)}) collective-permute-start(f32[256,256]{1,0:T(8,128)S(1)} %get-tuple-element.22), channel_id=1, source_target_pairs={{0,20},{24,16}} | collective-permute-start | bytes 786440 | tf_op jit(solution)/shard_map/ppermute | solution.py:37
  9.6 5.8 %copy-start = (f32[256,512]{1,0:T(8,128)S(1)}, f32[256,512]{1,0:T(8,128)}, u32[]{:S(2)}) copy-start(f32[256,512]{1,0:T(8,128)} %param.5) | copy-start | bytes 1572868
  10.8 7.4 %collective-permute-start.10 = (bf16[256,256]{1,0:T(8,128)(2,1)S(1)}, bf16[256,256]{1,0:T(8,128)(2,1)S(1)}, u32[]{:S(2)}, u32[]{:S(2)}) collective-permute-start(bf16[256,256]{1,0:T(8,128)(2,1)S(1)} %slice.36), channel_id=1, source_target_pairs={{0,20}} | collective-permute-start | bytes 393224 | tf_op jit(solution)/shard_map/ppermute | solution.py:37
  12.1 7.4 %collective-permute-start.8 = (bf16[256,256]{1,0:T(8,128)(2,1)S(1)}, bf16[256,256]{1,0:T(8,128)(2,1)S(1)}, u32[]{:S(2)}, u32[]{:S(2)}) collective-permute-start(bf16[256,256]{1,0:T(8,128)(2,1)S(1)} %slice.36), channel_id=1, source_target_pairs={{0,4}} | collective-permute-start | bytes 393224 | tf_op jit(solution)/shard_map/ppermute | solution.py:37
  13.5 6.8 %collective-permute-start.9 = (bf16[256,256]{1,0:T(8,128)(2,1)S(1)}, bf16[256,256]{1,0:T(8,128)(2,1)S(1)}, u32[]{:S(2)}, u32[]{:S(2)}) collective-permute-start(bf16[256,256]{1,0:T(8,128)(2,1)S(1)} %slice.36), channel_id=1, source_target_pairs={{0,16}} | collective-permute-start | bytes 393224 | tf_op jit(solution)/shard_map/ppermute | solution.py:37
  14.8 6.8 %collective-permute-start.12 = (bf16[256,512]{1,0:T(8,128)(2,1)S(1)}, bf16[256,512]{1,0:T(8,128)(2,1)S(1)}, u32[]{:S(2)}, u32[]{:S(2)}) collective-permute-start(bf16[256,512]{1,0:T(8,128)(2,1)S(1)} %get-tuple-element.28), channel_id=1, source_target_pairs={{2,10},{18,26},{1,17},{3,19},{5,21},{7,23}} | collective-permute-start | bytes 786440 | tf_op jit(solution)/shard_map/ppermute | solution.py:37
  16.9 5.4 %collective-permute-start.4 = (bf16[256,256]{1,0:T(8,128)(2,1)S(1)}, bf16[256,256]{1,0:T(8,128)(2,1)S(1)}, u32[]{:S(2)}, u32[]{:S(2)}) collective-permute-start(bf16[256,256]{1,0:T(8,128)(2,1)S(1)} %get-tuple-element.24), channel_id=1, source_target_pairs={{0,8},{4,12},{16,24},{20,28}} | collective-permute-start | bytes 393224 | tf_op jit(solution)/shard_map/ppermute | solution.py:37
  18.3 5.6 %collective-permute-start.5 = (bf16[256,256]{1,0:T(8,128)(2,1)S(1)}, bf16[256,256]{1,0:T(8,128)(2,1)S(1)}, u32[]{:S(2)}, u32[]{:S(2)}) collective-permute-start(bf16[256,256]{1,0:T(8,128)(2,1)S(1)} %get-tuple-element.24), channel_id=1, source_target_pairs={{0,10},{4,14},{16,26},{20,30}} | collective-permute-start | bytes 393224 | tf_op jit(solution)/shard_map/ppermute | solution.py:37
  19.6 2.8 %collective-permute-start.3 = (bf16[256,256]{1,0:T(8,128)(2,1)S(1)}, bf16[256,256]{1,0:T(8,128)(2,1)S(1)}, u32[]{:S(2)}, u32[]{:S(2)}) collective-permute-start(bf16[256,256]{1,0:T(8,128)(2,1)S(1)} %get-tuple-element.23), channel_id=1, source_target_pairs={{4,6},{16,18},{20,22}} | collective-permute-start | bytes 393224 | tf_op jit(solution)/shard_map/ppermute | solution.py:37
  20.3 6.4 %collective-permute-start.11 = (bf16[256,256]{1,0:T(8,128)(2,1)S(1)}, bf16[256,256]{1,0:T(8,128)(2,1)S(1)}, u32[]{:S(2)}, u32[]{:S(2)}) collective-permute-start(bf16[256,256]{1,0:T(8,128)(2,1)S(1)} %select_select_fusion.3), channel_id=1, source_target_pairs={{0,8},{4,12},{16,24},{20,28}} | collective-permute-start | bytes 393224 | tf_op jit(solution)/shard_map/ppermute | solution.py:37
  21.6 5.1 %collective-permute-start.13 = (bf16[256,512]{1,0:T(8,128)(2,1)S(1)}, bf16[256,512]{1,0:T(8,128)(2,1)S(1)}, u32[]{:S(2)}, u32[]{:S(2)}) collective-permute-start(bf16[256,512]{1,0:T(8,128)(2,1)S(1)} %broadcast_select_fusion), channel_id=1, source_target_pairs={{2,6},{18,22},{10,14},{26,30},{1,9},{3,11},{5,13},{7,15},{17,25},{... | collective-permute-start | bytes 786440 | tf_op jit(solution)/shard_map/ppermute | solution.py:37
  23.9 2.8 %collective-permute-start.6 = (bf16[256,256]{1,0:T(8,128)(2,1)S(1)}, bf16[256,256]{1,0:T(8,128)(2,1)S(1)}, u32[]{:S(2)}, u32[]{:S(2)}) collective-permute-start(bf16[256,256]{1,0:T(8,128)(2,1)S(1)} %select_select_fusion.4), channel_id=1, source_target_pairs={{4,5},{6,7},{8,9},{10,11},{12,13},{14,15},{16,17},{18,19},{20,21},... | collective-permute-start | bytes 393224 | tf_op jit(solution)/shard_map/ppermute | solution.py:37

commit v4 on v3

--- a/solution.py
+++ b/solution.py
@@ -46,15 +46,14 @@
     pivot_columns, first_upper = lax.cond(
         sends_columns | (row_here == 0), blocks, no_blocks, matrix
     )
-    upper = matrix.astype(jnp.bfloat16)
-    column_upper = upper[:, NB:]
+    upper = lax.optimization_barrier(jnp.where(row_here == 0, first_upper, 0))
 
     down = strides(n_row)
     orders = [down, [down[-1]] + down[:-1]]
     held = [[0], [0]]
 
-    def upper_step(value, step, sent):
-        pairs = []
+    def upper_step(value, step, sent, pairs=()):
+        pairs = list(pairs)
         takes = []
         for kind in range(2):
             stride = orders[kind][step]
@@ -65,13 +64,14 @@
             ]
             held[kind] = held[kind] + [h + stride for h in held[kind]]
         got = send(sent, pairs)
-        return jnp.where(jnp.where(col_here % 2 == 0, takes[0], takes[1]), got, value)
+        return jnp.where(jnp.where(col_here % 2 == 0, takes[0], takes[1]), got, value), got
 
     workers = [r for r in range(n_row) if r & APART == 0]
-    targets = workers[1:]
+    targets = workers[2:] + workers[1:2]
     square, partner = matrix[:, :NB], matrix[:, :NB]
-    near_upper = column_upper
-    upper, column_upper = lax.optimization_barrier((upper_step(upper, 0, first_upper), column_upper))
+    passed, got = upper_step(upper, 0, first_upper, [((0, 0), (1, 0))])
+    near_upper = jnp.where(row_here == 1, got[:, NB:], upper[:, NB:])
+    upper = passed
     for index, target in reversed(list(enumerate(targets))):
         served = [0, targets[-1]] if index == 0 else [targets[index - 1]]
         pairs = [((0, 0), (target, 0))] + [((r + APART, 0), (r, 0)) for r in served]
@@ -79,10 +79,16 @@
         square = jnp.where(row_here == target, got, square)
         for r in served:
             partner = jnp.where(row_here == r, got, partner)
-    for target in reversed(workers[1:]):
-        got = send(column_upper, [((0, 0), (target, 0))])
-        near_upper = jnp.where(row_here == target, got, near_upper)
-    upper = upper_step(upper, 1, upper)
+    near_sent = near_upper
+    for target in reversed(targets[:-1]):
+        pairs = [((1, 0), (target, 0))]
+        takes = row_here == target
+        if target == targets[-2]:
+            pairs += [((0, 0), (APART, 0))]
+            takes = takes | (row_here == APART)
+        got = send(near_sent, pairs)
+        near_upper = jnp.where(takes, got, near_upper)
+    upper, _ = upper_step(upper, 1, upper)
 
     def compute(square, partner):
         both = multipliers(square, jnp.concatenate([matrix[:, :NB], partner], axis=0))
@@ -105,10 +111,10 @@
         got = send(lower, [((r, 0), (r, c)) for r in targets])
         received = jnp.where((row_here & APART == 0) & (col_here == c), got, received)
     near_sent, _ = lax.optimization_barrier((near_upper, lower))
-    got = send(near_sent, [((r, 0), (r + APART, 0)) for r in workers])
-    near_upper = jnp.where(row_here & APART == 0, near_upper, got)
+    got = send(near_sent, [((r, 0), (r + APART, 0)) for r in workers[1:]])
+    near_upper = jnp.where((row_here & APART != 0) & (row_here != APART), got, near_upper)
     for step in range(2, len(down)):
-        upper = upper_step(upper, step, upper)
+        upper, _ = upper_step(upper, step, upper)
     got = send(
         received, [((r, c), (r, c + 1)) for r in range(1, n_row) for c in range(0, n_col, 2)]
     )

time: 28.2 us -> 27.1 us (0.961)
  the two profiles are of different devices: /device:TPU:0 before, /device:TPU:11 now
where the time goes in v4:
time: 27.1 us; the launch traced here: 26.8 us
  waiting for transfers between devices  14.8 us (55%)
  starting transfers between devices  10.1 us (37%)
  matrix products  1.07 us (4%)
  between operations  0.39 us (1%)
    ppermute x13, waiting for transfers between devices, send(): return lax.ppermute(value, ('row', 'col'), flat)  14.8 us
    ppermute x13, starting transfers between devices, send(): return lax.ppermute(value, ('row', 'col'), flat)  10.1 us
    dot_general x1, matrix products, shards(): return matrix - jnp.dot(received, upper, preferred_element_type=jnp.float32)  1.07 us
  transfers between devices with their start and end apart: 13, of which 2 were waited for; matrix products, arithmetic and copies ran while one was open for 1% of the time, Pallas kernels for 0%

profile of v4, /device:TPU:11, one launch (start us, length us, event | category | flops | bytes accessed | tf_op | source)
XLA Modules:
  0.0 26.8 jit_solution(7184180756617703629)
XLA Ops:
  0.0 0.1 conditional.2
  0.1 0.7 %collective-permute-start.7 = (bf16[256,512]{1,0:T(8,128)(2,1)S(1)}, bf16[256,512]{1,0:T(8,128)(2,1)S(1)}, u32[]{:S(2)}, u32[]{:S(2)}) collective-permute-start(bf16[256,512]{1,0:T(8,128)(2,1)S(1)} %get-tuple-element.23), channel_id=1, source_target_pairs={{0,4},{2,18},{1,5},{3,7}} | collective-permute-start | bytes 786440 | tf_op jit(solution)/shard_map/ppermute | solution.py:37
  0.7 0.7 %collective-permute-start = (f32[256,256]{1,0:T(8,128)S(1)}, f32[256,256]{1,0:T(8,128)S(1)}, u32[]{:S(2)}, u32[]{:S(2)}) collective-permute-start(f32[256,256]{1,0:T(8,128)S(1)} %get-tuple-element.20), channel_id=1, source_target_pairs={{0,16},{8,0},{12,4}} | collective-permute-start | bytes 786440 | tf_op jit(solution)/shard_map/ppermute | solution.py:37
  1.4 0.7 %collective-permute-start.1 = (f32[256,256]{1,0:T(8,128)S(1)}, f32[256,256]{1,0:T(8,128)S(1)}, u32[]{:S(2)}, u32[]{:S(2)}) collective-permute-start(f32[256,256]{1,0:T(8,128)S(1)} %get-tuple-element.20), channel_id=1, source_target_pairs={{0,20},{24,16}} | collective-permute-start | bytes 786440 | tf_op jit(solution)/shard_map/ppermute | solution.py:37
  2.1 0.7 %collective-permute-start.2 = (f32[256,256]{1,0:T(8,128)S(1)}, f32[256,256]{1,0:T(8,128)S(1)}, u32[]{:S(2)}, u32[]{:S(2)}) collective-permute-start(f32[256,256]{1,0:T(8,128)S(1)} %get-tuple-element.20), channel_id=1, source_target_pairs={{0,4},{28,20}} | collective-permute-start | bytes 786440 | tf_op jit(solution)/shard_map/ppermute | solution.py:37
  2.9 0.0 copy-start
  2.9 0.0 collective-permute-done.7
  2.9 0.8 %collective-permute-start.8 = (bf16[256,256]{1,0:T(8,128)(2,1)S(1)}, bf16[256,256]{1,0:T(8,128)(2,1)S(1)}, u32[]{:S(2)}, u32[]{:S(2)}) collective-permute-start(bf16[256,256]{1,0:T(8,128)(2,1)S(1)} %slice_select_fusion), channel_id=1, source_target_pairs={{4,16}} | collective-permute-start | bytes 393224 | tf_op jit(solution)/shard_map/ppermute | solution.py:37
  3.7 0.7 %collective-permute-start.9 = (bf16[256,256]{1,0:T(8,128)(2,1)S(1)}, bf16[256,256]{1,0:T(8,128)(2,1)S(1)}, u32[]{:S(2)}, u32[]{:S(2)}) collective-permute-start(bf16[256,256]{1,0:T(8,128)(2,1)S(1)} %slice_select_fusion), channel_id=1, source_target_pairs={{4,20},{0,8}} | collective-permute-start | bytes 393224 | tf_op jit(solution)/shard_map/ppermute | solution.py:37
  4.4 0.0 collective-permute-done
  4.4 0.7 %collective-permute-start.11 = (bf16[256,512]{1,0:T(8,128)(2,1)S(1)}, bf16[256,512]{1,0:T(8,128)(2,1)S(1)}, u32[]{:S(2)}, u32[]{:S(2)}) collective-permute-start(bf16[256,512]{1,0:T(8,128)(2,1)S(1)} %broadcast_select_fusion), channel_id=1, source_target_pairs={{2,10},{18,26},{1,17},{3,19},{5,21},{7,23}} | collective-permute-start | bytes 786440 | tf_op jit(solution)/shard_map/ppermute | solution.py:37
  5.1 0.0 copy-done
  5.2 0.0 collective-permute-done.1
  5.2 0.0 collective-permute-done.2
  5.4 0.1 conditional.3
  5.4 0.7 %collective-permute-start.4 = (bf16[256,256]{1,0:T(8,128)(2,1)S(1)}, bf16[256,256]{1,0:T(8,128)(2,1)S(1)}, u32[]{:S(2)}, u32[]{:S(2)}) collective-permute-start(bf16[256,256]{1,0:T(8,128)(2,1)S(1)} %get-tuple-element.22), channel_id=1, source_target_pairs={{0,8},{4,12},{16,24},{20,28}} | collective-permute-start | bytes 393224 | tf_op jit(solution)/shard_map/ppermute | solution.py:37
  6.1 0.7 %collective-permute-start.5 = (bf16[256,256]{1,0:T(8,128)(2,1)S(1)}, bf16[256,256]{1,0:T(8,128)(2,1)S(1)}, u32[]{:S(2)}, u32[]{:S(2)}) collective-permute-start(bf16[256,256]{1,0:T(8,128)(2,1)S(1)} %get-tuple-element.22), channel_id=1, source_target_pairs={{0,10},{4,14},{16,26},{20,30}} | collective-permute-start | bytes 393224 | tf_op jit(solution)/shard_map/ppermute | solution.py:37
  6.8 0.0 collective-permute-done.8
  6.8 0.7 %collective-permute-start.3 = (bf16[256,256]{1,0:T(8,128)(2,1)S(1)}, bf16[256,256]{1,0:T(8,128)(2,1)S(1)}, u32[]{:S(2)}, u32[]{:S(2)}) collective-permute-start(bf16[256,256]{1,0:T(8,128)(2,1)S(1)} %get-tuple-element.21), channel_id=1, source_target_pairs={{16,18},{20,22},{4,6}} | collective-permute-start | bytes 393224 | tf_op jit(solution)/shard_map/ppermute | solution.py:37
  7.5 0.0 collective-permute-done.9
  7.5 0.7 %collective-permute-start.10 = (bf16[256,256]{1,0:T(8,128)(2,1)S(1)}, bf16[256,256]{1,0:T(8,128)(2,1)S(1)}, u32[]{:S(2)}, u32[]{:S(2)}) collective-permute-start(bf16[256,256]{1,0:T(8,128)(2,1)S(1)} %select_select_fusion.3), channel_id=1, source_target_pairs={{4,12},{16,24},{20,28}} | collective-permute-start | bytes 393224 | tf_op jit(solution)/shard_map/ppermute | solution.py:37
  8.2 0.0 collective-permute-done.11
  8.2 1.3 %collective-permute-start.12 = (bf16[256,512]{1,0:T(8,128)(2,1)S(1)}, bf16[256,512]{1,0:T(8,128)(2,1)S(1)}, u32[]{:S(2)}, u32[]{:S(2)}) collective-permute-start(bf16[256,512]{1,0:T(8,128)(2,1)S(1)} %broadcast_select_fusion.1), channel_id=1, source_target_pairs={{2,6},{18,22},{10,14},{26,30},{1,9},{3,11},{5,13},{7,15},{17,25},{... | collective-permute-start | bytes 786440 | tf_op jit(solution)/shard_map/ppermute | solution.py:37
  9.5 0.0 collective-permute-done.3
  9.5 0.0 collective-permute-done.4
  9.6 0.0 collective-permute-done.5
  9.6 1.3 %collective-permute-start.6 = (bf16[256,256]{1,0:T(8,128)(2,1)S(1)}, bf16[256,256]{1,0:T(8,128)(2,1)S(1)}, u32[]{:S(2)}, u32[]{:S(2)}) collective-permute-start(bf16[256,256]{1,0:T(8,128)(2,1)S(1)} %select_select_fusion.4), channel_id=1, source_target_pairs={{4,5},{6,7},{8,9},{10,11},{12,13},{14,15},{16,17},{18,19},{20,21},... | collective-permute-start | bytes 393224 | tf_op jit(solution)/shard_map/ppermute | solution.py:37
  10.9 0.0 collective-permute-done.10
  10.9 11.9 %collective-permute-done.6 = bf16[256,256]{1,0:T(8,128)(2,1)S(1)} collective-permute-done((bf16[256,256]{1,0:T(8,128)(2,1)S(1)}, bf16[256,256]{1,0:T(8,128)(2,1)S(1)}, u32[]{:S(2)}, u32[]{:S(2)}) %collective-permute-start.6) | collective-permute-done | bytes 131104 | tf_op jit(solution)/shard_map/ppermute | solution.py:37
  22.8 2.9 %collective-permute-done.12 = bf16[256,512]{1,0:T(8,128)(2,1)S(1)} collective-permute-done((bf16[256,512]{1,0:T(8,128)(2,1)S(1)}, bf16[256,512]{1,0:T(8,128)(2,1)S(1)}, u32[]{:S(2)}, u32[]{:S(2)}) %collective-permute-start.12) | collective-permute-done | bytes 262176 | tf_op jit(solution)/shard_map/ppermute | solution.py:37
  25.7 1.1 %convolution_subtract_fusion = f32[256,512]{1,0:T(8,128)} fusion(f32[256,512]{1,0:T(8,128)S(1)} %copy-done, bf16[256,512]{1,0:T(8,128)(2,1)S(1)} %collective-permute-done.12, bf16[256,512]{1,0:T(8,128)(2,1)S(1)} %broadcast_select_fusion.1, bf16[256,256]{1,0:T(8,128)(2,1)S(1)} %broadcast_select_fusion.3, pred[]{:T(512)S(6)} %select_n.175, pred[]{:T(512)S(6)} %eq.78, ...), kind=kOutput, calls=%fused_computation.34 | convolution fusion | flops 67633152 | bytes 1966084 | tf_op jit(solution)/shard_map/dot_general | solution.py:126
  (16 shorter events, 0.4 us)
Async XLA Ops:
  0.1 2.8 %collective-permute-start.7 = (bf16[256,512]{1,0:T(8,128)(2,1)S(1)}, bf16[256,512]{1,0:T(8,128)(2,1)S(1)}, u32[]{:S(2)}, u32[]{:S(2)}) collective-permute-start(bf16[256,512]{1,0:T(8,128)(2,1)S(1)} %get-tuple-element.23), channel_id=1, source_target_pairs={{0,4},{2,18},{1,5},{3,7}} | collective-permute-start | bytes 786440 | tf_op jit(solution)/shard_map/ppermute | solution.py:37
  0.7 3.7 %collective-permute-start = (f32[256,256]{1,0:T(8,128)S(1)}, f32[256,256]{1,0:T(8,128)S(1)}, u32[]{:S(2)}, u32[]{:S(2)}) collective-permute-start(f32[256,256]{1,0:T(8,128)S(1)} %get-tuple-element.20), channel_id=1, source_target_pairs={{0,16},{8,0},{12,4}} | collective-permute-start | bytes 786440 | tf_op jit(solution)/shard_map/ppermute | solution.py:37
  1.4 3.8 %collective-permute-start.1 = (f32[256,256]{1,0:T(8,128)S(1)}, f32[256,256]{1,0:T(8,128)S(1)}, u32[]{:S(2)}, u32[]{:S(2)}) collective-permute-start(f32[256,256]{1,0:T(8,128)S(1)} %get-tuple-element.20), channel_id=1, source_target_pairs={{0,20},{24,16}} | collective-permute-start | bytes 786440 | tf_op jit(solution)/shard_map/ppermute | solution.py:37
  2.1 3.1 %collective-permute-start.2 = (f32[256,256]{1,0:T(8,128)S(1)}, f32[256,256]{1,0:T(8,128)S(1)}, u32[]{:S(2)}, u32[]{:S(2)}) collective-permute-start(f32[256,256]{1,0:T(8,128)S(1)} %get-tuple-element.20), channel_id=1, source_target_pairs={{0,4},{28,20}} | collective-permute-start | bytes 786440 | tf_op jit(solution)/shard_map/ppermute | solution.py:37
  2.9 2.3 %copy-start = (f32[256,512]{1,0:T(8,128)S(1)}, f32[256,512]{1,0:T(8,128)}, u32[]{:S(2)}) copy-start(f32[256,512]{1,0:T(8,128)} %param.5) | copy-start | bytes 1572868
  2.9 3.9 %collective-permute-start.8 = (bf16[256,256]{1,0:T(8,128)(2,1)S(1)}, bf16[256,256]{1,0:T(8,128)(2,1)S(1)}, u32[]{:S(2)}, u32[]{:S(2)}) collective-permute-start(bf16[256,256]{1,0:T(8,128)(2,1)S(1)} %slice_select_fusion), channel_id=1, source_target_pairs={{4,16}} | collective-permute-start | bytes 393224 | tf_op jit(solution)/shard_map/ppermute | solution.py:37
  3.7 3.7 %collective-permute-start.9 = (bf16[256,256]{1,0:T(8,128)(2,1)S(1)}, bf16[256,256]{1,0:T(8,128)(2,1)S(1)}, u32[]{:S(2)}, u32[]{:S(2)}) collective-permute-start(bf16[256,256]{1,0:T(8,128)(2,1)S(1)} %slice_select_fusion), channel_id=1, source_target_pairs={{4,20},{0,8}} | collective-permute-start | bytes 393224 | tf_op jit(solution)/shard_map/ppermute | solution.py:37
  4.4 3.7 %collective-permute-start.11 = (bf16[256,512]{1,0:T(8,128)(2,1)S(1)}, bf16[256,512]{1,0:T(8,128)(2,1)S(1)}, u32[]{:S(2)}, u32[]{:S(2)}) collective-permute-start(bf16[256,512]{1,0:T(8,128)(2,1)S(1)} %broadcast_select_fusion), channel_id=1, source_target_pairs={{2,10},{18,26},{1,17},{3,19},{5,21},{7,23}} | collective-permute-start | bytes 786440 | tf_op jit(solution)/shard_map/ppermute | solution.py:37
  5.4 4.1 %collective-permute-start.4 = (bf16[256,256]{1,0:T(8,128)(2,1)S(1)}, bf16[256,256]{1,0:T(8,128)(2,1)S(1)}, u32[]{:S(2)}, u32[]{:S(2)}) collective-permute-start(bf16[256,256]{1,0:T(8,128)(2,1)S(1)} %get-tuple-element.22), channel_id=1, source_target_pairs={{0,8},{4,12},{16,24},{20,28}} | collective-permute-start | bytes 393224 | tf_op jit(solution)/shard_map/ppermute | solution.py:37
  6.1 3.5 %collective-permute-start.5 = (bf16[256,256]{1,0:T(8,128)(2,1)S(1)}, bf16[256,256]{1,0:T(8,128)(2,1)S(1)}, u32[]{:S(2)}, u32[]{:S(2)}) collective-permute-start(bf16[256,256]{1,0:T(8,128)(2,1)S(1)} %get-tuple-element.22), channel_id=1, source_target_pairs={{0,10},{4,14},{16,26},{20,30}} | collective-permute-start | bytes 393224 | tf_op jit(solution)/shard_map/ppermute | solution.py:37
  6.8 2.7 %collective-permute-start.3 = (bf16[256,256]{1,0:T(8,128)(2,1)S(1)}, bf16[256,256]{1,0:T(8,128)(2,1)S(1)}, u32[]{:S(2)}, u32[]{:S(2)}) collective-permute-start(bf16[256,256]{1,0:T(8,128)(2,1)S(1)} %get-tuple-element.21), channel_id=1, source_target_pairs={{16,18},{20,22},{4,6}} | collective-permute-start | bytes 393224 | tf_op jit(solution)/shard_map/ppermute | solution.py:37
  7.5 3.4 %collective-permute-start.10 = (bf16[256,256]{1,0:T(8,128)(2,1)S(1)}, bf16[256,256]{1,0:T(8,128)(2,1)S(1)}, u32[]{:S(2)}, u32[]{:S(2)}) collective-permute-start(bf16[256,256]{1,0:T(8,128)(2,1)S(1)} %select_select_fusion.3), channel_id=1, source_target_pairs={{4,12},{16,24},{20,28}} | collective-permute-start | bytes 393224 | tf_op jit(solution)/shard_map/ppermute | solution.py:37
  8.2 17.5 %collective-permute-start.12 = (bf16[256,512]{1,0:T(8,128)(2,1)S(1)}, bf16[256,512]{1,0:T(8,128)(2,1)S(1)}, u32[]{:S(2)}, u32[]{:S(2)}) collective-permute-start(bf16[256,512]{1,0:T(8,128)(2,1)S(1)} %broadcast_select_fusion.1), channel_id=1, source_target_pairs={{2,6},{18,22},{10,14},{26,30},{1,9},{3,11},{5,13},{7,15},{17,25},{... | collective-permute-start | bytes 786440 | tf_op jit(solution)/shard_map/ppermute | solution.py:37
  9.6 13.2 %collective-permute-start.6 = (bf16[256,256]{1,0:T(8,128)(2,1)S(1)}, bf16[256,256]{1,0:T(8,128)(2,1)S(1)}, u32[]{:S(2)}, u32[]{:S(2)}) collective-permute-start(bf16[256,256]{1,0:T(8,128)(2,1)S(1)} %select_select_fusion.4), channel_id=1, source_target_pairs={{4,5},{6,7},{8,9},{10,11},{12,13},{14,15},{16,17},{18,19},{20,21},... | collective-permute-start | bytes 393224 | tf_op jit(solution)/shard_map/ppermute | solution.py:37

commit v5 on v4

--- a/solution.py
+++ b/solution.py
@@ -14,6 +14,17 @@
         out.append(stride)
         stride //= 2
     return out
+
+
+def two_terms(values, width):
+    high = lax.reduce_precision(values, exponent_bits=8, mantissa_bits=7)
+    terms = [high.astype(jnp.bfloat16), (values - high).astype(jnp.bfloat16)]
+    both = jnp.concatenate(terms, axis=1)
+    return jnp.pad(both, ((0, 0), (0, width - both.shape[1])))
+
+
+def summed(terms):
+    return terms[:, :NB].astype(jnp.float32) + terms[:, NB : 2 * NB].astype(jnp.float32)
 
 
 def multipliers(square, columns):
@@ -37,16 +48,19 @@
         return lax.ppermute(value, ("row", "col"), flat)
 
     def blocks(matrix):
-        return matrix[:, :NB], matrix.astype(jnp.bfloat16)
+        rows = matrix.astype(jnp.bfloat16)
+        return jnp.where(col_here == 0, two_terms(matrix[:, :NB], cols_dev), rows), rows[:, NB:]
 
     def no_blocks(matrix):
-        return jnp.zeros((NB, NB), matrix.dtype), jnp.zeros(matrix.shape, jnp.bfloat16)
+        return jnp.zeros(matrix.shape, jnp.bfloat16), jnp.zeros(
+            (rows_dev, cols_dev - NB), jnp.bfloat16
+        )
 
     sends_columns = (col_here == 0) & (row_here & APART != 0)
-    pivot_columns, first_upper = lax.cond(
+    first_sent, column_upper = lax.cond(
         sends_columns | (row_here == 0), blocks, no_blocks, matrix
     )
-    upper = lax.optimization_barrier(jnp.where(row_here == 0, first_upper, 0))
+    upper = lax.optimization_barrier(jnp.where(row_here == 0, first_sent, 0))
 
     down = strides(n_row)
     orders = [down, [down[-1]] + down[:-1]]
@@ -68,30 +82,34 @@
 
     workers = [r for r in range(n_row) if r & APART == 0]
     targets = workers[2:] + workers[1:2]
-    square, partner = matrix[:, :NB], matrix[:, :NB]
-    passed, got = upper_step(upper, 0, first_upper, [((0, 0), (1, 0))])
-    near_upper = jnp.where(row_here == 1, got[:, NB:], upper[:, NB:])
-    upper = passed
+    square = partner = first_sent
     for index, target in reversed(list(enumerate(targets))):
         served = [0, targets[-1]] if index == 0 else [targets[index - 1]]
         pairs = [((0, 0), (target, 0))] + [((r + APART, 0), (r, 0)) for r in served]
-        got = send(pivot_columns, pairs)
+        if index == 0:
+            upper, got = upper_step(upper, 0, first_sent, pairs)
+        else:
+            got = send(first_sent, pairs)
         square = jnp.where(row_here == target, got, square)
         for r in served:
             partner = jnp.where(row_here == r, got, partner)
+
+    got = send(column_upper, [((0, 0), (1, 0))])
+    near_upper = jnp.where(row_here == 1, got, column_upper)
     near_sent = near_upper
-    for target in reversed(targets[:-1]):
+    for target in reversed(targets[1:-1]):
         pairs = [((1, 0), (target, 0))]
         takes = row_here == target
-        if target == targets[-2]:
-            pairs += [((0, 0), (APART, 0))]
-            takes = takes | (row_here == APART)
+        if target == targets[1]:
+            pairs += [((0, 0), (targets[0], 0))]
+            takes = takes | (row_here == targets[0])
         got = send(near_sent, pairs)
         near_upper = jnp.where(takes, got, near_upper)
     upper, _ = upper_step(upper, 1, upper)
 
     def compute(square, partner):
-        both = multipliers(square, jnp.concatenate([matrix[:, :NB], partner], axis=0))
+        columns = jnp.concatenate([matrix[:, :NB], summed(partner)], axis=0)
+        both = multipliers(summed(square), columns)
         both = both.astype(jnp.bfloat16)
         return both[:NB], both[NB:]
 
@@ -111,8 +129,8 @@
         got = send(lower, [((r, 0), (r, c)) for r in targets])
         received = jnp.where((row_here & APART == 0) & (col_here == c), got, received)
     near_sent, _ = lax.optimization_barrier((near_upper, lower))
-    got = send(near_sent, [((r, 0), (r + APART, 0)) for r in workers[1:]])
-    near_upper = jnp.where((row_here & APART != 0) & (row_here != APART), got, near_upper)
+    got = send(near_sent, [((r, 0), (r + APART, 0)) for r in workers])
+    near_upper = jnp.where(row_here & APART != 0, got, near_upper)
     for step in range(2, len(down)):
         upper, _ = upper_step(upper, step, upper)
     got = send(

time: 27.1 us -> 28.9 us (1.066)
  the two profiles are of different devices: /device:TPU:11 before, /device:TPU:7 now
where the time goes in v5:
time: 28.9 us; the launch traced here: 28.6 us
  waiting for transfers between devices  16.2 us (56%)
  starting transfers between devices  10.7 us (37%)
  matrix products  1.08 us (4%)
  between operations  0.31 us (1%)
    ppermute x12, waiting for transfers between devices, send(): return lax.ppermute(value, ('row', 'col'), flat)  16.2 us
    ppermute x12, starting transfers between devices, send(): return lax.ppermute(value, ('row', 'col'), flat)  10.7 us
    dot_general x1, matrix products, shards(): return matrix - jnp.dot(received, upper, preferred_element_type=jnp.float32)  1.08 us
  transfers between devices with their start and end apart: 12, of which 3 were waited for; matrix products, arithmetic and copies ran while one was open for 1% of the time, Pallas kernels for 0%

profile of v5, /device:TPU:7, one launch (start us, length us, event | category | flops | bytes accessed | tf_op | source)
XLA Modules:
  0.0 28.6 jit_solution(10874629485248647621)
XLA Ops:
  0.1 1.3 %collective-permute-start = (bf16[256,512]{1,0:T(8,128)(2,1)S(1)}, bf16[256,512]{1,0:T(8,128)(2,1)S(1)}, u32[]{:S(2)}, u32[]{:S(2)}) collective-permute-start(bf16[256,512]{1,0:T(8,128)(2,1)S(1)} %get-tuple-element.100), channel_id=1, source_target_pairs={{0,16},{8,0},{12,4},{2,18},{1,5},{3,7}} | collective-permute-start | bytes 786440 | tf_op jit(solution)/shard_map/ppermute | solution.py:48
  1.4 0.7 %collective-permute-start.1 = (bf16[256,512]{1,0:T(8,128)(2,1)S(1)}, bf16[256,512]{1,0:T(8,128)(2,1)S(1)}, u32[]{:S(2)}, u32[]{:S(2)}) collective-permute-start(bf16[256,512]{1,0:T(8,128)(2,1)S(1)} %get-tuple-element.100), channel_id=1, source_target_pairs={{0,20},{24,16}} | collective-permute-start | bytes 786440 | tf_op jit(solution)/shard_map/ppermute | solution.py:48
  2.0 0.7 %collective-permute-start.2 = (bf16[256,512]{1,0:T(8,128)(2,1)S(1)}, bf16[256,512]{1,0:T(8,128)(2,1)S(1)}, u32[]{:S(2)}, u32[]{:S(2)}) collective-permute-start(bf16[256,512]{1,0:T(8,128)(2,1)S(1)} %get-tuple-element.100), channel_id=1, source_target_pairs={{0,4},{28,20}} | collective-permute-start | bytes 786440 | tf_op jit(solution)/shard_map/ppermute | solution.py:48
  2.7 0.7 %collective-permute-start.7 = (bf16[256,256]{1,0:T(8,128)(2,1)S(1)}, bf16[256,256]{1,0:T(8,128)(2,1)S(1)}, u32[]{:S(2)}, u32[]{:S(2)}) collective-permute-start(bf16[256,256]{1,0:T(8,128)(2,1)S(1)} %get-tuple-element.28), channel_id=1, source_target_pairs={{0,4}} | collective-permute-start | bytes 393224 | tf_op jit(solution)/shard_map/ppermute | solution.py:48
  3.5 0.0 collective-permute-done.7
  3.5 0.0 copy-start
  3.5 0.8 %collective-permute-start.8 = (bf16[256,256]{1,0:T(8,128)(2,1)S(1)}, bf16[256,256]{1,0:T(8,128)(2,1)S(1)}, u32[]{:S(2)}, u32[]{:S(2)}) collective-permute-start(bf16[256,256]{1,0:T(8,128)(2,1)S(1)} %broadcast_select_fusion.3), channel_id=1, source_target_pairs={{4,20},{0,16}} | collective-permute-start | bytes 393224 | tf_op jit(solution)/shard_map/ppermute | solution.py:48
  4.3 2.9 %collective-permute-done = bf16[256,512]{1,0:T(8,128)(2,1)S(1)} collective-permute-done((bf16[256,512]{1,0:T(8,128)(2,1)S(1)}, bf16[256,512]{1,0:T(8,128)(2,1)S(1)}, u32[]{:S(2)}, u32[]{:S(2)}) %collective-permute-start) | collective-permute-done | bytes 262176 | tf_op jit(solution)/shard_map/ppermute | solution.py:48
  7.2 1.3 %collective-permute-start.10 = (bf16[256,512]{1,0:T(8,128)(2,1)S(1)}, bf16[256,512]{1,0:T(8,128)(2,1)S(1)}, u32[]{:S(2)}, u32[]{:S(2)}) collective-permute-start(bf16[256,512]{1,0:T(8,128)(2,1)S(1)} %broadcast_select_fusion), channel_id=1, source_target_pairs={{2,10},{18,26},{1,17},{3,19},{5,21},{7,23}} | collective-permute-start | bytes 786440 | tf_op jit(solution)/shard_map/ppermute | solution.py:48
  8.6 0.0 collective-permute-done.1
  8.6 0.0 collective-permute-done.2
  8.6 0.0 copy-done
  8.6 0.1 conditional.3
  8.7 0.7 %collective-permute-start.4 = (bf16[256,256]{1,0:T(8,128)(2,1)S(1)}, bf16[256,256]{1,0:T(8,128)(2,1)S(1)}, u32[]{:S(2)}, u32[]{:S(2)}) collective-permute-start(bf16[256,256]{1,0:T(8,128)(2,1)S(1)} %get-tuple-element.27), channel_id=1, source_target_pairs={{0,8},{4,12},{16,24},{20,28}} | collective-permute-start | bytes 393224 | tf_op jit(solution)/shard_map/ppermute | solution.py:48
  9.4 0.7 %collective-permute-start.5 = (bf16[256,256]{1,0:T(8,128)(2,1)S(1)}, bf16[256,256]{1,0:T(8,128)(2,1)S(1)}, u32[]{:S(2)}, u32[]{:S(2)}) collective-permute-start(bf16[256,256]{1,0:T(8,128)(2,1)S(1)} %get-tuple-element.27), channel_id=1, source_target_pairs={{0,10},{4,14},{16,26},{20,30}} | collective-permute-start | bytes 393224 | tf_op jit(solution)/shard_map/ppermute | solution.py:48
  10.1 0.7 %collective-permute-start.3 = (bf16[256,256]{1,0:T(8,128)(2,1)S(1)}, bf16[256,256]{1,0:T(8,128)(2,1)S(1)}, u32[]{:S(2)}, u32[]{:S(2)}) collective-permute-start(bf16[256,256]{1,0:T(8,128)(2,1)S(1)} %get-tuple-element.26), channel_id=1, source_target_pairs={{16,18},{20,22},{4,6}} | collective-permute-start | bytes 393224 | tf_op jit(solution)/shard_map/ppermute | solution.py:48
  10.7 0.0 collective-permute-done.8
  10.8 0.7 %collective-permute-start.9 = (bf16[256,256]{1,0:T(8,128)(2,1)S(1)}, bf16[256,256]{1,0:T(8,128)(2,1)S(1)}, u32[]{:S(2)}, u32[]{:S(2)}) collective-permute-start(bf16[256,256]{1,0:T(8,128)(2,1)S(1)} %broadcast_select_fusion.4), channel_id=1, source_target_pairs={{0,8},{4,12},{16,24},{20,28}} | collective-permute-start | bytes 393224 | tf_op jit(solution)/shard_map/ppermute | solution.py:48
  11.4 0.4 %collective-permute-done.10 = bf16[256,512]{1,0:T(8,128)(2,1)S(1)} collective-permute-done((bf16[256,512]{1,0:T(8,128)(2,1)S(1)}, bf16[256,512]{1,0:T(8,128)(2,1)S(1)}, u32[]{:S(2)}, u32[]{:S(2)}) %collective-permute-start.10) | collective-permute-done | bytes 262176 | tf_op jit(solution)/shard_map/ppermute | solution.py:48
  11.8 1.3 %collective-permute-start.11 = (bf16[256,512]{1,0:T(8,128)(2,1)S(1)}, bf16[256,512]{1,0:T(8,128)(2,1)S(1)}, u32[]{:S(2)}, u32[]{:S(2)}) collective-permute-start(bf16[256,512]{1,0:T(8,128)(2,1)S(1)} %broadcast_select_fusion.1), channel_id=1, source_target_pairs={{2,6},{18,22},{10,14},{26,30},{1,9},{3,11},{5,13},{7,15},{17,25},{... | collective-permute-start | bytes 786440 | tf_op jit(solution)/shard_map/ppermute | solution.py:48
  13.1 0.0 collective-permute-done.3
  13.2 0.0 collective-permute-done.4
  13.2 0.0 collective-permute-done.5
  13.2 1.3 %collective-permute-start.6 = (bf16[256,256]{1,0:T(8,128)(2,1)S(1)}, bf16[256,256]{1,0:T(8,128)(2,1)S(1)}, u32[]{:S(2)}, u32[]{:S(2)}) collective-permute-start(bf16[256,256]{1,0:T(8,128)(2,1)S(1)} %select_select_fusion.3), channel_id=1, source_target_pairs={{4,5},{6,7},{8,9},{10,11},{12,13},{14,15},{16,17},{18,19},{20,21},... | collective-permute-start | bytes 393224 | tf_op jit(solution)/shard_map/ppermute | solution.py:48
  14.5 0.0 collective-permute-done.9
  14.6 13.0 %collective-permute-done.6 = bf16[256,256]{1,0:T(8,128)(2,1)S(1)} collective-permute-done((bf16[256,256]{1,0:T(8,128)(2,1)S(1)}, bf16[256,256]{1,0:T(8,128)(2,1)S(1)}, u32[]{:S(2)}, u32[]{:S(2)}) %collective-permute-start.6) | collective-permute-done | bytes 131104 | tf_op jit(solution)/shard_map/ppermute | solution.py:48
  27.5 0.0 collective-permute-done.11
  27.5 1.1 %convolution_subtract_fusion = f32[256,512]{1,0:T(8,128)} fusion(f32[256,512]{1,0:T(8,128)S(1)} %copy-done, bf16[256,512]{1,0:T(8,128)(2,1)S(1)} %collective-permute-done.11, bf16[256,512]{1,0:T(8,128)(2,1)S(1)} %broadcast_select_fusion.1, bf16[256,256]{1,0:T(8,128)(2,1)S(1)} %broadcast_select_fusion.5, pred[]{:T(512)S(6)} %select_n.176, pred[]{:T(512)S(6)} %eq.78, ...), kind=kOutput, calls=%fused_computation.40 | convolution fusion | flops 67633152 | bytes 1966084 | tf_op jit(solution)/shard_map/dot_general | solution.py:144
  (13 shorter events, 0.3 us)
Async XLA Ops:
  0.1 7.1 %collective-permute-start = (bf16[256,512]{1,0:T(8,128)(2,1)S(1)}, bf16[256,512]{1,0:T(8,128)(2,1)S(1)}, u32[]{:S(2)}, u32[]{:S(2)}) collective-permute-start(bf16[256,512]{1,0:T(8,128)(2,1)S(1)} %get-tuple-element.100), channel_id=1, source_target_pairs={{0,16},{8,0},{12,4},{2,18},{1,5},{3,7}} | collective-permute-start | bytes 786440 | tf_op jit(solution)/shard_map/ppermute | solution.py:48
  1.4 7.2 %collective-permute-start.1 = (bf16[256,512]{1,0:T(8,128)(2,1)S(1)}, bf16[256,512]{1,0:T(8,128)(2,1)S(1)}, u32[]{:S(2)}, u32[]{:S(2)}) collective-permute-start(bf16[256,512]{1,0:T(8,128)(2,1)S(1)} %get-tuple-element.100), channel_id=1, source_target_pairs={{0,20},{24,16}} | collective-permute-start | bytes 786440 | tf_op jit(solution)/shard_map/ppermute | solution.py:48
  2.0 6.5 %collective-permute-start.2 = (bf16[256,512]{1,0:T(8,128)(2,1)S(1)}, bf16[256,512]{1,0:T(8,128)(2,1)S(1)}, u32[]{:S(2)}, u32[]{:S(2)}) collective-permute-start(bf16[256,512]{1,0:T(8,128)(2,1)S(1)} %get-tuple-element.100), channel_id=1, source_target_pairs={{0,4},{28,20}} | collective-permute-start | bytes 786440 | tf_op jit(solution)/shard_map/ppermute | solution.py:48
  2.7 0.7 %collective-permute-start.7 = (bf16[256,256]{1,0:T(8,128)(2,1)S(1)}, bf16[256,256]{1,0:T(8,128)(2,1)S(1)}, u32[]{:S(2)}, u32[]{:S(2)}) collective-permute-start(bf16[256,256]{1,0:T(8,128)(2,1)S(1)} %get-tuple-element.28), channel_id=1, source_target_pairs={{0,4}} | collective-permute-start | bytes 393224 | tf_op jit(solution)/shard_map/ppermute | solution.py:48
  3.5 5.1 %copy-start = (f32[256,512]{1,0:T(8,128)S(1)}, f32[256,512]{1,0:T(8,128)}, u32[]{:S(2)}) copy-start(f32[256,512]{1,0:T(8,128)} %param.5) | copy-start | bytes 1572868
  3.5 7.2 %collective-permute-start.8 = (bf16[256,256]{1,0:T(8,128)(2,1)S(1)}, bf16[256,256]{1,0:T(8,128)(2,1)S(1)}, u32[]{:S(2)}, u32[]{:S(2)}) collective-permute-start(bf16[256,256]{1,0:T(8,128)(2,1)S(1)} %broadcast_select_fusion.3), channel_id=1, source_target_pairs={{4,20},{0,16}} | collective-permute-start | bytes 393224 | tf_op jit(solution)/shard_map/ppermute | solution.py:48
  7.2 4.6 %collective-permute-start.10 = (bf16[256,512]{1,0:T(8,128)(2,1)S(1)}, bf16[256,512]{1,0:T(8,128)(2,1)S(1)}, u32[]{:S(2)}, u32[]{:S(2)}) collective-permute-start(bf16[256,512]{1,0:T(8,128)(2,1)S(1)} %broadcast_select_fusion), channel_id=1, source_target_pairs={{2,10},{18,26},{1,17},{3,19},{5,21},{7,23}} | collective-permute-start | bytes 786440 | tf_op jit(solution)/shard_map/ppermute | solution.py:48
  8.7 4.5 %collective-permute-start.4 = (bf16[256,256]{1,0:T(8,128)(2,1)S(1)}, bf16[256,256]{1,0:T(8,128)(2,1)S(1)}, u32[]{:S(2)}, u32[]{:S(2)}) collective-permute-start(bf16[256,256]{1,0:T(8,128)(2,1)S(1)} %get-tuple-element.27), channel_id=1, source_target_pairs={{0,8},{4,12},{16,24},{20,28}} | collective-permute-start | bytes 393224 | tf_op jit(solution)/shard_map/ppermute | solution.py:48
  9.4 3.8 %collective-permute-start.5 = (bf16[256,256]{1,0:T(8,128)(2,1)S(1)}, bf16[256,256]{1,0:T(8,128)(2,1)S(1)}, u32[]{:S(2)}, u32[]{:S(2)}) collective-permute-start(bf16[256,256]{1,0:T(8,128)(2,1)S(1)} %get-tuple-element.27), channel_id=1, source_target_pairs={{0,10},{4,14},{16,26},{20,30}} | collective-permute-start | bytes 393224 | tf_op jit(solution)/shard_map/ppermute | solution.py:48
  10.1 3.1 %collective-permute-start.3 = (bf16[256,256]{1,0:T(8,128)(2,1)S(1)}, bf16[256,256]{1,0:T(8,128)(2,1)S(1)}, u32[]{:S(2)}, u32[]{:S(2)}) collective-permute-start(bf16[256,256]{1,0:T(8,128)(2,1)S(1)} %get-tuple-element.26), channel_id=1, source_target_pairs={{16,18},{20,22},{4,6}} | collective-permute-start | bytes 393224 | tf_op jit(solution)/shard_map/ppermute | solution.py:48
  10.8 3.8 %collective-permute-start.9 = (bf16[256,256]{1,0:T(8,128)(2,1)S(1)}, bf16[256,256]{1,0:T(8,128)(2,1)S(1)}, u32[]{:S(2)}, u32[]{:S(2)}) collective-permute-start(bf16[256,256]{1,0:T(8,128)(2,1)S(1)} %broadcast_select_fusion.4), channel_id=1, source_target_pairs={{0,8},{4,12},{16,24},{20,28}} | collective-permute-start | bytes 393224 | tf_op jit(solution)/shard_map/ppermute | solution.py:48
  11.8 15.7 %collective-permute-start.11 = (bf16[256,512]{1,0:T(8,128)(2,1)S(1)}, bf16[256,512]{1,0:T(8,128)(2,1)S(1)}, u32[]{:S(2)}, u32[]{:S(2)}) collective-permute-start(bf16[256,512]{1,0:T(8,128)(2,1)S(1)} %broadcast_select_fusion.1), channel_id=1, source_target_pairs={{2,6},{18,22},{10,14},{26,30},{1,9},{3,11},{5,13},{7,15},{17,25},{... | collective-permute-start | bytes 786440 | tf_op jit(solution)/shard_map/ppermute | solution.py:48
  13.2 14.3 %collective-permute-start.6 = (bf16[256,256]{1,0:T(8,128)(2,1)S(1)}, bf16[256,256]{1,0:T(8,128)(2,1)S(1)}, u32[]{:S(2)}, u32[]{:S(2)}) collective-permute-start(bf16[256,256]{1,0:T(8,128)(2,1)S(1)} %select_select_fusion.3), channel_id=1, source_target_pairs={{4,5},{6,7},{8,9},{10,11},{12,13},{14,15},{16,17},{18,19},{20,21},... | collective-permute-start | bytes 393224 | tf_op jit(solution)/shard_map/ppermute | solution.py:48

commit v6 on v5

--- a/solution.py
+++ b/solution.py
@@ -81,31 +81,38 @@
         return jnp.where(jnp.where(col_here % 2 == 0, takes[0], takes[1]), got, value), got
 
     workers = [r for r in range(n_row) if r & APART == 0]
-    targets = workers[2:] + workers[1:2]
-    square = partner = first_sent
+    targets = workers[:1:-1]
+    upper, got = upper_step(upper, 0, first_sent, [((0, 0), (1, 0)), ((APART, 0), (0, 0))])
+    square = jnp.where(row_here == 1, got, first_sent)
+    partner = got
     for index, target in reversed(list(enumerate(targets))):
-        served = [0, targets[-1]] if index == 0 else [targets[index - 1]]
+        served = [1, targets[-1]] if index == 0 else [targets[index - 1]]
         pairs = [((0, 0), (target, 0))] + [((r + APART, 0), (r, 0)) for r in served]
-        if index == 0:
-            upper, got = upper_step(upper, 0, first_sent, pairs)
-        else:
-            got = send(first_sent, pairs)
+        got = send(first_sent, pairs)
         square = jnp.where(row_here == target, got, square)
         for r in served:
             partner = jnp.where(row_here == r, got, partner)
 
-    got = send(column_upper, [((0, 0), (1, 0))])
-    near_upper = jnp.where(row_here == 1, got, column_upper)
-    near_sent = near_upper
-    for target in reversed(targets[1:-1]):
-        pairs = [((1, 0), (target, 0))]
-        takes = row_here == target
-        if target == targets[1]:
-            pairs += [((0, 0), (targets[0], 0))]
-            takes = takes | (row_here == targets[0])
-        got = send(near_sent, pairs)
-        near_upper = jnp.where(takes, got, near_upper)
+    upper, column_upper = lax.optimization_barrier((upper, column_upper))
+    got = send(column_upper, [((0, 0), (APART, 0))])
+    near_first = jnp.where(row_here == APART, got, column_upper)
+    near_upper, near_held = near_first, [0, APART]
     upper, _ = upper_step(upper, 1, upper)
+
+    def send_both(value, pairs, hops):
+        nonlocal near_upper
+        hops = [hop for hop in hops if hop[1] < n_row]
+        if value is not None and near_first.shape != value.shape:
+            return send(value, pairs)
+        if value is None:
+            value = near_first
+        for row, _ in hops:
+            value = jnp.where((row_here == row) & (col_here == 0), near_first, value)
+        got = send(value, pairs + [((a, 0), (b, 0)) for a, b in hops])
+        for _, row in hops:
+            near_upper = jnp.where(row_here == row, got, near_upper)
+            near_held.append(row)
+        return got
 
     def compute(square, partner):
         columns = jnp.concatenate([matrix[:, :NB], summed(partner)], axis=0)
@@ -119,18 +126,28 @@
 
     working = (row_here & APART == 0) & (col_here == 0)
     lower, lower_far = lax.cond(working, compute, none, square, partner)
+
     received = lower
     for c in range(2, n_col, 2):
-        got = send(lower_far, [((r, 0), (r + APART, c)) for r in workers])
+        pairs = [((r, 0), (r + APART, c)) for r in workers]
+        got = send_both(lower_far, pairs, [(APART, 4)] if c == 2 else [])
         received = jnp.where((row_here & APART != 0) & (col_here == c), got, received)
-    got = send(lower_far, [((r, 0), (r + APART, 0)) for r in workers])
+    pairs = [((r, 0), (r + APART, 0)) for r in workers]
+    got = send_both(lower_far, pairs, [(APART, 5)])
     received = jnp.where((row_here & APART != 0) & (col_here == 0), got, received)
     for c in range(2, n_col, 2):
-        got = send(lower, [((r, 0), (r, c)) for r in targets])
+        pairs = [((r, 0), (r, c)) for r in workers[1:]]
+        got = send_both(lower, pairs, [(APART, 7), (0, 1)] if c == 2 else [])
         received = jnp.where((row_here & APART == 0) & (col_here == c), got, received)
-    near_sent, _ = lax.optimization_barrier((near_upper, lower))
-    got = send(near_sent, [((r, 0), (r + APART, 0)) for r in workers])
-    near_upper = jnp.where(row_here & APART != 0, got, near_upper)
+    near_first, _ = lax.optimization_barrier((near_first, lower))
+    send_both(None, [], [(APART, 6), (0, 3)])
+    while len(near_held) < n_row:
+        missing = [r for r in range(n_row) if r not in near_held]
+        hops = list(zip(near_held, missing))
+        got = send(near_upper, [((a, 0), (b, 0)) for a, b in hops])
+        for _, row in hops:
+            near_upper = jnp.where(row_here == row, got, near_upper)
+            near_held.append(row)
     for step in range(2, len(down)):
         upper, _ = upper_step(upper, step, upper)
     got = send(

time: 28.9 us -> 33.1 us (1.15)
  the two profiles are of different devices: /device:TPU:7 before, /device:TPU:3 now
where the time goes in v6:
time: 33.1 us; the launch traced here: 32.8 us
  waiting for transfers between devices  21.3 us (64%)
  starting transfers between devices  9.9 us (30%)
  matrix products  1.08 us (3%)
    ppermute x11, waiting for transfers between devices, send(): return lax.ppermute(value, ('row', 'col'), flat)  21.3 us
    ppermute x11, starting transfers between devices, send(): return lax.ppermute(value, ('row', 'col'), flat)  9.9 us
    dot_general x1, matrix products, shards(): return matrix - jnp.dot(received, upper, preferred_element_type=jnp.float32)  1.08 us
  transfers between devices with their start and end apart: 11, of which 3 were waited for; matrix products, arithmetic and copies ran while one was open for 1% of the time, Pallas kernels for 0%

profile of v6, /device:TPU:3, one launch (start us, length us, event | category | flops | bytes accessed | tf_op | source)
XLA Modules:
  0.0 32.8 jit_solution(15956741688047568954)
XLA Ops:
  0.1 1.3 %collective-permute-start = (bf16[256,512]{1,0:T(8,128)(2,1)S(1)}, bf16[256,512]{1,0:T(8,128)(2,1)S(1)}, u32[]{:S(2)}, u32[]{:S(2)}) collective-permute-start(bf16[256,512]{1,0:T(8,128)(2,1)S(1)} %get-tuple-element.92), channel_id=1, source_target_pairs={{0,4},{8,0},{2,18},{1,5},{3,7}} | collective-permute-start | bytes 786440 | tf_op jit(solution)/shard_map/ppermute | solution.py:48
  1.4 0.7 %collective-permute-start.2 = (bf16[256,512]{1,0:T(8,128)(2,1)S(1)}, bf16[256,512]{1,0:T(8,128)(2,1)S(1)}, u32[]{:S(2)}, u32[]{:S(2)}) collective-permute-start(bf16[256,512]{1,0:T(8,128)(2,1)S(1)} %get-tuple-element.92), channel_id=1, source_target_pairs={{0,20},{12,4},{24,16}} | collective-permute-start | bytes 786440 | tf_op jit(solution)/shard_map/ppermute | solution.py:48
  2.0 0.7 %collective-permute-start.3 = (bf16[256,512]{1,0:T(8,128)(2,1)S(1)}, bf16[256,512]{1,0:T(8,128)(2,1)S(1)}, u32[]{:S(2)}, u32[]{:S(2)}) collective-permute-start(bf16[256,512]{1,0:T(8,128)(2,1)S(1)} %get-tuple-element.92), channel_id=1, source_target_pairs={{0,16},{28,20}} | collective-permute-start | bytes 786440 | tf_op jit(solution)/shard_map/ppermute | solution.py:48
  2.8 0.0 copy-start
  2.8 6.3 %collective-permute-done = bf16[256,512]{1,0:T(8,128)(2,1)S(1)} collective-permute-done((bf16[256,512]{1,0:T(8,128)(2,1)S(1)}, bf16[256,512]{1,0:T(8,128)(2,1)S(1)}, u32[]{:S(2)}, u32[]{:S(2)}) %collective-permute-start) | collective-permute-done | bytes 262176 | tf_op jit(solution)/shard_map/ppermute | solution.py:48
  9.2 0.7 %collective-permute-start.1 = (bf16[256,256]{1,0:T(8,128)(2,1)S(1)}, bf16[256,256]{1,0:T(8,128)(2,1)S(1)}, u32[]{:S(2)}, u32[]{:S(2)}) collective-permute-start(bf16[256,256]{1,0:T(8,128)(2,1)S(1)} %get-tuple-element.29), channel_id=1, source_target_pairs={{0,8}} | collective-permute-start | bytes 393224 | tf_op jit(solution)/shard_map/ppermute | solution.py:48
  9.9 1.3 %collective-permute-start.9 = (bf16[256,512]{1,0:T(8,128)(2,1)S(1)}, bf16[256,512]{1,0:T(8,128)(2,1)S(1)}, u32[]{:S(2)}, u32[]{:S(2)}) collective-permute-start(bf16[256,512]{1,0:T(8,128)(2,1)S(1)} %broadcast_select_fusion.2), channel_id=1, source_target_pairs={{2,10},{18,26},{1,17},{3,19},{5,21},{7,23}} | collective-permute-start | bytes 786440 | tf_op jit(solution)/shard_map/ppermute | solution.py:48
  11.2 0.0 collective-permute-done.2
  11.2 0.0 collective-permute-done.3
  11.2 0.0 copy-done
  11.2 0.1 conditional.3
  11.3 0.0 collective-permute-done.1
  11.3 0.7 %collective-permute-start.5 = (bf16[256,256]{1,0:T(8,128)(2,1)S(1)}, bf16[256,256]{1,0:T(8,128)(2,1)S(1)}, u32[]{:S(2)}, u32[]{:S(2)}) collective-permute-start(bf16[256,256]{1,0:T(8,128)(2,1)S(1)} %get-tuple-element.97), channel_id=1, source_target_pairs={{0,8},{4,12},{16,24},{20,28},{8,20}} | collective-permute-start | bytes 393224 | tf_op jit(solution)/shard_map/ppermute | solution.py:48
  12.0 0.7 %collective-permute-start.6 = (bf16[256,256]{1,0:T(8,128)(2,1)S(1)}, bf16[256,256]{1,0:T(8,128)(2,1)S(1)}, u32[]{:S(2)}, u32[]{:S(2)}) collective-permute-start(bf16[256,256]{1,0:T(8,128)(2,1)S(1)} %get-tuple-element.97), channel_id=1, source_target_pairs={{0,10},{4,14},{16,26},{20,30},{8,16}} | collective-permute-start | bytes 393224 | tf_op jit(solution)/shard_map/ppermute | solution.py:48
  12.7 0.7 %collective-permute-start.8 = (bf16[256,256]{1,0:T(8,128)(2,1)S(1)}, bf16[256,256]{1,0:T(8,128)(2,1)S(1)}, u32[]{:S(2)}, u32[]{:S(2)}) collective-permute-start(bf16[256,256]{1,0:T(8,128)(2,1)S(1)} %get-tuple-element.32), channel_id=1, source_target_pairs={{8,24},{0,12}} | collective-permute-start | bytes 393224 | tf_op jit(solution)/shard_map/ppermute | solution.py:48
  13.4 0.7 %collective-permute-start.4 = (bf16[256,256]{1,0:T(8,128)(2,1)S(1)}, bf16[256,256]{1,0:T(8,128)(2,1)S(1)}, u32[]{:S(2)}, u32[]{:S(2)}) collective-permute-start(bf16[256,256]{1,0:T(8,128)(2,1)S(1)} %select_select_fusion.4), channel_id=1, source_target_pairs={{4,6},{16,18},{20,22},{8,28},{0,4}} | collective-permute-start | bytes 393224 | tf_op jit(solution)/shard_map/ppermute | solution.py:48
  14.1 0.4 %collective-permute-done.9 = bf16[256,512]{1,0:T(8,128)(2,1)S(1)} collective-permute-done((bf16[256,512]{1,0:T(8,128)(2,1)S(1)}, bf16[256,512]{1,0:T(8,128)(2,1)S(1)}, u32[]{:S(2)}, u32[]{:S(2)}) %collective-permute-start.9) | collective-permute-done | bytes 262176 | tf_op jit(solution)/shard_map/ppermute | solution.py:48
  14.5 1.3 %collective-permute-start.10 = (bf16[256,512]{1,0:T(8,128)(2,1)S(1)}, bf16[256,512]{1,0:T(8,128)(2,1)S(1)}, u32[]{:S(2)}, u32[]{:S(2)}) collective-permute-start(bf16[256,512]{1,0:T(8,128)(2,1)S(1)} %broadcast_select_fusion), channel_id=1, source_target_pairs={{2,6},{18,22},{10,14},{26,30},{1,9},{3,11},{5,13},{7,15},{17,25},{... | collective-permute-start | bytes 786440 | tf_op jit(solution)/shard_map/ppermute | solution.py:48
  15.8 0.0 collective-permute-done.8
  15.8 0.0 collective-permute-done.4
  15.9 0.0 collective-permute-done.5
  15.9 0.0 collective-permute-done.6
  15.9 0.1 select_select_fusion.5
  15.9 1.3 %collective-permute-start.7 = (bf16[256,256]{1,0:T(8,128)(2,1)S(1)}, bf16[256,256]{1,0:T(8,128)(2,1)S(1)}, u32[]{:S(2)}, u32[]{:S(2)}) collective-permute-start(bf16[256,256]{1,0:T(8,128)(2,1)S(1)} %get-tuple-element.107), channel_id=1, source_target_pairs={{4,5},{6,7},{8,9},{10,11},{12,13},{14,15},{16,17},{18,19},{20,21},... | collective-permute-start | bytes 393224 | tf_op jit(solution)/shard_map/ppermute | solution.py:48
  17.3 14.5 %collective-permute-done.7 = bf16[256,256]{1,0:T(8,128)(2,1)S(1)} collective-permute-done((bf16[256,256]{1,0:T(8,128)(2,1)S(1)}, bf16[256,256]{1,0:T(8,128)(2,1)S(1)}, u32[]{:S(2)}, u32[]{:S(2)}) %collective-permute-start.7) | collective-permute-done | bytes 131104 | tf_op jit(solution)/shard_map/ppermute | solution.py:48
  31.7 0.0 collective-permute-done.10
  31.8 1.1 %convolution_subtract_fusion = f32[256,512]{1,0:T(8,128)} fusion(f32[256,512]{1,0:T(8,128)S(1)} %copy-done, bf16[256,512]{1,0:T(8,128)(2,1)S(1)} %collective-permute-done.10, bf16[256,512]{1,0:T(8,128)(2,1)S(1)} %broadcast_select_fusion, bf16[256,256]{1,0:T(8,128)(2,1)S(1)} %get-tuple-element.108, pred[]{:T(512)S(6)} %select_n.234, pred[]{:T(512)S(6)} %eq.101, ...), kind=kOutput, calls=%fused_computation.39 | convolution fusion | flops 67633152 | bytes 1966084 | tf_op jit(solution)/shard_map/dot_general | solution.py:161
  (10 shorter events, 0.2 us)
Async XLA Ops:
  0.1 9.1 %collective-permute-start = (bf16[256,512]{1,0:T(8,128)(2,1)S(1)}, bf16[256,512]{1,0:T(8,128)(2,1)S(1)}, u32[]{:S(2)}, u32[]{:S(2)}) collective-permute-start(bf16[256,512]{1,0:T(8,128)(2,1)S(1)} %get-tuple-element.92), channel_id=1, source_target_pairs={{0,4},{8,0},{2,18},{1,5},{3,7}} | collective-permute-start | bytes 786440 | tf_op jit(solution)/shard_map/ppermute | solution.py:48
  1.4 9.9 %collective-permute-start.2 = (bf16[256,512]{1,0:T(8,128)(2,1)S(1)}, bf16[256,512]{1,0:T(8,128)(2,1)S(1)}, u32[]{:S(2)}, u32[]{:S(2)}) collective-permute-start(bf16[256,512]{1,0:T(8,128)(2,1)S(1)} %get-tuple-element.92), channel_id=1, source_target_pairs={{0,20},{12,4},{24,16}} | collective-permute-start | bytes 786440 | tf_op jit(solution)/shard_map/ppermute | solution.py:48
  2.0 9.2 %collective-permute-start.3 = (bf16[256,512]{1,0:T(8,128)(2,1)S(1)}, bf16[256,512]{1,0:T(8,128)(2,1)S(1)}, u32[]{:S(2)}, u32[]{:S(2)}) collective-permute-start(bf16[256,512]{1,0:T(8,128)(2,1)S(1)} %get-tuple-element.92), channel_id=1, source_target_pairs={{0,16},{28,20}} | collective-permute-start | bytes 786440 | tf_op jit(solution)/shard_map/ppermute | solution.py:48
  2.8 8.4 %copy-start = (f32[256,512]{1,0:T(8,128)S(1)}, f32[256,512]{1,0:T(8,128)}, u32[]{:S(2)}) copy-start(f32[256,512]{1,0:T(8,128)} %param.5) | copy-start | bytes 1572868
  9.2 2.1 %collective-permute-start.1 = (bf16[256,256]{1,0:T(8,128)(2,1)S(1)}, bf16[256,256]{1,0:T(8,128)(2,1)S(1)}, u32[]{:S(2)}, u32[]{:S(2)}) collective-permute-start(bf16[256,256]{1,0:T(8,128)(2,1)S(1)} %get-tuple-element.29), channel_id=1, source_target_pairs={{0,8}} | collective-permute-start | bytes 393224 | tf_op jit(solution)/shard_map/ppermute | solution.py:48
  9.9 4.6 %collective-permute-start.9 = (bf16[256,512]{1,0:T(8,128)(2,1)S(1)}, bf16[256,512]{1,0:T(8,128)(2,1)S(1)}, u32[]{:S(2)}, u32[]{:S(2)}) collective-permute-start(bf16[256,512]{1,0:T(8,128)(2,1)S(1)} %broadcast_select_fusion.2), channel_id=1, source_target_pairs={{2,10},{18,26},{1,17},{3,19},{5,21},{7,23}} | collective-permute-start | bytes 786440 | tf_op jit(solution)/shard_map/ppermute | solution.py:48
  11.3 4.5 %collective-permute-start.5 = (bf16[256,256]{1,0:T(8,128)(2,1)S(1)}, bf16[256,256]{1,0:T(8,128)(2,1)S(1)}, u32[]{:S(2)}, u32[]{:S(2)}) collective-permute-start(bf16[256,256]{1,0:T(8,128)(2,1)S(1)} %get-tuple-element.97), channel_id=1, source_target_pairs={{0,8},{4,12},{16,24},{20,28},{8,20}} | collective-permute-start | bytes 393224 | tf_op jit(solution)/shard_map/ppermute | solution.py:48
  12.0 3.8 %collective-permute-start.6 = (bf16[256,256]{1,0:T(8,128)(2,1)S(1)}, bf16[256,256]{1,0:T(8,128)(2,1)S(1)}, u32[]{:S(2)}, u32[]{:S(2)}) collective-permute-start(bf16[256,256]{1,0:T(8,128)(2,1)S(1)} %get-tuple-element.97), channel_id=1, source_target_pairs={{0,10},{4,14},{16,26},{20,30},{8,16}} | collective-permute-start | bytes 393224 | tf_op jit(solution)/shard_map/ppermute | solution.py:48
  12.7 3.1 %collective-permute-start.8 = (bf16[256,256]{1,0:T(8,128)(2,1)S(1)}, bf16[256,256]{1,0:T(8,128)(2,1)S(1)}, u32[]{:S(2)}, u32[]{:S(2)}) collective-permute-start(bf16[256,256]{1,0:T(8,128)(2,1)S(1)} %get-tuple-element.32), channel_id=1, source_target_pairs={{8,24},{0,12}} | collective-permute-start | bytes 393224 | tf_op jit(solution)/shard_map/ppermute | solution.py:48
  13.4 2.4 %collective-permute-start.4 = (bf16[256,256]{1,0:T(8,128)(2,1)S(1)}, bf16[256,256]{1,0:T(8,128)(2,1)S(1)}, u32[]{:S(2)}, u32[]{:S(2)}) collective-permute-start(bf16[256,256]{1,0:T(8,128)(2,1)S(1)} %select_select_fusion.4), channel_id=1, source_target_pairs={{4,6},{16,18},{20,22},{8,28},{0,4}} | collective-permute-start | bytes 393224 | tf_op jit(solution)/shard_map/ppermute | solution.py:48
  14.5 17.2 %collective-permute-start.10 = (bf16[256,512]{1,0:T(8,128)(2,1)S(1)}, bf16[256,512]{1,0:T(8,128)(2,1)S(1)}, u32[]{:S(2)}, u32[]{:S(2)}) collective-permute-start(bf16[256,512]{1,0:T(8,128)(2,1)S(1)} %broadcast_select_fusion), channel_id=1, source_target_pairs={{2,6},{18,22},{10,14},{26,30},{1,9},{3,11},{5,13},{7,15},{17,25},{... | collective-permute-start | bytes 786440 | tf_op jit(solution)/shard_map/ppermute | solution.py:48
  15.9 15.8 %collective-permute-start.7 = (bf16[256,256]{1,0:T(8,128)(2,1)S(1)}, bf16[256,256]{1,0:T(8,128)(2,1)S(1)}, u32[]{:S(2)}, u32[]{:S(2)}) collective-permute-start(bf16[256,256]{1,0:T(8,128)(2,1)S(1)} %get-tuple-element.107), channel_id=1, source_target_pairs={{4,5},{6,7},{8,9},{10,11},{12,13},{14,15},{16,17},{18,19},{20,21},... | collective-permute-start | bytes 393224 | tf_op jit(solution)/shard_map/ppermute | solution.py:48

commit v7 on v4

--- a/solution.py
+++ b/solution.py
@@ -49,45 +49,47 @@
     upper = lax.optimization_barrier(jnp.where(row_here == 0, first_upper, 0))
 
     down = strides(n_row)
-    orders = [down, [down[-1]] + down[:-1]]
-    held = [[0], [0]]
+    orders = [[down[-1]] + down[:-1], down, down[:1] + down[-1:] + down[1:-1]]
+    kinds = [2 if c == 1 else c % 2 for c in range(n_col)]
+    kind_here = jnp.where(col_here == 1, 2, col_here % 2)
+    held = [[0], [0], [0]]
 
     def upper_step(value, step, sent, pairs=()):
         pairs = list(pairs)
-        takes = []
-        for kind in range(2):
+        takes = jnp.bool_(False)
+        for kind in range(3):
             stride = orders[kind][step]
             missing = sum(orders[kind][step + 1 :])
-            takes.append((row_here & (stride | missing)) == stride)
+            takes = takes | ((kind_here == kind) & ((row_here & (stride | missing)) == stride))
             pairs += [
-                ((h, c), (h + stride, c)) for h in held[kind] for c in range(1, n_col) if c % 2 == kind
+                ((h, c), (h + stride, c))
+                for h in held[kind]
+                for c in range(1, n_col)
+                if kinds[c] == kind
             ]
             held[kind] = held[kind] + [h + stride for h in held[kind]]
         got = send(sent, pairs)
-        return jnp.where(jnp.where(col_here % 2 == 0, takes[0], takes[1]), got, value), got
+        return jnp.where(takes, got, value), got
 
     workers = [r for r in range(n_row) if r & APART == 0]
-    targets = workers[2:] + workers[1:2]
+    targets = workers[1:2] + workers[:1:-1]
     square, partner = matrix[:, :NB], matrix[:, :NB]
     passed, got = upper_step(upper, 0, first_upper, [((0, 0), (1, 0))])
     near_upper = jnp.where(row_here == 1, got[:, NB:], upper[:, NB:])
     upper = passed
     for index, target in reversed(list(enumerate(targets))):
-        served = [0, targets[-1]] if index == 0 else [targets[index - 1]]
+        served = [targets[index - 1]] if index else [0]
+        if index == 1:
+            served += targets[-1:]
         pairs = [((0, 0), (target, 0))] + [((r + APART, 0), (r, 0)) for r in served]
         got = send(pivot_columns, pairs)
         square = jnp.where(row_here == target, got, square)
         for r in served:
             partner = jnp.where(row_here == r, got, partner)
     near_sent = near_upper
-    for target in reversed(targets[:-1]):
-        pairs = [((1, 0), (target, 0))]
-        takes = row_here == target
-        if target == targets[-2]:
-            pairs += [((0, 0), (APART, 0))]
-            takes = takes | (row_here == APART)
-        got = send(near_sent, pairs)
-        near_upper = jnp.where(takes, got, near_upper)
+    for target in targets[1:]:
+        got = send(near_sent, [((1, 0), (target, 0))])
+        near_upper = jnp.where(row_here == target, got, near_upper)
     upper, _ = upper_step(upper, 1, upper)
 
     def compute(square, partner):
@@ -111,8 +113,8 @@
         got = send(lower, [((r, 0), (r, c)) for r in targets])
         received = jnp.where((row_here & APART == 0) & (col_here == c), got, received)
     near_sent, _ = lax.optimization_barrier((near_upper, lower))
-    got = send(near_sent, [((r, 0), (r + APART, 0)) for r in workers[1:]])
-    near_upper = jnp.where((row_here & APART != 0) & (row_here != APART), got, near_upper)
+    got = send(near_sent, [((r, 0), (r + APART, 0)) for r in workers])
+    near_upper = jnp.where(row_here & APART != 0, got, near_upper)
     for step in range(2, len(down)):
         upper, _ = upper_step(upper, step, upper)
     got = send(

time: 27.1 us -> 27.3 us (level)
  the two profiles are of different devices: /device:TPU:11 before, /device:TPU:21 now
where the time goes in v7:
time: 27.3 us; the launch traced here: 26.9 us
  waiting for transfers between devices  13.8 us (51%)
  starting transfers between devices  11.2 us (41%)
  matrix products  1.07 us (4%)
  between operations  0.39 us (1%)
    ppermute x13, waiting for transfers between devices, send(): return lax.ppermute(value, ('row', 'col'), flat)  13.8 us
    ppermute x13, starting transfers between devices, send(): return lax.ppermute(value, ('row', 'col'), flat)  11.2 us
    dot_general x1, matrix products, shards(): return matrix - jnp.dot(received, upper, preferred_element_type=jnp.float32)  1.07 us
  transfers between devices with their start and end apart: 13, of which 3 were waited for; matrix products, arithmetic and copies ran while one was open for 1% of the time, Pallas kernels for 0%

profile of v7, /device:TPU:21, one launch (start us, length us, event | category | flops | bytes accessed | tf_op | source)
XLA Modules:
  0.0 26.9 jit_solution(10789894335203114293)
XLA Ops:
  0.0 0.1 conditional.2
  0.1 1.3 %collective-permute-start.7 = (bf16[256,512]{1,0:T(8,128)(2,1)S(1)}, bf16[256,512]{1,0:T(8,128)(2,1)S(1)}, u32[]{:S(2)}, u32[]{:S(2)}) collective-permute-start(bf16[256,512]{1,0:T(8,128)(2,1)S(1)} %get-tuple-element.23), channel_id=1, source_target_pairs={{0,4},{2,6},{3,19},{1,17}} | collective-permute-start | bytes 786440 | tf_op jit(solution)/shard_map/ppermute | solution.py:37
  1.4 0.7 %collective-permute-start = (f32[256,256]{1,0:T(8,128)S(1)}, f32[256,256]{1,0:T(8,128)S(1)}, u32[]{:S(2)}, u32[]{:S(2)}) collective-permute-start(f32[256,256]{1,0:T(8,128)S(1)} %get-tuple-element.20), channel_id=1, source_target_pairs={{0,4},{8,0}} | collective-permute-start | bytes 786440 | tf_op jit(solution)/shard_map/ppermute | solution.py:37
  2.0 0.7 %collective-permute-start.1 = (f32[256,256]{1,0:T(8,128)S(1)}, f32[256,256]{1,0:T(8,128)S(1)}, u32[]{:S(2)}, u32[]{:S(2)}) collective-permute-start(f32[256,256]{1,0:T(8,128)S(1)} %get-tuple-element.20), channel_id=1, source_target_pairs={{0,20},{12,4},{24,16}} | collective-permute-start | bytes 786440 | tf_op jit(solution)/shard_map/ppermute | solution.py:37
  2.7 0.7 %collective-permute-start.2 = (f32[256,256]{1,0:T(8,128)S(1)}, f32[256,256]{1,0:T(8,128)S(1)}, u32[]{:S(2)}, u32[]{:S(2)}) collective-permute-start(f32[256,256]{1,0:T(8,128)S(1)} %get-tuple-element.20), channel_id=1, source_target_pairs={{0,16},{28,20}} | collective-permute-start | bytes 786440 | tf_op jit(solution)/shard_map/ppermute | solution.py:37
  3.5 0.0 copy-start
  3.5 4.6 %collective-permute-done.7 = bf16[256,512]{1,0:T(8,128)(2,1)S(1)} collective-permute-done((bf16[256,512]{1,0:T(8,128)(2,1)S(1)}, bf16[256,512]{1,0:T(8,128)(2,1)S(1)}, u32[]{:S(2)}, u32[]{:S(2)}) %collective-permute-start.7) | collective-permute-done | bytes 262176 | tf_op jit(solution)/shard_map/ppermute | solution.py:37
  8.1 0.7 %collective-permute-start.8 = (bf16[256,256]{1,0:T(8,128)(2,1)S(1)}, bf16[256,256]{1,0:T(8,128)(2,1)S(1)}, u32[]{:S(2)}, u32[]{:S(2)}) collective-permute-start(bf16[256,256]{1,0:T(8,128)(2,1)S(1)} %slice_select_fusion), channel_id=1, source_target_pairs={{4,16}} | collective-permute-start | bytes 393224 | tf_op jit(solution)/shard_map/ppermute | solution.py:37
  8.8 0.7 %collective-permute-start.9 = (bf16[256,256]{1,0:T(8,128)(2,1)S(1)}, bf16[256,256]{1,0:T(8,128)(2,1)S(1)}, u32[]{:S(2)}, u32[]{:S(2)}) collective-permute-start(bf16[256,256]{1,0:T(8,128)(2,1)S(1)} %slice_select_fusion), channel_id=1, source_target_pairs={{4,20}} | collective-permute-start | bytes 393224 | tf_op jit(solution)/shard_map/ppermute | solution.py:37
  9.5 0.0 collective-permute-done
  9.5 1.3 %collective-permute-start.11 = (bf16[256,512]{1,0:T(8,128)(2,1)S(1)}, bf16[256,512]{1,0:T(8,128)(2,1)S(1)}, u32[]{:S(2)}, u32[]{:S(2)}) collective-permute-start(bf16[256,512]{1,0:T(8,128)(2,1)S(1)} %broadcast_select_fusion), channel_id=1, source_target_pairs={{2,18},{6,22},{3,11},{19,27},{1,5},{17,21}} | collective-permute-start | bytes 786440 | tf_op jit(solution)/shard_map/ppermute | solution.py:37
  10.8 0.0 copy-done
  10.9 0.0 collective-permute-done.1
  10.9 0.0 collective-permute-done.2
  11.0 0.1 conditional.3
  11.1 0.7 %collective-permute-start.4 = (bf16[256,256]{1,0:T(8,128)(2,1)S(1)}, bf16[256,256]{1,0:T(8,128)(2,1)S(1)}, u32[]{:S(2)}, u32[]{:S(2)}) collective-permute-start(bf16[256,256]{1,0:T(8,128)(2,1)S(1)} %get-tuple-element.22), channel_id=1, source_target_pairs={{0,8},{4,12},{16,24},{20,28}} | collective-permute-start | bytes 393224 | tf_op jit(solution)/shard_map/ppermute | solution.py:37
  11.8 0.7 %collective-permute-start.5 = (bf16[256,256]{1,0:T(8,128)(2,1)S(1)}, bf16[256,256]{1,0:T(8,128)(2,1)S(1)}, u32[]{:S(2)}, u32[]{:S(2)}) collective-permute-start(bf16[256,256]{1,0:T(8,128)(2,1)S(1)} %get-tuple-element.22), channel_id=1, source_target_pairs={{0,10},{4,14},{16,26},{20,30}} | collective-permute-start | bytes 393224 | tf_op jit(solution)/shard_map/ppermute | solution.py:37
  12.4 0.0 collective-permute-done.8
  12.5 0.7 %collective-permute-start.3 = (bf16[256,256]{1,0:T(8,128)(2,1)S(1)}, bf16[256,256]{1,0:T(8,128)(2,1)S(1)}, u32[]{:S(2)}, u32[]{:S(2)}) collective-permute-start(bf16[256,256]{1,0:T(8,128)(2,1)S(1)} %get-tuple-element.21), channel_id=1, source_target_pairs={{4,6},{20,22},{16,18}} | collective-permute-start | bytes 393224 | tf_op jit(solution)/shard_map/ppermute | solution.py:37
  13.1 0.0 collective-permute-done.9
  13.2 0.7 %collective-permute-start.10 = (bf16[256,256]{1,0:T(8,128)(2,1)S(1)}, bf16[256,256]{1,0:T(8,128)(2,1)S(1)}, u32[]{:S(2)}, u32[]{:S(2)}) collective-permute-start(bf16[256,256]{1,0:T(8,128)(2,1)S(1)} %select_select_fusion.2), channel_id=1, source_target_pairs={{0,8},{4,12},{16,24},{20,28}} | collective-permute-start | bytes 393224 | tf_op jit(solution)/shard_map/ppermute | solution.py:37
  13.8 0.2 collective-permute-done.11
  14.1 1.3 %collective-permute-start.12 = (bf16[256,512]{1,0:T(8,128)(2,1)S(1)}, bf16[256,512]{1,0:T(8,128)(2,1)S(1)}, u32[]{:S(2)}, u32[]{:S(2)}) collective-permute-start(bf16[256,512]{1,0:T(8,128)(2,1)S(1)} %broadcast_select_fusion.1), channel_id=1, source_target_pairs={{2,10},{6,14},{18,26},{22,30},{3,7},{19,23},{11,15},{27,31},{1,9},... | collective-permute-start | bytes 786440 | tf_op jit(solution)/shard_map/ppermute | solution.py:37
  15.4 0.0 collective-permute-done.3
  15.5 0.0 collective-permute-done.4
  15.5 0.0 collective-permute-done.5
  15.5 1.3 %collective-permute-start.6 = (bf16[256,256]{1,0:T(8,128)(2,1)S(1)}, bf16[256,256]{1,0:T(8,128)(2,1)S(1)}, u32[]{:S(2)}, u32[]{:S(2)}) collective-permute-start(bf16[256,256]{1,0:T(8,128)(2,1)S(1)} %select_select_fusion.3), channel_id=1, source_target_pairs={{4,5},{6,7},{8,9},{10,11},{12,13},{14,15},{16,17},{18,19},{20,21},... | collective-permute-start | bytes 393224 | tf_op jit(solution)/shard_map/ppermute | solution.py:37
  16.8 0.0 collective-permute-done.10
  16.9 9.0 %collective-permute-done.6 = bf16[256,256]{1,0:T(8,128)(2,1)S(1)} collective-permute-done((bf16[256,256]{1,0:T(8,128)(2,1)S(1)}, bf16[256,256]{1,0:T(8,128)(2,1)S(1)}, u32[]{:S(2)}, u32[]{:S(2)}) %collective-permute-start.6) | collective-permute-done | bytes 131104 | tf_op jit(solution)/shard_map/ppermute | solution.py:37
  25.8 0.0 collective-permute-done.12
  25.8 1.1 %convolution_subtract_fusion = f32[256,512]{1,0:T(8,128)} fusion(f32[256,512]{1,0:T(8,128)S(1)} %copy-done, bf16[256,512]{1,0:T(8,128)(2,1)S(1)} %collective-permute-done.12, bf16[256,512]{1,0:T(8,128)(2,1)S(1)} %broadcast_select_fusion.1, bf16[256,256]{1,0:T(8,128)(2,1)S(1)} %broadcast_select_fusion.3, pred[]{:T(512)S(6)} %or.23, pred[]{:T(512)S(6)} %eq.93, ...), kind=kOutput, calls=%fused_computation.34 | convolution fusion | flops 67633152 | bytes 1966084 | tf_op jit(solution)/shard_map/dot_general | solution.py:128
  (15 shorter events, 0.3 us)
Async XLA Ops:
  0.1 8.0 %collective-permute-start.7 = (bf16[256,512]{1,0:T(8,128)(2,1)S(1)}, bf16[256,512]{1,0:T(8,128)(2,1)S(1)}, u32[]{:S(2)}, u32[]{:S(2)}) collective-permute-start(bf16[256,512]{1,0:T(8,128)(2,1)S(1)} %get-tuple-element.23), channel_id=1, source_target_pairs={{0,4},{2,6},{3,19},{1,17}} | collective-permute-start | bytes 786440 | tf_op jit(solution)/shard_map/ppermute | solution.py:37
  1.4 8.1 %collective-permute-start = (f32[256,256]{1,0:T(8,128)S(1)}, f32[256,256]{1,0:T(8,128)S(1)}, u32[]{:S(2)}, u32[]{:S(2)}) collective-permute-start(f32[256,256]{1,0:T(8,128)S(1)} %get-tuple-element.20), channel_id=1, source_target_pairs={{0,4},{8,0}} | collective-permute-start | bytes 786440 | tf_op jit(solution)/shard_map/ppermute | solution.py:37
  2.0 8.9 %collective-permute-start.1 = (f32[256,256]{1,0:T(8,128)S(1)}, f32[256,256]{1,0:T(8,128)S(1)}, u32[]{:S(2)}, u32[]{:S(2)}) collective-permute-start(f32[256,256]{1,0:T(8,128)S(1)} %get-tuple-element.20), channel_id=1, source_target_pairs={{0,20},{12,4},{24,16}} | collective-permute-start | bytes 786440 | tf_op jit(solution)/shard_map/ppermute | solution.py:37
  2.7 8.2 %collective-permute-start.2 = (f32[256,256]{1,0:T(8,128)S(1)}, f32[256,256]{1,0:T(8,128)S(1)}, u32[]{:S(2)}, u32[]{:S(2)}) collective-permute-start(f32[256,256]{1,0:T(8,128)S(1)} %get-tuple-element.20), channel_id=1, source_target_pairs={{0,16},{28,20}} | collective-permute-start | bytes 786440 | tf_op jit(solution)/shard_map/ppermute | solution.py:37
  3.5 7.3 %copy-start = (f32[256,512]{1,0:T(8,128)S(1)}, f32[256,512]{1,0:T(8,128)}, u32[]{:S(2)}) copy-start(f32[256,512]{1,0:T(8,128)} %param.5) | copy-start | bytes 1572868
  8.1 4.4 %collective-permute-start.8 = (bf16[256,256]{1,0:T(8,128)(2,1)S(1)}, bf16[256,256]{1,0:T(8,128)(2,1)S(1)}, u32[]{:S(2)}, u32[]{:S(2)}) collective-permute-start(bf16[256,256]{1,0:T(8,128)(2,1)S(1)} %slice_select_fusion), channel_id=1, source_target_pairs={{4,16}} | collective-permute-start | bytes 393224 | tf_op jit(solution)/shard_map/ppermute | solution.py:37
  8.8 4.4 %collective-permute-start.9 = (bf16[256,256]{1,0:T(8,128)(2,1)S(1)}, bf16[256,256]{1,0:T(8,128)(2,1)S(1)}, u32[]{:S(2)}, u32[]{:S(2)}) collective-permute-start(bf16[256,256]{1,0:T(8,128)(2,1)S(1)} %slice_select_fusion), channel_id=1, source_target_pairs={{4,20}} | collective-permute-start | bytes 393224 | tf_op jit(solution)/shard_map/ppermute | solution.py:37
  9.5 4.6 %collective-permute-start.11 = (bf16[256,512]{1,0:T(8,128)(2,1)S(1)}, bf16[256,512]{1,0:T(8,128)(2,1)S(1)}, u32[]{:S(2)}, u32[]{:S(2)}) collective-permute-start(bf16[256,512]{1,0:T(8,128)(2,1)S(1)} %broadcast_select_fusion), channel_id=1, source_target_pairs={{2,18},{6,22},{3,11},{19,27},{1,5},{17,21}} | collective-permute-start | bytes 786440 | tf_op jit(solution)/shard_map/ppermute | solution.py:37
  11.1 4.4 %collective-permute-start.4 = (bf16[256,256]{1,0:T(8,128)(2,1)S(1)}, bf16[256,256]{1,0:T(8,128)(2,1)S(1)}, u32[]{:S(2)}, u32[]{:S(2)}) collective-permute-start(bf16[256,256]{1,0:T(8,128)(2,1)S(1)} %get-tuple-element.22), channel_id=1, source_target_pairs={{0,8},{4,12},{16,24},{20,28}} | collective-permute-start | bytes 393224 | tf_op jit(solution)/shard_map/ppermute | solution.py:37
  11.8 3.7 %collective-permute-start.5 = (bf16[256,256]{1,0:T(8,128)(2,1)S(1)}, bf16[256,256]{1,0:T(8,128)(2,1)S(1)}, u32[]{:S(2)}, u32[]{:S(2)}) collective-permute-start(bf16[256,256]{1,0:T(8,128)(2,1)S(1)} %get-tuple-element.22), channel_id=1, source_target_pairs={{0,10},{4,14},{16,26},{20,30}} | collective-permute-start | bytes 393224 | tf_op jit(solution)/shard_map/ppermute | solution.py:37
  12.5 3.0 %collective-permute-start.3 = (bf16[256,256]{1,0:T(8,128)(2,1)S(1)}, bf16[256,256]{1,0:T(8,128)(2,1)S(1)}, u32[]{:S(2)}, u32[]{:S(2)}) collective-permute-start(bf16[256,256]{1,0:T(8,128)(2,1)S(1)} %get-tuple-element.21), channel_id=1, source_target_pairs={{4,6},{20,22},{16,18}} | collective-permute-start | bytes 393224 | tf_op jit(solution)/shard_map/ppermute | solution.py:37
  13.2 3.6 %collective-permute-start.10 = (bf16[256,256]{1,0:T(8,128)(2,1)S(1)}, bf16[256,256]{1,0:T(8,128)(2,1)S(1)}, u32[]{:S(2)}, u32[]{:S(2)}) collective-permute-start(bf16[256,256]{1,0:T(8,128)(2,1)S(1)} %select_select_fusion.2), channel_id=1, source_target_pairs={{0,8},{4,12},{16,24},{20,28}} | collective-permute-start | bytes 393224 | tf_op jit(solution)/shard_map/ppermute | solution.py:37
  14.1 11.7 %collective-permute-start.12 = (bf16[256,512]{1,0:T(8,128)(2,1)S(1)}, bf16[256,512]{1,0:T(8,128)(2,1)S(1)}, u32[]{:S(2)}, u32[]{:S(2)}) collective-permute-start(bf16[256,512]{1,0:T(8,128)(2,1)S(1)} %broadcast_select_fusion.1), channel_id=1, source_target_pairs={{2,10},{6,14},{18,26},{22,30},{3,7},{19,23},{11,15},{27,31},{1,9},... | collective-permute-start | bytes 786440 | tf_op jit(solution)/shard_map/ppermute | solution.py:37
  15.5 10.3 %collective-permute-start.6 = (bf16[256,256]{1,0:T(8,128)(2,1)S(1)}, bf16[256,256]{1,0:T(8,128)(2,1)S(1)}, u32[]{:S(2)}, u32[]{:S(2)}) collective-permute-start(bf16[256,256]{1,0:T(8,128)(2,1)S(1)} %select_select_fusion.3), channel_id=1, source_target_pairs={{4,5},{6,7},{8,9},{10,11},{12,13},{14,15},{16,17},{18,19},{20,21},... | collective-permute-start | bytes 393224 | tf_op jit(solution)/shard_map/ppermute | solution.py:37

commit v8 on v7

--- a/solution.py
+++ b/solution.py
@@ -72,22 +72,21 @@
         return jnp.where(takes, got, value), got
 
     workers = [r for r in range(n_row) if r & APART == 0]
-    targets = workers[1:2] + workers[:1:-1]
+    targets = workers[:1:-1]
+    targets.insert(1, 1)
     square, partner = matrix[:, :NB], matrix[:, :NB]
     passed, got = upper_step(upper, 0, first_upper, [((0, 0), (1, 0))])
     near_upper = jnp.where(row_here == 1, got[:, NB:], upper[:, NB:])
     upper = passed
     for index, target in reversed(list(enumerate(targets))):
-        served = [targets[index - 1]] if index else [0]
-        if index == 1:
-            served += targets[-1:]
+        served = [] if index > 1 else targets[:1] if index else [0] + targets[1:]
         pairs = [((0, 0), (target, 0))] + [((r + APART, 0), (r, 0)) for r in served]
         got = send(pivot_columns, pairs)
         square = jnp.where(row_here == target, got, square)
         for r in served:
             partner = jnp.where(row_here == r, got, partner)
     near_sent = near_upper
-    for target in targets[1:]:
+    for target in workers[2:]:
         got = send(near_sent, [((1, 0), (target, 0))])
         near_upper = jnp.where(row_here == target, got, near_upper)
     upper, _ = upper_step(upper, 1, upper)

time: 27.3 us -> 27.4 us (level)
  the two profiles are of different devices: /device:TPU:21 before, /device:TPU:15 now
where the time goes in v8:
time: 27.4 us; the launch traced here: 27 us
  waiting for transfers between devices  15.1 us (55%)
  starting transfers between devices  10.1 us (37%)
  matrix products  1.07 us (4%)
  between operations  0.41 us (1%)
    ppermute x13, waiting for transfers between devices, send(): return lax.ppermute(value, ('row', 'col'), flat)  15.1 us
    ppermute x13, starting transfers between devices, send(): return lax.ppermute(value, ('row', 'col'), flat)  10.1 us
    dot_general x1, matrix products, shards(): return matrix - jnp.dot(received, upper, preferred_element_type=jnp.float32)  1.07 us
  transfers between devices with their start and end apart: 13, of which 1 were waited for; matrix products, arithmetic and copies ran while one was open for 1% of the time, Pallas kernels for 0%

profile of v8, /device:TPU:15, one launch (start us, length us, event | category | flops | bytes accessed | tf_op | source)
XLA Modules:
  0.0 27.0 jit_solution(9564128989287384185)
XLA Ops:
  0.0 0.1 conditional.2
  0.1 0.7 %collective-permute-start.7 = (bf16[256,512]{1,0:T(8,128)(2,1)S(1)}, bf16[256,512]{1,0:T(8,128)(2,1)S(1)}, u32[]{:S(2)}, u32[]{:S(2)}) collective-permute-start(bf16[256,512]{1,0:T(8,128)(2,1)S(1)} %get-tuple-element.23), channel_id=1, source_target_pairs={{0,4},{2,6},{3,19},{1,17}} | collective-permute-start | bytes 786440 | tf_op jit(solution)/shard_map/ppermute | solution.py:37
  0.7 0.7 %collective-permute-start = (f32[256,256]{1,0:T(8,128)S(1)}, f32[256,256]{1,0:T(8,128)S(1)}, u32[]{:S(2)}, u32[]{:S(2)}) collective-permute-start(f32[256,256]{1,0:T(8,128)S(1)} %get-tuple-element.20), channel_id=1, source_target_pairs={{0,20},{8,0},{12,4},{24,16}} | collective-permute-start | bytes 786440 | tf_op jit(solution)/shard_map/ppermute | solution.py:37
  1.4 0.7 %collective-permute-start.1 = (f32[256,256]{1,0:T(8,128)S(1)}, f32[256,256]{1,0:T(8,128)S(1)}, u32[]{:S(2)}, u32[]{:S(2)}) collective-permute-start(f32[256,256]{1,0:T(8,128)S(1)} %get-tuple-element.20), channel_id=1, source_target_pairs={{0,4},{28,20}} | collective-permute-start | bytes 786440 | tf_op jit(solution)/shard_map/ppermute | solution.py:37
  2.1 0.7 %collective-permute-start.2 = (f32[256,256]{1,0:T(8,128)S(1)}, f32[256,256]{1,0:T(8,128)S(1)}, u32[]{:S(2)}, u32[]{:S(2)}) collective-permute-start(f32[256,256]{1,0:T(8,128)S(1)} %get-tuple-element.20), channel_id=1, source_target_pairs={{0,16}} | collective-permute-start | bytes 786440 | tf_op jit(solution)/shard_map/ppermute | solution.py:37
  2.9 0.0 copy-start
  2.9 0.0 collective-permute-done.7
  2.9 0.8 %collective-permute-start.8 = (bf16[256,256]{1,0:T(8,128)(2,1)S(1)}, bf16[256,256]{1,0:T(8,128)(2,1)S(1)}, u32[]{:S(2)}, u32[]{:S(2)}) collective-permute-start(bf16[256,256]{1,0:T(8,128)(2,1)S(1)} %slice_select_fusion), channel_id=1, source_target_pairs={{4,20}} | collective-permute-start | bytes 393224 | tf_op jit(solution)/shard_map/ppermute | solution.py:37
  3.7 0.7 %collective-permute-start.9 = (bf16[256,256]{1,0:T(8,128)(2,1)S(1)}, bf16[256,256]{1,0:T(8,128)(2,1)S(1)}, u32[]{:S(2)}, u32[]{:S(2)}) collective-permute-start(bf16[256,256]{1,0:T(8,128)(2,1)S(1)} %slice_select_fusion), channel_id=1, source_target_pairs={{4,16}} | collective-permute-start | bytes 393224 | tf_op jit(solution)/shard_map/ppermute | solution.py:37
  4.5 0.0 collective-permute-done
  4.5 0.7 %collective-permute-start.11 = (bf16[256,512]{1,0:T(8,128)(2,1)S(1)}, bf16[256,512]{1,0:T(8,128)(2,1)S(1)}, u32[]{:S(2)}, u32[]{:S(2)}) collective-permute-start(bf16[256,512]{1,0:T(8,128)(2,1)S(1)} %broadcast_select_fusion), channel_id=1, source_target_pairs={{2,18},{6,22},{3,11},{19,27},{1,5},{17,21}} | collective-permute-start | bytes 786440 | tf_op jit(solution)/shard_map/ppermute | solution.py:37
  5.2 0.0 copy-done
  5.3 0.0 collective-permute-done.1
  5.3 0.0 collective-permute-done.2
  5.3 0.1 conditional.3
  5.4 0.7 %collective-permute-start.4 = (bf16[256,256]{1,0:T(8,128)(2,1)S(1)}, bf16[256,256]{1,0:T(8,128)(2,1)S(1)}, u32[]{:S(2)}, u32[]{:S(2)}) collective-permute-start(bf16[256,256]{1,0:T(8,128)(2,1)S(1)} %get-tuple-element.22), channel_id=1, source_target_pairs={{0,8},{4,12},{16,24},{20,28}} | collective-permute-start | bytes 393224 | tf_op jit(solution)/shard_map/ppermute | solution.py:37
  6.1 0.7 %collective-permute-start.5 = (bf16[256,256]{1,0:T(8,128)(2,1)S(1)}, bf16[256,256]{1,0:T(8,128)(2,1)S(1)}, u32[]{:S(2)}, u32[]{:S(2)}) collective-permute-start(bf16[256,256]{1,0:T(8,128)(2,1)S(1)} %get-tuple-element.22), channel_id=1, source_target_pairs={{0,10},{4,14},{16,26},{20,30}} | collective-permute-start | bytes 393224 | tf_op jit(solution)/shard_map/ppermute | solution.py:37
  6.8 0.0 collective-permute-done.8
  6.8 0.7 %collective-permute-start.3 = (bf16[256,256]{1,0:T(8,128)(2,1)S(1)}, bf16[256,256]{1,0:T(8,128)(2,1)S(1)}, u32[]{:S(2)}, u32[]{:S(2)}) collective-permute-start(bf16[256,256]{1,0:T(8,128)(2,1)S(1)} %get-tuple-element.21), channel_id=1, source_target_pairs={{20,22},{4,6},{16,18}} | collective-permute-start | bytes 393224 | tf_op jit(solution)/shard_map/ppermute | solution.py:37
  7.4 0.0 collective-permute-done.9
  7.5 0.7 %collective-permute-start.10 = (bf16[256,256]{1,0:T(8,128)(2,1)S(1)}, bf16[256,256]{1,0:T(8,128)(2,1)S(1)}, u32[]{:S(2)}, u32[]{:S(2)}) collective-permute-start(bf16[256,256]{1,0:T(8,128)(2,1)S(1)} %select_select_fusion.2), channel_id=1, source_target_pairs={{0,8},{4,12},{16,24},{20,28}} | collective-permute-start | bytes 393224 | tf_op jit(solution)/shard_map/ppermute | solution.py:37
  8.2 0.0 collective-permute-done.11
  8.2 1.3 %collective-permute-start.12 = (bf16[256,512]{1,0:T(8,128)(2,1)S(1)}, bf16[256,512]{1,0:T(8,128)(2,1)S(1)}, u32[]{:S(2)}, u32[]{:S(2)}) collective-permute-start(bf16[256,512]{1,0:T(8,128)(2,1)S(1)} %broadcast_select_fusion.1), channel_id=1, source_target_pairs={{2,10},{6,14},{18,26},{22,30},{3,7},{19,23},{11,15},{27,31},{1,9},... | collective-permute-start | bytes 786440 | tf_op jit(solution)/shard_map/ppermute | solution.py:37
  9.5 0.0 collective-permute-done.3
  9.5 0.0 collective-permute-done.4
  9.5 0.0 collective-permute-done.5
  9.6 1.3 %collective-permute-start.6 = (bf16[256,256]{1,0:T(8,128)(2,1)S(1)}, bf16[256,256]{1,0:T(8,128)(2,1)S(1)}, u32[]{:S(2)}, u32[]{:S(2)}) collective-permute-start(bf16[256,256]{1,0:T(8,128)(2,1)S(1)} %select_select_fusion.3), channel_id=1, source_target_pairs={{4,5},{6,7},{8,9},{10,11},{12,13},{14,15},{16,17},{18,19},{20,21},... | collective-permute-start | bytes 393224 | tf_op jit(solution)/shard_map/ppermute | solution.py:37
  10.9 0.0 collective-permute-done.10
  10.9 15.0 %collective-permute-done.6 = bf16[256,256]{1,0:T(8,128)(2,1)S(1)} collective-permute-done((bf16[256,256]{1,0:T(8,128)(2,1)S(1)}, bf16[256,256]{1,0:T(8,128)(2,1)S(1)}, u32[]{:S(2)}, u32[]{:S(2)}) %collective-permute-start.6) | collective-permute-done | bytes 131104 | tf_op jit(solution)/shard_map/ppermute | solution.py:37
  26.0 0.0 collective-permute-done.12
  26.0 1.1 %convolution_subtract_fusion = f32[256,512]{1,0:T(8,128)} fusion(f32[256,512]{1,0:T(8,128)S(1)} %copy-done, bf16[256,512]{1,0:T(8,128)(2,1)S(1)} %collective-permute-done.12, bf16[256,512]{1,0:T(8,128)(2,1)S(1)} %broadcast_select_fusion.1, bf16[256,256]{1,0:T(8,128)(2,1)S(1)} %broadcast_select_fusion.3, pred[]{:T(512)S(6)} %or.23, pred[]{:T(512)S(6)} %eq.93, ...), kind=kOutput, calls=%fused_computation.34 | convolution fusion | flops 67633152 | bytes 1966084 | tf_op jit(solution)/shard_map/dot_general | solution.py:127
  (14 shorter events, 0.3 us)
Async XLA Ops:
  0.1 2.8 %collective-permute-start.7 = (bf16[256,512]{1,0:T(8,128)(2,1)S(1)}, bf16[256,512]{1,0:T(8,128)(2,1)S(1)}, u32[]{:S(2)}, u32[]{:S(2)}) collective-permute-start(bf16[256,512]{1,0:T(8,128)(2,1)S(1)} %get-tuple-element.23), channel_id=1, source_target_pairs={{0,4},{2,6},{3,19},{1,17}} | collective-permute-start | bytes 786440 | tf_op jit(solution)/shard_map/ppermute | solution.py:37
  0.7 3.7 %collective-permute-start = (f32[256,256]{1,0:T(8,128)S(1)}, f32[256,256]{1,0:T(8,128)S(1)}, u32[]{:S(2)}, u32[]{:S(2)}) collective-permute-start(f32[256,256]{1,0:T(8,128)S(1)} %get-tuple-element.20), channel_id=1, source_target_pairs={{0,20},{8,0},{12,4},{24,16}} | collective-permute-start | bytes 786440 | tf_op jit(solution)/shard_map/ppermute | solution.py:37
  1.4 3.8 %collective-permute-start.1 = (f32[256,256]{1,0:T(8,128)S(1)}, f32[256,256]{1,0:T(8,128)S(1)}, u32[]{:S(2)}, u32[]{:S(2)}) collective-permute-start(f32[256,256]{1,0:T(8,128)S(1)} %get-tuple-element.20), channel_id=1, source_target_pairs={{0,4},{28,20}} | collective-permute-start | bytes 786440 | tf_op jit(solution)/shard_map/ppermute | solution.py:37
  2.1 3.2 %collective-permute-start.2 = (f32[256,256]{1,0:T(8,128)S(1)}, f32[256,256]{1,0:T(8,128)S(1)}, u32[]{:S(2)}, u32[]{:S(2)}) collective-permute-start(f32[256,256]{1,0:T(8,128)S(1)} %get-tuple-element.20), channel_id=1, source_target_pairs={{0,16}} | collective-permute-start | bytes 786440 | tf_op jit(solution)/shard_map/ppermute | solution.py:37
  2.9 2.3 %copy-start = (f32[256,512]{1,0:T(8,128)S(1)}, f32[256,512]{1,0:T(8,128)}, u32[]{:S(2)}) copy-start(f32[256,512]{1,0:T(8,128)} %param.5) | copy-start | bytes 1572868
  2.9 3.8 %collective-permute-start.8 = (bf16[256,256]{1,0:T(8,128)(2,1)S(1)}, bf16[256,256]{1,0:T(8,128)(2,1)S(1)}, u32[]{:S(2)}, u32[]{:S(2)}) collective-permute-start(bf16[256,256]{1,0:T(8,128)(2,1)S(1)} %slice_select_fusion), channel_id=1, source_target_pairs={{4,20}} | collective-permute-start | bytes 393224 | tf_op jit(solution)/shard_map/ppermute | solution.py:37
  3.7 3.7 %collective-permute-start.9 = (bf16[256,256]{1,0:T(8,128)(2,1)S(1)}, bf16[256,256]{1,0:T(8,128)(2,1)S(1)}, u32[]{:S(2)}, u32[]{:S(2)}) collective-permute-start(bf16[256,256]{1,0:T(8,128)(2,1)S(1)} %slice_select_fusion), channel_id=1, source_target_pairs={{4,16}} | collective-permute-start | bytes 393224 | tf_op jit(solution)/shard_map/ppermute | solution.py:37
  4.5 3.7 %collective-permute-start.11 = (bf16[256,512]{1,0:T(8,128)(2,1)S(1)}, bf16[256,512]{1,0:T(8,128)(2,1)S(1)}, u32[]{:S(2)}, u32[]{:S(2)}) collective-permute-start(bf16[256,512]{1,0:T(8,128)(2,1)S(1)} %broadcast_select_fusion), channel_id=1, source_target_pairs={{2,18},{6,22},{3,11},{19,27},{1,5},{17,21}} | collective-permute-start | bytes 786440 | tf_op jit(solution)/shard_map/ppermute | solution.py:37
  5.4 4.1 %collective-permute-start.4 = (bf16[256,256]{1,0:T(8,128)(2,1)S(1)}, bf16[256,256]{1,0:T(8,128)(2,1)S(1)}, u32[]{:S(2)}, u32[]{:S(2)}) collective-permute-start(bf16[256,256]{1,0:T(8,128)(2,1)S(1)} %get-tuple-element.22), channel_id=1, source_target_pairs={{0,8},{4,12},{16,24},{20,28}} | collective-permute-start | bytes 393224 | tf_op jit(solution)/shard_map/ppermute | solution.py:37
  6.1 3.5 %collective-permute-start.5 = (bf16[256,256]{1,0:T(8,128)(2,1)S(1)}, bf16[256,256]{1,0:T(8,128)(2,1)S(1)}, u32[]{:S(2)}, u32[]{:S(2)}) collective-permute-start(bf16[256,256]{1,0:T(8,128)(2,1)S(1)} %get-tuple-element.22), channel_id=1, source_target_pairs={{0,10},{4,14},{16,26},{20,30}} | collective-permute-start | bytes 393224 | tf_op jit(solution)/shard_map/ppermute | solution.py:37
  6.8 2.7 %collective-permute-start.3 = (bf16[256,256]{1,0:T(8,128)(2,1)S(1)}, bf16[256,256]{1,0:T(8,128)(2,1)S(1)}, u32[]{:S(2)}, u32[]{:S(2)}) collective-permute-start(bf16[256,256]{1,0:T(8,128)(2,1)S(1)} %get-tuple-element.21), channel_id=1, source_target_pairs={{20,22},{4,6},{16,18}} | collective-permute-start | bytes 393224 | tf_op jit(solution)/shard_map/ppermute | solution.py:37
  7.5 3.4 %collective-permute-start.10 = (bf16[256,256]{1,0:T(8,128)(2,1)S(1)}, bf16[256,256]{1,0:T(8,128)(2,1)S(1)}, u32[]{:S(2)}, u32[]{:S(2)}) collective-permute-start(bf16[256,256]{1,0:T(8,128)(2,1)S(1)} %select_select_fusion.2), channel_id=1, source_target_pairs={{0,8},{4,12},{16,24},{20,28}} | collective-permute-start | bytes 393224 | tf_op jit(solution)/shard_map/ppermute | solution.py:37
  8.2 17.8 %collective-permute-start.12 = (bf16[256,512]{1,0:T(8,128)(2,1)S(1)}, bf16[256,512]{1,0:T(8,128)(2,1)S(1)}, u32[]{:S(2)}, u32[]{:S(2)}) collective-permute-start(bf16[256,512]{1,0:T(8,128)(2,1)S(1)} %broadcast_select_fusion.1), channel_id=1, source_target_pairs={{2,10},{6,14},{18,26},{22,30},{3,7},{19,23},{11,15},{27,31},{1,9},... | collective-permute-start | bytes 786440 | tf_op jit(solution)/shard_map/ppermute | solution.py:37
  9.6 16.4 %collective-permute-start.6 = (bf16[256,256]{1,0:T(8,128)(2,1)S(1)}, bf16[256,256]{1,0:T(8,128)(2,1)S(1)}, u32[]{:S(2)}, u32[]{:S(2)}) collective-permute-start(bf16[256,256]{1,0:T(8,128)(2,1)S(1)} %select_select_fusion.3), channel_id=1, source_target_pairs={{4,5},{6,7},{8,9},{10,11},{12,13},{14,15},{16,17},{18,19},{20,21},... | collective-permute-start | bytes 393224 | tf_op jit(solution)/shard_map/ppermute | solution.py:37

commit v9 on v7

--- a/solution.py
+++ b/solution.py
@@ -54,8 +54,8 @@
     kind_here = jnp.where(col_here == 1, 2, col_here % 2)
     held = [[0], [0], [0]]
 
-    def upper_step(value, step, sent, pairs=()):
-        pairs = list(pairs)
+    def upper_step(value, step, sent):
+        pairs = []
         takes = jnp.bool_(False)
         for kind in range(3):
             stride = orders[kind][step]
@@ -69,14 +69,13 @@
             ]
             held[kind] = held[kind] + [h + stride for h in held[kind]]
         got = send(sent, pairs)
-        return jnp.where(takes, got, value), got
+        return jnp.where(takes, got, value)
 
     workers = [r for r in range(n_row) if r & APART == 0]
     targets = workers[1:2] + workers[:1:-1]
     square, partner = matrix[:, :NB], matrix[:, :NB]
-    passed, got = upper_step(upper, 0, first_upper, [((0, 0), (1, 0))])
-    near_upper = jnp.where(row_here == 1, got[:, NB:], upper[:, NB:])
-    upper = passed
+    near_upper = upper[:, NB:]
+    upper = upper_step(upper, 0, first_upper)
     for index, target in reversed(list(enumerate(targets))):
         served = [targets[index - 1]] if index else [0]
         if index == 1:
@@ -86,11 +85,19 @@
         square = jnp.where(row_here == target, got, square)
         for r in served:
             partner = jnp.where(row_here == r, got, partner)
+    def near_step(near, sent, hops):
+        got = send(sent, [((a, 0), (b, 0)) for a, b in hops])
+        near_held.extend([b for _, b in hops])
+        for _, row in hops:
+            near = jnp.where(row_here == row, got, near)
+        return near
+
+    near_held = [0]
     near_sent = near_upper
-    for target in targets[1:]:
-        got = send(near_sent, [((1, 0), (target, 0))])
-        near_upper = jnp.where(row_here == target, got, near_upper)
-    upper, _ = upper_step(upper, 1, upper)
+    for row in (down[0], 1):
+        near_upper = near_step(near_upper, near_sent, [(0, row)])
+    near_held = [0, 1, down[0]]
+    upper = upper_step(upper, 1, upper)
 
     def compute(square, partner):
         both = multipliers(square, jnp.concatenate([matrix[:, :NB], partner], axis=0))
@@ -113,10 +120,15 @@
         got = send(lower, [((r, 0), (r, c)) for r in targets])
         received = jnp.where((row_here & APART == 0) & (col_here == c), got, received)
     near_sent, _ = lax.optimization_barrier((near_upper, lower))
-    got = send(near_sent, [((r, 0), (r + APART, 0)) for r in workers])
-    near_upper = jnp.where(row_here & APART != 0, got, near_upper)
+    hops = [(0, APART), (1, n_row - 1), (down[0], down[0] + APART)]
+    near_upper = near_step(near_upper, near_sent, hops)
+    while len(near_held) < n_row:
+        missing = [r for r in range(n_row) if r not in near_held]
+        if len(missing) > 2:
+            near_sent = near_upper
+        near_upper = near_step(near_upper, near_sent, list(zip(near_held, missing)))
     for step in range(2, len(down)):
-        upper, _ = upper_step(upper, step, upper)
+        upper = upper_step(upper, step, upper)
     got = send(
         received, [((r, c), (r, c + 1)) for r in range(1, n_row) for c in range(0, n_col, 2)]
     )

time: 27.3 us -> 32 us (1.17)
  the two profiles are of different devices: /device:TPU:21 before, /device:TPU:28 now
where the time goes in v9:
time: 32 us; the launch traced here: 31.6 us
  waiting for transfers between devices  18.3 us (57%)
  starting transfers between devices  11.4 us (36%)
  matrix products  1.07 us (3%)
  between operations  0.43 us (1%)
    ppermute x14, waiting for transfers between devices, send(): return lax.ppermute(value, ('row', 'col'), flat)  18.3 us
    ppermute x14, starting transfers between devices, send(): return lax.ppermute(value, ('row', 'col'), flat)  11.4 us
    dot_general x1, matrix products, shards(): return matrix - jnp.dot(received, upper, preferred_element_type=jnp.float32)  1.07 us
  transfers between devices with their start and end apart: 14, of which 3 were waited for; matrix products, arithmetic and copies ran while one was open for 1% of the time, Pallas kernels for 0%

profile of v9, /device:TPU:28, one launch (start us, length us, event | category | flops | bytes accessed | tf_op | source)
XLA Modules:
  0.0 31.6 jit_solution(17877827010014809769)
XLA Ops:
  0.0 0.1 conditional.2
  0.1 0.7 %collective-permute-start.11 = (bf16[256,512]{1,0:T(8,128)(2,1)S(1)}, bf16[256,512]{1,0:T(8,128)(2,1)S(1)}, u32[]{:S(2)}, u32[]{:S(2)}) collective-permute-start(bf16[256,512]{1,0:T(8,128)(2,1)S(1)} %get-tuple-element.23), channel_id=1, source_target_pairs={{2,6},{3,19},{1,17}} | collective-permute-start | bytes 786440 | tf_op jit(solution)/shard_map/ppermute | solution.py:37
  0.7 0.7 %collective-permute-start = (f32[256,256]{1,0:T(8,128)S(1)}, f32[256,256]{1,0:T(8,128)S(1)}, u32[]{:S(2)}, u32[]{:S(2)}) collective-permute-start(f32[256,256]{1,0:T(8,128)S(1)} %get-tuple-element.20), channel_id=1, source_target_pairs={{0,4},{8,0}} | collective-permute-start | bytes 786440 | tf_op jit(solution)/shard_map/ppermute | solution.py:37
  1.4 0.7 %collective-permute-start.1 = (f32[256,256]{1,0:T(8,128)S(1)}, f32[256,256]{1,0:T(8,128)S(1)}, u32[]{:S(2)}, u32[]{:S(2)}) collective-permute-start(f32[256,256]{1,0:T(8,128)S(1)} %get-tuple-element.20), channel_id=1, source_target_pairs={{0,20},{12,4},{24,16}} | collective-permute-start | bytes 786440 | tf_op jit(solution)/shard_map/ppermute | solution.py:37
  2.1 0.7 %collective-permute-start.2 = (f32[256,256]{1,0:T(8,128)S(1)}, f32[256,256]{1,0:T(8,128)S(1)}, u32[]{:S(2)}, u32[]{:S(2)}) collective-permute-start(f32[256,256]{1,0:T(8,128)S(1)} %get-tuple-element.20), channel_id=1, source_target_pairs={{0,16},{28,20}} | collective-permute-start | bytes 786440 | tf_op jit(solution)/shard_map/ppermute | solution.py:37
  2.8 0.0 copy-start
  2.9 0.8 %collective-permute-start.7 = (bf16[256,256]{1,0:T(8,128)(2,1)S(1)}, bf16[256,256]{1,0:T(8,128)(2,1)S(1)}, u32[]{:S(2)}, u32[]{:S(2)}) collective-permute-start(bf16[256,256]{1,0:T(8,128)(2,1)S(1)} %slice.36), channel_id=1, source_target_pairs={{0,4}} | collective-permute-start | bytes 393224 | tf_op jit(solution)/shard_map/ppermute | solution.py:37
  3.7 0.0 collective-permute-done.11
  3.7 0.7 %collective-permute-start.8 = (bf16[256,256]{1,0:T(8,128)(2,1)S(1)}, bf16[256,256]{1,0:T(8,128)(2,1)S(1)}, u32[]{:S(2)}, u32[]{:S(2)}) collective-permute-start(bf16[256,256]{1,0:T(8,128)(2,1)S(1)} %slice.36), channel_id=1, source_target_pairs={{0,16}} | collective-permute-start | bytes 393224 | tf_op jit(solution)/shard_map/ppermute | solution.py:37
  4.4 0.0 collective-permute-done.7
  4.4 0.7 %collective-permute-start.12 = (bf16[256,512]{1,0:T(8,128)(2,1)S(1)}, bf16[256,512]{1,0:T(8,128)(2,1)S(1)}, u32[]{:S(2)}, u32[]{:S(2)}) collective-permute-start(bf16[256,512]{1,0:T(8,128)(2,1)S(1)} %broadcast_select_fusion), channel_id=1, source_target_pairs={{2,18},{6,22},{3,11},{19,27},{1,5},{17,21}} | collective-permute-start | bytes 786440 | tf_op jit(solution)/shard_map/ppermute | solution.py:37
  5.1 0.0 copy-done
  5.2 0.0 collective-permute-done.8
  5.3 0.0 collective-permute-done
  5.3 0.0 collective-permute-done.1
  5.3 0.0 collective-permute-done.2
  5.4 0.1 conditional.3
  5.5 0.7 %collective-permute-start.4 = (bf16[256,256]{1,0:T(8,128)(2,1)S(1)}, bf16[256,256]{1,0:T(8,128)(2,1)S(1)}, u32[]{:S(2)}, u32[]{:S(2)}) collective-permute-start(bf16[256,256]{1,0:T(8,128)(2,1)S(1)} %get-tuple-element.22), channel_id=1, source_target_pairs={{0,8},{4,12},{16,24},{20,28}} | collective-permute-start | bytes 393224 | tf_op jit(solution)/shard_map/ppermute | solution.py:37
  6.1 1.3 %collective-permute-start.5 = (bf16[256,256]{1,0:T(8,128)(2,1)S(1)}, bf16[256,256]{1,0:T(8,128)(2,1)S(1)}, u32[]{:S(2)}, u32[]{:S(2)}) collective-permute-start(bf16[256,256]{1,0:T(8,128)(2,1)S(1)} %get-tuple-element.22), channel_id=1, source_target_pairs={{0,10},{4,14},{16,26},{20,30}} | collective-permute-start | bytes 393224 | tf_op jit(solution)/shard_map/ppermute | solution.py:37
  7.4 0.7 %collective-permute-start.3 = (bf16[256,256]{1,0:T(8,128)(2,1)S(1)}, bf16[256,256]{1,0:T(8,128)(2,1)S(1)}, u32[]{:S(2)}, u32[]{:S(2)}) collective-permute-start(bf16[256,256]{1,0:T(8,128)(2,1)S(1)} %get-tuple-element.21), channel_id=1, source_target_pairs={{4,6},{20,22},{16,18}} | collective-permute-start | bytes 393224 | tf_op jit(solution)/shard_map/ppermute | solution.py:37
  8.1 0.7 %collective-permute-start.10 = (bf16[256,256]{1,0:T(8,128)(2,1)S(1)}, bf16[256,256]{1,0:T(8,128)(2,1)S(1)}, u32[]{:S(2)}, u32[]{:S(2)}) collective-permute-start(bf16[256,256]{1,0:T(8,128)(2,1)S(1)} %select_select_fusion.4), channel_id=1, source_target_pairs={{0,8},{4,28},{16,24}} | collective-permute-start | bytes 393224 | tf_op jit(solution)/shard_map/ppermute | solution.py:37
  8.8 0.0 collective-permute-done.12
  8.8 0.7 %collective-permute-start.9 = (bf16[256,256]{1,0:T(8,128)(2,1)S(1)}, bf16[256,256]{1,0:T(8,128)(2,1)S(1)}, u32[]{:S(2)}, u32[]{:S(2)}) collective-permute-start(bf16[256,256]{1,0:T(8,128)(2,1)S(1)} %select_select_fusion.4), channel_id=1, source_target_pairs={{0,12},{4,20}} | collective-permute-start | bytes 393224 | tf_op jit(solution)/shard_map/ppermute | solution.py:37
  9.5 0.0 collective-permute-done.3
  9.5 1.3 %collective-permute-start.13 = (bf16[256,512]{1,0:T(8,128)(2,1)S(1)}, bf16[256,512]{1,0:T(8,128)(2,1)S(1)}, u32[]{:S(2)}, u32[]{:S(2)}) collective-permute-start(bf16[256,512]{1,0:T(8,128)(2,1)S(1)} %broadcast_select_fusion.1), channel_id=1, source_target_pairs={{2,10},{6,14},{18,26},{22,30},{3,7},{19,23},{11,15},{27,31},{1,9},... | collective-permute-start | bytes 786440 | tf_op jit(solution)/shard_map/ppermute | solution.py:37
  10.8 0.0 collective-permute-done.4
  10.8 12.3 %collective-permute-done.5 = bf16[256,256]{1,0:T(8,128)(2,1)S(1)} collective-permute-done((bf16[256,256]{1,0:T(8,128)(2,1)S(1)}, bf16[256,256]{1,0:T(8,128)(2,1)S(1)}, u32[]{:S(2)}, u32[]{:S(2)}) %collective-permute-start.5) | collective-permute-done | bytes 131104 | tf_op jit(solution)/shard_map/ppermute | solution.py:37
  23.2 1.3 %collective-permute-start.6 = (bf16[256,256]{1,0:T(8,128)(2,1)S(1)}, bf16[256,256]{1,0:T(8,128)(2,1)S(1)}, u32[]{:S(2)}, u32[]{:S(2)}) collective-permute-start(bf16[256,256]{1,0:T(8,128)(2,1)S(1)} %select_select_fusion.5), channel_id=1, source_target_pairs={{4,5},{6,7},{8,9},{10,11},{12,13},{14,15},{16,17},{18,19},{20,21},... | collective-permute-start | bytes 393224 | tf_op jit(solution)/shard_map/ppermute | solution.py:37
  24.5 0.0 collective-permute-done.10
  24.5 0.0 collective-permute-done.9
  24.5 0.9 %collective-permute-done.6 = bf16[256,256]{1,0:T(8,128)(2,1)S(1)} collective-permute-done((bf16[256,256]{1,0:T(8,128)(2,1)S(1)}, bf16[256,256]{1,0:T(8,128)(2,1)S(1)}, u32[]{:S(2)}, u32[]{:S(2)}) %collective-permute-start.6) | collective-permute-done | bytes 131104 | tf_op jit(solution)/shard_map/ppermute | solution.py:37
  25.4 5.1 %collective-permute-done.13 = bf16[256,512]{1,0:T(8,128)(2,1)S(1)} collective-permute-done((bf16[256,512]{1,0:T(8,128)(2,1)S(1)}, bf16[256,512]{1,0:T(8,128)(2,1)S(1)}, u32[]{:S(2)}, u32[]{:S(2)}) %collective-permute-start.13) | collective-permute-done | bytes 262176 | tf_op jit(solution)/shard_map/ppermute | solution.py:37
  30.5 1.1 %convolution_subtract_fusion = f32[256,512]{1,0:T(8,128)} fusion(f32[256,512]{1,0:T(8,128)S(1)} %copy-done, bf16[256,512]{1,0:T(8,128)(2,1)S(1)} %collective-permute-done.13, bf16[256,512]{1,0:T(8,128)(2,1)S(1)} %broadcast_select_fusion.1, bf16[256,256]{1,0:T(8,128)(2,1)S(1)} %select_select_fusion.2, pred[]{:T(512)S(6)} %or.23, pred[]{:T(512)S(6)} %eq.105, ...), kind=kOutput, calls=%fused_computation.34 | convolution fusion | flops 67633152 | bytes 1966084 | tf_op jit(solution)/shard_map/dot_general | solution.py:140
  (15 shorter events, 0.3 us)
Async XLA Ops:
  0.1 3.6 %collective-permute-start.11 = (bf16[256,512]{1,0:T(8,128)(2,1)S(1)}, bf16[256,512]{1,0:T(8,128)(2,1)S(1)}, u32[]{:S(2)}, u32[]{:S(2)}) collective-permute-start(bf16[256,512]{1,0:T(8,128)(2,1)S(1)} %get-tuple-element.23), channel_id=1, source_target_pairs={{2,6},{3,19},{1,17}} | collective-permute-start | bytes 786440 | tf_op jit(solution)/shard_map/ppermute | solution.py:37
  0.7 4.5 %collective-permute-start = (f32[256,256]{1,0:T(8,128)S(1)}, f32[256,256]{1,0:T(8,128)S(1)}, u32[]{:S(2)}, u32[]{:S(2)}) collective-permute-start(f32[256,256]{1,0:T(8,128)S(1)} %get-tuple-element.20), channel_id=1, source_target_pairs={{0,4},{8,0}} | collective-permute-start | bytes 786440 | tf_op jit(solution)/shard_map/ppermute | solution.py:37
  1.4 3.9 %collective-permute-start.1 = (f32[256,256]{1,0:T(8,128)S(1)}, f32[256,256]{1,0:T(8,128)S(1)}, u32[]{:S(2)}, u32[]{:S(2)}) collective-permute-start(f32[256,256]{1,0:T(8,128)S(1)} %get-tuple-element.20), channel_id=1, source_target_pairs={{0,20},{12,4},{24,16}} | collective-permute-start | bytes 786440 | tf_op jit(solution)/shard_map/ppermute | solution.py:37
  2.1 3.2 %collective-permute-start.2 = (f32[256,256]{1,0:T(8,128)S(1)}, f32[256,256]{1,0:T(8,128)S(1)}, u32[]{:S(2)}, u32[]{:S(2)}) collective-permute-start(f32[256,256]{1,0:T(8,128)S(1)} %get-tuple-element.20), channel_id=1, source_target_pairs={{0,16},{28,20}} | collective-permute-start | bytes 786440 | tf_op jit(solution)/shard_map/ppermute | solution.py:37
  2.8 2.3 %copy-start = (f32[256,512]{1,0:T(8,128)S(1)}, f32[256,512]{1,0:T(8,128)}, u32[]{:S(2)}) copy-start(f32[256,512]{1,0:T(8,128)} %param.5) | copy-start | bytes 1572868
  2.9 1.6 %collective-permute-start.7 = (bf16[256,256]{1,0:T(8,128)(2,1)S(1)}, bf16[256,256]{1,0:T(8,128)(2,1)S(1)}, u32[]{:S(2)}, u32[]{:S(2)}) collective-permute-start(bf16[256,256]{1,0:T(8,128)(2,1)S(1)} %slice.36), channel_id=1, source_target_pairs={{0,4}} | collective-permute-start | bytes 393224 | tf_op jit(solution)/shard_map/ppermute | solution.py:37
  3.7 1.5 %collective-permute-start.8 = (bf16[256,256]{1,0:T(8,128)(2,1)S(1)}, bf16[256,256]{1,0:T(8,128)(2,1)S(1)}, u32[]{:S(2)}, u32[]{:S(2)}) collective-permute-start(bf16[256,256]{1,0:T(8,128)(2,1)S(1)} %slice.36), channel_id=1, source_target_pairs={{0,16}} | collective-permute-start | bytes 393224 | tf_op jit(solution)/shard_map/ppermute | solution.py:37
  4.4 4.4 %collective-permute-start.12 = (bf16[256,512]{1,0:T(8,128)(2,1)S(1)}, bf16[256,512]{1,0:T(8,128)(2,1)S(1)}, u32[]{:S(2)}, u32[]{:S(2)}) collective-permute-start(bf16[256,512]{1,0:T(8,128)(2,1)S(1)} %broadcast_select_fusion), channel_id=1, source_target_pairs={{2,18},{6,22},{3,11},{19,27},{1,5},{17,21}} | collective-permute-start | bytes 786440 | tf_op jit(solution)/shard_map/ppermute | solution.py:37
  5.5 5.4 %collective-permute-start.4 = (bf16[256,256]{1,0:T(8,128)(2,1)S(1)}, bf16[256,256]{1,0:T(8,128)(2,1)S(1)}, u32[]{:S(2)}, u32[]{:S(2)}) collective-permute-start(bf16[256,256]{1,0:T(8,128)(2,1)S(1)} %get-tuple-element.22), channel_id=1, source_target_pairs={{0,8},{4,12},{16,24},{20,28}} | collective-permute-start | bytes 393224 | tf_op jit(solution)/shard_map/ppermute | solution.py:37
  6.1 17.0 %collective-permute-start.5 = (bf16[256,256]{1,0:T(8,128)(2,1)S(1)}, bf16[256,256]{1,0:T(8,128)(2,1)S(1)}, u32[]{:S(2)}, u32[]{:S(2)}) collective-permute-start(bf16[256,256]{1,0:T(8,128)(2,1)S(1)} %get-tuple-element.22), channel_id=1, source_target_pairs={{0,10},{4,14},{16,26},{20,30}} | collective-permute-start | bytes 393224 | tf_op jit(solution)/shard_map/ppermute | solution.py:37
  7.4 2.1 %collective-permute-start.3 = (bf16[256,256]{1,0:T(8,128)(2,1)S(1)}, bf16[256,256]{1,0:T(8,128)(2,1)S(1)}, u32[]{:S(2)}, u32[]{:S(2)}) collective-permute-start(bf16[256,256]{1,0:T(8,128)(2,1)S(1)} %get-tuple-element.21), channel_id=1, source_target_pairs={{4,6},{20,22},{16,18}} | collective-permute-start | bytes 393224 | tf_op jit(solution)/shard_map/ppermute | solution.py:37
  8.1 16.4 %collective-permute-start.10 = (bf16[256,256]{1,0:T(8,128)(2,1)S(1)}, bf16[256,256]{1,0:T(8,128)(2,1)S(1)}, u32[]{:S(2)}, u32[]{:S(2)}) collective-permute-start(bf16[256,256]{1,0:T(8,128)(2,1)S(1)} %select_select_fusion.4), channel_id=1, source_target_pairs={{0,8},{4,28},{16,24}} | collective-permute-start | bytes 393224 | tf_op jit(solution)/shard_map/ppermute | solution.py:37
  8.8 15.7 %collective-permute-start.9 = (bf16[256,256]{1,0:T(8,128)(2,1)S(1)}, bf16[256,256]{1,0:T(8,128)(2,1)S(1)}, u32[]{:S(2)}, u32[]{:S(2)}) collective-permute-start(bf16[256,256]{1,0:T(8,128)(2,1)S(1)} %select_select_fusion.4), channel_id=1, source_target_pairs={{0,12},{4,20}} | collective-permute-start | bytes 393224 | tf_op jit(solution)/shard_map/ppermute | solution.py:37
  9.5 21.0 %collective-permute-start.13 = (bf16[256,512]{1,0:T(8,128)(2,1)S(1)}, bf16[256,512]{1,0:T(8,128)(2,1)S(1)}, u32[]{:S(2)}, u32[]{:S(2)}) collective-permute-start(bf16[256,512]{1,0:T(8,128)(2,1)S(1)} %broadcast_select_fusion.1), channel_id=1, source_target_pairs={{2,10},{6,14},{18,26},{22,30},{3,7},{19,23},{11,15},{27,31},{1,9},... | collective-permute-start | bytes 786440 | tf_op jit(solution)/shard_map/ppermute | solution.py:37
  23.2 2.3 %collective-permute-start.6 = (bf16[256,256]{1,0:T(8,128)(2,1)S(1)}, bf16[256,256]{1,0:T(8,128)(2,1)S(1)}, u32[]{:S(2)}, u32[]{:S(2)}) collective-permute-start(bf16[256,256]{1,0:T(8,128)(2,1)S(1)} %select_select_fusion.5), channel_id=1, source_target_pairs={{4,5},{6,7},{8,9},{10,11},{12,13},{14,15},{16,17},{18,19},{20,21},... | collective-permute-start | bytes 393224 | tf_op jit(solution)/shard_map/ppermute | solution.py:37

commit v10 on v5

--- a/solution.py
+++ b/solution.py
@@ -81,10 +81,11 @@
         return jnp.where(jnp.where(col_here % 2 == 0, takes[0], takes[1]), got, value), got
 
     workers = [r for r in range(n_row) if r & APART == 0]
-    targets = workers[2:] + workers[1:2]
+    targets = workers[:1:-1]
+    targets.insert(1, 1)
     square = partner = first_sent
     for index, target in reversed(list(enumerate(targets))):
-        served = [0, targets[-1]] if index == 0 else [targets[index - 1]]
+        served = [[], [0] + [r for r in workers[2:]], [1]][min(index, 2)] if index < 3 else []
         pairs = [((0, 0), (target, 0))] + [((r + APART, 0), (r, 0)) for r in served]
         if index == 0:
             upper, got = upper_step(upper, 0, first_sent, pairs)
@@ -94,17 +95,11 @@
         for r in served:
             partner = jnp.where(row_here == r, got, partner)
 
-    got = send(column_upper, [((0, 0), (1, 0))])
-    near_upper = jnp.where(row_here == 1, got, column_upper)
-    near_sent = near_upper
-    for target in reversed(targets[1:-1]):
-        pairs = [((1, 0), (target, 0))]
-        takes = row_here == target
-        if target == targets[1]:
-            pairs += [((0, 0), (targets[0], 0))]
-            takes = takes | (row_here == targets[0])
-        got = send(near_sent, pairs)
-        near_upper = jnp.where(takes, got, near_upper)
+    upper, column_upper = lax.optimization_barrier((upper, column_upper))
+    near_upper = column_upper
+    for target in targets:
+        got = send(column_upper, [((0, 0), (target, 0))])
+        near_upper = jnp.where(row_here == target, got, near_upper)
     upper, _ = upper_step(upper, 1, upper)
 
     def compute(square, partner):

time: 28.9 us -> 29.6 us (1.024)
  the two profiles are of different devices: /device:TPU:7 before, /device:TPU:13 now
where the time goes in v10:
time: 29.6 us; the launch traced here: 29.3 us
  waiting for transfers between devices  17.5 us (59%)
  starting transfers between devices  10.1 us (34%)
  matrix products  1.07 us (4%)
  between operations  0.33 us (1%)
    ppermute x13, waiting for transfers between devices, send(): return lax.ppermute(value, ('row', 'col'), flat)  17.5 us
    ppermute x13, starting transfers between devices, send(): return lax.ppermute(value, ('row', 'col'), flat)  10.1 us
    dot_general x1, matrix products, shards(): return matrix - jnp.dot(received, upper, preferred_element_type=jnp.float32)  1.07 us
  transfers between devices with their start and end apart: 13, of which 1 were waited for; matrix products, arithmetic and copies ran while one was open for 1% of the time, Pallas kernels for 0%

profile of v10, /device:TPU:13, one launch (start us, length us, event | category | flops | bytes accessed | tf_op | source)
XLA Modules:
  0.0 29.3 jit_solution(1923164970733652386)
XLA Ops:
  0.1 0.7 %collective-permute-start = (bf16[256,512]{1,0:T(8,128)(2,1)S(1)}, bf16[256,512]{1,0:T(8,128)(2,1)S(1)}, u32[]{:S(2)}, u32[]{:S(2)}) collective-permute-start(bf16[256,512]{1,0:T(8,128)(2,1)S(1)} %get-tuple-element.101), channel_id=1, source_target_pairs={{0,20},{2,18},{1,5},{3,7}} | collective-permute-start | bytes 786440 | tf_op jit(solution)/shard_map/ppermute | solution.py:48
  0.7 0.7 %collective-permute-start.1 = (bf16[256,512]{1,0:T(8,128)(2,1)S(1)}, bf16[256,512]{1,0:T(8,128)(2,1)S(1)}, u32[]{:S(2)}, u32[]{:S(2)}) collective-permute-start(bf16[256,512]{1,0:T(8,128)(2,1)S(1)} %get-tuple-element.101), channel_id=1, source_target_pairs={{0,4},{8,0},{24,16},{28,20}} | collective-permute-start | bytes 786440 | tf_op jit(solution)/shard_map/ppermute | solution.py:48
  1.4 0.7 %collective-permute-start.2 = (bf16[256,512]{1,0:T(8,128)(2,1)S(1)}, bf16[256,512]{1,0:T(8,128)(2,1)S(1)}, u32[]{:S(2)}, u32[]{:S(2)}) collective-permute-start(bf16[256,512]{1,0:T(8,128)(2,1)S(1)} %get-tuple-element.101), channel_id=1, source_target_pairs={{0,16},{12,4}} | collective-permute-start | bytes 786440 | tf_op jit(solution)/shard_map/ppermute | solution.py:48
  2.2 0.0 copy-start
  2.2 0.0 collective-permute-done
  2.2 0.8 %collective-permute-start.7 = (bf16[256,256]{1,0:T(8,128)(2,1)S(1)}, bf16[256,256]{1,0:T(8,128)(2,1)S(1)}, u32[]{:S(2)}, u32[]{:S(2)}) collective-permute-start(bf16[256,256]{1,0:T(8,128)(2,1)S(1)} %get-tuple-element.31), channel_id=1, source_target_pairs={{0,16}} | collective-permute-start | bytes 393224 | tf_op jit(solution)/shard_map/ppermute | solution.py:48
  3.0 0.7 %collective-permute-start.8 = (bf16[256,256]{1,0:T(8,128)(2,1)S(1)}, bf16[256,256]{1,0:T(8,128)(2,1)S(1)}, u32[]{:S(2)}, u32[]{:S(2)}) collective-permute-start(bf16[256,256]{1,0:T(8,128)(2,1)S(1)} %get-tuple-element.31), channel_id=1, source_target_pairs={{0,4}} | collective-permute-start | bytes 393224 | tf_op jit(solution)/shard_map/ppermute | solution.py:48
  3.7 0.7 %collective-permute-start.9 = (bf16[256,256]{1,0:T(8,128)(2,1)S(1)}, bf16[256,256]{1,0:T(8,128)(2,1)S(1)}, u32[]{:S(2)}, u32[]{:S(2)}) collective-permute-start(bf16[256,256]{1,0:T(8,128)(2,1)S(1)} %get-tuple-element.31), channel_id=1, source_target_pairs={{0,20}} | collective-permute-start | bytes 393224 | tf_op jit(solution)/shard_map/ppermute | solution.py:48
  4.4 0.0 collective-permute-done.1
  4.4 0.7 %collective-permute-start.11 = (bf16[256,512]{1,0:T(8,128)(2,1)S(1)}, bf16[256,512]{1,0:T(8,128)(2,1)S(1)}, u32[]{:S(2)}, u32[]{:S(2)}) collective-permute-start(bf16[256,512]{1,0:T(8,128)(2,1)S(1)} %broadcast_select_fusion.1), channel_id=1, source_target_pairs={{2,10},{18,26},{1,17},{3,19},{5,21},{7,23}} | collective-permute-start | bytes 786440 | tf_op jit(solution)/shard_map/ppermute | solution.py:48
  5.1 0.0 collective-permute-done.2
  5.1 0.0 copy-done
  5.2 0.1 conditional.3
  5.2 0.7 %collective-permute-start.4 = (bf16[256,256]{1,0:T(8,128)(2,1)S(1)}, bf16[256,256]{1,0:T(8,128)(2,1)S(1)}, u32[]{:S(2)}, u32[]{:S(2)}) collective-permute-start(bf16[256,256]{1,0:T(8,128)(2,1)S(1)} %get-tuple-element.29), channel_id=1, source_target_pairs={{0,8},{4,12},{16,24},{20,28}} | collective-permute-start | bytes 393224 | tf_op jit(solution)/shard_map/ppermute | solution.py:48
  5.9 0.0 collective-permute-done.7
  5.9 0.7 %collective-permute-start.5 = (bf16[256,256]{1,0:T(8,128)(2,1)S(1)}, bf16[256,256]{1,0:T(8,128)(2,1)S(1)}, u32[]{:S(2)}, u32[]{:S(2)}) collective-permute-start(bf16[256,256]{1,0:T(8,128)(2,1)S(1)} %get-tuple-element.29), channel_id=1, source_target_pairs={{0,10},{4,14},{16,26},{20,30}} | collective-permute-start | bytes 393224 | tf_op jit(solution)/shard_map/ppermute | solution.py:48
  6.6 0.0 collective-permute-done.8
  6.6 0.7 %collective-permute-start.3 = (bf16[256,256]{1,0:T(8,128)(2,1)S(1)}, bf16[256,256]{1,0:T(8,128)(2,1)S(1)}, u32[]{:S(2)}, u32[]{:S(2)}) collective-permute-start(bf16[256,256]{1,0:T(8,128)(2,1)S(1)} %get-tuple-element.28), channel_id=1, source_target_pairs={{20,22},{4,6},{16,18}} | collective-permute-start | bytes 393224 | tf_op jit(solution)/shard_map/ppermute | solution.py:48
  7.3 0.0 collective-permute-done.9
  7.3 0.7 %collective-permute-start.10 = (bf16[256,256]{1,0:T(8,128)(2,1)S(1)}, bf16[256,256]{1,0:T(8,128)(2,1)S(1)}, u32[]{:S(2)}, u32[]{:S(2)}) collective-permute-start(bf16[256,256]{1,0:T(8,128)(2,1)S(1)} %select_select_fusion.2), channel_id=1, source_target_pairs={{0,8},{4,12},{16,24},{20,28}} | collective-permute-start | bytes 393224 | tf_op jit(solution)/shard_map/ppermute | solution.py:48
  8.0 0.0 collective-permute-done.11
  8.0 1.3 %collective-permute-start.12 = (bf16[256,512]{1,0:T(8,128)(2,1)S(1)}, bf16[256,512]{1,0:T(8,128)(2,1)S(1)}, u32[]{:S(2)}, u32[]{:S(2)}) collective-permute-start(bf16[256,512]{1,0:T(8,128)(2,1)S(1)} %broadcast_select_fusion), channel_id=1, source_target_pairs={{2,6},{18,22},{10,14},{26,30},{1,9},{3,11},{5,13},{7,15},{17,25},{... | collective-permute-start | bytes 786440 | tf_op jit(solution)/shard_map/ppermute | solution.py:48
  9.3 0.0 collective-permute-done.3
  9.3 0.0 collective-permute-done.4
  9.4 0.0 collective-permute-done.5
  9.4 1.3 %collective-permute-start.6 = (bf16[256,256]{1,0:T(8,128)(2,1)S(1)}, bf16[256,256]{1,0:T(8,128)(2,1)S(1)}, u32[]{:S(2)}, u32[]{:S(2)}) collective-permute-start(bf16[256,256]{1,0:T(8,128)(2,1)S(1)} %select_select_fusion.3), channel_id=1, source_target_pairs={{4,5},{6,7},{8,9},{10,11},{12,13},{14,15},{16,17},{18,19},{20,21},... | collective-permute-start | bytes 393224 | tf_op jit(solution)/shard_map/ppermute | solution.py:48
  10.7 0.0 collective-permute-done.10
  10.7 17.4 %collective-permute-done.6 = bf16[256,256]{1,0:T(8,128)(2,1)S(1)} collective-permute-done((bf16[256,256]{1,0:T(8,128)(2,1)S(1)}, bf16[256,256]{1,0:T(8,128)(2,1)S(1)}, u32[]{:S(2)}, u32[]{:S(2)}) %collective-permute-start.6) | collective-permute-done | bytes 131104 | tf_op jit(solution)/shard_map/ppermute | solution.py:48
  28.2 0.0 collective-permute-done.12
  28.2 1.1 %convolution_subtract_fusion = f32[256,512]{1,0:T(8,128)} fusion(f32[256,512]{1,0:T(8,128)S(1)} %copy-done, bf16[256,512]{1,0:T(8,128)(2,1)S(1)} %collective-permute-done.12, bf16[256,512]{1,0:T(8,128)(2,1)S(1)} %broadcast_select_fusion, bf16[256,256]{1,0:T(8,128)(2,1)S(1)} %broadcast_select_fusion.3, pred[]{:T(512)S(6)} %select_n.188, pred[]{:T(512)S(6)} %eq.78, ...), kind=kOutput, calls=%fused_computation.40 | convolution fusion | flops 67633152 | bytes 1966084 | tf_op jit(solution)/shard_map/dot_general | solution.py:139
  (11 shorter events, 0.3 us)
Async XLA Ops:
  0.1 2.1 %collective-permute-start = (bf16[256,512]{1,0:T(8,128)(2,1)S(1)}, bf16[256,512]{1,0:T(8,128)(2,1)S(1)}, u32[]{:S(2)}, u32[]{:S(2)}) collective-permute-start(bf16[256,512]{1,0:T(8,128)(2,1)S(1)} %get-tuple-element.101), channel_id=1, source_target_pairs={{0,20},{2,18},{1,5},{3,7}} | collective-permute-start | bytes 786440 | tf_op jit(solution)/shard_map/ppermute | solution.py:48
  0.7 3.7 %collective-permute-start.1 = (bf16[256,512]{1,0:T(8,128)(2,1)S(1)}, bf16[256,512]{1,0:T(8,128)(2,1)S(1)}, u32[]{:S(2)}, u32[]{:S(2)}) collective-permute-start(bf16[256,512]{1,0:T(8,128)(2,1)S(1)} %get-tuple-element.101), channel_id=1, source_target_pairs={{0,4},{8,0},{24,16},{28,20}} | collective-permute-start | bytes 786440 | tf_op jit(solution)/shard_map/ppermute | solution.py:48
  1.4 3.7 %collective-permute-start.2 = (bf16[256,512]{1,0:T(8,128)(2,1)S(1)}, bf16[256,512]{1,0:T(8,128)(2,1)S(1)}, u32[]{:S(2)}, u32[]{:S(2)}) collective-permute-start(bf16[256,512]{1,0:T(8,128)(2,1)S(1)} %get-tuple-element.101), channel_id=1, source_target_pairs={{0,16},{12,4}} | collective-permute-start | bytes 786440 | tf_op jit(solution)/shard_map/ppermute | solution.py:48
  2.2 3.0 %copy-start = (f32[256,512]{1,0:T(8,128)S(1)}, f32[256,512]{1,0:T(8,128)}, u32[]{:S(2)}) copy-start(f32[256,512]{1,0:T(8,128)} %param.5) | copy-start | bytes 1572868
  2.2 3.7 %collective-permute-start.7 = (bf16[256,256]{1,0:T(8,128)(2,1)S(1)}, bf16[256,256]{1,0:T(8,128)(2,1)S(1)}, u32[]{:S(2)}, u32[]{:S(2)}) collective-permute-start(bf16[256,256]{1,0:T(8,128)(2,1)S(1)} %get-tuple-element.31), channel_id=1, source_target_pairs={{0,16}} | collective-permute-start | bytes 393224 | tf_op jit(solution)/shard_map/ppermute | solution.py:48
  3.0 3.5 %collective-permute-start.8 = (bf16[256,256]{1,0:T(8,128)(2,1)S(1)}, bf16[256,256]{1,0:T(8,128)(2,1)S(1)}, u32[]{:S(2)}, u32[]{:S(2)}) collective-permute-start(bf16[256,256]{1,0:T(8,128)(2,1)S(1)} %get-tuple-element.31), channel_id=1, source_target_pairs={{0,4}} | collective-permute-start | bytes 393224 | tf_op jit(solution)/shard_map/ppermute | solution.py:48
  3.7 3.6 %collective-permute-start.9 = (bf16[256,256]{1,0:T(8,128)(2,1)S(1)}, bf16[256,256]{1,0:T(8,128)(2,1)S(1)}, u32[]{:S(2)}, u32[]{:S(2)}) collective-permute-start(bf16[256,256]{1,0:T(8,128)(2,1)S(1)} %get-tuple-element.31), channel_id=1, source_target_pairs={{0,20}} | collective-permute-start | bytes 393224 | tf_op jit(solution)/shard_map/ppermute | solution.py:48
  4.4 3.6 %collective-permute-start.11 = (bf16[256,512]{1,0:T(8,128)(2,1)S(1)}, bf16[256,512]{1,0:T(8,128)(2,1)S(1)}, u32[]{:S(2)}, u32[]{:S(2)}) collective-permute-start(bf16[256,512]{1,0:T(8,128)(2,1)S(1)} %broadcast_select_fusion.1), channel_id=1, source_target_pairs={{2,10},{18,26},{1,17},{3,19},{5,21},{7,23}} | collective-permute-start | bytes 786440 | tf_op jit(solution)/shard_map/ppermute | solution.py:48
  5.2 4.1 %collective-permute-start.4 = (bf16[256,256]{1,0:T(8,128)(2,1)S(1)}, bf16[256,256]{1,0:T(8,128)(2,1)S(1)}, u32[]{:S(2)}, u32[]{:S(2)}) collective-permute-start(bf16[256,256]{1,0:T(8,128)(2,1)S(1)} %get-tuple-element.29), channel_id=1, source_target_pairs={{0,8},{4,12},{16,24},{20,28}} | collective-permute-start | bytes 393224 | tf_op jit(solution)/shard_map/ppermute | solution.py:48
  5.9 3.5 %collective-permute-start.5 = (bf16[256,256]{1,0:T(8,128)(2,1)S(1)}, bf16[256,256]{1,0:T(8,128)(2,1)S(1)}, u32[]{:S(2)}, u32[]{:S(2)}) collective-permute-start(bf16[256,256]{1,0:T(8,128)(2,1)S(1)} %get-tuple-element.29), channel_id=1, source_target_pairs={{0,10},{4,14},{16,26},{20,30}} | collective-permute-start | bytes 393224 | tf_op jit(solution)/shard_map/ppermute | solution.py:48
  6.6 2.8 %collective-permute-start.3 = (bf16[256,256]{1,0:T(8,128)(2,1)S(1)}, bf16[256,256]{1,0:T(8,128)(2,1)S(1)}, u32[]{:S(2)}, u32[]{:S(2)}) collective-permute-start(bf16[256,256]{1,0:T(8,128)(2,1)S(1)} %get-tuple-element.28), channel_id=1, source_target_pairs={{20,22},{4,6},{16,18}} | collective-permute-start | bytes 393224 | tf_op jit(solution)/shard_map/ppermute | solution.py:48
  7.3 3.4 %collective-permute-start.10 = (bf16[256,256]{1,0:T(8,128)(2,1)S(1)}, bf16[256,256]{1,0:T(8,128)(2,1)S(1)}, u32[]{:S(2)}, u32[]{:S(2)}) collective-permute-start(bf16[256,256]{1,0:T(8,128)(2,1)S(1)} %select_select_fusion.2), channel_id=1, source_target_pairs={{0,8},{4,12},{16,24},{20,28}} | collective-permute-start | bytes 393224 | tf_op jit(solution)/shard_map/ppermute | solution.py:48
  8.0 20.2 %collective-permute-start.12 = (bf16[256,512]{1,0:T(8,128)(2,1)S(1)}, bf16[256,512]{1,0:T(8,128)(2,1)S(1)}, u32[]{:S(2)}, u32[]{:S(2)}) collective-permute-start(bf16[256,512]{1,0:T(8,128)(2,1)S(1)} %broadcast_select_fusion), channel_id=1, source_target_pairs={{2,6},{18,22},{10,14},{26,30},{1,9},{3,11},{5,13},{7,15},{17,25},{... | collective-permute-start | bytes 786440 | tf_op jit(solution)/shard_map/ppermute | solution.py:48
  9.4 18.8 %collective-permute-start.6 = (bf16[256,256]{1,0:T(8,128)(2,1)S(1)}, bf16[256,256]{1,0:T(8,128)(2,1)S(1)}, u32[]{:S(2)}, u32[]{:S(2)}) collective-permute-start(bf16[256,256]{1,0:T(8,128)(2,1)S(1)} %select_select_fusion.3), channel_id=1, source_target_pairs={{4,5},{6,7},{8,9},{10,11},{12,13},{14,15},{16,17},{18,19},{20,21},... | collective-permute-start | bytes 393224 | tf_op jit(solution)/shard_map/ppermute | solution.py:48

commit v11 on v8

--- a/solution.py
+++ b/solution.py
@@ -103,11 +103,9 @@
     working = (row_here & APART == 0) & (col_here == 0)
     lower, lower_far = lax.cond(working, compute, none, square, partner)
     received = lower
-    for c in range(2, n_col, 2):
+    for c in range(0, n_col, 2):
         got = send(lower_far, [((r, 0), (r + APART, c)) for r in workers])
         received = jnp.where((row_here & APART != 0) & (col_here == c), got, received)
-    got = send(lower_far, [((r, 0), (r + APART, 0)) for r in workers])
-    received = jnp.where((row_here & APART != 0) & (col_here == 0), got, received)
     for c in range(2, n_col, 2):
         got = send(lower, [((r, 0), (r, c)) for r in targets])
         received = jnp.where((row_here & APART == 0) & (col_here == c), got, received)

time: 27.4 us -> 27.4 us (level)
  the two profiles are of different devices: /device:TPU:15 before, /device:TPU:11 now
where the time goes in v11:
time: 27.4 us; the launch traced here: 27.1 us
  waiting for transfers between devices  15.1 us (55%)
  starting transfers between devices  10.1 us (37%)
  matrix products  1.07 us (4%)
  between operations  0.41 us (1%)
    ppermute x13, waiting for transfers between devices, send(): return lax.ppermute(value, ('row', 'col'), flat)  15.1 us
    ppermute x13, starting transfers between devices, send(): return lax.ppermute(value, ('row', 'col'), flat)  10.1 us
    dot_general x1, matrix products, shards(): return matrix - jnp.dot(received, upper, preferred_element_type=jnp.float32)  1.07 us
  transfers between devices with their start and end apart: 13, of which 1 were waited for; matrix products, arithmetic and copies ran while one was open for 1% of the time, Pallas kernels for 0%

profile of v11, /device:TPU:11, one launch (start us, length us, event | category | flops | bytes accessed | tf_op | source)
XLA Modules:
  0.0 27.1 jit_solution(7473279364785498108)
XLA Ops:
  0.0 0.1 conditional.2
  0.1 0.7 %collective-permute-start.7 = (bf16[256,512]{1,0:T(8,128)(2,1)S(1)}, bf16[256,512]{1,0:T(8,128)(2,1)S(1)}, u32[]{:S(2)}, u32[]{:S(2)}) collective-permute-start(bf16[256,512]{1,0:T(8,128)(2,1)S(1)} %get-tuple-element.23), channel_id=1, source_target_pairs={{0,4},{2,6},{3,19},{1,17}} | collective-permute-start | bytes 786440 | tf_op jit(solution)/shard_map/ppermute | solution.py:37
  0.7 0.7 %collective-permute-start = (f32[256,256]{1,0:T(8,128)S(1)}, f32[256,256]{1,0:T(8,128)S(1)}, u32[]{:S(2)}, u32[]{:S(2)}) collective-permute-start(f32[256,256]{1,0:T(8,128)S(1)} %get-tuple-element.20), channel_id=1, source_target_pairs={{0,20},{8,0},{12,4},{24,16}} | collective-permute-start | bytes 786440 | tf_op jit(solution)/shard_map/ppermute | solution.py:37
  1.4 0.7 %collective-permute-start.1 = (f32[256,256]{1,0:T(8,128)S(1)}, f32[256,256]{1,0:T(8,128)S(1)}, u32[]{:S(2)}, u32[]{:S(2)}) collective-permute-start(f32[256,256]{1,0:T(8,128)S(1)} %get-tuple-element.20), channel_id=1, source_target_pairs={{0,4},{28,20}} | collective-permute-start | bytes 786440 | tf_op jit(solution)/shard_map/ppermute | solution.py:37
  2.1 0.7 %collective-permute-start.2 = (f32[256,256]{1,0:T(8,128)S(1)}, f32[256,256]{1,0:T(8,128)S(1)}, u32[]{:S(2)}, u32[]{:S(2)}) collective-permute-start(f32[256,256]{1,0:T(8,128)S(1)} %get-tuple-element.20), channel_id=1, source_target_pairs={{0,16}} | collective-permute-start | bytes 786440 | tf_op jit(solution)/shard_map/ppermute | solution.py:37
  2.9 0.0 copy-start
  2.9 0.0 collective-permute-done.7
  2.9 0.8 %collective-permute-start.8 = (bf16[256,256]{1,0:T(8,128)(2,1)S(1)}, bf16[256,256]{1,0:T(8,128)(2,1)S(1)}, u32[]{:S(2)}, u32[]{:S(2)}) collective-permute-start(bf16[256,256]{1,0:T(8,128)(2,1)S(1)} %slice_select_fusion), channel_id=1, source_target_pairs={{4,20}} | collective-permute-start | bytes 393224 | tf_op jit(solution)/shard_map/ppermute | solution.py:37
  3.7 0.7 %collective-permute-start.9 = (bf16[256,256]{1,0:T(8,128)(2,1)S(1)}, bf16[256,256]{1,0:T(8,128)(2,1)S(1)}, u32[]{:S(2)}, u32[]{:S(2)}) collective-permute-start(bf16[256,256]{1,0:T(8,128)(2,1)S(1)} %slice_select_fusion), channel_id=1, source_target_pairs={{4,16}} | collective-permute-start | bytes 393224 | tf_op jit(solution)/shard_map/ppermute | solution.py:37
  4.5 0.0 collective-permute-done
  4.5 0.7 %collective-permute-start.11 = (bf16[256,512]{1,0:T(8,128)(2,1)S(1)}, bf16[256,512]{1,0:T(8,128)(2,1)S(1)}, u32[]{:S(2)}, u32[]{:S(2)}) collective-permute-start(bf16[256,512]{1,0:T(8,128)(2,1)S(1)} %broadcast_select_fusion), channel_id=1, source_target_pairs={{2,18},{6,22},{3,11},{19,27},{1,5},{17,21}} | collective-permute-start | bytes 786440 | tf_op jit(solution)/shard_map/ppermute | solution.py:37
  5.2 0.0 copy-done
  5.3 0.0 collective-permute-done.1
  5.3 0.0 collective-permute-done.2
  5.3 0.1 conditional.3
  5.4 0.7 %collective-permute-start.4 = (bf16[256,256]{1,0:T(8,128)(2,1)S(1)}, bf16[256,256]{1,0:T(8,128)(2,1)S(1)}, u32[]{:S(2)}, u32[]{:S(2)}) collective-permute-start(bf16[256,256]{1,0:T(8,128)(2,1)S(1)} %get-tuple-element.22), channel_id=1, source_target_pairs={{0,10},{4,14},{16,26},{20,30}} | collective-permute-start | bytes 393224 | tf_op jit(solution)/shard_map/ppermute | solution.py:37
  6.1 0.7 %collective-permute-start.5 = (bf16[256,256]{1,0:T(8,128)(2,1)S(1)}, bf16[256,256]{1,0:T(8,128)(2,1)S(1)}, u32[]{:S(2)}, u32[]{:S(2)}) collective-permute-start(bf16[256,256]{1,0:T(8,128)(2,1)S(1)} %get-tuple-element.22), channel_id=1, source_target_pairs={{0,8},{4,12},{16,24},{20,28}} | collective-permute-start | bytes 393224 | tf_op jit(solution)/shard_map/ppermute | solution.py:37
  6.8 0.0 collective-permute-done.8
  6.8 0.7 %collective-permute-start.3 = (bf16[256,256]{1,0:T(8,128)(2,1)S(1)}, bf16[256,256]{1,0:T(8,128)(2,1)S(1)}, u32[]{:S(2)}, u32[]{:S(2)}) collective-permute-start(bf16[256,256]{1,0:T(8,128)(2,1)S(1)} %get-tuple-element.21), channel_id=1, source_target_pairs={{20,22},{4,6},{16,18}} | collective-permute-start | bytes 393224 | tf_op jit(solution)/shard_map/ppermute | solution.py:37
  7.4 0.0 collective-permute-done.9
  7.5 0.7 %collective-permute-start.10 = (bf16[256,256]{1,0:T(8,128)(2,1)S(1)}, bf16[256,256]{1,0:T(8,128)(2,1)S(1)}, u32[]{:S(2)}, u32[]{:S(2)}) collective-permute-start(bf16[256,256]{1,0:T(8,128)(2,1)S(1)} %select_select_fusion.2), channel_id=1, source_target_pairs={{0,8},{4,12},{16,24},{20,28}} | collective-permute-start | bytes 393224 | tf_op jit(solution)/shard_map/ppermute | solution.py:37
  8.2 0.0 collective-permute-done.11
  8.2 1.3 %collective-permute-start.12 = (bf16[256,512]{1,0:T(8,128)(2,1)S(1)}, bf16[256,512]{1,0:T(8,128)(2,1)S(1)}, u32[]{:S(2)}, u32[]{:S(2)}) collective-permute-start(bf16[256,512]{1,0:T(8,128)(2,1)S(1)} %broadcast_select_fusion.1), channel_id=1, source_target_pairs={{2,10},{6,14},{18,26},{22,30},{3,7},{19,23},{11,15},{27,31},{1,9},... | collective-permute-start | bytes 786440 | tf_op jit(solution)/shard_map/ppermute | solution.py:37
  9.5 0.0 collective-permute-done.3
  9.5 0.0 collective-permute-done.4
  9.5 0.0 collective-permute-done.5
  9.6 1.3 %collective-permute-start.6 = (bf16[256,256]{1,0:T(8,128)(2,1)S(1)}, bf16[256,256]{1,0:T(8,128)(2,1)S(1)}, u32[]{:S(2)}, u32[]{:S(2)}) collective-permute-start(bf16[256,256]{1,0:T(8,128)(2,1)S(1)} %select_select_fusion.3), channel_id=1, source_target_pairs={{4,5},{6,7},{8,9},{10,11},{12,13},{14,15},{16,17},{18,19},{20,21},... | collective-permute-start | bytes 393224 | tf_op jit(solution)/shard_map/ppermute | solution.py:37
  10.9 0.0 collective-permute-done.10
  10.9 15.1 %collective-permute-done.6 = bf16[256,256]{1,0:T(8,128)(2,1)S(1)} collective-permute-done((bf16[256,256]{1,0:T(8,128)(2,1)S(1)}, bf16[256,256]{1,0:T(8,128)(2,1)S(1)}, u32[]{:S(2)}, u32[]{:S(2)}) %collective-permute-start.6) | collective-permute-done | bytes 131104 | tf_op jit(solution)/shard_map/ppermute | solution.py:37
  26.0 0.0 collective-permute-done.12
  26.0 1.1 %convolution_subtract_fusion = f32[256,512]{1,0:T(8,128)} fusion(f32[256,512]{1,0:T(8,128)S(1)} %copy-done, bf16[256,512]{1,0:T(8,128)(2,1)S(1)} %collective-permute-done.12, bf16[256,512]{1,0:T(8,128)(2,1)S(1)} %broadcast_select_fusion.1, bf16[256,256]{1,0:T(8,128)(2,1)S(1)} %broadcast_select_fusion.3, pred[]{:T(512)S(6)} %or.23, pred[]{:T(512)S(6)} %eq.93, ...), kind=kOutput, calls=%fused_computation.34 | convolution fusion | flops 67633152 | bytes 1966084 | tf_op jit(solution)/shard_map/dot_general | solution.py:125
  (14 shorter events, 0.3 us)
Async XLA Ops:
  0.1 2.8 %collective-permute-start.7 = (bf16[256,512]{1,0:T(8,128)(2,1)S(1)}, bf16[256,512]{1,0:T(8,128)(2,1)S(1)}, u32[]{:S(2)}, u32[]{:S(2)}) collective-permute-start(bf16[256,512]{1,0:T(8,128)(2,1)S(1)} %get-tuple-element.23), channel_id=1, source_target_pairs={{0,4},{2,6},{3,19},{1,17}} | collective-permute-start | bytes 786440 | tf_op jit(solution)/shard_map/ppermute | solution.py:37
  0.7 3.7 %collective-permute-start = (f32[256,256]{1,0:T(8,128)S(1)}, f32[256,256]{1,0:T(8,128)S(1)}, u32[]{:S(2)}, u32[]{:S(2)}) collective-permute-start(f32[256,256]{1,0:T(8,128)S(1)} %get-tuple-element.20), channel_id=1, source_target_pairs={{0,20},{8,0},{12,4},{24,16}} | collective-permute-start | bytes 786440 | tf_op jit(solution)/shard_map/ppermute | solution.py:37
  1.4 3.8 %collective-permute-start.1 = (f32[256,256]{1,0:T(8,128)S(1)}, f32[256,256]{1,0:T(8,128)S(1)}, u32[]{:S(2)}, u32[]{:S(2)}) collective-permute-start(f32[256,256]{1,0:T(8,128)S(1)} %get-tuple-element.20), channel_id=1, source_target_pairs={{0,4},{28,20}} | collective-permute-start | bytes 786440 | tf_op jit(solution)/shard_map/ppermute | solution.py:37
  2.1 3.2 %collective-permute-start.2 = (f32[256,256]{1,0:T(8,128)S(1)}, f32[256,256]{1,0:T(8,128)S(1)}, u32[]{:S(2)}, u32[]{:S(2)}) collective-permute-start(f32[256,256]{1,0:T(8,128)S(1)} %get-tuple-element.20), channel_id=1, source_target_pairs={{0,16}} | collective-permute-start | bytes 786440 | tf_op jit(solution)/shard_map/ppermute | solution.py:37
  2.9 2.3 %copy-start = (f32[256,512]{1,0:T(8,128)S(1)}, f32[256,512]{1,0:T(8,128)}, u32[]{:S(2)}) copy-start(f32[256,512]{1,0:T(8,128)} %param.5) | copy-start | bytes 1572868
  2.9 3.8 %collective-permute-start.8 = (bf16[256,256]{1,0:T(8,128)(2,1)S(1)}, bf16[256,256]{1,0:T(8,128)(2,1)S(1)}, u32[]{:S(2)}, u32[]{:S(2)}) collective-permute-start(bf16[256,256]{1,0:T(8,128)(2,1)S(1)} %slice_select_fusion), channel_id=1, source_target_pairs={{4,20}} | collective-permute-start | bytes 393224 | tf_op jit(solution)/shard_map/ppermute | solution.py:37
  3.7 3.7 %collective-permute-start.9 = (bf16[256,256]{1,0:T(8,128)(2,1)S(1)}, bf16[256,256]{1,0:T(8,128)(2,1)S(1)}, u32[]{:S(2)}, u32[]{:S(2)}) collective-permute-start(bf16[256,256]{1,0:T(8,128)(2,1)S(1)} %slice_select_fusion), channel_id=1, source_target_pairs={{4,16}} | collective-permute-start | bytes 393224 | tf_op jit(solution)/shard_map/ppermute | solution.py:37
  4.5 3.7 %collective-permute-start.11 = (bf16[256,512]{1,0:T(8,128)(2,1)S(1)}, bf16[256,512]{1,0:T(8,128)(2,1)S(1)}, u32[]{:S(2)}, u32[]{:S(2)}) collective-permute-start(bf16[256,512]{1,0:T(8,128)(2,1)S(1)} %broadcast_select_fusion), channel_id=1, source_target_pairs={{2,18},{6,22},{3,11},{19,27},{1,5},{17,21}} | collective-permute-start | bytes 786440 | tf_op jit(solution)/shard_map/ppermute | solution.py:37
  5.4 4.1 %collective-permute-start.4 = (bf16[256,256]{1,0:T(8,128)(2,1)S(1)}, bf16[256,256]{1,0:T(8,128)(2,1)S(1)}, u32[]{:S(2)}, u32[]{:S(2)}) collective-permute-start(bf16[256,256]{1,0:T(8,128)(2,1)S(1)} %get-tuple-element.22), channel_id=1, source_target_pairs={{0,10},{4,14},{16,26},{20,30}} | collective-permute-start | bytes 393224 | tf_op jit(solution)/shard_map/ppermute | solution.py:37
  6.1 3.5 %collective-permute-start.5 = (bf16[256,256]{1,0:T(8,128)(2,1)S(1)}, bf16[256,256]{1,0:T(8,128)(2,1)S(1)}, u32[]{:S(2)}, u32[]{:S(2)}) collective-permute-start(bf16[256,256]{1,0:T(8,128)(2,1)S(1)} %get-tuple-element.22), channel_id=1, source_target_pairs={{0,8},{4,12},{16,24},{20,28}} | collective-permute-start | bytes 393224 | tf_op jit(solution)/shard_map/ppermute | solution.py:37
  6.8 2.7 %collective-permute-start.3 = (bf16[256,256]{1,0:T(8,128)(2,1)S(1)}, bf16[256,256]{1,0:T(8,128)(2,1)S(1)}, u32[]{:S(2)}, u32[]{:S(2)}) collective-permute-start(bf16[256,256]{1,0:T(8,128)(2,1)S(1)} %get-tuple-element.21), channel_id=1, source_target_pairs={{20,22},{4,6},{16,18}} | collective-permute-start | bytes 393224 | tf_op jit(solution)/shard_map/ppermute | solution.py:37
  7.5 3.4 %collective-permute-start.10 = (bf16[256,256]{1,0:T(8,128)(2,1)S(1)}, bf16[256,256]{1,0:T(8,128)(2,1)S(1)}, u32[]{:S(2)}, u32[]{:S(2)}) collective-permute-start(bf16[256,256]{1,0:T(8,128)(2,1)S(1)} %select_select_fusion.2), channel_id=1, source_target_pairs={{0,8},{4,12},{16,24},{20,28}} | collective-permute-start | bytes 393224 | tf_op jit(solution)/shard_map/ppermute | solution.py:37
  8.2 17.8 %collective-permute-start.12 = (bf16[256,512]{1,0:T(8,128)(2,1)S(1)}, bf16[256,512]{1,0:T(8,128)(2,1)S(1)}, u32[]{:S(2)}, u32[]{:S(2)}) collective-permute-start(bf16[256,512]{1,0:T(8,128)(2,1)S(1)} %broadcast_select_fusion.1), channel_id=1, source_target_pairs={{2,10},{6,14},{18,26},{22,30},{3,7},{19,23},{11,15},{27,31},{1,9},... | collective-permute-start | bytes 786440 | tf_op jit(solution)/shard_map/ppermute | solution.py:37
  9.6 16.4 %collective-permute-start.6 = (bf16[256,256]{1,0:T(8,128)(2,1)S(1)}, bf16[256,256]{1,0:T(8,128)(2,1)S(1)}, u32[]{:S(2)}, u32[]{:S(2)}) collective-permute-start(bf16[256,256]{1,0:T(8,128)(2,1)S(1)} %select_select_fusion.3), channel_id=1, source_target_pairs={{4,5},{6,7},{8,9},{10,11},{12,13},{14,15},{16,17},{18,19},{20,21},... | collective-permute-start | bytes 393224 | tf_op jit(solution)/shard_map/ppermute | solution.py:37

commit v12 on v11

--- a/solution.py
+++ b/solution.py
@@ -89,6 +89,7 @@
     for target in workers[2:]:
         got = send(near_sent, [((1, 0), (target, 0))])
         near_upper = jnp.where(row_here == target, got, near_upper)
+    near_first = send(near_sent, [((r, 0), (r + APART, 0)) for r in workers[:2]])
     upper, _ = upper_step(upper, 1, upper)
 
     def compute(square, partner):
@@ -110,8 +111,9 @@
         got = send(lower, [((r, 0), (r, c)) for r in targets])
         received = jnp.where((row_here & APART == 0) & (col_here == c), got, received)
     near_sent, _ = lax.optimization_barrier((near_upper, lower))
-    got = send(near_sent, [((r, 0), (r + APART, 0)) for r in workers])
+    got = send(near_sent, [((r, 0), (r + APART, 0)) for r in workers[2:]])
     near_upper = jnp.where(row_here & APART != 0, got, near_upper)
+    near_upper = jnp.where((row_here | 1) == APART + 1, near_first, near_upper)
     for step in range(2, len(down)):
         upper, _ = upper_step(upper, step, upper)
     got = send(

time: 27.4 us -> 30.5 us (1.11)
  the two profiles are of different devices: /device:TPU:11 before, /device:TPU:14 now
where the time goes in v12:
time: 30.5 us; the launch traced here: 30.2 us
  waiting for transfers between devices  16.9 us (55%)
  starting transfers between devices  11.4 us (37%)
  matrix products  1.07 us (4%)
  between operations  0.42 us (1%)
    ppermute x14, waiting for transfers between devices, send(): return lax.ppermute(value, ('row', 'col'), flat)  16.9 us
    ppermute x14, starting transfers between devices, send(): return lax.ppermute(value, ('row', 'col'), flat)  11.4 us
    dot_general x1, matrix products, shards(): return matrix - jnp.dot(received, upper, preferred_element_type=jnp.float32)  1.07 us
  transfers between devices with their start and end apart: 14, of which 3 were waited for; matrix products, arithmetic and copies ran while one was open for 1% of the time, Pallas kernels for 0%

profile of v12, /device:TPU:14, one launch (start us, length us, event | category | flops | bytes accessed | tf_op | source)
XLA Modules:
  0.0 30.2 jit_solution(8324561801383084006)
XLA Ops:
  0.0 0.1 conditional.2
  0.1 0.7 %collective-permute-start.7 = (bf16[256,512]{1,0:T(8,128)(2,1)S(1)}, bf16[256,512]{1,0:T(8,128)(2,1)S(1)}, u32[]{:S(2)}, u32[]{:S(2)}) collective-permute-start(bf16[256,512]{1,0:T(8,128)(2,1)S(1)} %get-tuple-element.23), channel_id=1, source_target_pairs={{0,4},{2,6},{3,19},{1,17}} | collective-permute-start | bytes 786440 | tf_op jit(solution)/shard_map/ppermute | solution.py:37
  0.7 0.7 %collective-permute-start = (f32[256,256]{1,0:T(8,128)S(1)}, f32[256,256]{1,0:T(8,128)S(1)}, u32[]{:S(2)}, u32[]{:S(2)}) collective-permute-start(f32[256,256]{1,0:T(8,128)S(1)} %get-tuple-element.20), channel_id=1, source_target_pairs={{0,20},{8,0},{12,4},{24,16}} | collective-permute-start | bytes 786440 | tf_op jit(solution)/shard_map/ppermute | solution.py:37
  1.4 0.7 %collective-permute-start.1 = (f32[256,256]{1,0:T(8,128)S(1)}, f32[256,256]{1,0:T(8,128)S(1)}, u32[]{:S(2)}, u32[]{:S(2)}) collective-permute-start(f32[256,256]{1,0:T(8,128)S(1)} %get-tuple-element.20), channel_id=1, source_target_pairs={{0,4},{28,20}} | collective-permute-start | bytes 786440 | tf_op jit(solution)/shard_map/ppermute | solution.py:37
  2.1 0.7 %collective-permute-start.2 = (f32[256,256]{1,0:T(8,128)S(1)}, f32[256,256]{1,0:T(8,128)S(1)}, u32[]{:S(2)}, u32[]{:S(2)}) collective-permute-start(f32[256,256]{1,0:T(8,128)S(1)} %get-tuple-element.20), channel_id=1, source_target_pairs={{0,16}} | collective-permute-start | bytes 786440 | tf_op jit(solution)/shard_map/ppermute | solution.py:37
  2.9 0.0 copy-start
  2.9 0.0 collective-permute-done.7
  2.9 0.8 %collective-permute-start.10 = (bf16[256,256]{1,0:T(8,128)(2,1)S(1)}, bf16[256,256]{1,0:T(8,128)(2,1)S(1)}, u32[]{:S(2)}, u32[]{:S(2)}) collective-permute-start(bf16[256,256]{1,0:T(8,128)(2,1)S(1)} %slice_select_fusion), channel_id=1, source_target_pairs={{4,16}} | collective-permute-start | bytes 393224 | tf_op jit(solution)/shard_map/ppermute | solution.py:37
  3.7 0.7 %collective-permute-start.9 = (bf16[256,256]{1,0:T(8,128)(2,1)S(1)}, bf16[256,256]{1,0:T(8,128)(2,1)S(1)}, u32[]{:S(2)}, u32[]{:S(2)}) collective-permute-start(bf16[256,256]{1,0:T(8,128)(2,1)S(1)} %slice_select_fusion), channel_id=1, source_target_pairs={{4,20}} | collective-permute-start | bytes 393224 | tf_op jit(solution)/shard_map/ppermute | solution.py:37
  4.5 0.0 collective-permute-done
  4.5 0.7 %collective-permute-start.12 = (bf16[256,512]{1,0:T(8,128)(2,1)S(1)}, bf16[256,512]{1,0:T(8,128)(2,1)S(1)}, u32[]{:S(2)}, u32[]{:S(2)}) collective-permute-start(bf16[256,512]{1,0:T(8,128)(2,1)S(1)} %broadcast_select_fusion), channel_id=1, source_target_pairs={{2,18},{6,22},{3,11},{19,27},{1,5},{17,21}} | collective-permute-start | bytes 786440 | tf_op jit(solution)/shard_map/ppermute | solution.py:37
  5.2 0.0 copy-done
  5.3 0.0 collective-permute-done.1
  5.3 0.0 collective-permute-done.2
  5.3 0.1 conditional.3
  5.4 1.3 %collective-permute-start.4 = (bf16[256,256]{1,0:T(8,128)(2,1)S(1)}, bf16[256,256]{1,0:T(8,128)(2,1)S(1)}, u32[]{:S(2)}, u32[]{:S(2)}) collective-permute-start(bf16[256,256]{1,0:T(8,128)(2,1)S(1)} %get-tuple-element.22), channel_id=1, source_target_pairs={{0,10},{4,14},{16,26},{20,30}} | collective-permute-start | bytes 393224 | tf_op jit(solution)/shard_map/ppermute | solution.py:37
  6.7 0.7 %collective-permute-start.5 = (bf16[256,256]{1,0:T(8,128)(2,1)S(1)}, bf16[256,256]{1,0:T(8,128)(2,1)S(1)}, u32[]{:S(2)}, u32[]{:S(2)}) collective-permute-start(bf16[256,256]{1,0:T(8,128)(2,1)S(1)} %get-tuple-element.22), channel_id=1, source_target_pairs={{0,8},{4,12},{16,24},{20,28}} | collective-permute-start | bytes 393224 | tf_op jit(solution)/shard_map/ppermute | solution.py:37
  7.4 0.0 collective-permute-done.10
  7.4 0.7 %collective-permute-start.8 = (bf16[256,256]{1,0:T(8,128)(2,1)S(1)}, bf16[256,256]{1,0:T(8,128)(2,1)S(1)}, u32[]{:S(2)}, u32[]{:S(2)}) collective-permute-start(bf16[256,256]{1,0:T(8,128)(2,1)S(1)} %slice_select_fusion), channel_id=1, source_target_pairs={{0,8},{4,12}} | collective-permute-start | bytes 393224 | tf_op jit(solution)/shard_map/ppermute | solution.py:37
  8.1 0.0 collective-permute-done.9
  8.1 0.7 %collective-permute-start.3 = (bf16[256,256]{1,0:T(8,128)(2,1)S(1)}, bf16[256,256]{1,0:T(8,128)(2,1)S(1)}, u32[]{:S(2)}, u32[]{:S(2)}) collective-permute-start(bf16[256,256]{1,0:T(8,128)(2,1)S(1)} %get-tuple-element.21), channel_id=1, source_target_pairs={{20,22},{4,6},{16,18}} | collective-permute-start | bytes 393224 | tf_op jit(solution)/shard_map/ppermute | solution.py:37
  8.8 0.0 collective-permute-done.12
  8.8 0.7 %collective-permute-start.11 = (bf16[256,256]{1,0:T(8,128)(2,1)S(1)}, bf16[256,256]{1,0:T(8,128)(2,1)S(1)}, u32[]{:S(2)}, u32[]{:S(2)}) collective-permute-start(bf16[256,256]{1,0:T(8,128)(2,1)S(1)} %select_select_fusion.3), channel_id=1, source_target_pairs={{16,24},{20,28}} | collective-permute-start | bytes 393224 | tf_op jit(solution)/shard_map/ppermute | solution.py:37
  9.5 0.0 collective-permute-done.3
  9.5 1.3 %collective-permute-start.13 = (bf16[256,512]{1,0:T(8,128)(2,1)S(1)}, bf16[256,512]{1,0:T(8,128)(2,1)S(1)}, u32[]{:S(2)}, u32[]{:S(2)}) collective-permute-start(bf16[256,512]{1,0:T(8,128)(2,1)S(1)} %broadcast_select_fusion.1), channel_id=1, source_target_pairs={{2,10},{6,14},{18,26},{22,30},{3,7},{19,23},{11,15},{27,31},{1,9},... | collective-permute-start | bytes 786440 | tf_op jit(solution)/shard_map/ppermute | solution.py:37
  10.8 9.0 %collective-permute-done.4 = bf16[256,256]{1,0:T(8,128)(2,1)S(1)} collective-permute-done((bf16[256,256]{1,0:T(8,128)(2,1)S(1)}, bf16[256,256]{1,0:T(8,128)(2,1)S(1)}, u32[]{:S(2)}, u32[]{:S(2)}) %collective-permute-start.4) | collective-permute-done | bytes 131104 | tf_op jit(solution)/shard_map/ppermute | solution.py:37
  19.9 0.0 collective-permute-done.5
  19.9 1.3 %collective-permute-start.6 = (bf16[256,256]{1,0:T(8,128)(2,1)S(1)}, bf16[256,256]{1,0:T(8,128)(2,1)S(1)}, u32[]{:S(2)}, u32[]{:S(2)}) collective-permute-start(bf16[256,256]{1,0:T(8,128)(2,1)S(1)} %select_select_fusion.4), channel_id=1, source_target_pairs={{4,5},{6,7},{8,9},{10,11},{12,13},{14,15},{16,17},{18,19},{20,21},... | collective-permute-start | bytes 393224 | tf_op jit(solution)/shard_map/ppermute | solution.py:37
  21.2 0.0 collective-permute-done.8
  21.2 0.0 collective-permute-done.11
  21.3 0.9 %collective-permute-done.6 = bf16[256,256]{1,0:T(8,128)(2,1)S(1)} collective-permute-done((bf16[256,256]{1,0:T(8,128)(2,1)S(1)}, bf16[256,256]{1,0:T(8,128)(2,1)S(1)}, u32[]{:S(2)}, u32[]{:S(2)}) %collective-permute-start.6) | collective-permute-done | bytes 131104 | tf_op jit(solution)/shard_map/ppermute | solution.py:37
  22.2 7.0 %collective-permute-done.13 = bf16[256,512]{1,0:T(8,128)(2,1)S(1)} collective-permute-done((bf16[256,512]{1,0:T(8,128)(2,1)S(1)}, bf16[256,512]{1,0:T(8,128)(2,1)S(1)}, u32[]{:S(2)}, u32[]{:S(2)}) %collective-permute-start.13) | collective-permute-done | bytes 262176 | tf_op jit(solution)/shard_map/ppermute | solution.py:37
  29.1 1.1 %convolution_subtract_fusion = f32[256,512]{1,0:T(8,128)} fusion(f32[256,512]{1,0:T(8,128)S(1)} %copy-done, bf16[256,512]{1,0:T(8,128)(2,1)S(1)} %collective-permute-done.13, bf16[256,512]{1,0:T(8,128)(2,1)S(1)} %broadcast_select_fusion.1, bf16[256,256]{1,0:T(8,128)(2,1)S(1)} %select_select_fusion.2, pred[]{:T(512)S(6)} %or.27, pred[]{:T(512)S(6)} %eq.96, ...), kind=kOutput, calls=%fused_computation.34 | convolution fusion | flops 67633152 | bytes 1966084 | tf_op jit(solution)/shard_map/dot_general | solution.py:127
  (14 shorter events, 0.3 us)
Async XLA Ops:
  0.1 2.8 %collective-permute-start.7 = (bf16[256,512]{1,0:T(8,128)(2,1)S(1)}, bf16[256,512]{1,0:T(8,128)(2,1)S(1)}, u32[]{:S(2)}, u32[]{:S(2)}) collective-permute-start(bf16[256,512]{1,0:T(8,128)(2,1)S(1)} %get-tuple-element.23), channel_id=1, source_target_pairs={{0,4},{2,6},{3,19},{1,17}} | collective-permute-start | bytes 786440 | tf_op jit(solution)/shard_map/ppermute | solution.py:37
  0.7 3.7 %collective-permute-start = (f32[256,256]{1,0:T(8,128)S(1)}, f32[256,256]{1,0:T(8,128)S(1)}, u32[]{:S(2)}, u32[]{:S(2)}) collective-permute-start(f32[256,256]{1,0:T(8,128)S(1)} %get-tuple-element.20), channel_id=1, source_target_pairs={{0,20},{8,0},{12,4},{24,16}} | collective-permute-start | bytes 786440 | tf_op jit(solution)/shard_map/ppermute | solution.py:37
  1.4 3.8 %collective-permute-start.1 = (f32[256,256]{1,0:T(8,128)S(1)}, f32[256,256]{1,0:T(8,128)S(1)}, u32[]{:S(2)}, u32[]{:S(2)}) collective-permute-start(f32[256,256]{1,0:T(8,128)S(1)} %get-tuple-element.20), channel_id=1, source_target_pairs={{0,4},{28,20}} | collective-permute-start | bytes 786440 | tf_op jit(solution)/shard_map/ppermute | solution.py:37
  2.1 3.2 %collective-permute-start.2 = (f32[256,256]{1,0:T(8,128)S(1)}, f32[256,256]{1,0:T(8,128)S(1)}, u32[]{:S(2)}, u32[]{:S(2)}) collective-permute-start(f32[256,256]{1,0:T(8,128)S(1)} %get-tuple-element.20), channel_id=1, source_target_pairs={{0,16}} | collective-permute-start | bytes 786440 | tf_op jit(solution)/shard_map/ppermute | solution.py:37
  2.9 2.3 %copy-start = (f32[256,512]{1,0:T(8,128)S(1)}, f32[256,512]{1,0:T(8,128)}, u32[]{:S(2)}) copy-start(f32[256,512]{1,0:T(8,128)} %param.5) | copy-start | bytes 1572868
  2.9 4.5 %collective-permute-start.10 = (bf16[256,256]{1,0:T(8,128)(2,1)S(1)}, bf16[256,256]{1,0:T(8,128)(2,1)S(1)}, u32[]{:S(2)}, u32[]{:S(2)}) collective-permute-start(bf16[256,256]{1,0:T(8,128)(2,1)S(1)} %slice_select_fusion), channel_id=1, source_target_pairs={{4,16}} | collective-permute-start | bytes 393224 | tf_op jit(solution)/shard_map/ppermute | solution.py:37
  3.7 4.3 %collective-permute-start.9 = (bf16[256,256]{1,0:T(8,128)(2,1)S(1)}, bf16[256,256]{1,0:T(8,128)(2,1)S(1)}, u32[]{:S(2)}, u32[]{:S(2)}) collective-permute-start(bf16[256,256]{1,0:T(8,128)(2,1)S(1)} %slice_select_fusion), channel_id=1, source_target_pairs={{4,20}} | collective-permute-start | bytes 393224 | tf_op jit(solution)/shard_map/ppermute | solution.py:37
  4.5 4.3 %collective-permute-start.12 = (bf16[256,512]{1,0:T(8,128)(2,1)S(1)}, bf16[256,512]{1,0:T(8,128)(2,1)S(1)}, u32[]{:S(2)}, u32[]{:S(2)}) collective-permute-start(bf16[256,512]{1,0:T(8,128)(2,1)S(1)} %broadcast_select_fusion), channel_id=1, source_target_pairs={{2,18},{6,22},{3,11},{19,27},{1,5},{17,21}} | collective-permute-start | bytes 786440 | tf_op jit(solution)/shard_map/ppermute | solution.py:37
  5.4 14.5 %collective-permute-start.4 = (bf16[256,256]{1,0:T(8,128)(2,1)S(1)}, bf16[256,256]{1,0:T(8,128)(2,1)S(1)}, u32[]{:S(2)}, u32[]{:S(2)}) collective-permute-start(bf16[256,256]{1,0:T(8,128)(2,1)S(1)} %get-tuple-element.22), channel_id=1, source_target_pairs={{0,10},{4,14},{16,26},{20,30}} | collective-permute-start | bytes 393224 | tf_op jit(solution)/shard_map/ppermute | solution.py:37
  6.7 13.2 %collective-permute-start.5 = (bf16[256,256]{1,0:T(8,128)(2,1)S(1)}, bf16[256,256]{1,0:T(8,128)(2,1)S(1)}, u32[]{:S(2)}, u32[]{:S(2)}) collective-permute-start(bf16[256,256]{1,0:T(8,128)(2,1)S(1)} %get-tuple-element.22), channel_id=1, source_target_pairs={{0,8},{4,12},{16,24},{20,28}} | collective-permute-start | bytes 393224 | tf_op jit(solution)/shard_map/ppermute | solution.py:37
  7.4 13.8 %collective-permute-start.8 = (bf16[256,256]{1,0:T(8,128)(2,1)S(1)}, bf16[256,256]{1,0:T(8,128)(2,1)S(1)}, u32[]{:S(2)}, u32[]{:S(2)}) collective-permute-start(bf16[256,256]{1,0:T(8,128)(2,1)S(1)} %slice_select_fusion), channel_id=1, source_target_pairs={{0,8},{4,12}} | collective-permute-start | bytes 393224 | tf_op jit(solution)/shard_map/ppermute | solution.py:37
  8.1 1.4 %collective-permute-start.3 = (bf16[256,256]{1,0:T(8,128)(2,1)S(1)}, bf16[256,256]{1,0:T(8,128)(2,1)S(1)}, u32[]{:S(2)}, u32[]{:S(2)}) collective-permute-start(bf16[256,256]{1,0:T(8,128)(2,1)S(1)} %get-tuple-element.21), channel_id=1, source_target_pairs={{20,22},{4,6},{16,18}} | collective-permute-start | bytes 393224 | tf_op jit(solution)/shard_map/ppermute | solution.py:37
  8.8 12.4 %collective-permute-start.11 = (bf16[256,256]{1,0:T(8,128)(2,1)S(1)}, bf16[256,256]{1,0:T(8,128)(2,1)S(1)}, u32[]{:S(2)}, u32[]{:S(2)}) collective-permute-start(bf16[256,256]{1,0:T(8,128)(2,1)S(1)} %select_select_fusion.3), channel_id=1, source_target_pairs={{16,24},{20,28}} | collective-permute-start | bytes 393224 | tf_op jit(solution)/shard_map/ppermute | solution.py:37
  9.5 19.6 %collective-permute-start.13 = (bf16[256,512]{1,0:T(8,128)(2,1)S(1)}, bf16[256,512]{1,0:T(8,128)(2,1)S(1)}, u32[]{:S(2)}, u32[]{:S(2)}) collective-permute-start(bf16[256,512]{1,0:T(8,128)(2,1)S(1)} %broadcast_select_fusion.1), channel_id=1, source_target_pairs={{2,10},{6,14},{18,26},{22,30},{3,7},{19,23},{11,15},{27,31},{1,9},... | collective-permute-start | bytes 786440 | tf_op jit(solution)/shard_map/ppermute | solution.py:37
  19.9 2.3 %collective-permute-start.6 = (bf16[256,256]{1,0:T(8,128)(2,1)S(1)}, bf16[256,256]{1,0:T(8,128)(2,1)S(1)}, u32[]{:S(2)}, u32[]{:S(2)}) collective-permute-start(bf16[256,256]{1,0:T(8,128)(2,1)S(1)} %select_select_fusion.4), channel_id=1, source_target_pairs={{4,5},{6,7},{8,9},{10,11},{12,13},{14,15},{16,17},{18,19},{20,21},... | collective-permute-start | bytes 393224 | tf_op jit(solution)/shard_map/ppermute | solution.py:37

commit v13 on v11

--- a/solution.py
+++ b/solution.py
@@ -103,15 +103,16 @@
     working = (row_here & APART == 0) & (col_here == 0)
     lower, lower_far = lax.cond(working, compute, none, square, partner)
     received = lower
+    both = jnp.concatenate([lower_far, near_upper], axis=1)
     for c in range(0, n_col, 2):
-        got = send(lower_far, [((r, 0), (r + APART, c)) for r in workers])
-        received = jnp.where((row_here & APART != 0) & (col_here == c), got, received)
+        got = send(lower_far if c else both, [((r, 0), (r + APART, c)) for r in workers])
+        if c == 0:
+            near_upper = jnp.where(row_here & APART != 0, got[:, NB:], near_upper)
+        takes = (row_here & APART != 0) & (col_here == c)
+        received = jnp.where(takes, got[:, :NB], received)
     for c in range(2, n_col, 2):
         got = send(lower, [((r, 0), (r, c)) for r in targets])
         received = jnp.where((row_here & APART == 0) & (col_here == c), got, received)
-    near_sent, _ = lax.optimization_barrier((near_upper, lower))
-    got = send(near_sent, [((r, 0), (r + APART, 0)) for r in workers])
-    near_upper = jnp.where(row_here & APART != 0, got, near_upper)
     for step in range(2, len(down)):
         upper, _ = upper_step(upper, step, upper)
     got = send(

time: 27.4 us -> 29.6 us (1.080)
  the two profiles are of different devices: /device:TPU:11 before, /device:TPU:31 now
where the time goes in v13:
time: 29.6 us; the launch traced here: 29.2 us
  waiting for transfers between devices  17 us (57%)
  starting transfers between devices  9.46 us (32%)
  local copies, waits for them, and re-layouts  1.08 us (4%)
  matrix products  1.07 us (4%)
  between operations  0.42 us (1%)
    ppermute x12, waiting for transfers between devices, send(): return lax.ppermute(value, ('row', 'col'), flat)  17 us
    ppermute x12, starting transfers between devices, send(): return lax.ppermute(value, ('row', 'col'), flat)  9.46 us
    dot_general x1, matrix products, shards(): return matrix - jnp.dot(received, upper, preferred_element_type=jnp.float32)  1.07 us
    slice x1, local copies, waits for them, and re-layouts, shards(): square, partner = (matrix[:, :NB], matrix[:, :NB])  0.97 us
  transfers between devices with their start and end apart: 12, of which 2 were waited for; matrix products, arithmetic and copies ran while one was open for 4% of the time, Pallas kernels for 0%

profile of v13, /device:TPU:31, one launch (start us, length us, event | category | flops | bytes accessed | tf_op | source)
XLA Modules:
  0.0 29.2 jit_solution(9299610401245712005)
XLA Ops:
  0.0 0.1 conditional.2
  0.1 0.7 %collective-permute-start.5 = (bf16[256,512]{1,0:T(8,128)(2,1)S(1)}, bf16[256,512]{1,0:T(8,128)(2,1)S(1)}, u32[]{:S(2)}, u32[]{:S(2)}) collective-permute-start(bf16[256,512]{1,0:T(8,128)(2,1)S(1)} %get-tuple-element.22), channel_id=1, source_target_pairs={{0,4},{2,6},{3,19},{1,17}} | collective-permute-start | bytes 786440 | tf_op jit(solution)/shard_map/ppermute | solution.py:37
  0.7 0.7 %collective-permute-start.2 = (f32[256,256]{1,0:T(8,128)S(1)}, f32[256,256]{1,0:T(8,128)S(1)}, u32[]{:S(2)}, u32[]{:S(2)}) collective-permute-start(f32[256,256]{1,0:T(8,128)S(1)} %get-tuple-element.19), channel_id=1, source_target_pairs={{0,16}} | collective-permute-start | bytes 786440 | tf_op jit(solution)/shard_map/ppermute | solution.py:37
  1.4 0.7 %collective-permute-start.1 = (f32[256,256]{1,0:T(8,128)S(1)}, f32[256,256]{1,0:T(8,128)S(1)}, u32[]{:S(2)}, u32[]{:S(2)}) collective-permute-start(f32[256,256]{1,0:T(8,128)S(1)} %get-tuple-element.19), channel_id=1, source_target_pairs={{0,4},{28,20}} | collective-permute-start | bytes 786440 | tf_op jit(solution)/shard_map/ppermute | solution.py:37
  2.1 0.7 %collective-permute-start = (f32[256,256]{1,0:T(8,128)S(1)}, f32[256,256]{1,0:T(8,128)S(1)}, u32[]{:S(2)}, u32[]{:S(2)}) collective-permute-start(f32[256,256]{1,0:T(8,128)S(1)} %get-tuple-element.19), channel_id=1, source_target_pairs={{0,20},{8,0},{12,4},{24,16}} | collective-permute-start | bytes 786440 | tf_op jit(solution)/shard_map/ppermute | solution.py:37
  2.8 1.0 %slice.34 = f32[256,256]{1,0:T(8,128)S(1)} slice(f32[256,512]{1,0:T(8,128)} %param.5), slice={[0:256], [0:256]} | slice | bytes 524288 | tf_op jit(solution)/shard_map/slice | solution.py:77
  3.9 0.0 collective-permute-done.5
  3.9 0.0 copy-start
  3.9 0.8 %collective-permute-start.7 = (bf16[256,256]{1,0:T(8,128)(2,1)S(1)}, bf16[256,256]{1,0:T(8,128)(2,1)S(1)}, u32[]{:S(2)}, u32[]{:S(2)}) collective-permute-start(bf16[256,256]{1,0:T(8,128)(2,1)S(1)} %slice_select_fusion.2), channel_id=1, source_target_pairs={{4,16}} | collective-permute-start | bytes 393224 | tf_op jit(solution)/shard_map/ppermute | solution.py:37
  4.7 0.7 %collective-permute-start.6 = (bf16[256,256]{1,0:T(8,128)(2,1)S(1)}, bf16[256,256]{1,0:T(8,128)(2,1)S(1)}, u32[]{:S(2)}, u32[]{:S(2)}) collective-permute-start(bf16[256,256]{1,0:T(8,128)(2,1)S(1)} %slice_select_fusion.2), channel_id=1, source_target_pairs={{4,20}} | collective-permute-start | bytes 393224 | tf_op jit(solution)/shard_map/ppermute | solution.py:37
  5.5 0.0 collective-permute-done.2
  5.5 0.7 %collective-permute-start.10 = (bf16[256,512]{1,0:T(8,128)(2,1)S(1)}, bf16[256,512]{1,0:T(8,128)(2,1)S(1)}, u32[]{:S(2)}, u32[]{:S(2)}) collective-permute-start(bf16[256,512]{1,0:T(8,128)(2,1)S(1)} %broadcast_select_fusion), channel_id=1, source_target_pairs={{2,18},{6,22},{3,11},{19,27},{1,5},{17,21}} | collective-permute-start | bytes 786440 | tf_op jit(solution)/shard_map/ppermute | solution.py:37
  6.2 0.0 collective-permute-done.1
  6.2 0.0 collective-permute-done
  6.2 0.0 copy-done
  6.2 0.1 conditional.3
  6.3 0.0 collective-permute-done.7
  6.3 0.0 collective-permute-done.6
  6.4 0.7 %collective-permute-start.8 = (bf16[256,512]{1,0:T(8,128)(2,1)S(1)}, bf16[256,512]{1,0:T(8,128)(2,1)S(1)}, u32[]{:S(2)}, u32[]{:S(2)}) collective-permute-start(bf16[256,512]{1,0:T(8,128)(2,1)S(1)} %pad_maximum_fusion), channel_id=1, source_target_pairs={{0,8},{4,12},{16,24},{20,28}} | collective-permute-start | bytes 786440 | tf_op jit(solution)/shard_map/ppermute | solution.py:37
  7.1 0.7 %collective-permute-start.4 = (bf16[256,256]{1,0:T(8,128)(2,1)S(1)}, bf16[256,256]{1,0:T(8,128)(2,1)S(1)}, u32[]{:S(2)}, u32[]{:S(2)}) collective-permute-start(bf16[256,256]{1,0:T(8,128)(2,1)S(1)} %get-tuple-element.21), channel_id=1, source_target_pairs={{0,10},{4,14},{16,26},{20,30}} | collective-permute-start | bytes 393224 | tf_op jit(solution)/shard_map/ppermute | solution.py:37
  7.8 0.7 %collective-permute-start.3 = (bf16[256,256]{1,0:T(8,128)(2,1)S(1)}, bf16[256,256]{1,0:T(8,128)(2,1)S(1)}, u32[]{:S(2)}, u32[]{:S(2)}) collective-permute-start(bf16[256,256]{1,0:T(8,128)(2,1)S(1)} %get-tuple-element.20), channel_id=1, source_target_pairs={{20,22},{4,6},{16,18}} | collective-permute-start | bytes 393224 | tf_op jit(solution)/shard_map/ppermute | solution.py:37
  8.5 0.0 collective-permute-done.10
  8.5 1.3 %collective-permute-start.11 = (bf16[256,512]{1,0:T(8,128)(2,1)S(1)}, bf16[256,512]{1,0:T(8,128)(2,1)S(1)}, u32[]{:S(2)}, u32[]{:S(2)}) collective-permute-start(bf16[256,512]{1,0:T(8,128)(2,1)S(1)} %broadcast_select_fusion.1), channel_id=1, source_target_pairs={{2,10},{6,14},{18,26},{22,30},{3,7},{19,23},{11,15},{27,31},{1,9},... | collective-permute-start | bytes 786440 | tf_op jit(solution)/shard_map/ppermute | solution.py:37
  9.8 0.0 collective-permute-done.3
  9.8 0.0 collective-permute-done.4
  9.8 0.0 collective-permute-done.8
  9.9 1.3 %collective-permute-start.9 = (bf16[256,256]{1,0:T(8,128)(2,1)S(1)}, bf16[256,256]{1,0:T(8,128)(2,1)S(1)}, u32[]{:S(2)}, u32[]{:S(2)}) collective-permute-start(bf16[256,256]{1,0:T(8,128)(2,1)S(1)} %get-tuple-element.81), channel_id=1, source_target_pairs={{4,5},{6,7},{8,9},{10,11},{12,13},{14,15},{16,17},{18,19},{20,21},... | collective-permute-start | bytes 393224 | tf_op jit(solution)/shard_map/ppermute | solution.py:37
  11.2 9.2 %collective-permute-done.11 = bf16[256,512]{1,0:T(8,128)(2,1)S(1)} collective-permute-done((bf16[256,512]{1,0:T(8,128)(2,1)S(1)}, bf16[256,512]{1,0:T(8,128)(2,1)S(1)}, u32[]{:S(2)}, u32[]{:S(2)}) %collective-permute-start.11) | collective-permute-done | bytes 262176 | tf_op jit(solution)/shard_map/ppermute | solution.py:37
  20.5 7.7 %collective-permute-done.9 = bf16[256,256]{1,0:T(8,128)(2,1)S(1)} collective-permute-done((bf16[256,256]{1,0:T(8,128)(2,1)S(1)}, bf16[256,256]{1,0:T(8,128)(2,1)S(1)}, u32[]{:S(2)}, u32[]{:S(2)}) %collective-permute-start.9) | collective-permute-done | bytes 131104 | tf_op jit(solution)/shard_map/ppermute | solution.py:37
  28.2 1.1 %convolution_subtract_fusion = f32[256,512]{1,0:T(8,128)} fusion(f32[256,512]{1,0:T(8,128)S(1)} %copy-done, bf16[256,512]{1,0:T(8,128)(2,1)S(1)} %collective-permute-done.11, bf16[256,512]{1,0:T(8,128)(2,1)S(1)} %broadcast_select_fusion.1, bf16[256,256]{1,0:T(8,128)(2,1)S(1)} %get-tuple-element.82, pred[]{:T(512)S(6)} %or.23, pred[]{:T(512)S(6)} %eq.93, ...), kind=kOutput, calls=%fused_computation.34 | convolution fusion | flops 67633152 | bytes 1966084 | tf_op jit(solution)/shard_map/dot_general | solution.py:126
  (13 shorter events, 0.3 us)
Async XLA Ops:
  0.1 3.8 %collective-permute-start.5 = (bf16[256,512]{1,0:T(8,128)(2,1)S(1)}, bf16[256,512]{1,0:T(8,128)(2,1)S(1)}, u32[]{:S(2)}, u32[]{:S(2)}) collective-permute-start(bf16[256,512]{1,0:T(8,128)(2,1)S(1)} %get-tuple-element.22), channel_id=1, source_target_pairs={{0,4},{2,6},{3,19},{1,17}} | collective-permute-start | bytes 786440 | tf_op jit(solution)/shard_map/ppermute | solution.py:37
  0.7 4.7 %collective-permute-start.2 = (f32[256,256]{1,0:T(8,128)S(1)}, f32[256,256]{1,0:T(8,128)S(1)}, u32[]{:S(2)}, u32[]{:S(2)}) collective-permute-start(f32[256,256]{1,0:T(8,128)S(1)} %get-tuple-element.19), channel_id=1, source_target_pairs={{0,16}} | collective-permute-start | bytes 786440 | tf_op jit(solution)/shard_map/ppermute | solution.py:37
  1.4 4.7 %collective-permute-start.1 = (f32[256,256]{1,0:T(8,128)S(1)}, f32[256,256]{1,0:T(8,128)S(1)}, u32[]{:S(2)}, u32[]{:S(2)}) collective-permute-start(f32[256,256]{1,0:T(8,128)S(1)} %get-tuple-element.19), channel_id=1, source_target_pairs={{0,4},{28,20}} | collective-permute-start | bytes 786440 | tf_op jit(solution)/shard_map/ppermute | solution.py:37
  2.1 4.1 %collective-permute-start = (f32[256,256]{1,0:T(8,128)S(1)}, f32[256,256]{1,0:T(8,128)S(1)}, u32[]{:S(2)}, u32[]{:S(2)}) collective-permute-start(f32[256,256]{1,0:T(8,128)S(1)} %get-tuple-element.19), channel_id=1, source_target_pairs={{0,20},{8,0},{12,4},{24,16}} | collective-permute-start | bytes 786440 | tf_op jit(solution)/shard_map/ppermute | solution.py:37
  3.9 2.3 %copy-start = (f32[256,512]{1,0:T(8,128)S(1)}, f32[256,512]{1,0:T(8,128)}, u32[]{:S(2)}) copy-start(f32[256,512]{1,0:T(8,128)} %param.5) | copy-start | bytes 1572868
  3.9 2.4 %collective-permute-start.7 = (bf16[256,256]{1,0:T(8,128)(2,1)S(1)}, bf16[256,256]{1,0:T(8,128)(2,1)S(1)}, u32[]{:S(2)}, u32[]{:S(2)}) collective-permute-start(bf16[256,256]{1,0:T(8,128)(2,1)S(1)} %slice_select_fusion.2), channel_id=1, source_target_pairs={{4,16}} | collective-permute-start | bytes 393224 | tf_op jit(solution)/shard_map/ppermute | solution.py:37
  4.7 1.6 %collective-permute-start.6 = (bf16[256,256]{1,0:T(8,128)(2,1)S(1)}, bf16[256,256]{1,0:T(8,128)(2,1)S(1)}, u32[]{:S(2)}, u32[]{:S(2)}) collective-permute-start(bf16[256,256]{1,0:T(8,128)(2,1)S(1)} %slice_select_fusion.2), channel_id=1, source_target_pairs={{4,20}} | collective-permute-start | bytes 393224 | tf_op jit(solution)/shard_map/ppermute | solution.py:37
  5.5 3.0 %collective-permute-start.10 = (bf16[256,512]{1,0:T(8,128)(2,1)S(1)}, bf16[256,512]{1,0:T(8,128)(2,1)S(1)}, u32[]{:S(2)}, u32[]{:S(2)}) collective-permute-start(bf16[256,512]{1,0:T(8,128)(2,1)S(1)} %broadcast_select_fusion), channel_id=1, source_target_pairs={{2,18},{6,22},{3,11},{19,27},{1,5},{17,21}} | collective-permute-start | bytes 786440 | tf_op jit(solution)/shard_map/ppermute | solution.py:37
  6.4 3.5 %collective-permute-start.8 = (bf16[256,512]{1,0:T(8,128)(2,1)S(1)}, bf16[256,512]{1,0:T(8,128)(2,1)S(1)}, u32[]{:S(2)}, u32[]{:S(2)}) collective-permute-start(bf16[256,512]{1,0:T(8,128)(2,1)S(1)} %pad_maximum_fusion), channel_id=1, source_target_pairs={{0,8},{4,12},{16,24},{20,28}} | collective-permute-start | bytes 786440 | tf_op jit(solution)/shard_map/ppermute | solution.py:37
  7.1 2.7 %collective-permute-start.4 = (bf16[256,256]{1,0:T(8,128)(2,1)S(1)}, bf16[256,256]{1,0:T(8,128)(2,1)S(1)}, u32[]{:S(2)}, u32[]{:S(2)}) collective-permute-start(bf16[256,256]{1,0:T(8,128)(2,1)S(1)} %get-tuple-element.21), channel_id=1, source_target_pairs={{0,10},{4,14},{16,26},{20,30}} | collective-permute-start | bytes 393224 | tf_op jit(solution)/shard_map/ppermute | solution.py:37
  7.8 2.0 %collective-permute-start.3 = (bf16[256,256]{1,0:T(8,128)(2,1)S(1)}, bf16[256,256]{1,0:T(8,128)(2,1)S(1)}, u32[]{:S(2)}, u32[]{:S(2)}) collective-permute-start(bf16[256,256]{1,0:T(8,128)(2,1)S(1)} %get-tuple-element.20), channel_id=1, source_target_pairs={{20,22},{4,6},{16,18}} | collective-permute-start | bytes 393224 | tf_op jit(solution)/shard_map/ppermute | solution.py:37
  8.5 12.0 %collective-permute-start.11 = (bf16[256,512]{1,0:T(8,128)(2,1)S(1)}, bf16[256,512]{1,0:T(8,128)(2,1)S(1)}, u32[]{:S(2)}, u32[]{:S(2)}) collective-permute-start(bf16[256,512]{1,0:T(8,128)(2,1)S(1)} %broadcast_select_fusion.1), channel_id=1, source_target_pairs={{2,10},{6,14},{18,26},{22,30},{3,7},{19,23},{11,15},{27,31},{1,9},... | collective-permute-start | bytes 786440 | tf_op jit(solution)/shard_map/ppermute | solution.py:37
  9.9 18.3 %collective-permute-start.9 = (bf16[256,256]{1,0:T(8,128)(2,1)S(1)}, bf16[256,256]{1,0:T(8,128)(2,1)S(1)}, u32[]{:S(2)}, u32[]{:S(2)}) collective-permute-start(bf16[256,256]{1,0:T(8,128)(2,1)S(1)} %get-tuple-element.81), channel_id=1, source_target_pairs={{4,5},{6,7},{8,9},{10,11},{12,13},{14,15},{16,17},{18,19},{20,21},... | collective-permute-start | bytes 393224 | tf_op jit(solution)/shard_map/ppermute | solution.py:37

commit v14 on v11

--- a/solution.py
+++ b/solution.py
@@ -86,9 +86,9 @@
         for r in served:
             partner = jnp.where(row_here == r, got, partner)
     near_sent = near_upper
-    for target in workers[2:]:
-        got = send(near_sent, [((1, 0), (target, 0))])
-        near_upper = jnp.where(row_here == target, got, near_upper)
+    for even, odd in zip(workers[2::2], workers[3::2]):
+        got = send(near_sent, [((0, 0), (even, 0)), ((1, 0), (odd, 0))])
+        near_upper = jnp.where((row_here | 1) == odd, got, near_upper)
     upper, _ = upper_step(upper, 1, upper)
 
     def compute(square, partner):

time: 27.4 us -> 27.4 us (level)
  waiting for transfers between devices: 15.1 us -> 15.8 us
  starting transfers between devices: 10.1 us -> 9.45 us
    ppermute x13 -> x12, waiting for transfers between devices: 15.1 us -> 15.8 us  [send(): return lax.ppermute(value, ('row', 'col'), flat)]
    ppermute x13 -> x12, starting transfers between devices: 10.1 us -> 9.45 us  [send(): return lax.ppermute(value, ('row', 'col'), flat)]
  transfers between devices with their start and end apart: 13 -> 12, of which waited for: 1 -> 1; matrix products, arithmetic and copies ran while one was open for 1% -> 1% of each run, Pallas kernels for 0% -> 0%
where the time goes in v14:
time: 27.4 us; the launch traced here: 27.1 us
  waiting for transfers between devices  15.8 us (58%)
  starting transfers between devices  9.45 us (34%)
  matrix products  1.07 us (4%)
  between operations  0.41 us (1%)
    ppermute x12, waiting for transfers between devices, send(): return lax.ppermute(value, ('row', 'col'), flat)  15.8 us
    ppermute x12, starting transfers between devices, send(): return lax.ppermute(value, ('row', 'col'), flat)  9.45 us
    dot_general x1, matrix products, shards(): return matrix - jnp.dot(received, upper, preferred_element_type=jnp.float32)  1.07 us
  transfers between devices with their start and end apart: 12, of which 1 were waited for; matrix products, arithmetic and copies ran while one was open for 1% of the time, Pallas kernels for 0%

profile of v14, /device:TPU:11, one launch (start us, length us, event | category | flops | bytes accessed | tf_op | source)
XLA Modules:
  0.0 27.1 jit_solution(9104421967078721824)
XLA Ops:
  0.0 0.1 conditional.2
  0.1 0.7 %collective-permute-start.7 = (bf16[256,512]{1,0:T(8,128)(2,1)S(1)}, bf16[256,512]{1,0:T(8,128)(2,1)S(1)}, u32[]{:S(2)}, u32[]{:S(2)}) collective-permute-start(bf16[256,512]{1,0:T(8,128)(2,1)S(1)} %get-tuple-element.23), channel_id=1, source_target_pairs={{0,4},{2,6},{3,19},{1,17}} | collective-permute-start | bytes 786440 | tf_op jit(solution)/shard_map/ppermute | solution.py:37
  0.7 0.7 %collective-permute-start = (f32[256,256]{1,0:T(8,128)S(1)}, f32[256,256]{1,0:T(8,128)S(1)}, u32[]{:S(2)}, u32[]{:S(2)}) collective-permute-start(f32[256,256]{1,0:T(8,128)S(1)} %get-tuple-element.20), channel_id=1, source_target_pairs={{0,20},{8,0},{12,4},{24,16}} | collective-permute-start | bytes 786440 | tf_op jit(solution)/shard_map/ppermute | solution.py:37
  1.4 0.7 %collective-permute-start.1 = (f32[256,256]{1,0:T(8,128)S(1)}, f32[256,256]{1,0:T(8,128)S(1)}, u32[]{:S(2)}, u32[]{:S(2)}) collective-permute-start(f32[256,256]{1,0:T(8,128)S(1)} %get-tuple-element.20), channel_id=1, source_target_pairs={{0,4},{28,20}} | collective-permute-start | bytes 786440 | tf_op jit(solution)/shard_map/ppermute | solution.py:37
  2.1 0.7 %collective-permute-start.2 = (f32[256,256]{1,0:T(8,128)S(1)}, f32[256,256]{1,0:T(8,128)S(1)}, u32[]{:S(2)}, u32[]{:S(2)}) collective-permute-start(f32[256,256]{1,0:T(8,128)S(1)} %get-tuple-element.20), channel_id=1, source_target_pairs={{0,16}} | collective-permute-start | bytes 786440 | tf_op jit(solution)/shard_map/ppermute | solution.py:37
  2.9 0.0 copy-start
  2.9 0.0 collective-permute-done.7
  2.9 0.8 %collective-permute-start.8 = (bf16[256,256]{1,0:T(8,128)(2,1)S(1)}, bf16[256,256]{1,0:T(8,128)(2,1)S(1)}, u32[]{:S(2)}, u32[]{:S(2)}) collective-permute-start(bf16[256,256]{1,0:T(8,128)(2,1)S(1)} %slice_select_fusion), channel_id=1, source_target_pairs={{0,16},{4,20}} | collective-permute-start | bytes 393224 | tf_op jit(solution)/shard_map/ppermute | solution.py:37
  3.8 0.7 %collective-permute-start.10 = (bf16[256,512]{1,0:T(8,128)(2,1)S(1)}, bf16[256,512]{1,0:T(8,128)(2,1)S(1)}, u32[]{:S(2)}, u32[]{:S(2)}) collective-permute-start(bf16[256,512]{1,0:T(8,128)(2,1)S(1)} %broadcast_select_fusion), channel_id=1, source_target_pairs={{2,18},{6,22},{3,11},{19,27},{1,5},{17,21}} | collective-permute-start | bytes 786440 | tf_op jit(solution)/shard_map/ppermute | solution.py:37
  4.5 0.0 copy-done
  4.6 0.0 collective-permute-done
  4.6 0.0 collective-permute-done.1
  4.6 0.0 collective-permute-done.2
  4.7 0.1 conditional.3
  4.7 0.7 %collective-permute-start.4 = (bf16[256,256]{1,0:T(8,128)(2,1)S(1)}, bf16[256,256]{1,0:T(8,128)(2,1)S(1)}, u32[]{:S(2)}, u32[]{:S(2)}) collective-permute-start(bf16[256,256]{1,0:T(8,128)(2,1)S(1)} %get-tuple-element.22), channel_id=1, source_target_pairs={{0,10},{4,14},{16,26},{20,30}} | collective-permute-start | bytes 393224 | tf_op jit(solution)/shard_map/ppermute | solution.py:37
  5.4 0.7 %collective-permute-start.5 = (bf16[256,256]{1,0:T(8,128)(2,1)S(1)}, bf16[256,256]{1,0:T(8,128)(2,1)S(1)}, u32[]{:S(2)}, u32[]{:S(2)}) collective-permute-start(bf16[256,256]{1,0:T(8,128)(2,1)S(1)} %get-tuple-element.22), channel_id=1, source_target_pairs={{0,8},{4,12},{16,24},{20,28}} | collective-permute-start | bytes 393224 | tf_op jit(solution)/shard_map/ppermute | solution.py:37
  6.1 0.7 %collective-permute-start.3 = (bf16[256,256]{1,0:T(8,128)(2,1)S(1)}, bf16[256,256]{1,0:T(8,128)(2,1)S(1)}, u32[]{:S(2)}, u32[]{:S(2)}) collective-permute-start(bf16[256,256]{1,0:T(8,128)(2,1)S(1)} %get-tuple-element.21), channel_id=1, source_target_pairs={{20,22},{4,6},{16,18}} | collective-permute-start | bytes 393224 | tf_op jit(solution)/shard_map/ppermute | solution.py:37
  6.8 0.0 collective-permute-done.8
  6.8 0.7 %collective-permute-start.9 = (bf16[256,256]{1,0:T(8,128)(2,1)S(1)}, bf16[256,256]{1,0:T(8,128)(2,1)S(1)}, u32[]{:S(2)}, u32[]{:S(2)}) collective-permute-start(bf16[256,256]{1,0:T(8,128)(2,1)S(1)} %broadcast_select_fusion.3), channel_id=1, source_target_pairs={{0,8},{4,12},{16,24},{20,28}} | collective-permute-start | bytes 393224 | tf_op jit(solution)/shard_map/ppermute | solution.py:37
  7.5 0.0 collective-permute-done.10
  7.5 1.3 %collective-permute-start.11 = (bf16[256,512]{1,0:T(8,128)(2,1)S(1)}, bf16[256,512]{1,0:T(8,128)(2,1)S(1)}, u32[]{:S(2)}, u32[]{:S(2)}) collective-permute-start(bf16[256,512]{1,0:T(8,128)(2,1)S(1)} %broadcast_select_fusion.1), channel_id=1, source_target_pairs={{2,10},{6,14},{18,26},{22,30},{3,7},{19,23},{11,15},{27,31},{1,9},... | collective-permute-start | bytes 786440 | tf_op jit(solution)/shard_map/ppermute | solution.py:37
  8.8 0.0 collective-permute-done.3
  8.8 0.0 collective-permute-done.4
  8.8 0.0 collective-permute-done.5
  8.9 1.3 %collective-permute-start.6 = (bf16[256,256]{1,0:T(8,128)(2,1)S(1)}, bf16[256,256]{1,0:T(8,128)(2,1)S(1)}, u32[]{:S(2)}, u32[]{:S(2)}) collective-permute-start(bf16[256,256]{1,0:T(8,128)(2,1)S(1)} %select_select_fusion.2), channel_id=1, source_target_pairs={{4,5},{6,7},{8,9},{10,11},{12,13},{14,15},{16,17},{18,19},{20,21},... | collective-permute-start | bytes 393224 | tf_op jit(solution)/shard_map/ppermute | solution.py:37
  10.2 0.0 collective-permute-done.9
  10.2 15.8 %collective-permute-done.6 = bf16[256,256]{1,0:T(8,128)(2,1)S(1)} collective-permute-done((bf16[256,256]{1,0:T(8,128)(2,1)S(1)}, bf16[256,256]{1,0:T(8,128)(2,1)S(1)}, u32[]{:S(2)}, u32[]{:S(2)}) %collective-permute-start.6) | collective-permute-done | bytes 131104 | tf_op jit(solution)/shard_map/ppermute | solution.py:37
  26.0 0.0 collective-permute-done.11
  26.0 1.1 %convolution_subtract_fusion = f32[256,512]{1,0:T(8,128)} fusion(f32[256,512]{1,0:T(8,128)S(1)} %copy-done, bf16[256,512]{1,0:T(8,128)(2,1)S(1)} %collective-permute-done.11, bf16[256,512]{1,0:T(8,128)(2,1)S(1)} %broadcast_select_fusion.1, bf16[256,256]{1,0:T(8,128)(2,1)S(1)} %broadcast_select_fusion.4, pred[]{:T(512)S(6)} %or.27, pred[]{:T(512)S(6)} %eq.94, ...), kind=kOutput, calls=%fused_computation.34 | convolution fusion | flops 67633152 | bytes 1966084 | tf_op jit(solution)/shard_map/dot_general | solution.py:125
  (14 shorter events, 0.3 us)
Async XLA Ops:
  0.1 2.8 %collective-permute-start.7 = (bf16[256,512]{1,0:T(8,128)(2,1)S(1)}, bf16[256,512]{1,0:T(8,128)(2,1)S(1)}, u32[]{:S(2)}, u32[]{:S(2)}) collective-permute-start(bf16[256,512]{1,0:T(8,128)(2,1)S(1)} %get-tuple-element.23), channel_id=1, source_target_pairs={{0,4},{2,6},{3,19},{1,17}} | collective-permute-start | bytes 786440 | tf_op jit(solution)/shard_map/ppermute | solution.py:37
  0.7 3.8 %collective-permute-start = (f32[256,256]{1,0:T(8,128)S(1)}, f32[256,256]{1,0:T(8,128)S(1)}, u32[]{:S(2)}, u32[]{:S(2)}) collective-permute-start(f32[256,256]{1,0:T(8,128)S(1)} %get-tuple-element.20), channel_id=1, source_target_pairs={{0,20},{8,0},{12,4},{24,16}} | collective-permute-start | bytes 786440 | tf_op jit(solution)/shard_map/ppermute | solution.py:37
  1.4 3.2 %collective-permute-start.1 = (f32[256,256]{1,0:T(8,128)S(1)}, f32[256,256]{1,0:T(8,128)S(1)}, u32[]{:S(2)}, u32[]{:S(2)}) collective-permute-start(f32[256,256]{1,0:T(8,128)S(1)} %get-tuple-element.20), channel_id=1, source_target_pairs={{0,4},{28,20}} | collective-permute-start | bytes 786440 | tf_op jit(solution)/shard_map/ppermute | solution.py:37
  2.1 2.5 %collective-permute-start.2 = (f32[256,256]{1,0:T(8,128)S(1)}, f32[256,256]{1,0:T(8,128)S(1)}, u32[]{:S(2)}, u32[]{:S(2)}) collective-permute-start(f32[256,256]{1,0:T(8,128)S(1)} %get-tuple-element.20), channel_id=1, source_target_pairs={{0,16}} | collective-permute-start | bytes 786440 | tf_op jit(solution)/shard_map/ppermute | solution.py:37
  2.9 1.6 %copy-start = (f32[256,512]{1,0:T(8,128)S(1)}, f32[256,512]{1,0:T(8,128)}, u32[]{:S(2)}) copy-start(f32[256,512]{1,0:T(8,128)} %param.5) | copy-start | bytes 1572868
  2.9 3.8 %collective-permute-start.8 = (bf16[256,256]{1,0:T(8,128)(2,1)S(1)}, bf16[256,256]{1,0:T(8,128)(2,1)S(1)}, u32[]{:S(2)}, u32[]{:S(2)}) collective-permute-start(bf16[256,256]{1,0:T(8,128)(2,1)S(1)} %slice_select_fusion), channel_id=1, source_target_pairs={{0,16},{4,20}} | collective-permute-start | bytes 393224 | tf_op jit(solution)/shard_map/ppermute | solution.py:37
  3.8 3.7 %collective-permute-start.10 = (bf16[256,512]{1,0:T(8,128)(2,1)S(1)}, bf16[256,512]{1,0:T(8,128)(2,1)S(1)}, u32[]{:S(2)}, u32[]{:S(2)}) collective-permute-start(bf16[256,512]{1,0:T(8,128)(2,1)S(1)} %broadcast_select_fusion), channel_id=1, source_target_pairs={{2,18},{6,22},{3,11},{19,27},{1,5},{17,21}} | collective-permute-start | bytes 786440 | tf_op jit(solution)/shard_map/ppermute | solution.py:37
  4.7 4.1 %collective-permute-start.4 = (bf16[256,256]{1,0:T(8,128)(2,1)S(1)}, bf16[256,256]{1,0:T(8,128)(2,1)S(1)}, u32[]{:S(2)}, u32[]{:S(2)}) collective-permute-start(bf16[256,256]{1,0:T(8,128)(2,1)S(1)} %get-tuple-element.22), channel_id=1, source_target_pairs={{0,10},{4,14},{16,26},{20,30}} | collective-permute-start | bytes 393224 | tf_op jit(solution)/shard_map/ppermute | solution.py:37
  5.4 3.4 %collective-permute-start.5 = (bf16[256,256]{1,0:T(8,128)(2,1)S(1)}, bf16[256,256]{1,0:T(8,128)(2,1)S(1)}, u32[]{:S(2)}, u32[]{:S(2)}) collective-permute-start(bf16[256,256]{1,0:T(8,128)(2,1)S(1)} %get-tuple-element.22), channel_id=1, source_target_pairs={{0,8},{4,12},{16,24},{20,28}} | collective-permute-start | bytes 393224 | tf_op jit(solution)/shard_map/ppermute | solution.py:37
  6.1 2.7 %collective-permute-start.3 = (bf16[256,256]{1,0:T(8,128)(2,1)S(1)}, bf16[256,256]{1,0:T(8,128)(2,1)S(1)}, u32[]{:S(2)}, u32[]{:S(2)}) collective-permute-start(bf16[256,256]{1,0:T(8,128)(2,1)S(1)} %get-tuple-element.21), channel_id=1, source_target_pairs={{20,22},{4,6},{16,18}} | collective-permute-start | bytes 393224 | tf_op jit(solution)/shard_map/ppermute | solution.py:37
  6.8 3.4 %collective-permute-start.9 = (bf16[256,256]{1,0:T(8,128)(2,1)S(1)}, bf16[256,256]{1,0:T(8,128)(2,1)S(1)}, u32[]{:S(2)}, u32[]{:S(2)}) collective-permute-start(bf16[256,256]{1,0:T(8,128)(2,1)S(1)} %broadcast_select_fusion.3), channel_id=1, source_target_pairs={{0,8},{4,12},{16,24},{20,28}} | collective-permute-start | bytes 393224 | tf_op jit(solution)/shard_map/ppermute | solution.py:37
  7.5 18.5 %collective-permute-start.11 = (bf16[256,512]{1,0:T(8,128)(2,1)S(1)}, bf16[256,512]{1,0:T(8,128)(2,1)S(1)}, u32[]{:S(2)}, u32[]{:S(2)}) collective-permute-start(bf16[256,512]{1,0:T(8,128)(2,1)S(1)} %broadcast_select_fusion.1), channel_id=1, source_target_pairs={{2,10},{6,14},{18,26},{22,30},{3,7},{19,23},{11,15},{27,31},{1,9},... | collective-permute-start | bytes 786440 | tf_op jit(solution)/shard_map/ppermute | solution.py:37
  8.9 17.1 %collective-permute-start.6 = (bf16[256,256]{1,0:T(8,128)(2,1)S(1)}, bf16[256,256]{1,0:T(8,128)(2,1)S(1)}, u32[]{:S(2)}, u32[]{:S(2)}) collective-permute-start(bf16[256,256]{1,0:T(8,128)(2,1)S(1)} %select_select_fusion.2), channel_id=1, source_target_pairs={{4,5},{6,7},{8,9},{10,11},{12,13},{14,15},{16,17},{18,19},{20,21},... | collective-permute-start | bytes 393224 | tf_op jit(solution)/shard_map/ppermute | solution.py:37

commit v15 on v3

--- a/solution.py
+++ b/solution.py
@@ -46,42 +46,57 @@
     pivot_columns, first_upper = lax.cond(
         sends_columns | (row_here == 0), blocks, no_blocks, matrix
     )
-    upper = matrix.astype(jnp.bfloat16)
-    column_upper = upper[:, NB:]
+    upper = lax.optimization_barrier(jnp.where(row_here == 0, first_upper, 0))
 
     down = strides(n_row)
-    orders = [down, [down[-1]] + down[:-1]]
+    middle = n_row // 2
+    orders = [[down[-1]] + down[:-1], down]
     held = [[0], [0]]
+    beside_steps = [[(0, middle)], [(middle, middle + 1)]]
+    for stride in down[1:-1]:
+        far = [b for step in beside_steps for _, b in step]
+        beside_steps.append([(h, h + stride) for h in far])
+    beside_steps[-1].append((0, 1))
+    beside_back = [(middle + r - 2, r) for r in range(2, middle)]
+
+    def among(rows):
+        found = jnp.bool_(False)
+        for row in rows:
+            found = found | (row_here == row)
+        return found
 
     def upper_step(value, step, sent):
-        pairs = []
-        takes = []
+        pairs = [((a, 1), (b, 1)) for a, b in beside_steps[step]]
+        takes = (col_here == 1) & among([b for _, b in beside_steps[step]])
         for kind in range(2):
             stride = orders[kind][step]
             missing = sum(orders[kind][step + 1 :])
-            takes.append((row_here & (stride | missing)) == stride)
+            takes = takes | (
+                (col_here != 1)
+                & (col_here % 2 == kind)
+                & ((row_here & (stride | missing)) == stride)
+            )
             pairs += [
-                ((h, c), (h + stride, c)) for h in held[kind] for c in range(1, n_col) if c % 2 == kind
+                ((h, c), (h + stride, c))
+                for h in held[kind]
+                for c in range(3 * kind, n_col, 2)
             ]
             held[kind] = held[kind] + [h + stride for h in held[kind]]
         got = send(sent, pairs)
-        return jnp.where(jnp.where(col_here % 2 == 0, takes[0], takes[1]), got, value)
+        return jnp.where(takes, got, value)
 
     workers = [r for r in range(n_row) if r & APART == 0]
-    targets = workers[1:]
+    targets = workers[:1:-1]
+    targets.insert(1, 1)
     square, partner = matrix[:, :NB], matrix[:, :NB]
-    near_upper = column_upper
-    upper, column_upper = lax.optimization_barrier((upper_step(upper, 0, first_upper), column_upper))
+    upper = upper_step(upper, 0, first_upper)
     for index, target in reversed(list(enumerate(targets))):
-        served = [0, targets[-1]] if index == 0 else [targets[index - 1]]
+        served = [] if index > 1 else targets[:1] if index else [0] + targets[1:]
         pairs = [((0, 0), (target, 0))] + [((r + APART, 0), (r, 0)) for r in served]
         got = send(pivot_columns, pairs)
         square = jnp.where(row_here == target, got, square)
         for r in served:
             partner = jnp.where(row_here == r, got, partner)
-    for target in reversed(workers[1:]):
-        got = send(column_upper, [((0, 0), (target, 0))])
-        near_upper = jnp.where(row_here == target, got, near_upper)
     upper = upper_step(upper, 1, upper)
 
     def compute(square, partner):
@@ -96,27 +111,27 @@
     working = (row_here & APART == 0) & (col_here == 0)
     lower, lower_far = lax.cond(working, compute, none, square, partner)
     received = lower
-    for c in range(2, n_col, 2):
+    for c in range(0, n_col, 2):
         got = send(lower_far, [((r, 0), (r + APART, c)) for r in workers])
         received = jnp.where((row_here & APART != 0) & (col_here == c), got, received)
-    got = send(lower_far, [((r, 0), (r + APART, 0)) for r in workers])
-    received = jnp.where((row_here & APART != 0) & (col_here == 0), got, received)
     for c in range(2, n_col, 2):
         got = send(lower, [((r, 0), (r, c)) for r in targets])
         received = jnp.where((row_here & APART == 0) & (col_here == c), got, received)
-    near_sent, _ = lax.optimization_barrier((near_upper, lower))
-    got = send(near_sent, [((r, 0), (r + APART, 0)) for r in workers])
-    near_upper = jnp.where(row_here & APART == 0, near_upper, got)
+    sent = upper
     for step in range(2, len(down)):
         upper = upper_step(upper, step, upper)
+    if len(beside_back) > 2:
+        sent = upper
+    got = send(sent, [((a, 1), (b, 1)) for a, b in beside_back])
+    upper = jnp.where((col_here == 1) & (row_here > 1) & (row_here < middle), got, upper)
     got = send(
         received, [((r, c), (r, c + 1)) for r in range(1, n_row) for c in range(0, n_col, 2)]
     )
     received = jnp.where(col_here % 2 == 0, received, got)
     received = jnp.where(row_here == 0, jnp.zeros_like(received), received)
 
-    column_upper = jnp.concatenate([jnp.zeros((NB, NB), jnp.bfloat16), near_upper], axis=1)
-    upper = jnp.where(col_here == 0, column_upper, upper)
+    col_done = col_here * cols_dev + jnp.arange(cols_dev, dtype=jnp.int32) < NB
+    upper = jnp.where(col_done[None, :], jnp.zeros_like(upper), upper)
     return matrix - jnp.dot(received, upper, preferred_element_type=jnp.float32)
 
 

time: 28.2 us -> 26.5 us (0.940)
  the two profiles are of different devices: /device:TPU:0 before, /device:TPU:21 now
where the time goes in v15:
time: 26.5 us; the launch traced here: 26.2 us
  waiting for transfers between devices  14.6 us (55%)
  starting transfers between devices  9.91 us (37%)
  matrix products  1.04 us (4%)
  between operations  0.37 us (1%)
    ppermute x11, waiting for transfers between devices, send(): return lax.ppermute(value, ('row', 'col'), flat)  14.6 us
    ppermute x11, starting transfers between devices, send(): return lax.ppermute(value, ('row', 'col'), flat)  9.91 us
    dot_general x1, matrix products, shards(): return matrix - jnp.dot(received, upper, preferred_element_type=jnp.float32)  1.04 us
  transfers between devices with their start and end apart: 11, of which 3 were waited for; matrix products, arithmetic and copies ran while one was open for 1% of the time, Pallas kernels for 0%

profile of v15, /device:TPU:21, one launch (start us, length us, event | category | flops | bytes accessed | tf_op | source)
XLA Modules:
  0.0 26.2 jit_solution(11122671498112962358)
XLA Ops:
  0.0 0.1 conditional.2
  0.1 1.3 %collective-permute-start.7 = (bf16[256,512]{1,0:T(8,128)(2,1)S(1)}, bf16[256,512]{1,0:T(8,128)(2,1)S(1)}, u32[]{:S(2)}, u32[]{:S(2)}) collective-permute-start(bf16[256,512]{1,0:T(8,128)(2,1)S(1)} %get-tuple-element.22), channel_id=1, source_target_pairs={{1,17},{0,4},{2,6},{3,19}} | collective-permute-start | bytes 786440 | tf_op jit(solution)/shard_map/ppermute | solution.py:37
  1.4 0.7 %collective-permute-start = (f32[256,256]{1,0:T(8,128)S(1)}, f32[256,256]{1,0:T(8,128)S(1)}, u32[]{:S(2)}, u32[]{:S(2)}) collective-permute-start(f32[256,256]{1,0:T(8,128)S(1)} %get-tuple-element.19), channel_id=1, source_target_pairs={{0,20},{8,0},{12,4},{24,16}} | collective-permute-start | bytes 786440 | tf_op jit(solution)/shard_map/ppermute | solution.py:37
  2.0 0.7 %collective-permute-start.1 = (f32[256,256]{1,0:T(8,128)S(1)}, f32[256,256]{1,0:T(8,128)S(1)}, u32[]{:S(2)}, u32[]{:S(2)}) collective-permute-start(f32[256,256]{1,0:T(8,128)S(1)} %get-tuple-element.19), channel_id=1, source_target_pairs={{0,4},{28,20}} | collective-permute-start | bytes 786440 | tf_op jit(solution)/shard_map/ppermute | solution.py:37
  2.7 0.7 %collective-permute-start.2 = (f32[256,256]{1,0:T(8,128)S(1)}, f32[256,256]{1,0:T(8,128)S(1)}, u32[]{:S(2)}, u32[]{:S(2)}) collective-permute-start(f32[256,256]{1,0:T(8,128)S(1)} %get-tuple-element.19), channel_id=1, source_target_pairs={{0,16}} | collective-permute-start | bytes 786440 | tf_op jit(solution)/shard_map/ppermute | solution.py:37
  3.5 0.0 copy-start
  3.5 4.6 %collective-permute-done.7 = bf16[256,512]{1,0:T(8,128)(2,1)S(1)} collective-permute-done((bf16[256,512]{1,0:T(8,128)(2,1)S(1)}, bf16[256,512]{1,0:T(8,128)(2,1)S(1)}, u32[]{:S(2)}, u32[]{:S(2)}) %collective-permute-start.7) | collective-permute-done | bytes 262176 | tf_op jit(solution)/shard_map/ppermute | solution.py:37
  8.1 1.3 %collective-permute-start.8 = (bf16[256,512]{1,0:T(8,128)(2,1)S(1)}, bf16[256,512]{1,0:T(8,128)(2,1)S(1)}, u32[]{:S(2)}, u32[]{:S(2)}) collective-permute-start(bf16[256,512]{1,0:T(8,128)(2,1)S(1)} %broadcast_select_fusion.1), channel_id=1, source_target_pairs={{17,21},{0,16},{2,18},{4,20},{6,22},{3,11},{19,27}} | collective-permute-start | bytes 786440 | tf_op jit(solution)/shard_map/ppermute | solution.py:37
  9.4 0.0 copy-done
  9.5 0.0 collective-permute-done
  9.5 0.0 collective-permute-done.1
  9.5 0.0 collective-permute-done.2
  9.6 0.1 conditional.3
  9.7 0.7 %collective-permute-start.4 = (bf16[256,256]{1,0:T(8,128)(2,1)S(1)}, bf16[256,256]{1,0:T(8,128)(2,1)S(1)}, u32[]{:S(2)}, u32[]{:S(2)}) collective-permute-start(bf16[256,256]{1,0:T(8,128)(2,1)S(1)} %get-tuple-element.21), channel_id=1, source_target_pairs={{0,10},{4,14},{16,26},{20,30}} | collective-permute-start | bytes 393224 | tf_op jit(solution)/shard_map/ppermute | solution.py:37
  10.3 0.7 %collective-permute-start.5 = (bf16[256,256]{1,0:T(8,128)(2,1)S(1)}, bf16[256,256]{1,0:T(8,128)(2,1)S(1)}, u32[]{:S(2)}, u32[]{:S(2)}) collective-permute-start(bf16[256,256]{1,0:T(8,128)(2,1)S(1)} %get-tuple-element.21), channel_id=1, source_target_pairs={{0,8},{4,12},{16,24},{20,28}} | collective-permute-start | bytes 393224 | tf_op jit(solution)/shard_map/ppermute | solution.py:37
  11.0 0.7 %collective-permute-start.3 = (bf16[256,256]{1,0:T(8,128)(2,1)S(1)}, bf16[256,256]{1,0:T(8,128)(2,1)S(1)}, u32[]{:S(2)}, u32[]{:S(2)}) collective-permute-start(bf16[256,256]{1,0:T(8,128)(2,1)S(1)} %get-tuple-element.20), channel_id=1, source_target_pairs={{20,22},{4,6},{16,18}} | collective-permute-start | bytes 393224 | tf_op jit(solution)/shard_map/ppermute | solution.py:37
  11.7 1.0 %collective-permute-done.8 = bf16[256,512]{1,0:T(8,128)(2,1)S(1)} collective-permute-done((bf16[256,512]{1,0:T(8,128)(2,1)S(1)}, bf16[256,512]{1,0:T(8,128)(2,1)S(1)}, u32[]{:S(2)}, u32[]{:S(2)}) %collective-permute-start.8) | collective-permute-done | bytes 262176 | tf_op jit(solution)/shard_map/ppermute | solution.py:37
  12.7 1.3 %collective-permute-start.10 = (bf16[256,512]{1,0:T(8,128)(2,1)S(1)}, bf16[256,512]{1,0:T(8,128)(2,1)S(1)}, u32[]{:S(2)}, u32[]{:S(2)}) collective-permute-start(bf16[256,512]{1,0:T(8,128)(2,1)S(1)} %broadcast_select_fusion.2), channel_id=1, source_target_pairs={{17,25},{21,29},{1,5},{0,8},{2,10},{4,12},{6,14},{16,24},{18,26},{... | collective-permute-start | bytes 786440 | tf_op jit(solution)/shard_map/ppermute | solution.py:37
  14.1 0.7 %collective-permute-start.9 = (bf16[256,512]{1,0:T(8,128)(2,1)S(1)}, bf16[256,512]{1,0:T(8,128)(2,1)S(1)}, u32[]{:S(2)}, u32[]{:S(2)}) collective-permute-start(bf16[256,512]{1,0:T(8,128)(2,1)S(1)} %broadcast_select_fusion.2), channel_id=1, source_target_pairs={{17,9},{21,13}} | collective-permute-start | bytes 786440 | tf_op jit(solution)/shard_map/ppermute | solution.py:37
  14.7 0.0 collective-permute-done.3
  14.7 0.0 collective-permute-done.4
  14.8 0.0 collective-permute-done.5
  14.8 1.3 %collective-permute-start.6 = (bf16[256,256]{1,0:T(8,128)(2,1)S(1)}, bf16[256,256]{1,0:T(8,128)(2,1)S(1)}, u32[]{:S(2)}, u32[]{:S(2)}) collective-permute-start(bf16[256,256]{1,0:T(8,128)(2,1)S(1)} %select_select_fusion.2), channel_id=1, source_target_pairs={{4,5},{6,7},{8,9},{10,11},{12,13},{14,15},{16,17},{18,19},{20,21},... | collective-permute-start | bytes 393224 | tf_op jit(solution)/shard_map/ppermute | solution.py:37
  16.2 9.0 %collective-permute-done.6 = bf16[256,256]{1,0:T(8,128)(2,1)S(1)} collective-permute-done((bf16[256,256]{1,0:T(8,128)(2,1)S(1)}, bf16[256,256]{1,0:T(8,128)(2,1)S(1)}, u32[]{:S(2)}, u32[]{:S(2)}) %collective-permute-start.6) | collective-permute-done | bytes 131104 | tf_op jit(solution)/shard_map/ppermute | solution.py:37
  25.2 0.0 collective-permute-done.10
  25.2 0.0 collective-permute-done.9
  25.2 1.0 %convolution_subtract_fusion = f32[256,512]{1,0:T(8,128)} fusion(f32[256,512]{1,0:T(8,128)S(1)} %copy-done, bf16[256,512]{1,0:T(8,128)(2,1)S(1)} %collective-permute-done.9, bf16[256,512]{1,0:T(8,128)(2,1)S(1)} %collective-permute-done.10, bf16[256,512]{1,0:T(8,128)(2,1)S(1)} %broadcast_select_fusion.2, pred[]{:T(512)S(6)} %or.35, pred[]{:T(512)S(6)} %and.97, ...), kind=kOutput, calls=%fused_computation.34 | convolution fusion | flops 67764224 | bytes 2097668 | tf_op jit(solution)/shard_map/dot_general | solution.py:135
  (12 shorter events, 0.2 us)
Async XLA Ops:
  0.1 8.0 %collective-permute-start.7 = (bf16[256,512]{1,0:T(8,128)(2,1)S(1)}, bf16[256,512]{1,0:T(8,128)(2,1)S(1)}, u32[]{:S(2)}, u32[]{:S(2)}) collective-permute-start(bf16[256,512]{1,0:T(8,128)(2,1)S(1)} %get-tuple-element.22), channel_id=1, source_target_pairs={{1,17},{0,4},{2,6},{3,19}} | collective-permute-start | bytes 786440 | tf_op jit(solution)/shard_map/ppermute | solution.py:37
  1.4 8.2 %collective-permute-start = (f32[256,256]{1,0:T(8,128)S(1)}, f32[256,256]{1,0:T(8,128)S(1)}, u32[]{:S(2)}, u32[]{:S(2)}) collective-permute-start(f32[256,256]{1,0:T(8,128)S(1)} %get-tuple-element.19), channel_id=1, source_target_pairs={{0,20},{8,0},{12,4},{24,16}} | collective-permute-start | bytes 786440 | tf_op jit(solution)/shard_map/ppermute | solution.py:37
  2.0 7.5 %collective-permute-start.1 = (f32[256,256]{1,0:T(8,128)S(1)}, f32[256,256]{1,0:T(8,128)S(1)}, u32[]{:S(2)}, u32[]{:S(2)}) collective-permute-start(f32[256,256]{1,0:T(8,128)S(1)} %get-tuple-element.19), channel_id=1, source_target_pairs={{0,4},{28,20}} | collective-permute-start | bytes 786440 | tf_op jit(solution)/shard_map/ppermute | solution.py:37
  2.7 6.8 %collective-permute-start.2 = (f32[256,256]{1,0:T(8,128)S(1)}, f32[256,256]{1,0:T(8,128)S(1)}, u32[]{:S(2)}, u32[]{:S(2)}) collective-permute-start(f32[256,256]{1,0:T(8,128)S(1)} %get-tuple-element.19), channel_id=1, source_target_pairs={{0,16}} | collective-permute-start | bytes 786440 | tf_op jit(solution)/shard_map/ppermute | solution.py:37
  3.5 6.0 %copy-start = (f32[256,512]{1,0:T(8,128)S(1)}, f32[256,512]{1,0:T(8,128)}, u32[]{:S(2)}) copy-start(f32[256,512]{1,0:T(8,128)} %param.5) | copy-start | bytes 1572868
  8.1 4.6 %collective-permute-start.8 = (bf16[256,512]{1,0:T(8,128)(2,1)S(1)}, bf16[256,512]{1,0:T(8,128)(2,1)S(1)}, u32[]{:S(2)}, u32[]{:S(2)}) collective-permute-start(bf16[256,512]{1,0:T(8,128)(2,1)S(1)} %broadcast_select_fusion.1), channel_id=1, source_target_pairs={{17,21},{0,16},{2,18},{4,20},{6,22},{3,11},{19,27}} | collective-permute-start | bytes 786440 | tf_op jit(solution)/shard_map/ppermute | solution.py:37
  9.7 5.1 %collective-permute-start.4 = (bf16[256,256]{1,0:T(8,128)(2,1)S(1)}, bf16[256,256]{1,0:T(8,128)(2,1)S(1)}, u32[]{:S(2)}, u32[]{:S(2)}) collective-permute-start(bf16[256,256]{1,0:T(8,128)(2,1)S(1)} %get-tuple-element.21), channel_id=1, source_target_pairs={{0,10},{4,14},{16,26},{20,30}} | collective-permute-start | bytes 393224 | tf_op jit(solution)/shard_map/ppermute | solution.py:37
  10.3 4.4 %collective-permute-start.5 = (bf16[256,256]{1,0:T(8,128)(2,1)S(1)}, bf16[256,256]{1,0:T(8,128)(2,1)S(1)}, u32[]{:S(2)}, u32[]{:S(2)}) collective-permute-start(bf16[256,256]{1,0:T(8,128)(2,1)S(1)} %get-tuple-element.21), channel_id=1, source_target_pairs={{0,8},{4,12},{16,24},{20,28}} | collective-permute-start | bytes 393224 | tf_op jit(solution)/shard_map/ppermute | solution.py:37
  11.0 3.7 %collective-permute-start.3 = (bf16[256,256]{1,0:T(8,128)(2,1)S(1)}, bf16[256,256]{1,0:T(8,128)(2,1)S(1)}, u32[]{:S(2)}, u32[]{:S(2)}) collective-permute-start(bf16[256,256]{1,0:T(8,128)(2,1)S(1)} %get-tuple-element.20), channel_id=1, source_target_pairs={{20,22},{4,6},{16,18}} | collective-permute-start | bytes 393224 | tf_op jit(solution)/shard_map/ppermute | solution.py:37
  12.7 12.4 %collective-permute-start.10 = (bf16[256,512]{1,0:T(8,128)(2,1)S(1)}, bf16[256,512]{1,0:T(8,128)(2,1)S(1)}, u32[]{:S(2)}, u32[]{:S(2)}) collective-permute-start(bf16[256,512]{1,0:T(8,128)(2,1)S(1)} %broadcast_select_fusion.2), channel_id=1, source_target_pairs={{17,25},{21,29},{1,5},{0,8},{2,10},{4,12},{6,14},{16,24},{18,26},{... | collective-permute-start | bytes 786440 | tf_op jit(solution)/shard_map/ppermute | solution.py:37
  14.1 11.1 %collective-permute-start.9 = (bf16[256,512]{1,0:T(8,128)(2,1)S(1)}, bf16[256,512]{1,0:T(8,128)(2,1)S(1)}, u32[]{:S(2)}, u32[]{:S(2)}) collective-permute-start(bf16[256,512]{1,0:T(8,128)(2,1)S(1)} %broadcast_select_fusion.2), channel_id=1, source_target_pairs={{17,9},{21,13}} | collective-permute-start | bytes 786440 | tf_op jit(solution)/shard_map/ppermute | solution.py:37
  14.8 10.4 %collective-permute-start.6 = (bf16[256,256]{1,0:T(8,128)(2,1)S(1)}, bf16[256,256]{1,0:T(8,128)(2,1)S(1)}, u32[]{:S(2)}, u32[]{:S(2)}) collective-permute-start(bf16[256,256]{1,0:T(8,128)(2,1)S(1)} %select_select_fusion.2), channel_id=1, source_target_pairs={{4,5},{6,7},{8,9},{10,11},{12,13},{14,15},{16,17},{18,19},{20,21},... | collective-permute-start | bytes 393224 | tf_op jit(solution)/shard_map/ppermute | solution.py:37

commit v16 on v15

--- a/solution.py
+++ b/solution.py
@@ -58,6 +58,7 @@
         beside_steps.append([(h, h + stride) for h in far])
     beside_steps[-1].append((0, 1))
     beside_back = [(middle + r - 2, r) for r in range(2, middle)]
+    relieved = middle + APART
 
     def among(rows):
         found = jnp.bool_(False)
@@ -80,6 +81,7 @@
                 ((h, c), (h + stride, c))
                 for h in held[kind]
                 for c in range(3 * kind, n_col, 2)
+                if c or h + stride != relieved
             ]
             held[kind] = held[kind] + [h + stride for h in held[kind]]
         got = send(sent, pairs)
@@ -117,17 +119,29 @@
     for c in range(2, n_col, 2):
         got = send(lower, [((r, 0), (r, c)) for r in targets])
         received = jnp.where((row_here & APART == 0) & (col_here == c), got, received)
+    got = send(lower, [((middle, 0), (middle, 3))])
+    direct = (row_here == middle) & (col_here == 3)
+    received = jnp.where(direct, got, received)
     sent = upper
     for step in range(2, len(down)):
         upper = upper_step(upper, step, upper)
     if len(beside_back) > 2:
         sent = upper
-    got = send(sent, [((a, 1), (b, 1)) for a, b in beside_back])
-    upper = jnp.where((col_here == 1) & (row_here > 1) & (row_here < middle), got, upper)
+    pairs = [((a, 1), (b, 1)) for a, b in beside_back] + [((middle + 1, 0), (relieved, 0))]
+    got = send(sent, pairs)
+    takes = (col_here == 1) & (row_here > 1) & (row_here < middle)
+    takes = takes | ((col_here == 0) & (row_here == relieved))
+    upper = jnp.where(takes, got, upper)
     got = send(
-        received, [((r, c), (r, c + 1)) for r in range(1, n_row) for c in range(0, n_col, 2)]
+        received,
+        [
+            ((r, c), (r, c + 1))
+            for r in range(1, n_row)
+            for c in range(0, n_col, 2)
+            if (r, c) != (middle, 2)
+        ],
     )
-    received = jnp.where(col_here % 2 == 0, received, got)
+    received = jnp.where((col_here % 2 == 0) | direct, received, got)
     received = jnp.where(row_here == 0, jnp.zeros_like(received), received)
 
     col_done = col_here * cols_dev + jnp.arange(cols_dev, dtype=jnp.int32) < NB

time: 26.5 us -> 30 us (1.13)
  the two profiles are of different devices: /device:TPU:21 before, /device:TPU:26 now
where the time goes in v16:
time: 30 us; the launch traced here: 29.7 us
  waiting for transfers between devices  15.5 us (52%)
  starting transfers between devices  11.2 us (37%)
  other arithmetic  1.27 us (4%)
  matrix products  1.03 us (3%)
  between operations  0.38 us (1%)
  local copies, waits for them, and re-layouts  0.3 us (1%)
    ppermute x12, waiting for transfers between devices, send(): return lax.ppermute(value, ('row', 'col'), flat)  15.5 us
    ppermute x12, starting transfers between devices, send(): return lax.ppermute(value, ('row', 'col'), flat)  11.2 us
    convert_element_type x1, other arithmetic, blocks(): return (matrix[:, :NB], matrix.astype(jnp.bfloat16))  1.15 us
    dot_general x1, matrix products, shards(): return matrix - jnp.dot(received, upper, preferred_element_type=jnp.float32)  1.03 us
  transfers between devices with their start and end apart: 12, of which 4 were waited for; matrix products, arithmetic and copies ran while one was open for 1% of the time, Pallas kernels for 0%

profile of v16, /device:TPU:26, one launch (start us, length us, event | category | flops | bytes accessed | tf_op | source)
XLA Modules:
  0.0 29.7 jit_solution(6636317697984329626)
XLA Ops:
  0.0 1.2 %conditional.2 = (f32[256,256]{1,0:T(8,128)S(1)}, bf16[256,512]{1,0:T(8,128)(2,1)S(1)}) conditional(s32[]{:T(128)} %convert_element_type.16, () %tuple.22, f32[256,512]{1,0:T(8,128)} %param.5), branch_computations={%region_0.0_spmd, %region_1.0_spmd} | conditional | flops 131072 | bytes 3407916 | solution.py:46
  0.0 0.0 copy-start.1
  0.0 1.1 %convert_element_type.1 = bf16[256,512]{1,0:T(8,128)(2,1)S(1)} convert(f32[256,512]{1,0:T(8,128)} %param.1) | non-fusion elementwise | flops 131072 | bytes 786432 | tf_op jit(solution)/shard_map/cond/branch_1_fun/convert_element_type | solution.py:40
  1.2 0.0 copy-done.1
  1.2 0.7 %collective-permute-start.8 = (bf16[256,512]{1,0:T(8,128)(2,1)S(1)}, bf16[256,512]{1,0:T(8,128)(2,1)S(1)}, u32[]{:S(2)}, u32[]{:S(2)}) collective-permute-start(bf16[256,512]{1,0:T(8,128)(2,1)S(1)} %get-tuple-element.22), channel_id=1, source_target_pairs={{1,17},{0,4},{2,6},{3,19}} | collective-permute-start | bytes 786440 | tf_op jit(solution)/shard_map/ppermute | solution.py:37
  1.9 0.7 %collective-permute-start = (f32[256,256]{1,0:T(8,128)S(1)}, f32[256,256]{1,0:T(8,128)S(1)}, u32[]{:S(2)}, u32[]{:S(2)}) collective-permute-start(f32[256,256]{1,0:T(8,128)S(1)} %get-tuple-element.19), channel_id=1, source_target_pairs={{0,20},{8,0},{12,4},{24,16}} | collective-permute-start | bytes 786440 | tf_op jit(solution)/shard_map/ppermute | solution.py:37
  2.6 1.8 %collective-permute-start.1 = (f32[256,256]{1,0:T(8,128)S(1)}, f32[256,256]{1,0:T(8,128)S(1)}, u32[]{:S(2)}, u32[]{:S(2)}) collective-permute-start(f32[256,256]{1,0:T(8,128)S(1)} %get-tuple-element.19), channel_id=1, source_target_pairs={{0,4},{28,20}} | collective-permute-start | bytes 786440 | tf_op jit(solution)/shard_map/ppermute | solution.py:37
  4.4 0.7 %collective-permute-start.2 = (f32[256,256]{1,0:T(8,128)S(1)}, f32[256,256]{1,0:T(8,128)S(1)}, u32[]{:S(2)}, u32[]{:S(2)}) collective-permute-start(f32[256,256]{1,0:T(8,128)S(1)} %get-tuple-element.19), channel_id=1, source_target_pairs={{0,16}} | collective-permute-start | bytes 786440 | tf_op jit(solution)/shard_map/ppermute | solution.py:37
  5.2 0.0 copy-start
  5.2 0.0 collective-permute-done.8
  5.2 0.8 %collective-permute-start.9 = (bf16[256,512]{1,0:T(8,128)(2,1)S(1)}, bf16[256,512]{1,0:T(8,128)(2,1)S(1)}, u32[]{:S(2)}, u32[]{:S(2)}) collective-permute-start(bf16[256,512]{1,0:T(8,128)(2,1)S(1)} %broadcast_select_fusion.1), channel_id=1, source_target_pairs={{17,21},{0,16},{2,18},{4,20},{6,22},{3,11},{19,27}} | collective-permute-start | bytes 786440 | tf_op jit(solution)/shard_map/ppermute | solution.py:37
  6.1 0.1 copy-done
  6.3 0.0 collective-permute-done
  6.3 2.0 %collective-permute-done.1 = f32[256,256]{1,0:T(8,128)S(1)} collective-permute-done((f32[256,256]{1,0:T(8,128)S(1)}, f32[256,256]{1,0:T(8,128)S(1)}, u32[]{:S(2)}, u32[]{:S(2)}) %collective-permute-start.1) | collective-permute-done | bytes 262176 | tf_op jit(solution)/shard_map/ppermute | solution.py:37
  8.3 0.0 collective-permute-done.2
  8.3 0.1 conditional.3
  8.4 0.7 %collective-permute-start.3 = (bf16[256,256]{1,0:T(8,128)(2,1)S(1)}, bf16[256,256]{1,0:T(8,128)(2,1)S(1)}, u32[]{:S(2)}, u32[]{:S(2)}) collective-permute-start(bf16[256,256]{1,0:T(8,128)(2,1)S(1)} %get-tuple-element.20), channel_id=1, source_target_pairs={{16,19}} | collective-permute-start | bytes 393224 | tf_op jit(solution)/shard_map/ppermute | solution.py:37
  9.1 0.7 %collective-permute-start.4 = (bf16[256,256]{1,0:T(8,128)(2,1)S(1)}, bf16[256,256]{1,0:T(8,128)(2,1)S(1)}, u32[]{:S(2)}, u32[]{:S(2)}) collective-permute-start(bf16[256,256]{1,0:T(8,128)(2,1)S(1)} %get-tuple-element.20), channel_id=1, source_target_pairs={{20,22},{4,6},{16,18}} | collective-permute-start | bytes 393224 | tf_op jit(solution)/shard_map/ppermute | solution.py:37
  9.8 0.7 %collective-permute-start.5 = (bf16[256,256]{1,0:T(8,128)(2,1)S(1)}, bf16[256,256]{1,0:T(8,128)(2,1)S(1)}, u32[]{:S(2)}, u32[]{:S(2)}) collective-permute-start(bf16[256,256]{1,0:T(8,128)(2,1)S(1)} %get-tuple-element.21), channel_id=1, source_target_pairs={{0,10},{4,14},{16,26},{20,30}} | collective-permute-start | bytes 393224 | tf_op jit(solution)/shard_map/ppermute | solution.py:37
  10.4 1.3 %collective-permute-start.6 = (bf16[256,256]{1,0:T(8,128)(2,1)S(1)}, bf16[256,256]{1,0:T(8,128)(2,1)S(1)}, u32[]{:S(2)}, u32[]{:S(2)}) collective-permute-start(bf16[256,256]{1,0:T(8,128)(2,1)S(1)} %get-tuple-element.21), channel_id=1, source_target_pairs={{0,8},{4,12},{16,24},{20,28}} | collective-permute-start | bytes 393224 | tf_op jit(solution)/shard_map/ppermute | solution.py:37
  11.7 0.0 collective-permute-done.9
  11.8 0.7 %collective-permute-start.10 = (bf16[256,512]{1,0:T(8,128)(2,1)S(1)}, bf16[256,512]{1,0:T(8,128)(2,1)S(1)}, u32[]{:S(2)}, u32[]{:S(2)}) collective-permute-start(bf16[256,512]{1,0:T(8,128)(2,1)S(1)} %broadcast_select_fusion.2), channel_id=1, source_target_pairs={{17,9},{21,13},{20,24}} | collective-permute-start | bytes 786440 | tf_op jit(solution)/shard_map/ppermute | solution.py:37
  12.5 0.0 collective-permute-done.3
  12.5 1.3 %collective-permute-start.11 = (bf16[256,512]{1,0:T(8,128)(2,1)S(1)}, bf16[256,512]{1,0:T(8,128)(2,1)S(1)}, u32[]{:S(2)}, u32[]{:S(2)}) collective-permute-start(bf16[256,512]{1,0:T(8,128)(2,1)S(1)} %broadcast_select_fusion.2), channel_id=1, source_target_pairs={{17,25},{21,29},{1,5},{0,8},{2,10},{4,12},{6,14},{18,26},{20,28},{... | collective-permute-start | bytes 786440 | tf_op jit(solution)/shard_map/ppermute | solution.py:37
  13.8 0.0 collective-permute-done.4
  13.8 0.0 collective-permute-done.5
  13.8 9.0 %collective-permute-done.6 = bf16[256,256]{1,0:T(8,128)(2,1)S(1)} collective-permute-done((bf16[256,256]{1,0:T(8,128)(2,1)S(1)}, bf16[256,256]{1,0:T(8,128)(2,1)S(1)}, u32[]{:S(2)}, u32[]{:S(2)}) %collective-permute-start.6) | collective-permute-done | bytes 131104 | tf_op jit(solution)/shard_map/ppermute | solution.py:37
  22.8 1.3 %collective-permute-start.7 = (bf16[256,256]{1,0:T(8,128)(2,1)S(1)}, bf16[256,256]{1,0:T(8,128)(2,1)S(1)}, u32[]{:S(2)}, u32[]{:S(2)}) collective-permute-start(bf16[256,256]{1,0:T(8,128)(2,1)S(1)} %select_select_fusion.2), channel_id=1, source_target_pairs={{4,5},{6,7},{8,9},{10,11},{12,13},{14,15},{16,17},{20,21},{22,23},... | collective-permute-start | bytes 393224 | tf_op jit(solution)/shard_map/ppermute | solution.py:37
  24.2 0.9 %collective-permute-done.7 = bf16[256,256]{1,0:T(8,128)(2,1)S(1)} collective-permute-done((bf16[256,256]{1,0:T(8,128)(2,1)S(1)}, bf16[256,256]{1,0:T(8,128)(2,1)S(1)}, u32[]{:S(2)}, u32[]{:S(2)}) %collective-permute-start.7) | collective-permute-done | bytes 131104 | tf_op jit(solution)/shard_map/ppermute | solution.py:37
  25.1 0.0 collective-permute-done.10
  25.1 3.6 %collective-permute-done.11 = bf16[256,512]{1,0:T(8,128)(2,1)S(1)} collective-permute-done((bf16[256,512]{1,0:T(8,128)(2,1)S(1)}, bf16[256,512]{1,0:T(8,128)(2,1)S(1)}, u32[]{:S(2)}, u32[]{:S(2)}) %collective-permute-start.11) | collective-permute-done | bytes 262176 | tf_op jit(solution)/shard_map/ppermute | solution.py:37
  28.7 1.0 %convolution_subtract_fusion = f32[256,512]{1,0:T(8,128)} fusion(f32[256,512]{1,0:T(8,128)S(1)} %copy-done, bf16[256,512]{1,0:T(8,128)(2,1)S(1)} %collective-permute-done.10, bf16[256,512]{1,0:T(8,128)(2,1)S(1)} %collective-permute-done.11, bf16[256,512]{1,0:T(8,128)(2,1)S(1)} %broadcast_select_fusion.2, pred[]{:T(512)S(6)} %or.43, pred[]{:T(512)S(6)} %or.35, ...), kind=kOutput, calls=%fused_computation.34 | convolution fusion | flops 67764224 | bytes 2097668 | tf_op jit(solution)/shard_map/dot_general | solution.py:149
  (11 shorter events, 0.2 us)
Async XLA Ops:
  0.0 1.2 %copy-start.1 = (f32[256,512]{1,0:T(8,128)S(1)}, f32[256,512]{1,0:T(8,128)}, u32[]{:S(2)}) copy-start(f32[256,512]{1,0:T(8,128)} %param.1) | copy-start | bytes 1572868 | tf_op jit(solution)/shard_map/cond
  1.2 4.0 %collective-permute-start.8 = (bf16[256,512]{1,0:T(8,128)(2,1)S(1)}, bf16[256,512]{1,0:T(8,128)(2,1)S(1)}, u32[]{:S(2)}, u32[]{:S(2)}) collective-permute-start(bf16[256,512]{1,0:T(8,128)(2,1)S(1)} %get-tuple-element.22), channel_id=1, source_target_pairs={{1,17},{0,4},{2,6},{3,19}} | collective-permute-start | bytes 786440 | tf_op jit(solution)/shard_map/ppermute | solution.py:37
  1.9 4.4 %collective-permute-start = (f32[256,256]{1,0:T(8,128)S(1)}, f32[256,256]{1,0:T(8,128)S(1)}, u32[]{:S(2)}, u32[]{:S(2)}) collective-permute-start(f32[256,256]{1,0:T(8,128)S(1)} %get-tuple-element.19), channel_id=1, source_target_pairs={{0,20},{8,0},{12,4},{24,16}} | collective-permute-start | bytes 786440 | tf_op jit(solution)/shard_map/ppermute | solution.py:37
  2.6 5.7 %collective-permute-start.1 = (f32[256,256]{1,0:T(8,128)S(1)}, f32[256,256]{1,0:T(8,128)S(1)}, u32[]{:S(2)}, u32[]{:S(2)}) collective-permute-start(f32[256,256]{1,0:T(8,128)S(1)} %get-tuple-element.19), channel_id=1, source_target_pairs={{0,4},{28,20}} | collective-permute-start | bytes 786440 | tf_op jit(solution)/shard_map/ppermute | solution.py:37
  4.4 3.9 %collective-permute-start.2 = (f32[256,256]{1,0:T(8,128)S(1)}, f32[256,256]{1,0:T(8,128)S(1)}, u32[]{:S(2)}, u32[]{:S(2)}) collective-permute-start(f32[256,256]{1,0:T(8,128)S(1)} %get-tuple-element.19), channel_id=1, source_target_pairs={{0,16}} | collective-permute-start | bytes 786440 | tf_op jit(solution)/shard_map/ppermute | solution.py:37
  5.2 1.0 %copy-start = (f32[256,512]{1,0:T(8,128)S(1)}, f32[256,512]{1,0:T(8,128)}, u32[]{:S(2)}) copy-start(f32[256,512]{1,0:T(8,128)} %param.5) | copy-start | bytes 1572868
  5.2 6.5 %collective-permute-start.9 = (bf16[256,512]{1,0:T(8,128)(2,1)S(1)}, bf16[256,512]{1,0:T(8,128)(2,1)S(1)}, u32[]{:S(2)}, u32[]{:S(2)}) collective-permute-start(bf16[256,512]{1,0:T(8,128)(2,1)S(1)} %broadcast_select_fusion.1), channel_id=1, source_target_pairs={{17,21},{0,16},{2,18},{4,20},{6,22},{3,11},{19,27}} | collective-permute-start | bytes 786440 | tf_op jit(solution)/shard_map/ppermute | solution.py:37
  8.4 4.1 %collective-permute-start.3 = (bf16[256,256]{1,0:T(8,128)(2,1)S(1)}, bf16[256,256]{1,0:T(8,128)(2,1)S(1)}, u32[]{:S(2)}, u32[]{:S(2)}) collective-permute-start(bf16[256,256]{1,0:T(8,128)(2,1)S(1)} %get-tuple-element.20), channel_id=1, source_target_pairs={{16,19}} | collective-permute-start | bytes 393224 | tf_op jit(solution)/shard_map/ppermute | solution.py:37
  9.1 4.7 %collective-permute-start.4 = (bf16[256,256]{1,0:T(8,128)(2,1)S(1)}, bf16[256,256]{1,0:T(8,128)(2,1)S(1)}, u32[]{:S(2)}, u32[]{:S(2)}) collective-permute-start(bf16[256,256]{1,0:T(8,128)(2,1)S(1)} %get-tuple-element.20), channel_id=1, source_target_pairs={{20,22},{4,6},{16,18}} | collective-permute-start | bytes 393224 | tf_op jit(solution)/shard_map/ppermute | solution.py:37
  9.8 4.0 %collective-permute-start.5 = (bf16[256,256]{1,0:T(8,128)(2,1)S(1)}, bf16[256,256]{1,0:T(8,128)(2,1)S(1)}, u32[]{:S(2)}, u32[]{:S(2)}) collective-permute-start(bf16[256,256]{1,0:T(8,128)(2,1)S(1)} %get-tuple-element.21), channel_id=1, source_target_pairs={{0,10},{4,14},{16,26},{20,30}} | collective-permute-start | bytes 393224 | tf_op jit(solution)/shard_map/ppermute | solution.py:37
  10.4 12.3 %collective-permute-start.6 = (bf16[256,256]{1,0:T(8,128)(2,1)S(1)}, bf16[256,256]{1,0:T(8,128)(2,1)S(1)}, u32[]{:S(2)}, u32[]{:S(2)}) collective-permute-start(bf16[256,256]{1,0:T(8,128)(2,1)S(1)} %get-tuple-element.21), channel_id=1, source_target_pairs={{0,8},{4,12},{16,24},{20,28}} | collective-permute-start | bytes 393224 | tf_op jit(solution)/shard_map/ppermute | solution.py:37
  11.8 13.3 %collective-permute-start.10 = (bf16[256,512]{1,0:T(8,128)(2,1)S(1)}, bf16[256,512]{1,0:T(8,128)(2,1)S(1)}, u32[]{:S(2)}, u32[]{:S(2)}) collective-permute-start(bf16[256,512]{1,0:T(8,128)(2,1)S(1)} %broadcast_select_fusion.2), channel_id=1, source_target_pairs={{17,9},{21,13},{20,24}} | collective-permute-start | bytes 786440 | tf_op jit(solution)/shard_map/ppermute | solution.py:37
  12.5 16.2 %collective-permute-start.11 = (bf16[256,512]{1,0:T(8,128)(2,1)S(1)}, bf16[256,512]{1,0:T(8,128)(2,1)S(1)}, u32[]{:S(2)}, u32[]{:S(2)}) collective-permute-start(bf16[256,512]{1,0:T(8,128)(2,1)S(1)} %broadcast_select_fusion.2), channel_id=1, source_target_pairs={{17,25},{21,29},{1,5},{0,8},{2,10},{4,12},{6,14},{18,26},{20,28},{... | collective-permute-start | bytes 786440 | tf_op jit(solution)/shard_map/ppermute | solution.py:37
  22.8 2.3 %collective-permute-start.7 = (bf16[256,256]{1,0:T(8,128)(2,1)S(1)}, bf16[256,256]{1,0:T(8,128)(2,1)S(1)}, u32[]{:S(2)}, u32[]{:S(2)}) collective-permute-start(bf16[256,256]{1,0:T(8,128)(2,1)S(1)} %select_select_fusion.2), channel_id=1, source_target_pairs={{4,5},{6,7},{8,9},{10,11},{12,13},{14,15},{16,17},{20,21},{22,23},... | collective-permute-start | bytes 393224 | tf_op jit(solution)/shard_map/ppermute | solution.py:37

commit v17 on v15

--- a/solution.py
+++ b/solution.py
@@ -14,6 +14,17 @@
         out.append(stride)
         stride //= 2
     return out
+
+
+def two_terms(values, width):
+    high = lax.reduce_precision(values, exponent_bits=8, mantissa_bits=7)
+    terms = [high.astype(jnp.bfloat16), (values - high).astype(jnp.bfloat16)]
+    both = jnp.concatenate(terms, axis=1)
+    return jnp.pad(both, ((0, 0), (0, width - both.shape[1])))
+
+
+def summed(terms):
+    return terms[:, :NB].astype(jnp.float32) + terms[:, NB : 2 * NB].astype(jnp.float32)
 
 
 def multipliers(square, columns):
@@ -36,8 +47,12 @@
         flat = [(r0 * n_col + c0, r1 * n_col + c1) for (r0, c0), (r1, c1) in pairs]
         return lax.ppermute(value, ("row", "col"), flat)
 
+    middle = n_row // 2
+    shared = middle + APART
+
     def blocks(matrix):
-        return matrix[:, :NB], matrix.astype(jnp.bfloat16)
+        columns, rows = matrix[:, :NB], matrix.astype(jnp.bfloat16)
+        return columns, jnp.where(row_here == shared, two_terms(columns, cols_dev), rows)
 
     def no_blocks(matrix):
         return jnp.zeros((NB, NB), matrix.dtype), jnp.zeros(matrix.shape, jnp.bfloat16)
@@ -49,7 +64,6 @@
     upper = lax.optimization_barrier(jnp.where(row_here == 0, first_upper, 0))
 
     down = strides(n_row)
-    middle = n_row // 2
     orders = [[down[-1]] + down[:-1], down]
     held = [[0], [0]]
     beside_steps = [[(0, middle)], [(middle, middle + 1)]]
@@ -65,8 +79,8 @@
             found = found | (row_here == row)
         return found
 
-    def upper_step(value, step, sent):
-        pairs = [((a, 1), (b, 1)) for a, b in beside_steps[step]]
+    def upper_step(value, step, sent, pairs=()):
+        pairs = list(pairs) + [((a, 1), (b, 1)) for a, b in beside_steps[step]]
         takes = (col_here == 1) & among([b for _, b in beside_steps[step]])
         for kind in range(2):
             stride = orders[kind][step]
@@ -83,43 +97,63 @@
             ]
             held[kind] = held[kind] + [h + stride for h in held[kind]]
         got = send(sent, pairs)
-        return jnp.where(takes, got, value)
+        return jnp.where(takes, got, value), got
 
     workers = [r for r in range(n_row) if r & APART == 0]
     targets = workers[:1:-1]
     targets.insert(1, 1)
     square, partner = matrix[:, :NB], matrix[:, :NB]
-    upper = upper_step(upper, 0, first_upper)
-    for index, target in reversed(list(enumerate(targets))):
+    upper, got = upper_step(upper, 0, first_upper, [((shared, 0), (0, 0))])
+    own = jnp.where(row_here == 0, summed(got), matrix[:, :NB])
+    for index, target in enumerate(targets):
         served = [] if index > 1 else targets[:1] if index else [0] + targets[1:]
         pairs = [((0, 0), (target, 0))] + [((r + APART, 0), (r, 0)) for r in served]
         got = send(pivot_columns, pairs)
         square = jnp.where(row_here == target, got, square)
         for r in served:
             partner = jnp.where(row_here == r, got, partner)
-    upper = upper_step(upper, 1, upper)
+    upper, _ = upper_step(upper, 1, upper)
 
-    def compute(square, partner):
-        both = multipliers(square, jnp.concatenate([matrix[:, :NB], partner], axis=0))
+    def compute(square, own, partner):
+        both = multipliers(square, jnp.concatenate([own, partner], axis=0))
         both = both.astype(jnp.bfloat16)
         return both[:NB], both[NB:]
 
-    def none(square, partner):
+    def none(square, own, partner):
         zero = jnp.zeros((NB, NB), jnp.bfloat16)
         return zero, zero
 
     working = (row_here & APART == 0) & (col_here == 0)
-    lower, lower_far = lax.cond(working, compute, none, square, partner)
+    lower, lower_far = lax.cond(working, compute, none, square, own, partner)
+    others = [r for r in workers if r not in (0, middle)]
+    far = row_here & APART != 0
     received = lower
-    for c in range(0, n_col, 2):
-        got = send(lower_far, [((r, 0), (r + APART, c)) for r in workers])
-        received = jnp.where((row_here & APART != 0) & (col_here == c), got, received)
-    for c in range(2, n_col, 2):
-        got = send(lower, [((r, 0), (r, c)) for r in targets])
-        received = jnp.where((row_here & APART == 0) & (col_here == c), got, received)
+
+    def send_near(c):
+        pairs = [((r, 0), (r + APART, 0)) for r in workers]
+        return send(lower_far, pairs), far & (col_here == 0)
+
+    def send_cross(c):
+        sent = jnp.where((row_here == 0) | (row_here == middle), lower, lower_far)
+        pairs = [((0, 0), (shared, c)), ((middle, 0), (middle, c))]
+        pairs += [((r, 0), (r + APART, c)) for r in others]
+        takes = (far & (row_here != APART)) | (row_here == middle)
+        return send(sent, pairs), takes & (col_here == c)
+
+    def send_own(c):
+        pairs = [((0, 0), (APART, c))] + [((r, 0), (r, c)) for r in others]
+        takes = (~far & (row_here != middle)) | (row_here == APART)
+        sent = jnp.where(row_here == 0, lower_far, lower)
+        return send(sent, pairs), takes & (col_here == c)
+
+    even = range(2, n_col, 2)
+    for step, columns in ((send_near, [0]), (send_own, even), (send_cross, even)):
+        for c in columns:
+            got, takes = step(c)
+            received = jnp.where(takes, got, received)
     sent = upper
     for step in range(2, len(down)):
-        upper = upper_step(upper, step, upper)
+        upper, _ = upper_step(upper, step, upper)
     if len(beside_back) > 2:
         sent = upper
     got = send(sent, [((a, 1), (b, 1)) for a, b in beside_back])

time: 26.5 us -> 28.3 us (1.068)
  the two profiles are of different devices: /device:TPU:21 before, /device:TPU:0 now
where the time goes in v17:
time: 28.3 us; the launch traced here: 28 us
  starting transfers between devices  16.1 us (57%)
  waiting for transfers between devices  6.28 us (22%)
  other arithmetic  3.15 us (11%)
  matrix products  1.99 us (7%)
  between operations  0.36 us (1%)
    ppermute x11, starting transfers between devices, send(): return lax.ppermute(value, ('row', 'col'), flat)  16.1 us
    ppermute x11, waiting for transfers between devices, send(): return lax.ppermute(value, ('row', 'col'), flat)  6.28 us
    convert_element_type x2, other arithmetic, two_terms(): terms = [high.astype(jnp.bfloat16), (values - high).astype(jnp.bfloat16)]  2.73 us
    dot_general x1, matrix products, shards(): return matrix - jnp.dot(received, upper, preferred_element_type=jnp.float32)  1.03 us
  transfers between devices with their start and end apart: 11, of which 4 were waited for; matrix products, arithmetic and copies ran while one was open for 5% of the time, Pallas kernels for 0%

profile of v17, /device:TPU:0, one launch (start us, length us, event | category | flops | bytes accessed | tf_op | source)
XLA Modules:
  0.0 28.0 jit_solution(2201160064681526219)
XLA Ops:
  0.0 2.8 %conditional.2 = (f32[256,256]{1,0:T(8,128)}, bf16[256,512]{1,0:T(8,128)(2,1)S(1)}) conditional(s32[]{:T(128)} %convert_element_type.30, () %tuple.29, (f32[256,512]{1,0:T(8,128)}, s32[]{:T(128)}) %tuple.30), branch_computations={%region_0.0_spmd, %region_1.2_spmd} | conditional | flops 1114113 | bytes 4194358 | solution.py:61
  0.0 0.0 copy-start.1
  0.0 1.7 %reduce-precision_convert_fusion = (bf16[256,256]{1,0:T(8,128)(2,1)S(1)}, f32[256,256]{1,0:T(8,128)}) fusion(f32[256,512]{1,0:T(8,128)} %get-tuple-element.108), kind=kLoop, calls=%fused_computation.1 | loop fusion | flops 131072 | bytes 655360 | tf_op jit(solution)/shard_map/cond/branch_1_fun/convert_element_type | solution.py:21
  1.8 1.0 %fusion = bf16[256,256]{1,0:T(8,128)(2,1)S(1)} fusion(f32[256,256]{1,0:T(8,128)} %get-tuple-element.145), kind=kLoop, calls=%fused_computation.2 | loop fusion | flops 196608 | bytes 393216 | tf_op jit(solution)/shard_map/cond/branch_1_fun/convert_element_type | solution.py:21
  2.7 0.0 copy-done.1
  2.7 0.1 maximum_select_fusion
  2.8 2.8 %collective-permute-start.3 = (bf16[256,512]{1,0:T(8,128)(2,1)S(1)}, bf16[256,512]{1,0:T(8,128)(2,1)S(1)}, u32[]{:S(2)}, u32[]{:S(2)}) collective-permute-start(bf16[256,512]{1,0:T(8,128)(2,1)S(1)} %get-tuple-element.125), channel_id=1, source_target_pairs={{24,0},{1,17},{0,4},{2,6},{3,19}} | collective-permute-start | bytes 786440 | tf_op jit(solution)/shard_map/ppermute | solution.py:48
  5.6 2.7 %collective-permute-start = (f32[256,256]{1,0:T(8,128)}, f32[256,256]{1,0:T(8,128)S(1)}, u32[]{:S(2)}, u32[]{:S(2)}) collective-permute-start(f32[256,256]{1,0:T(8,128)} %get-tuple-element.124), channel_id=1, source_target_pairs={{0,20},{8,0},{12,4},{24,16}} | collective-permute-start | bytes 786440 | tf_op jit(solution)/shard_map/ppermute | solution.py:48
  8.3 1.3 %collective-permute-start.1 = (f32[256,256]{1,0:T(8,128)}, f32[256,256]{1,0:T(8,128)S(1)}, u32[]{:S(2)}, u32[]{:S(2)}) collective-permute-start(f32[256,256]{1,0:T(8,128)} %get-tuple-element.124), channel_id=1, source_target_pairs={{0,4},{28,20}} | collective-permute-start | bytes 786440 | tf_op jit(solution)/shard_map/ppermute | solution.py:48
  9.6 1.3 %collective-permute-start.2 = (f32[256,256]{1,0:T(8,128)}, f32[256,256]{1,0:T(8,128)S(1)}, u32[]{:S(2)}, u32[]{:S(2)}) collective-permute-start(f32[256,256]{1,0:T(8,128)} %get-tuple-element.124), channel_id=1, source_target_pairs={{0,16}} | collective-permute-start | bytes 786440 | tf_op jit(solution)/shard_map/ppermute | solution.py:48
  11.1 2.5 %collective-permute-done.3 = bf16[256,512]{1,0:T(8,128)(2,1)S(1)} collective-permute-done((bf16[256,512]{1,0:T(8,128)(2,1)S(1)}, bf16[256,512]{1,0:T(8,128)(2,1)S(1)}, u32[]{:S(2)}, u32[]{:S(2)}) %collective-permute-start.3) | collective-permute-done | bytes 262176 | tf_op jit(solution)/shard_map/ppermute | solution.py:48
  13.6 0.0 copy-start
  13.6 1.4 %collective-permute-start.8 = (bf16[256,512]{1,0:T(8,128)(2,1)S(1)}, bf16[256,512]{1,0:T(8,128)(2,1)S(1)}, u32[]{:S(2)}, u32[]{:S(2)}) collective-permute-start(bf16[256,512]{1,0:T(8,128)(2,1)S(1)} %broadcast_select_fusion.1), channel_id=1, source_target_pairs={{17,21},{0,16},{2,18},{4,20},{6,22},{3,11},{19,27}} | collective-permute-start | bytes 786440 | tf_op jit(solution)/shard_map/ppermute | solution.py:48
  15.1 1.2 %collective-permute-done = f32[256,256]{1,0:T(8,128)S(1)} collective-permute-done((f32[256,256]{1,0:T(8,128)}, f32[256,256]{1,0:T(8,128)S(1)}, u32[]{:S(2)}, u32[]{:S(2)}) %collective-permute-start) | collective-permute-done | bytes 262176 | tf_op jit(solution)/shard_map/ppermute | solution.py:48
  16.3 0.0 collective-permute-done.1
  16.3 0.0 collective-permute-done.2
  16.3 0.0 copy-done
  16.3 1.2 %conditional.3 = (bf16[256,256]{1,0:T(8,128)(2,1)S(1)}, bf16[256,256]{1,0:T(8,128)(2,1)S(1)}) conditional(s32[]{:T(128)} %convert_element_type.29, () %tuple.28, (pred[]{:T(512)}, pred[]{:T(512)}, pred[]{:T(512)}, f32[256,512]{1,0:T(8,128)S(1)}, f32[256,256]{1,0:T(8,128)S(1)}, /*index=5*/f32[256,256]{1,0:T(8,128)S(1)}, f32[256,256]{1,0:T(8,128)S(1)}, ...), branch_computations={%region_2.3_spmd, %region_3.6_spmd} | conditional | flops 505217024 | bytes 5578771 | solution.py:127
  16.4 0.2 fusion.15
  16.5 0.6 %fusion.1 = f32[768,256]{1,0:T(8,128)S(1)} fusion(f32[256,256]{1,0:T(8,128)S(1)} %get-tuple-element.133, f32[256,256]{1,0:T(8,128)S(1)} %get-tuple-element.134, f32[256,256]{1,0:T(8,128)S(1)} %get-tuple-element.132, f32[256]{0:T(256)S(1)} %get-tuple-element.137, f32[256]{0:T(256)S(1)} %get-tuple-element.138), kind=kOutput, calls=%fused_computation.5 | convolution fusion | flops 302710784 | bytes 1574912 | tf_op jit(solution)/shard_map/cond/branch_1_fun/dot_general | solution.py:36
  17.1 0.4 %convolution_convert_fusion = bf16[512,256]{1,0:T(8,128)(2,1)S(1)} fusion(f32[768,256]{1,0:T(8,128)S(1)} %fusion.1), kind=kOutput, calls=%fused_computation.4 | convolution fusion | flops 201654272 | bytes 1048576 | tf_op jit(solution)/shard_map/cond/branch_1_fun/dot_general | solution.py:37
  17.5 1.3 %collective-permute-start.6 = (bf16[256,256]{1,0:T(8,128)(2,1)S(1)}, bf16[256,256]{1,0:T(8,128)(2,1)S(1)}, u32[]{:S(2)}, u32[]{:S(2)}) collective-permute-start(bf16[256,256]{1,0:T(8,128)(2,1)S(1)} %get-tuple-element.127), channel_id=1, source_target_pairs={{0,8},{4,12},{16,24},{20,28}} | collective-permute-start | bytes 393224 | tf_op jit(solution)/shard_map/ppermute | solution.py:48
  18.9 1.3 %collective-permute-start.4 = (bf16[256,256]{1,0:T(8,128)(2,1)S(1)}, bf16[256,256]{1,0:T(8,128)(2,1)S(1)}, u32[]{:S(2)}, u32[]{:S(2)}) collective-permute-start(bf16[256,256]{1,0:T(8,128)(2,1)S(1)} %get-tuple-element.140), channel_id=1, source_target_pairs={{0,26},{16,18},{4,14},{20,30}} | collective-permute-start | bytes 393224 | tf_op jit(solution)/shard_map/ppermute | solution.py:48
  20.2 1.3 %collective-permute-start.5 = (bf16[256,256]{1,0:T(8,128)(2,1)S(1)}, bf16[256,256]{1,0:T(8,128)(2,1)S(1)}, u32[]{:S(2)}, u32[]{:S(2)}) collective-permute-start(bf16[256,256]{1,0:T(8,128)(2,1)S(1)} %get-tuple-element.139), channel_id=1, source_target_pairs={{0,10},{4,6},{20,22}} | collective-permute-start | bytes 393224 | tf_op jit(solution)/shard_map/ppermute | solution.py:48
  21.5 0.0 collective-permute-done.8
  21.5 1.3 %collective-permute-start.10 = (bf16[256,512]{1,0:T(8,128)(2,1)S(1)}, bf16[256,512]{1,0:T(8,128)(2,1)S(1)}, u32[]{:S(2)}, u32[]{:S(2)}) collective-permute-start(bf16[256,512]{1,0:T(8,128)(2,1)S(1)} %broadcast_select_fusion.2), channel_id=1, source_target_pairs={{17,25},{21,29},{1,5},{0,8},{2,10},{4,12},{6,14},{16,24},{18,26},{... | collective-permute-start | bytes 786440 | tf_op jit(solution)/shard_map/ppermute | solution.py:48
  22.9 0.7 %collective-permute-start.9 = (bf16[256,512]{1,0:T(8,128)(2,1)S(1)}, bf16[256,512]{1,0:T(8,128)(2,1)S(1)}, u32[]{:S(2)}, u32[]{:S(2)}) collective-permute-start(bf16[256,512]{1,0:T(8,128)(2,1)S(1)} %broadcast_select_fusion.2), channel_id=1, source_target_pairs={{17,9},{21,13}} | collective-permute-start | bytes 786440 | tf_op jit(solution)/shard_map/ppermute | solution.py:48
  23.5 0.0 collective-permute-done.4
  23.6 0.6 %collective-permute-done.5 = bf16[256,256]{1,0:T(8,128)(2,1)S(1)} collective-permute-done((bf16[256,256]{1,0:T(8,128)(2,1)S(1)}, bf16[256,256]{1,0:T(8,128)(2,1)S(1)}, u32[]{:S(2)}, u32[]{:S(2)}) %collective-permute-start.5) | collective-permute-done | bytes 131104 | tf_op jit(solution)/shard_map/ppermute | solution.py:48
  24.1 0.0 collective-permute-done.6
  24.2 0.7 %collective-permute-start.7 = (bf16[256,256]{1,0:T(8,128)(2,1)S(1)}, bf16[256,256]{1,0:T(8,128)(2,1)S(1)}, u32[]{:S(2)}, u32[]{:S(2)}) collective-permute-start(bf16[256,256]{1,0:T(8,128)(2,1)S(1)} %select_select_fusion.2), channel_id=1, source_target_pairs={{4,5},{6,7},{8,9},{10,11},{12,13},{14,15},{16,17},{18,19},{20,21},... | collective-permute-start | bytes 393224 | tf_op jit(solution)/shard_map/ppermute | solution.py:48
  24.9 0.0 collective-permute-done.7
  24.9 2.0 %collective-permute-done.10 = bf16[256,512]{1,0:T(8,128)(2,1)S(1)} collective-permute-done((bf16[256,512]{1,0:T(8,128)(2,1)S(1)}, bf16[256,512]{1,0:T(8,128)(2,1)S(1)}, u32[]{:S(2)}, u32[]{:S(2)}) %collective-permute-start.10) | collective-permute-done | bytes 262176 | tf_op jit(solution)/shard_map/ppermute | solution.py:48
  26.9 0.0 collective-permute-done.9
  26.9 1.0 %convolution_subtract_fusion = f32[256,512]{1,0:T(8,128)} fusion(f32[256,512]{1,0:T(8,128)S(1)} %copy-done, bf16[256,512]{1,0:T(8,128)(2,1)S(1)} %collective-permute-done.9, bf16[256,512]{1,0:T(8,128)(2,1)S(1)} %collective-permute-done.10, bf16[256,512]{1,0:T(8,128)(2,1)S(1)} %broadcast_select_fusion.2, pred[]{:T(512)S(6)} %or.47, pred[]{:T(512)S(6)} %and.103, ...), kind=kOutput, calls=%fused_computation.38 | convolution fusion | flops 67764224 | bytes 2097668 | tf_op jit(solution)/shard_map/dot_general | solution.py:169
  (10 shorter events, 0.2 us)
Async XLA Ops:
  0.0 2.7 %copy-start.1 = (f32[256,512]{1,0:T(8,128)S(1)}, f32[256,512]{1,0:T(8,128)}, u32[]{:S(2)}) copy-start(f32[256,512]{1,0:T(8,128)} %get-tuple-element.108) | copy-start | bytes 1572868 | tf_op jit(solution)/shard_map/cond
  2.8 10.8 %collective-permute-start.3 = (bf16[256,512]{1,0:T(8,128)(2,1)S(1)}, bf16[256,512]{1,0:T(8,128)(2,1)S(1)}, u32[]{:S(2)}, u32[]{:S(2)}) collective-permute-start(bf16[256,512]{1,0:T(8,128)(2,1)S(1)} %get-tuple-element.125), channel_id=1, source_target_pairs={{24,0},{1,17},{0,4},{2,6},{3,19}} | collective-permute-start | bytes 786440 | tf_op jit(solution)/shard_map/ppermute | solution.py:48
  5.6 10.7 %collective-permute-start = (f32[256,256]{1,0:T(8,128)}, f32[256,256]{1,0:T(8,128)S(1)}, u32[]{:S(2)}, u32[]{:S(2)}) collective-permute-start(f32[256,256]{1,0:T(8,128)} %get-tuple-element.124), channel_id=1, source_target_pairs={{0,20},{8,0},{12,4},{24,16}} | collective-permute-start | bytes 786440 | tf_op jit(solution)/shard_map/ppermute | solution.py:48
  8.3 8.0 %collective-permute-start.1 = (f32[256,256]{1,0:T(8,128)}, f32[256,256]{1,0:T(8,128)S(1)}, u32[]{:S(2)}, u32[]{:S(2)}) collective-permute-start(f32[256,256]{1,0:T(8,128)} %get-tuple-element.124), channel_id=1, source_target_pairs={{0,4},{28,20}} | collective-permute-start | bytes 786440 | tf_op jit(solution)/shard_map/ppermute | solution.py:48
  9.6 6.7 %collective-permute-start.2 = (f32[256,256]{1,0:T(8,128)}, f32[256,256]{1,0:T(8,128)S(1)}, u32[]{:S(2)}, u32[]{:S(2)}) collective-permute-start(f32[256,256]{1,0:T(8,128)} %get-tuple-element.124), channel_id=1, source_target_pairs={{0,16}} | collective-permute-start | bytes 786440 | tf_op jit(solution)/shard_map/ppermute | solution.py:48
  13.6 2.7 %copy-start = (f32[256,512]{1,0:T(8,128)S(1)}, f32[256,512]{1,0:T(8,128)}, u32[]{:S(2)}) copy-start(f32[256,512]{1,0:T(8,128)} %param.5) | copy-start | bytes 1572868
  13.6 7.8 %collective-permute-start.8 = (bf16[256,512]{1,0:T(8,128)(2,1)S(1)}, bf16[256,512]{1,0:T(8,128)(2,1)S(1)}, u32[]{:S(2)}, u32[]{:S(2)}) collective-permute-start(bf16[256,512]{1,0:T(8,128)(2,1)S(1)} %broadcast_select_fusion.1), channel_id=1, source_target_pairs={{17,21},{0,16},{2,18},{4,20},{6,22},{3,11},{19,27}} | collective-permute-start | bytes 786440 | tf_op jit(solution)/shard_map/ppermute | solution.py:48
  17.5 6.6 %collective-permute-start.6 = (bf16[256,256]{1,0:T(8,128)(2,1)S(1)}, bf16[256,256]{1,0:T(8,128)(2,1)S(1)}, u32[]{:S(2)}, u32[]{:S(2)}) collective-permute-start(bf16[256,256]{1,0:T(8,128)(2,1)S(1)} %get-tuple-element.127), channel_id=1, source_target_pairs={{0,8},{4,12},{16,24},{20,28}} | collective-permute-start | bytes 393224 | tf_op jit(solution)/shard_map/ppermute | solution.py:48
  18.9 4.7 %collective-permute-start.4 = (bf16[256,256]{1,0:T(8,128)(2,1)S(1)}, bf16[256,256]{1,0:T(8,128)(2,1)S(1)}, u32[]{:S(2)}, u32[]{:S(2)}) collective-permute-start(bf16[256,256]{1,0:T(8,128)(2,1)S(1)} %get-tuple-element.140), channel_id=1, source_target_pairs={{0,26},{16,18},{4,14},{20,30}} | collective-permute-start | bytes 393224 | tf_op jit(solution)/shard_map/ppermute | solution.py:48
  20.2 3.9 %collective-permute-start.5 = (bf16[256,256]{1,0:T(8,128)(2,1)S(1)}, bf16[256,256]{1,0:T(8,128)(2,1)S(1)}, u32[]{:S(2)}, u32[]{:S(2)}) collective-permute-start(bf16[256,256]{1,0:T(8,128)(2,1)S(1)} %get-tuple-element.139), channel_id=1, source_target_pairs={{0,10},{4,6},{20,22}} | collective-permute-start | bytes 393224 | tf_op jit(solution)/shard_map/ppermute | solution.py:48
  21.5 5.4 %collective-permute-start.10 = (bf16[256,512]{1,0:T(8,128)(2,1)S(1)}, bf16[256,512]{1,0:T(8,128)(2,1)S(1)}, u32[]{:S(2)}, u32[]{:S(2)}) collective-permute-start(bf16[256,512]{1,0:T(8,128)(2,1)S(1)} %broadcast_select_fusion.2), channel_id=1, source_target_pairs={{17,25},{21,29},{1,5},{0,8},{2,10},{4,12},{6,14},{16,24},{18,26},{... | collective-permute-start | bytes 786440 | tf_op jit(solution)/shard_map/ppermute | solution.py:48
  22.9 4.1 %collective-permute-start.9 = (bf16[256,512]{1,0:T(8,128)(2,1)S(1)}, bf16[256,512]{1,0:T(8,128)(2,1)S(1)}, u32[]{:S(2)}, u32[]{:S(2)}) collective-permute-start(bf16[256,512]{1,0:T(8,128)(2,1)S(1)} %broadcast_select_fusion.2), channel_id=1, source_target_pairs={{17,9},{21,13}} | collective-permute-start | bytes 786440 | tf_op jit(solution)/shard_map/ppermute | solution.py:48
  24.2 0.7 %collective-permute-start.7 = (bf16[256,256]{1,0:T(8,128)(2,1)S(1)}, bf16[256,256]{1,0:T(8,128)(2,1)S(1)}, u32[]{:S(2)}, u32[]{:S(2)}) collective-permute-start(bf16[256,256]{1,0:T(8,128)(2,1)S(1)} %select_select_fusion.2), channel_id=1, source_target_pairs={{4,5},{6,7},{8,9},{10,11},{12,13},{14,15},{16,17},{18,19},{20,21},... | collective-permute-start | bytes 393224 | tf_op jit(solution)/shard_map/ppermute | solution.py:48

commit v18 on v17

--- a/solution.py
+++ b/solution.py
@@ -51,11 +51,11 @@
     shared = middle + APART
 
     def blocks(matrix):
-        columns, rows = matrix[:, :NB], matrix.astype(jnp.bfloat16)
-        return columns, jnp.where(row_here == shared, two_terms(columns, cols_dev), rows)
+        terms, rows = two_terms(matrix[:, :NB], cols_dev), matrix.astype(jnp.bfloat16)
+        return terms, jnp.where(row_here == shared, terms, rows)
 
     def no_blocks(matrix):
-        return jnp.zeros((NB, NB), matrix.dtype), jnp.zeros(matrix.shape, jnp.bfloat16)
+        return jnp.zeros(matrix.shape, jnp.bfloat16), jnp.zeros(matrix.shape, jnp.bfloat16)
 
     sends_columns = (col_here == 0) & (row_here & APART != 0)
     pivot_columns, first_upper = lax.cond(
@@ -102,7 +102,7 @@
     workers = [r for r in range(n_row) if r & APART == 0]
     targets = workers[:1:-1]
     targets.insert(1, 1)
-    square, partner = matrix[:, :NB], matrix[:, :NB]
+    square = partner = pivot_columns
     upper, got = upper_step(upper, 0, first_upper, [((shared, 0), (0, 0))])
     own = jnp.where(row_here == 0, summed(got), matrix[:, :NB])
     for index, target in enumerate(targets):
@@ -115,7 +115,8 @@
     upper, _ = upper_step(upper, 1, upper)
 
     def compute(square, own, partner):
-        both = multipliers(square, jnp.concatenate([own, partner], axis=0))
+        columns = jnp.concatenate([own, summed(partner)], axis=0)
+        both = multipliers(summed(square), columns)
         both = both.astype(jnp.bfloat16)
         return both[:NB], both[NB:]
 

time: 28.3 us -> 26.8 us (0.947)
  other arithmetic: 3.15 us -> 1.57 us
  waiting for transfers between devices: 6.28 us -> 5.35 us
  starting transfers between devices: 16.1 us -> 17 us
    convert_element_type x2 -> x1, other arithmetic: 2.73 us -> 1.05 us  [two_terms(): terms = [high.astype(jnp.bfloat16), (values - high).astype(jnp.bfloat16)]]
    ppermute x11, starting transfers between devices: 16.1 us -> 17 us  [send(): return lax.ppermute(value, ('row', 'col'), flat)]
    ppermute x11, waiting for transfers between devices: 6.28 us -> 5.35 us  [send(): return lax.ppermute(value, ('row', 'col'), flat)]
where the time goes in v18:
time: 26.8 us; the launch traced here: 26.5 us
  starting transfers between devices  17 us (63%)
  waiting for transfers between devices  5.35 us (20%)
  matrix products  1.99 us (7%)
  other arithmetic  1.57 us (6%)
  between operations  0.36 us (1%)
    ppermute x11, starting transfers between devices, send(): return lax.ppermute(value, ('row', 'col'), flat)  17 us
    ppermute x11, waiting for transfers between devices, send(): return lax.ppermute(value, ('row', 'col'), flat)  5.35 us
    convert_element_type x1, other arithmetic, two_terms(): terms = [high.astype(jnp.bfloat16), (values - high).astype(jnp.bfloat16)]  1.05 us
    dot_general x1, matrix products, shards(): return matrix - jnp.dot(received, upper, preferred_element_type=jnp.float32)  1.03 us
    dot_general x1, matrix products, multipliers(): jnp.dot(jnp.concatenate([square, columns], axis=0), approx, precision=HIGH)  0.56 us
  transfers between devices with their start and end apart: 11, of which 4 were waited for; matrix products, arithmetic and copies ran while one was open for 5% of the time, Pallas kernels for 0%

profile of v18, /device:TPU:0, one launch (start us, length us, event | category | flops | bytes accessed | tf_op | source)
XLA Modules:
  0.0 26.5 jit_solution(8293894997657679664)
XLA Ops:
  0.0 1.2 %conditional.2 = (bf16[256,512]{1,0:T(8,128)(2,1)S(1)}, bf16[256,512]{1,0:T(8,128)(2,1)S(1)}) conditional(s32[]{:T(128)} %convert_element_type.50, () %tuple.29, (f32[256,512]{1,0:T(8,128)}, s32[]{:T(128)}) %tuple.30), branch_computations={%region_0.0_spmd, %region_1.2_spmd} | conditional | flops 1048577 | bytes 3932214 | solution.py:61
  0.0 0.0 copy-start.1
  0.0 1.1 %reduce-precision_convert_fusion = (bf16[256,256]{1,0:T(8,128)(2,1)S(1)}, bf16[256,256]{1,0:T(8,128)(2,1)S(1)}) fusion(f32[256,512]{1,0:T(8,128)} %get-tuple-element.110), kind=kLoop, calls=%fused_computation.1 | loop fusion | flops 262144 | bytes 524288 | tf_op jit(solution)/shard_map/cond/branch_1_fun/convert_element_type | solution.py:21
  1.1 0.1 copy-done.1
  1.1 0.1 convert_select_fusion
  1.2 3.7 %collective-permute-start.3 = (bf16[256,512]{1,0:T(8,128)(2,1)S(1)}, bf16[256,512]{1,0:T(8,128)(2,1)S(1)}, u32[]{:S(2)}, u32[]{:S(2)}) collective-permute-start(bf16[256,512]{1,0:T(8,128)(2,1)S(1)} %get-tuple-element.129), channel_id=1, source_target_pairs={{24,0},{1,17},{0,4},{2,6},{3,19}} | collective-permute-start | bytes 786440 | tf_op jit(solution)/shard_map/ppermute | solution.py:48
  4.9 2.7 %collective-permute-start = (bf16[256,512]{1,0:T(8,128)(2,1)S(1)}, bf16[256,512]{1,0:T(8,128)(2,1)S(1)}, u32[]{:S(2)}, u32[]{:S(2)}) collective-permute-start(bf16[256,512]{1,0:T(8,128)(2,1)S(1)} %get-tuple-element.128), channel_id=1, source_target_pairs={{0,20},{8,0},{12,4},{24,16}} | collective-permute-start | bytes 786440 | tf_op jit(solution)/shard_map/ppermute | solution.py:48
  7.6 1.3 %collective-permute-start.1 = (bf16[256,512]{1,0:T(8,128)(2,1)S(1)}, bf16[256,512]{1,0:T(8,128)(2,1)S(1)}, u32[]{:S(2)}, u32[]{:S(2)}) collective-permute-start(bf16[256,512]{1,0:T(8,128)(2,1)S(1)} %get-tuple-element.128), channel_id=1, source_target_pairs={{0,4},{28,20}} | collective-permute-start | bytes 786440 | tf_op jit(solution)/shard_map/ppermute | solution.py:48
  8.9 1.3 %collective-permute-start.2 = (bf16[256,512]{1,0:T(8,128)(2,1)S(1)}, bf16[256,512]{1,0:T(8,128)(2,1)S(1)}, u32[]{:S(2)}, u32[]{:S(2)}) collective-permute-start(bf16[256,512]{1,0:T(8,128)(2,1)S(1)} %get-tuple-element.128), channel_id=1, source_target_pairs={{0,16}} | collective-permute-start | bytes 786440 | tf_op jit(solution)/shard_map/ppermute | solution.py:48
  10.4 1.6 %collective-permute-done.3 = bf16[256,512]{1,0:T(8,128)(2,1)S(1)} collective-permute-done((bf16[256,512]{1,0:T(8,128)(2,1)S(1)}, bf16[256,512]{1,0:T(8,128)(2,1)S(1)}, u32[]{:S(2)}, u32[]{:S(2)}) %collective-permute-start.3) | collective-permute-done | bytes 262176 | tf_op jit(solution)/shard_map/ppermute | solution.py:48
  12.0 0.0 copy-start
  12.0 1.4 %collective-permute-start.8 = (bf16[256,512]{1,0:T(8,128)(2,1)S(1)}, bf16[256,512]{1,0:T(8,128)(2,1)S(1)}, u32[]{:S(2)}, u32[]{:S(2)}) collective-permute-start(bf16[256,512]{1,0:T(8,128)(2,1)S(1)} %broadcast_select_fusion.1), channel_id=1, source_target_pairs={{17,21},{0,16},{2,18},{4,20},{6,22},{3,11},{19,27}} | collective-permute-start | bytes 786440 | tf_op jit(solution)/shard_map/ppermute | solution.py:48
  13.5 1.2 %collective-permute-done = bf16[256,512]{1,0:T(8,128)(2,1)S(1)} collective-permute-done((bf16[256,512]{1,0:T(8,128)(2,1)S(1)}, bf16[256,512]{1,0:T(8,128)(2,1)S(1)}, u32[]{:S(2)}, u32[]{:S(2)}) %collective-permute-start) | collective-permute-done | bytes 262176 | tf_op jit(solution)/shard_map/ppermute | solution.py:48
  14.7 0.0 collective-permute-done.1
  14.7 0.0 collective-permute-done.2
  14.7 0.0 copy-done
  14.7 1.3 %conditional.3 = (bf16[256,256]{1,0:T(8,128)(2,1)S(1)}, bf16[256,256]{1,0:T(8,128)(2,1)S(1)}) conditional(s32[]{:T(128)} %convert_element_type.49, () %tuple.28, (pred[]{:T(512)}, pred[]{:T(512)}, pred[]{:T(512)}, bf16[256,512]{1,0:T(8,128)(2,1)S(1)}, bf16[256,512]{1,0:T(8,128)(2,1)S(1)}, /*index=5*/bf16[256,512]{1,0:T(8,128)(2,1)S(1)}, ...), branch_computations={%region_2.3_spmd, %region_3.6_spmd} | conditional | flops 506068992 | bytes 6889492 | solution.py:128
  14.7 0.1 select_select_fusion.1
  14.8 0.1 fusion.15
  15.0 0.1 slice_select_fusion
  15.0 0.6 %fusion.1 = f32[768,256]{1,0:T(8,128)S(1)} fusion(f32[256,256]{1,0:T(8,128)S(1)} %get-tuple-element.141, f32[256,256]{1,0:T(8,128)S(1)} %slice_select_fusion, f32[256,256]{1,0:T(8,128)S(1)} %get-tuple-element.140, f32[256]{0:T(256)S(1)} %broadcast_divide_fusion, f32[256]{0:T(256)S(1)} %broadcast_divide_fusion.1), kind=kOutput, calls=%fused_computation.6 | convolution fusion | flops 302710784 | bytes 1574912 | tf_op jit(solution)/shard_map/cond/branch_1_fun/dot_general | solution.py:36
  15.6 0.4 %convolution_convert_fusion = bf16[512,256]{1,0:T(8,128)(2,1)S(1)} fusion(f32[768,256]{1,0:T(8,128)S(1)} %fusion.1), kind=kOutput, calls=%fused_computation.5 | convolution fusion | flops 201654272 | bytes 1048576 | tf_op jit(solution)/shard_map/cond/branch_1_fun/dot_general | solution.py:37
  16.0 1.3 %collective-permute-start.6 = (bf16[256,256]{1,0:T(8,128)(2,1)S(1)}, bf16[256,256]{1,0:T(8,128)(2,1)S(1)}, u32[]{:S(2)}, u32[]{:S(2)}) collective-permute-start(bf16[256,256]{1,0:T(8,128)(2,1)S(1)} %get-tuple-element.131), channel_id=1, source_target_pairs={{0,8},{4,12},{16,24},{20,28}} | collective-permute-start | bytes 393224 | tf_op jit(solution)/shard_map/ppermute | solution.py:48
  17.4 1.3 %collective-permute-start.4 = (bf16[256,256]{1,0:T(8,128)(2,1)S(1)}, bf16[256,256]{1,0:T(8,128)(2,1)S(1)}, u32[]{:S(2)}, u32[]{:S(2)}) collective-permute-start(bf16[256,256]{1,0:T(8,128)(2,1)S(1)} %get-tuple-element.145), channel_id=1, source_target_pairs={{0,26},{16,18},{4,14},{20,30}} | collective-permute-start | bytes 393224 | tf_op jit(solution)/shard_map/ppermute | solution.py:48
  18.7 1.3 %collective-permute-start.5 = (bf16[256,256]{1,0:T(8,128)(2,1)S(1)}, bf16[256,256]{1,0:T(8,128)(2,1)S(1)}, u32[]{:S(2)}, u32[]{:S(2)}) collective-permute-start(bf16[256,256]{1,0:T(8,128)(2,1)S(1)} %get-tuple-element.144), channel_id=1, source_target_pairs={{0,10},{4,6},{20,22}} | collective-permute-start | bytes 393224 | tf_op jit(solution)/shard_map/ppermute | solution.py:48
  20.0 0.0 collective-permute-done.8
  20.0 1.3 %collective-permute-start.10 = (bf16[256,512]{1,0:T(8,128)(2,1)S(1)}, bf16[256,512]{1,0:T(8,128)(2,1)S(1)}, u32[]{:S(2)}, u32[]{:S(2)}) collective-permute-start(bf16[256,512]{1,0:T(8,128)(2,1)S(1)} %broadcast_select_fusion.2), channel_id=1, source_target_pairs={{17,25},{21,29},{1,5},{0,8},{2,10},{4,12},{6,14},{16,24},{18,26},{... | collective-permute-start | bytes 786440 | tf_op jit(solution)/shard_map/ppermute | solution.py:48
  21.4 0.7 %collective-permute-start.9 = (bf16[256,512]{1,0:T(8,128)(2,1)S(1)}, bf16[256,512]{1,0:T(8,128)(2,1)S(1)}, u32[]{:S(2)}, u32[]{:S(2)}) collective-permute-start(bf16[256,512]{1,0:T(8,128)(2,1)S(1)} %broadcast_select_fusion.2), channel_id=1, source_target_pairs={{17,9},{21,13}} | collective-permute-start | bytes 786440 | tf_op jit(solution)/shard_map/ppermute | solution.py:48
  22.0 0.0 collective-permute-done.4
  22.0 0.6 %collective-permute-done.5 = bf16[256,256]{1,0:T(8,128)(2,1)S(1)} collective-permute-done((bf16[256,256]{1,0:T(8,128)(2,1)S(1)}, bf16[256,256]{1,0:T(8,128)(2,1)S(1)}, u32[]{:S(2)}, u32[]{:S(2)}) %collective-permute-start.5) | collective-permute-done | bytes 131104 | tf_op jit(solution)/shard_map/ppermute | solution.py:48
  22.6 0.0 collective-permute-done.6
  22.6 0.7 %collective-permute-start.7 = (bf16[256,256]{1,0:T(8,128)(2,1)S(1)}, bf16[256,256]{1,0:T(8,128)(2,1)S(1)}, u32[]{:S(2)}, u32[]{:S(2)}) collective-permute-start(bf16[256,256]{1,0:T(8,128)(2,1)S(1)} %select_select_fusion.2), channel_id=1, source_target_pairs={{4,5},{6,7},{8,9},{10,11},{12,13},{14,15},{16,17},{18,19},{20,21},... | collective-permute-start | bytes 393224 | tf_op jit(solution)/shard_map/ppermute | solution.py:48
  23.4 0.0 collective-permute-done.7
  23.4 2.0 %collective-permute-done.10 = bf16[256,512]{1,0:T(8,128)(2,1)S(1)} collective-permute-done((bf16[256,512]{1,0:T(8,128)(2,1)S(1)}, bf16[256,512]{1,0:T(8,128)(2,1)S(1)}, u32[]{:S(2)}, u32[]{:S(2)}) %collective-permute-start.10) | collective-permute-done | bytes 262176 | tf_op jit(solution)/shard_map/ppermute | solution.py:48
  25.4 0.0 collective-permute-done.9
  25.4 1.0 %convolution_subtract_fusion = f32[256,512]{1,0:T(8,128)} fusion(f32[256,512]{1,0:T(8,128)S(1)} %copy-done, bf16[256,512]{1,0:T(8,128)(2,1)S(1)} %collective-permute-done.9, bf16[256,512]{1,0:T(8,128)(2,1)S(1)} %collective-permute-done.10, bf16[256,512]{1,0:T(8,128)(2,1)S(1)} %broadcast_select_fusion.2, pred[]{:T(512)S(6)} %or.47, pred[]{:T(512)S(6)} %and.103, ...), kind=kOutput, calls=%fused_computation.41 | convolution fusion | flops 67764224 | bytes 2097668 | tf_op jit(solution)/shard_map/dot_general | solution.py:170
  (11 shorter events, 0.2 us)
Async XLA Ops:
  0.0 1.1 %copy-start.1 = (f32[256,512]{1,0:T(8,128)S(1)}, f32[256,512]{1,0:T(8,128)}, u32[]{:S(2)}) copy-start(f32[256,512]{1,0:T(8,128)} %get-tuple-element.110) | copy-start | bytes 1572868 | tf_op jit(solution)/shard_map/cond
  1.2 10.8 %collective-permute-start.3 = (bf16[256,512]{1,0:T(8,128)(2,1)S(1)}, bf16[256,512]{1,0:T(8,128)(2,1)S(1)}, u32[]{:S(2)}, u32[]{:S(2)}) collective-permute-start(bf16[256,512]{1,0:T(8,128)(2,1)S(1)} %get-tuple-element.129), channel_id=1, source_target_pairs={{24,0},{1,17},{0,4},{2,6},{3,19}} | collective-permute-start | bytes 786440 | tf_op jit(solution)/shard_map/ppermute | solution.py:48
  4.9 9.8 %collective-permute-start = (bf16[256,512]{1,0:T(8,128)(2,1)S(1)}, bf16[256,512]{1,0:T(8,128)(2,1)S(1)}, u32[]{:S(2)}, u32[]{:S(2)}) collective-permute-start(bf16[256,512]{1,0:T(8,128)(2,1)S(1)} %get-tuple-element.128), channel_id=1, source_target_pairs={{0,20},{8,0},{12,4},{24,16}} | collective-permute-start | bytes 786440 | tf_op jit(solution)/shard_map/ppermute | solution.py:48
  7.6 7.1 %collective-permute-start.1 = (bf16[256,512]{1,0:T(8,128)(2,1)S(1)}, bf16[256,512]{1,0:T(8,128)(2,1)S(1)}, u32[]{:S(2)}, u32[]{:S(2)}) collective-permute-start(bf16[256,512]{1,0:T(8,128)(2,1)S(1)} %get-tuple-element.128), channel_id=1, source_target_pairs={{0,4},{28,20}} | collective-permute-start | bytes 786440 | tf_op jit(solution)/shard_map/ppermute | solution.py:48
  8.9 5.7 %collective-permute-start.2 = (bf16[256,512]{1,0:T(8,128)(2,1)S(1)}, bf16[256,512]{1,0:T(8,128)(2,1)S(1)}, u32[]{:S(2)}, u32[]{:S(2)}) collective-permute-start(bf16[256,512]{1,0:T(8,128)(2,1)S(1)} %get-tuple-element.128), channel_id=1, source_target_pairs={{0,16}} | collective-permute-start | bytes 786440 | tf_op jit(solution)/shard_map/ppermute | solution.py:48
  12.0 2.7 %copy-start = (f32[256,512]{1,0:T(8,128)S(1)}, f32[256,512]{1,0:T(8,128)}, u32[]{:S(2)}) copy-start(f32[256,512]{1,0:T(8,128)} %param.5) | copy-start | bytes 1572868
  12.0 8.0 %collective-permute-start.8 = (bf16[256,512]{1,0:T(8,128)(2,1)S(1)}, bf16[256,512]{1,0:T(8,128)(2,1)S(1)}, u32[]{:S(2)}, u32[]{:S(2)}) collective-permute-start(bf16[256,512]{1,0:T(8,128)(2,1)S(1)} %broadcast_select_fusion.1), channel_id=1, source_target_pairs={{17,21},{0,16},{2,18},{4,20},{6,22},{3,11},{19,27}} | collective-permute-start | bytes 786440 | tf_op jit(solution)/shard_map/ppermute | solution.py:48
  16.0 6.6 %collective-permute-start.6 = (bf16[256,256]{1,0:T(8,128)(2,1)S(1)}, bf16[256,256]{1,0:T(8,128)(2,1)S(1)}, u32[]{:S(2)}, u32[]{:S(2)}) collective-permute-start(bf16[256,256]{1,0:T(8,128)(2,1)S(1)} %get-tuple-element.131), channel_id=1, source_target_pairs={{0,8},{4,12},{16,24},{20,28}} | collective-permute-start | bytes 393224 | tf_op jit(solution)/shard_map/ppermute | solution.py:48
  17.4 4.7 %collective-permute-start.4 = (bf16[256,256]{1,0:T(8,128)(2,1)S(1)}, bf16[256,256]{1,0:T(8,128)(2,1)S(1)}, u32[]{:S(2)}, u32[]{:S(2)}) collective-permute-start(bf16[256,256]{1,0:T(8,128)(2,1)S(1)} %get-tuple-element.145), channel_id=1, source_target_pairs={{0,26},{16,18},{4,14},{20,30}} | collective-permute-start | bytes 393224 | tf_op jit(solution)/shard_map/ppermute | solution.py:48
  18.7 3.9 %collective-permute-start.5 = (bf16[256,256]{1,0:T(8,128)(2,1)S(1)}, bf16[256,256]{1,0:T(8,128)(2,1)S(1)}, u32[]{:S(2)}, u32[]{:S(2)}) collective-permute-start(bf16[256,256]{1,0:T(8,128)(2,1)S(1)} %get-tuple-element.144), channel_id=1, source_target_pairs={{0,10},{4,6},{20,22}} | collective-permute-start | bytes 393224 | tf_op jit(solution)/shard_map/ppermute | solution.py:48
  20.0 5.4 %collective-permute-start.10 = (bf16[256,512]{1,0:T(8,128)(2,1)S(1)}, bf16[256,512]{1,0:T(8,128)(2,1)S(1)}, u32[]{:S(2)}, u32[]{:S(2)}) collective-permute-start(bf16[256,512]{1,0:T(8,128)(2,1)S(1)} %broadcast_select_fusion.2), channel_id=1, source_target_pairs={{17,25},{21,29},{1,5},{0,8},{2,10},{4,12},{6,14},{16,24},{18,26},{... | collective-permute-start | bytes 786440 | tf_op jit(solution)/shard_map/ppermute | solution.py:48
  21.4 4.1 %collective-permute-start.9 = (bf16[256,512]{1,0:T(8,128)(2,1)S(1)}, bf16[256,512]{1,0:T(8,128)(2,1)S(1)}, u32[]{:S(2)}, u32[]{:S(2)}) collective-permute-start(bf16[256,512]{1,0:T(8,128)(2,1)S(1)} %broadcast_select_fusion.2), channel_id=1, source_target_pairs={{17,9},{21,13}} | collective-permute-start | bytes 786440 | tf_op jit(solution)/shard_map/ppermute | solution.py:48
  22.6 0.7 %collective-permute-start.7 = (bf16[256,256]{1,0:T(8,128)(2,1)S(1)}, bf16[256,256]{1,0:T(8,128)(2,1)S(1)}, u32[]{:S(2)}, u32[]{:S(2)}) collective-permute-start(bf16[256,256]{1,0:T(8,128)(2,1)S(1)} %select_select_fusion.2), channel_id=1, source_target_pairs={{4,5},{6,7},{8,9},{10,11},{12,13},{14,15},{16,17},{18,19},{20,21},... | collective-permute-start | bytes 393224 | tf_op jit(solution)/shard_map/ppermute | solution.py:48

commit v19 on v18

--- a/solution.py
+++ b/solution.py
@@ -72,6 +72,18 @@
         beside_steps.append([(h, h + stride) for h in far])
     beside_steps[-1].append((0, 1))
     beside_back = [(middle + r - 2, r) for r in range(2, middle)]
+    first_steps = [[(0, 1)], [(0, APART), (1, middle + 1)]]
+    first_held = [0, 1, APART, middle + 1]
+    for step in range(2, len(down)):
+        hops = []
+        for source in first_held[step == len(down) - 1 :]:
+            missing = [r for r in range(n_row) if r not in first_held + [b for _, b in hops]]
+            near = [r for r in missing if r == source + APART]
+            hops += [(source, r) for r in (near or missing)[:1]]
+        first_steps.append(hops)
+        first_held = first_held + [b for _, b in hops]
+    first_back = [(APART, r) for r in range(n_row) if r not in first_held]
+    assert len(first_back) == 1
 
     def among(rows):
         found = jnp.bool_(False)
@@ -81,19 +93,21 @@
 
     def upper_step(value, step, sent, pairs=()):
         pairs = list(pairs) + [((a, 1), (b, 1)) for a, b in beside_steps[step]]
+        pairs += [((a, 0), (b, 0)) for a, b in first_steps[step]]
         takes = (col_here == 1) & among([b for _, b in beside_steps[step]])
+        takes = takes | ((col_here == 0) & among([b for _, b in first_steps[step]]))
         for kind in range(2):
             stride = orders[kind][step]
             missing = sum(orders[kind][step + 1 :])
             takes = takes | (
-                (col_here != 1)
+                (col_here > 1)
                 & (col_here % 2 == kind)
                 & ((row_here & (stride | missing)) == stride)
             )
             pairs += [
                 ((h, c), (h + stride, c))
                 for h in held[kind]
-                for c in range(3 * kind, n_col, 2)
+                for c in range(2 + kind, n_col, 2)
             ]
             held[kind] = held[kind] + [h + stride for h in held[kind]]
         got = send(sent, pairs)
@@ -157,8 +171,11 @@
         upper, _ = upper_step(upper, step, upper)
     if len(beside_back) > 2:
         sent = upper
-    got = send(sent, [((a, 1), (b, 1)) for a, b in beside_back])
-    upper = jnp.where((col_here == 1) & (row_here > 1) & (row_here < middle), got, upper)
+    pairs = [((a, 1), (b, 1)) for a, b in beside_back] + [((a, 0), (b, 0)) for a, b in first_back]
+    got = send(sent, pairs)
+    takes = (col_here == 1) & (row_here > 1) & (row_here < middle)
+    takes = takes | ((col_here == 0) & among([b for _, b in first_back]))
+    upper = jnp.where(takes, got, upper)
     got = send(
         received, [((r, c), (r, c + 1)) for r in range(1, n_row) for c in range(0, n_col, 2)]
     )

time: 26.8 us -> 30.8 us (1.15)
  the two profiles are of different devices: /device:TPU:0 before, /device:TPU:24 now
where the time goes in v19:
time: 30.8 us; the launch traced here: 30.4 us
  waiting for transfers between devices  16.9 us (55%)
  starting transfers between devices  10.7 us (35%)
  other arithmetic  1.3 us (4%)
  matrix products  1.03 us (3%)
  between operations  0.39 us (1%)
    ppermute x11, waiting for transfers between devices, send(): return lax.ppermute(value, ('row', 'col'), flat)  16.9 us
    ppermute x11, starting transfers between devices, send(): return lax.ppermute(value, ('row', 'col'), flat)  10.7 us
    convert_element_type x1, other arithmetic, two_terms(): terms = [high.astype(jnp.bfloat16), (values - high).astype(jnp.bfloat16)]  1.05 us
    dot_general x1, matrix products, shards(): return matrix - jnp.dot(received, upper, preferred_element_type=jnp.float32)  1.03 us
  transfers between devices with their start and end apart: 11, of which 5 were waited for; matrix products, arithmetic and copies ran while one was open for 1% of the time, Pallas kernels for 0%

profile of v19, /device:TPU:24, one launch (start us, length us, event | category | flops | bytes accessed | tf_op | source)
XLA Modules:
  0.0 30.4 jit_solution(14440982886150544536)
XLA Ops:
  0.0 1.2 %conditional.2 = (bf16[256,512]{1,0:T(8,128)(2,1)S(1)}, bf16[256,512]{1,0:T(8,128)(2,1)S(1)}) conditional(s32[]{:T(128)} %convert_element_type.50, () %tuple.29, (f32[256,512]{1,0:T(8,128)}, s32[]{:T(128)}) %tuple.30), branch_computations={%region_0.0_spmd, %region_1.2_spmd} | conditional | flops 1048577 | bytes 3932214 | solution.py:61
  0.0 0.0 copy-start.1
  0.0 1.1 %reduce-precision_convert_fusion = (bf16[256,256]{1,0:T(8,128)(2,1)S(1)}, bf16[256,256]{1,0:T(8,128)(2,1)S(1)}) fusion(f32[256,512]{1,0:T(8,128)} %get-tuple-element.110), kind=kLoop, calls=%fused_computation.1 | loop fusion | flops 262144 | bytes 524288 | tf_op jit(solution)/shard_map/cond/branch_1_fun/convert_element_type | solution.py:21
  1.1 0.1 copy-done.1
  1.1 0.1 convert_select_fusion
  1.2 1.3 %collective-permute-start.3 = (bf16[256,512]{1,0:T(8,128)(2,1)S(1)}, bf16[256,512]{1,0:T(8,128)(2,1)S(1)}, u32[]{:S(2)}, u32[]{:S(2)}) collective-permute-start(bf16[256,512]{1,0:T(8,128)(2,1)S(1)} %get-tuple-element.129), channel_id=1, source_target_pairs={{24,0},{1,17},{0,4},{2,6},{3,19}} | collective-permute-start | bytes 786440 | tf_op jit(solution)/shard_map/ppermute | solution.py:48
  2.5 1.3 %collective-permute-start = (bf16[256,512]{1,0:T(8,128)(2,1)S(1)}, bf16[256,512]{1,0:T(8,128)(2,1)S(1)}, u32[]{:S(2)}, u32[]{:S(2)}) collective-permute-start(bf16[256,512]{1,0:T(8,128)(2,1)S(1)} %get-tuple-element.128), channel_id=1, source_target_pairs={{0,20},{8,0},{12,4},{24,16}} | collective-permute-start | bytes 786440 | tf_op jit(solution)/shard_map/ppermute | solution.py:48
  3.8 0.7 %collective-permute-start.1 = (bf16[256,512]{1,0:T(8,128)(2,1)S(1)}, bf16[256,512]{1,0:T(8,128)(2,1)S(1)}, u32[]{:S(2)}, u32[]{:S(2)}) collective-permute-start(bf16[256,512]{1,0:T(8,128)(2,1)S(1)} %get-tuple-element.128), channel_id=1, source_target_pairs={{0,4},{28,20}} | collective-permute-start | bytes 786440 | tf_op jit(solution)/shard_map/ppermute | solution.py:48
  4.5 0.7 %collective-permute-start.2 = (bf16[256,512]{1,0:T(8,128)(2,1)S(1)}, bf16[256,512]{1,0:T(8,128)(2,1)S(1)}, u32[]{:S(2)}, u32[]{:S(2)}) collective-permute-start(bf16[256,512]{1,0:T(8,128)(2,1)S(1)} %get-tuple-element.128), channel_id=1, source_target_pairs={{0,16}} | collective-permute-start | bytes 786440 | tf_op jit(solution)/shard_map/ppermute | solution.py:48
  5.4 1.0 %collective-permute-done.3 = bf16[256,512]{1,0:T(8,128)(2,1)S(1)} collective-permute-done((bf16[256,512]{1,0:T(8,128)(2,1)S(1)}, bf16[256,512]{1,0:T(8,128)(2,1)S(1)}, u32[]{:S(2)}, u32[]{:S(2)}) %collective-permute-start.3) | collective-permute-done | bytes 262176 | tf_op jit(solution)/shard_map/ppermute | solution.py:48
  6.4 0.0 copy-start
  6.4 0.8 %collective-permute-start.8 = (bf16[256,512]{1,0:T(8,128)(2,1)S(1)}, bf16[256,512]{1,0:T(8,128)(2,1)S(1)}, u32[]{:S(2)}, u32[]{:S(2)}) collective-permute-start(bf16[256,512]{1,0:T(8,128)(2,1)S(1)} %broadcast_select_fusion.1), channel_id=1, source_target_pairs={{17,21},{0,8},{4,20},{2,18},{6,22},{3,11},{19,27}} | collective-permute-start | bytes 786440 | tf_op jit(solution)/shard_map/ppermute | solution.py:48
  7.3 1.9 %collective-permute-done = bf16[256,512]{1,0:T(8,128)(2,1)S(1)} collective-permute-done((bf16[256,512]{1,0:T(8,128)(2,1)S(1)}, bf16[256,512]{1,0:T(8,128)(2,1)S(1)}, u32[]{:S(2)}, u32[]{:S(2)}) %collective-permute-start) | collective-permute-done | bytes 262176 | tf_op jit(solution)/shard_map/ppermute | solution.py:48
  9.2 0.0 collective-permute-done.1
  9.2 0.0 collective-permute-done.2
  9.2 0.0 copy-done
  9.2 0.1 conditional.3
  9.3 1.3 %collective-permute-start.6 = (bf16[256,256]{1,0:T(8,128)(2,1)S(1)}, bf16[256,256]{1,0:T(8,128)(2,1)S(1)}, u32[]{:S(2)}, u32[]{:S(2)}) collective-permute-start(bf16[256,256]{1,0:T(8,128)(2,1)S(1)} %get-tuple-element.131), channel_id=1, source_target_pairs={{0,8},{4,12},{16,24},{20,28}} | collective-permute-start | bytes 393224 | tf_op jit(solution)/shard_map/ppermute | solution.py:48
  10.6 0.7 %collective-permute-start.4 = (bf16[256,256]{1,0:T(8,128)(2,1)S(1)}, bf16[256,256]{1,0:T(8,128)(2,1)S(1)}, u32[]{:S(2)}, u32[]{:S(2)}) collective-permute-start(bf16[256,256]{1,0:T(8,128)(2,1)S(1)} %get-tuple-element.145), channel_id=1, source_target_pairs={{0,26},{16,18},{4,14},{20,30}} | collective-permute-start | bytes 393224 | tf_op jit(solution)/shard_map/ppermute | solution.py:48
  11.3 0.7 %collective-permute-start.5 = (bf16[256,256]{1,0:T(8,128)(2,1)S(1)}, bf16[256,256]{1,0:T(8,128)(2,1)S(1)}, u32[]{:S(2)}, u32[]{:S(2)}) collective-permute-start(bf16[256,256]{1,0:T(8,128)(2,1)S(1)} %get-tuple-element.144), channel_id=1, source_target_pairs={{0,10},{4,6},{20,22}} | collective-permute-start | bytes 393224 | tf_op jit(solution)/shard_map/ppermute | solution.py:48
  12.0 0.0 collective-permute-done.8
  12.0 0.7 %collective-permute-start.10 = (bf16[256,512]{1,0:T(8,128)(2,1)S(1)}, bf16[256,512]{1,0:T(8,128)(2,1)S(1)}, u32[]{:S(2)}, u32[]{:S(2)}) collective-permute-start(bf16[256,512]{1,0:T(8,128)(2,1)S(1)} %broadcast_select_fusion.2), channel_id=1, source_target_pairs={{17,25},{21,29},{1,5},{4,12},{8,16},{20,28},{2,10},{6,14},{18,26},... | collective-permute-start | bytes 786440 | tf_op jit(solution)/shard_map/ppermute | solution.py:48
  12.7 1.3 %collective-permute-start.9 = (bf16[256,512]{1,0:T(8,128)(2,1)S(1)}, bf16[256,512]{1,0:T(8,128)(2,1)S(1)}, u32[]{:S(2)}, u32[]{:S(2)}) collective-permute-start(bf16[256,512]{1,0:T(8,128)(2,1)S(1)} %broadcast_select_fusion.2), channel_id=1, source_target_pairs={{17,9},{21,13},{8,24}} | collective-permute-start | bytes 786440 | tf_op jit(solution)/shard_map/ppermute | solution.py:48
  14.0 0.0 collective-permute-done.4
  14.0 0.0 collective-permute-done.5
  14.0 7.1 %collective-permute-done.6 = bf16[256,256]{1,0:T(8,128)(2,1)S(1)} collective-permute-done((bf16[256,256]{1,0:T(8,128)(2,1)S(1)}, bf16[256,256]{1,0:T(8,128)(2,1)S(1)}, u32[]{:S(2)}, u32[]{:S(2)}) %collective-permute-start.6) | collective-permute-done | bytes 131104 | tf_op jit(solution)/shard_map/ppermute | solution.py:48
  21.2 1.3 %collective-permute-start.7 = (bf16[256,256]{1,0:T(8,128)(2,1)S(1)}, bf16[256,256]{1,0:T(8,128)(2,1)S(1)}, u32[]{:S(2)}, u32[]{:S(2)}) collective-permute-start(bf16[256,256]{1,0:T(8,128)(2,1)S(1)} %select_select_fusion.2), channel_id=1, source_target_pairs={{4,5},{6,7},{8,9},{10,11},{12,13},{14,15},{16,17},{18,19},{20,21},... | collective-permute-start | bytes 393224 | tf_op jit(solution)/shard_map/ppermute | solution.py:48
  22.5 0.9 %collective-permute-done.7 = bf16[256,256]{1,0:T(8,128)(2,1)S(1)} collective-permute-done((bf16[256,256]{1,0:T(8,128)(2,1)S(1)}, bf16[256,256]{1,0:T(8,128)(2,1)S(1)}, u32[]{:S(2)}, u32[]{:S(2)}) %collective-permute-start.7) | collective-permute-done | bytes 131104 | tf_op jit(solution)/shard_map/ppermute | solution.py:48
  23.4 0.0 collective-permute-done.10
  23.4 6.0 %collective-permute-done.9 = bf16[256,512]{1,0:T(8,128)(2,1)S(1)} collective-permute-done((bf16[256,512]{1,0:T(8,128)(2,1)S(1)}, bf16[256,512]{1,0:T(8,128)(2,1)S(1)}, u32[]{:S(2)}, u32[]{:S(2)}) %collective-permute-start.9) | collective-permute-done | bytes 262176 | tf_op jit(solution)/shard_map/ppermute | solution.py:48
  29.4 1.0 %convolution_subtract_fusion = f32[256,512]{1,0:T(8,128)} fusion(f32[256,512]{1,0:T(8,128)S(1)} %copy-done, bf16[256,512]{1,0:T(8,128)(2,1)S(1)} %collective-permute-done.9, bf16[256,512]{1,0:T(8,128)(2,1)S(1)} %collective-permute-done.10, bf16[256,512]{1,0:T(8,128)(2,1)S(1)} %broadcast_select_fusion.2, pred[]{:T(512)S(6)} %or.75, pred[]{:T(512)S(6)} %or.61, ...), kind=kOutput, calls=%fused_computation.41 | convolution fusion | flops 67764224 | bytes 2097668 | tf_op jit(solution)/shard_map/dot_general | solution.py:187
  (10 shorter events, 0.2 us)
Async XLA Ops:
  0.0 1.1 %copy-start.1 = (f32[256,512]{1,0:T(8,128)S(1)}, f32[256,512]{1,0:T(8,128)}, u32[]{:S(2)}) copy-start(f32[256,512]{1,0:T(8,128)} %get-tuple-element.110) | copy-start | bytes 1572868 | tf_op jit(solution)/shard_map/cond
  1.2 5.2 %collective-permute-start.3 = (bf16[256,512]{1,0:T(8,128)(2,1)S(1)}, bf16[256,512]{1,0:T(8,128)(2,1)S(1)}, u32[]{:S(2)}, u32[]{:S(2)}) collective-permute-start(bf16[256,512]{1,0:T(8,128)(2,1)S(1)} %get-tuple-element.129), channel_id=1, source_target_pairs={{24,0},{1,17},{0,4},{2,6},{3,19}} | collective-permute-start | bytes 786440 | tf_op jit(solution)/shard_map/ppermute | solution.py:48
  2.5 6.7 %collective-permute-start = (bf16[256,512]{1,0:T(8,128)(2,1)S(1)}, bf16[256,512]{1,0:T(8,128)(2,1)S(1)}, u32[]{:S(2)}, u32[]{:S(2)}) collective-permute-start(bf16[256,512]{1,0:T(8,128)(2,1)S(1)} %get-tuple-element.128), channel_id=1, source_target_pairs={{0,20},{8,0},{12,4},{24,16}} | collective-permute-start | bytes 786440 | tf_op jit(solution)/shard_map/ppermute | solution.py:48
  3.8 5.4 %collective-permute-start.1 = (bf16[256,512]{1,0:T(8,128)(2,1)S(1)}, bf16[256,512]{1,0:T(8,128)(2,1)S(1)}, u32[]{:S(2)}, u32[]{:S(2)}) collective-permute-start(bf16[256,512]{1,0:T(8,128)(2,1)S(1)} %get-tuple-element.128), channel_id=1, source_target_pairs={{0,4},{28,20}} | collective-permute-start | bytes 786440 | tf_op jit(solution)/shard_map/ppermute | solution.py:48
  4.5 4.7 %collective-permute-start.2 = (bf16[256,512]{1,0:T(8,128)(2,1)S(1)}, bf16[256,512]{1,0:T(8,128)(2,1)S(1)}, u32[]{:S(2)}, u32[]{:S(2)}) collective-permute-start(bf16[256,512]{1,0:T(8,128)(2,1)S(1)} %get-tuple-element.128), channel_id=1, source_target_pairs={{0,16}} | collective-permute-start | bytes 786440 | tf_op jit(solution)/shard_map/ppermute | solution.py:48
  6.4 2.8 %copy-start = (f32[256,512]{1,0:T(8,128)S(1)}, f32[256,512]{1,0:T(8,128)}, u32[]{:S(2)}) copy-start(f32[256,512]{1,0:T(8,128)} %param.5) | copy-start | bytes 1572868
  6.4 5.6 %collective-permute-start.8 = (bf16[256,512]{1,0:T(8,128)(2,1)S(1)}, bf16[256,512]{1,0:T(8,128)(2,1)S(1)}, u32[]{:S(2)}, u32[]{:S(2)}) collective-permute-start(bf16[256,512]{1,0:T(8,128)(2,1)S(1)} %broadcast_select_fusion.1), channel_id=1, source_target_pairs={{17,21},{0,8},{4,20},{2,18},{6,22},{3,11},{19,27}} | collective-permute-start | bytes 786440 | tf_op jit(solution)/shard_map/ppermute | solution.py:48
  9.3 11.9 %collective-permute-start.6 = (bf16[256,256]{1,0:T(8,128)(2,1)S(1)}, bf16[256,256]{1,0:T(8,128)(2,1)S(1)}, u32[]{:S(2)}, u32[]{:S(2)}) collective-permute-start(bf16[256,256]{1,0:T(8,128)(2,1)S(1)} %get-tuple-element.131), channel_id=1, source_target_pairs={{0,8},{4,12},{16,24},{20,28}} | collective-permute-start | bytes 393224 | tf_op jit(solution)/shard_map/ppermute | solution.py:48
  10.6 3.4 %collective-permute-start.4 = (bf16[256,256]{1,0:T(8,128)(2,1)S(1)}, bf16[256,256]{1,0:T(8,128)(2,1)S(1)}, u32[]{:S(2)}, u32[]{:S(2)}) collective-permute-start(bf16[256,256]{1,0:T(8,128)(2,1)S(1)} %get-tuple-element.145), channel_id=1, source_target_pairs={{0,26},{16,18},{4,14},{20,30}} | collective-permute-start | bytes 393224 | tf_op jit(solution)/shard_map/ppermute | solution.py:48
  11.3 2.7 %collective-permute-start.5 = (bf16[256,256]{1,0:T(8,128)(2,1)S(1)}, bf16[256,256]{1,0:T(8,128)(2,1)S(1)}, u32[]{:S(2)}, u32[]{:S(2)}) collective-permute-start(bf16[256,256]{1,0:T(8,128)(2,1)S(1)} %get-tuple-element.144), channel_id=1, source_target_pairs={{0,10},{4,6},{20,22}} | collective-permute-start | bytes 393224 | tf_op jit(solution)/shard_map/ppermute | solution.py:48
  12.0 11.4 %collective-permute-start.10 = (bf16[256,512]{1,0:T(8,128)(2,1)S(1)}, bf16[256,512]{1,0:T(8,128)(2,1)S(1)}, u32[]{:S(2)}, u32[]{:S(2)}) collective-permute-start(bf16[256,512]{1,0:T(8,128)(2,1)S(1)} %broadcast_select_fusion.2), channel_id=1, source_target_pairs={{17,25},{21,29},{1,5},{4,12},{8,16},{20,28},{2,10},{6,14},{18,26},... | collective-permute-start | bytes 786440 | tf_op jit(solution)/shard_map/ppermute | solution.py:48
  12.7 16.7 %collective-permute-start.9 = (bf16[256,512]{1,0:T(8,128)(2,1)S(1)}, bf16[256,512]{1,0:T(8,128)(2,1)S(1)}, u32[]{:S(2)}, u32[]{:S(2)}) collective-permute-start(bf16[256,512]{1,0:T(8,128)(2,1)S(1)} %broadcast_select_fusion.2), channel_id=1, source_target_pairs={{17,9},{21,13},{8,24}} | collective-permute-start | bytes 786440 | tf_op jit(solution)/shard_map/ppermute | solution.py:48
  21.2 2.3 %collective-permute-start.7 = (bf16[256,256]{1,0:T(8,128)(2,1)S(1)}, bf16[256,256]{1,0:T(8,128)(2,1)S(1)}, u32[]{:S(2)}, u32[]{:S(2)}) collective-permute-start(bf16[256,256]{1,0:T(8,128)(2,1)S(1)} %select_select_fusion.2), channel_id=1, source_target_pairs={{4,5},{6,7},{8,9},{10,11},{12,13},{14,15},{16,17},{18,19},{20,21},... | collective-permute-start | bytes 393224 | tf_op jit(solution)/shard_map/ppermute | solution.py:48

commit v20 on v15

--- a/solution.py
+++ b/solution.py
@@ -58,6 +58,7 @@
         beside_steps.append([(h, h + stride) for h in far])
     beside_steps[-1].append((0, 1))
     beside_back = [(middle + r - 2, r) for r in range(2, middle)]
+    relieved = middle + APART
 
     def among(rows):
         found = jnp.bool_(False)
@@ -80,6 +81,7 @@
                 ((h, c), (h + stride, c))
                 for h in held[kind]
                 for c in range(3 * kind, n_col, 2)
+                if c or h + stride != relieved
             ]
             held[kind] = held[kind] + [h + stride for h in held[kind]]
         got = send(sent, pairs)
@@ -111,19 +113,39 @@
     working = (row_here & APART == 0) & (col_here == 0)
     lower, lower_far = lax.cond(working, compute, none, square, partner)
     received = lower
-    for c in range(0, n_col, 2):
-        got = send(lower_far, [((r, 0), (r + APART, c)) for r in workers])
-        received = jnp.where((row_here & APART != 0) & (col_here == c), got, received)
-    for c in range(2, n_col, 2):
-        got = send(lower, [((r, 0), (r, c)) for r in targets])
-        received = jnp.where((row_here & APART == 0) & (col_here == c), got, received)
+    far = row_here & APART != 0
+    swapped = (row_here == middle) | (row_here == relieved)
+
+    def route(rows, c, own):
+        return [((r, 0), (r if own != (r == middle) else r + APART, c)) for r in rows]
+
+    def send_far(c):
+        sent = jnp.where(row_here == middle, lower, lower_far)
+        return send(sent, route(workers, c, False)), (far != swapped) & (col_here == c)
+
+    def send_own(c):
+        sent = jnp.where(row_here == middle, lower_far, lower)
+        return send(sent, route(targets, c, True)), (~far != swapped) & (col_here == c)
+
+    def send_near(c):
+        pairs = [((r, 0), (r + APART, 0)) for r in workers]
+        return send(lower_far, pairs), far & (col_here == 0)
+
+    even = range(2, n_col, 2)
+    for step, columns in ((send_near, [0]), (send_own, even), (send_far, even)):
+        for c in columns:
+            got, takes = step(c)
+            received = jnp.where(takes, got, received)
     sent = upper
     for step in range(2, len(down)):
         upper = upper_step(upper, step, upper)
     if len(beside_back) > 2:
         sent = upper
-    got = send(sent, [((a, 1), (b, 1)) for a, b in beside_back])
-    upper = jnp.where((col_here == 1) & (row_here > 1) & (row_here < middle), got, upper)
+    pairs = [((a, 1), (b, 1)) for a, b in beside_back] + [((middle + 1, 0), (relieved, 0))]
+    got = send(sent, pairs)
+    takes = (col_here == 1) & (row_here > 1) & (row_here < middle)
+    takes = takes | ((col_here == 0) & (row_here == relieved))
+    upper = jnp.where(takes, got, upper)
     got = send(
         received, [((r, c), (r, c + 1)) for r in range(1, n_row) for c in range(0, n_col, 2)]
     )

time: 26.5 us -> 29 us (1.094)
  the two profiles are of different devices: /device:TPU:21 before, /device:TPU:24 now
where the time goes in v20:
time: 29 us; the launch traced here: 28.7 us
  waiting for transfers between devices  15.6 us (54%)
  starting transfers between devices  10 us (34%)
  other arithmetic  1.29 us (4%)
  matrix products  1.03 us (4%)
  between operations  0.36 us (1%)
  local copies, waits for them, and re-layouts  0.3 us (1%)
    ppermute x11, waiting for transfers between devices, send(): return lax.ppermute(value, ('row', 'col'), flat)  15.6 us
    ppermute x11, starting transfers between devices, send(): return lax.ppermute(value, ('row', 'col'), flat)  10 us
    convert_element_type x1, other arithmetic, blocks(): return (matrix[:, :NB], matrix.astype(jnp.bfloat16))  1.15 us
    dot_general x1, matrix products, shards(): return matrix - jnp.dot(received, upper, preferred_element_type=jnp.float32)  1.03 us
  transfers between devices with their start and end apart: 11, of which 4 were waited for; matrix products, arithmetic and copies ran while one was open for 1% of the time, Pallas kernels for 0%

profile of v20, /device:TPU:24, one launch (start us, length us, event | category | flops | bytes accessed | tf_op | source)
XLA Modules:
  0.0 28.7 jit_solution(14873769852477449256)
XLA Ops:
  0.0 1.2 %conditional.2 = (f32[256,256]{1,0:T(8,128)S(1)}, bf16[256,512]{1,0:T(8,128)(2,1)S(1)}) conditional(s32[]{:T(128)} %convert_element_type.16, () %tuple.22, f32[256,512]{1,0:T(8,128)} %param.5), branch_computations={%region_0.0_spmd, %region_1.0_spmd} | conditional | flops 131072 | bytes 3407916 | solution.py:46
  0.0 0.0 copy-start.1
  0.0 1.1 %convert_element_type.1 = bf16[256,512]{1,0:T(8,128)(2,1)S(1)} convert(f32[256,512]{1,0:T(8,128)} %param.1) | non-fusion elementwise | flops 131072 | bytes 786432 | tf_op jit(solution)/shard_map/cond/branch_1_fun/convert_element_type | solution.py:40
  1.2 0.0 copy-done.1
  1.2 0.7 %collective-permute-start.7 = (bf16[256,512]{1,0:T(8,128)(2,1)S(1)}, bf16[256,512]{1,0:T(8,128)(2,1)S(1)}, u32[]{:S(2)}, u32[]{:S(2)}) collective-permute-start(bf16[256,512]{1,0:T(8,128)(2,1)S(1)} %get-tuple-element.22), channel_id=1, source_target_pairs={{1,17},{0,4},{2,6},{3,19}} | collective-permute-start | bytes 786440 | tf_op jit(solution)/shard_map/ppermute | solution.py:37
  1.9 1.3 %collective-permute-start = (f32[256,256]{1,0:T(8,128)S(1)}, f32[256,256]{1,0:T(8,128)S(1)}, u32[]{:S(2)}, u32[]{:S(2)}) collective-permute-start(f32[256,256]{1,0:T(8,128)S(1)} %get-tuple-element.19), channel_id=1, source_target_pairs={{0,20},{8,0},{12,4},{24,16}} | collective-permute-start | bytes 786440 | tf_op jit(solution)/shard_map/ppermute | solution.py:37
  3.2 0.7 %collective-permute-start.1 = (f32[256,256]{1,0:T(8,128)S(1)}, f32[256,256]{1,0:T(8,128)S(1)}, u32[]{:S(2)}, u32[]{:S(2)}) collective-permute-start(f32[256,256]{1,0:T(8,128)S(1)} %get-tuple-element.19), channel_id=1, source_target_pairs={{0,4},{28,20}} | collective-permute-start | bytes 786440 | tf_op jit(solution)/shard_map/ppermute | solution.py:37
  3.9 0.7 %collective-permute-start.2 = (f32[256,256]{1,0:T(8,128)S(1)}, f32[256,256]{1,0:T(8,128)S(1)}, u32[]{:S(2)}, u32[]{:S(2)}) collective-permute-start(f32[256,256]{1,0:T(8,128)S(1)} %get-tuple-element.19), channel_id=1, source_target_pairs={{0,16}} | collective-permute-start | bytes 786440 | tf_op jit(solution)/shard_map/ppermute | solution.py:37
  4.7 0.0 copy-start
  4.7 0.0 collective-permute-done.7
  4.7 0.8 %collective-permute-start.8 = (bf16[256,512]{1,0:T(8,128)(2,1)S(1)}, bf16[256,512]{1,0:T(8,128)(2,1)S(1)}, u32[]{:S(2)}, u32[]{:S(2)}) collective-permute-start(bf16[256,512]{1,0:T(8,128)(2,1)S(1)} %broadcast_select_fusion.1), channel_id=1, source_target_pairs={{17,21},{0,16},{2,18},{4,20},{6,22},{3,11},{19,27}} | collective-permute-start | bytes 786440 | tf_op jit(solution)/shard_map/ppermute | solution.py:37
  5.6 0.1 copy-done
  5.8 1.3 %collective-permute-done = f32[256,256]{1,0:T(8,128)S(1)} collective-permute-done((f32[256,256]{1,0:T(8,128)S(1)}, f32[256,256]{1,0:T(8,128)S(1)}, u32[]{:S(2)}, u32[]{:S(2)}) %collective-permute-start) | collective-permute-done | bytes 262176 | tf_op jit(solution)/shard_map/ppermute | solution.py:37
  7.1 0.0 collective-permute-done.1
  7.1 0.0 collective-permute-done.2
  7.1 0.1 conditional.3
  7.2 1.3 %collective-permute-start.5 = (bf16[256,256]{1,0:T(8,128)(2,1)S(1)}, bf16[256,256]{1,0:T(8,128)(2,1)S(1)}, u32[]{:S(2)}, u32[]{:S(2)}) collective-permute-start(bf16[256,256]{1,0:T(8,128)(2,1)S(1)} %get-tuple-element.21), channel_id=1, source_target_pairs={{0,8},{4,12},{16,24},{20,28}} | collective-permute-start | bytes 393224 | tf_op jit(solution)/shard_map/ppermute | solution.py:37
  8.5 0.7 %collective-permute-start.3 = (bf16[256,256]{1,0:T(8,128)(2,1)S(1)}, bf16[256,256]{1,0:T(8,128)(2,1)S(1)}, u32[]{:S(2)}, u32[]{:S(2)}) collective-permute-start(bf16[256,256]{1,0:T(8,128)(2,1)S(1)} %get-tuple-element.82), channel_id=1, source_target_pairs={{0,10},{4,14},{16,18},{20,30}} | collective-permute-start | bytes 393224 | tf_op jit(solution)/shard_map/ppermute | solution.py:37
  9.2 0.7 %collective-permute-start.4 = (bf16[256,256]{1,0:T(8,128)(2,1)S(1)}, bf16[256,256]{1,0:T(8,128)(2,1)S(1)}, u32[]{:S(2)}, u32[]{:S(2)}) collective-permute-start(bf16[256,256]{1,0:T(8,128)(2,1)S(1)} %get-tuple-element.81), channel_id=1, source_target_pairs={{20,22},{4,6},{16,26}} | collective-permute-start | bytes 393224 | tf_op jit(solution)/shard_map/ppermute | solution.py:37
  9.9 0.0 collective-permute-done.8
  9.9 0.7 %collective-permute-start.10 = (bf16[256,512]{1,0:T(8,128)(2,1)S(1)}, bf16[256,512]{1,0:T(8,128)(2,1)S(1)}, u32[]{:S(2)}, u32[]{:S(2)}) collective-permute-start(bf16[256,512]{1,0:T(8,128)(2,1)S(1)} %broadcast_select_fusion.2), channel_id=1, source_target_pairs={{17,25},{21,29},{1,5},{0,8},{2,10},{4,12},{6,14},{18,26},{20,28},{... | collective-permute-start | bytes 786440 | tf_op jit(solution)/shard_map/ppermute | solution.py:37
  10.6 1.3 %collective-permute-start.9 = (bf16[256,512]{1,0:T(8,128)(2,1)S(1)}, bf16[256,512]{1,0:T(8,128)(2,1)S(1)}, u32[]{:S(2)}, u32[]{:S(2)}) collective-permute-start(bf16[256,512]{1,0:T(8,128)(2,1)S(1)} %broadcast_select_fusion.2), channel_id=1, source_target_pairs={{17,9},{21,13},{20,24}} | collective-permute-start | bytes 786440 | tf_op jit(solution)/shard_map/ppermute | solution.py:37
  11.9 0.0 collective-permute-done.3
  11.9 0.0 collective-permute-done.4
  11.9 7.7 %collective-permute-done.5 = bf16[256,256]{1,0:T(8,128)(2,1)S(1)} collective-permute-done((bf16[256,256]{1,0:T(8,128)(2,1)S(1)}, bf16[256,256]{1,0:T(8,128)(2,1)S(1)}, u32[]{:S(2)}, u32[]{:S(2)}) %collective-permute-start.5) | collective-permute-done | bytes 131104 | tf_op jit(solution)/shard_map/ppermute | solution.py:37
  19.7 1.3 %collective-permute-start.6 = (bf16[256,256]{1,0:T(8,128)(2,1)S(1)}, bf16[256,256]{1,0:T(8,128)(2,1)S(1)}, u32[]{:S(2)}, u32[]{:S(2)}) collective-permute-start(bf16[256,256]{1,0:T(8,128)(2,1)S(1)} %select_select_fusion.2), channel_id=1, source_target_pairs={{4,5},{6,7},{8,9},{10,11},{12,13},{14,15},{16,17},{18,19},{20,21},... | collective-permute-start | bytes 393224 | tf_op jit(solution)/shard_map/ppermute | solution.py:37
  21.1 0.9 %collective-permute-done.6 = bf16[256,256]{1,0:T(8,128)(2,1)S(1)} collective-permute-done((bf16[256,256]{1,0:T(8,128)(2,1)S(1)}, bf16[256,256]{1,0:T(8,128)(2,1)S(1)}, u32[]{:S(2)}, u32[]{:S(2)}) %collective-permute-start.6) | collective-permute-done | bytes 131104 | tf_op jit(solution)/shard_map/ppermute | solution.py:37
  22.0 0.0 collective-permute-done.10
  22.0 5.7 %collective-permute-done.9 = bf16[256,512]{1,0:T(8,128)(2,1)S(1)} collective-permute-done((bf16[256,512]{1,0:T(8,128)(2,1)S(1)}, bf16[256,512]{1,0:T(8,128)(2,1)S(1)}, u32[]{:S(2)}, u32[]{:S(2)}) %collective-permute-start.9) | collective-permute-done | bytes 262176 | tf_op jit(solution)/shard_map/ppermute | solution.py:37
  27.6 1.0 %convolution_subtract_fusion = f32[256,512]{1,0:T(8,128)} fusion(f32[256,512]{1,0:T(8,128)S(1)} %copy-done, bf16[256,512]{1,0:T(8,128)(2,1)S(1)} %collective-permute-done.9, bf16[256,512]{1,0:T(8,128)(2,1)S(1)} %collective-permute-done.10, bf16[256,512]{1,0:T(8,128)(2,1)S(1)} %broadcast_select_fusion.2, pred[]{:T(512)S(6)} %or.43, pred[]{:T(512)S(6)} %or.35, ...), kind=kOutput, calls=%fused_computation.34 | convolution fusion | flops 67764224 | bytes 2097668 | tf_op jit(solution)/shard_map/dot_general | solution.py:157
  (12 shorter events, 0.2 us)
Async XLA Ops:
  0.0 1.2 %copy-start.1 = (f32[256,512]{1,0:T(8,128)S(1)}, f32[256,512]{1,0:T(8,128)}, u32[]{:S(2)}) copy-start(f32[256,512]{1,0:T(8,128)} %param.1) | copy-start | bytes 1572868 | tf_op jit(solution)/shard_map/cond
  1.2 3.5 %collective-permute-start.7 = (bf16[256,512]{1,0:T(8,128)(2,1)S(1)}, bf16[256,512]{1,0:T(8,128)(2,1)S(1)}, u32[]{:S(2)}, u32[]{:S(2)}) collective-permute-start(bf16[256,512]{1,0:T(8,128)(2,1)S(1)} %get-tuple-element.22), channel_id=1, source_target_pairs={{1,17},{0,4},{2,6},{3,19}} | collective-permute-start | bytes 786440 | tf_op jit(solution)/shard_map/ppermute | solution.py:37
  1.9 5.2 %collective-permute-start = (f32[256,256]{1,0:T(8,128)S(1)}, f32[256,256]{1,0:T(8,128)S(1)}, u32[]{:S(2)}, u32[]{:S(2)}) collective-permute-start(f32[256,256]{1,0:T(8,128)S(1)} %get-tuple-element.19), channel_id=1, source_target_pairs={{0,20},{8,0},{12,4},{24,16}} | collective-permute-start | bytes 786440 | tf_op jit(solution)/shard_map/ppermute | solution.py:37
  3.2 3.9 %collective-permute-start.1 = (f32[256,256]{1,0:T(8,128)S(1)}, f32[256,256]{1,0:T(8,128)S(1)}, u32[]{:S(2)}, u32[]{:S(2)}) collective-permute-start(f32[256,256]{1,0:T(8,128)S(1)} %get-tuple-element.19), channel_id=1, source_target_pairs={{0,4},{28,20}} | collective-permute-start | bytes 786440 | tf_op jit(solution)/shard_map/ppermute | solution.py:37
  3.9 3.2 %collective-permute-start.2 = (f32[256,256]{1,0:T(8,128)S(1)}, f32[256,256]{1,0:T(8,128)S(1)}, u32[]{:S(2)}, u32[]{:S(2)}) collective-permute-start(f32[256,256]{1,0:T(8,128)S(1)} %get-tuple-element.19), channel_id=1, source_target_pairs={{0,16}} | collective-permute-start | bytes 786440 | tf_op jit(solution)/shard_map/ppermute | solution.py:37
  4.7 1.0 %copy-start = (f32[256,512]{1,0:T(8,128)S(1)}, f32[256,512]{1,0:T(8,128)}, u32[]{:S(2)}) copy-start(f32[256,512]{1,0:T(8,128)} %param.5) | copy-start | bytes 1572868
  4.7 5.2 %collective-permute-start.8 = (bf16[256,512]{1,0:T(8,128)(2,1)S(1)}, bf16[256,512]{1,0:T(8,128)(2,1)S(1)}, u32[]{:S(2)}, u32[]{:S(2)}) collective-permute-start(bf16[256,512]{1,0:T(8,128)(2,1)S(1)} %broadcast_select_fusion.1), channel_id=1, source_target_pairs={{17,21},{0,16},{2,18},{4,20},{6,22},{3,11},{19,27}} | collective-permute-start | bytes 786440 | tf_op jit(solution)/shard_map/ppermute | solution.py:37
  7.2 12.5 %collective-permute-start.5 = (bf16[256,256]{1,0:T(8,128)(2,1)S(1)}, bf16[256,256]{1,0:T(8,128)(2,1)S(1)}, u32[]{:S(2)}, u32[]{:S(2)}) collective-permute-start(bf16[256,256]{1,0:T(8,128)(2,1)S(1)} %get-tuple-element.21), channel_id=1, source_target_pairs={{0,8},{4,12},{16,24},{20,28}} | collective-permute-start | bytes 393224 | tf_op jit(solution)/shard_map/ppermute | solution.py:37
  8.5 3.4 %collective-permute-start.3 = (bf16[256,256]{1,0:T(8,128)(2,1)S(1)}, bf16[256,256]{1,0:T(8,128)(2,1)S(1)}, u32[]{:S(2)}, u32[]{:S(2)}) collective-permute-start(bf16[256,256]{1,0:T(8,128)(2,1)S(1)} %get-tuple-element.82), channel_id=1, source_target_pairs={{0,10},{4,14},{16,18},{20,30}} | collective-permute-start | bytes 393224 | tf_op jit(solution)/shard_map/ppermute | solution.py:37
  9.2 2.7 %collective-permute-start.4 = (bf16[256,256]{1,0:T(8,128)(2,1)S(1)}, bf16[256,256]{1,0:T(8,128)(2,1)S(1)}, u32[]{:S(2)}, u32[]{:S(2)}) collective-permute-start(bf16[256,256]{1,0:T(8,128)(2,1)S(1)} %get-tuple-element.81), channel_id=1, source_target_pairs={{20,22},{4,6},{16,26}} | collective-permute-start | bytes 393224 | tf_op jit(solution)/shard_map/ppermute | solution.py:37
  9.9 12.0 %collective-permute-start.10 = (bf16[256,512]{1,0:T(8,128)(2,1)S(1)}, bf16[256,512]{1,0:T(8,128)(2,1)S(1)}, u32[]{:S(2)}, u32[]{:S(2)}) collective-permute-start(bf16[256,512]{1,0:T(8,128)(2,1)S(1)} %broadcast_select_fusion.2), channel_id=1, source_target_pairs={{17,25},{21,29},{1,5},{0,8},{2,10},{4,12},{6,14},{18,26},{20,28},{... | collective-permute-start | bytes 786440 | tf_op jit(solution)/shard_map/ppermute | solution.py:37
  10.6 17.0 %collective-permute-start.9 = (bf16[256,512]{1,0:T(8,128)(2,1)S(1)}, bf16[256,512]{1,0:T(8,128)(2,1)S(1)}, u32[]{:S(2)}, u32[]{:S(2)}) collective-permute-start(bf16[256,512]{1,0:T(8,128)(2,1)S(1)} %broadcast_select_fusion.2), channel_id=1, source_target_pairs={{17,9},{21,13},{20,24}} | collective-permute-start | bytes 786440 | tf_op jit(solution)/shard_map/ppermute | solution.py:37
  19.7 2.3 %collective-permute-start.6 = (bf16[256,256]{1,0:T(8,128)(2,1)S(1)}, bf16[256,256]{1,0:T(8,128)(2,1)S(1)}, u32[]{:S(2)}, u32[]{:S(2)}) collective-permute-start(bf16[256,256]{1,0:T(8,128)(2,1)S(1)} %select_select_fusion.2), channel_id=1, source_target_pairs={{4,5},{6,7},{8,9},{10,11},{12,13},{14,15},{16,17},{18,19},{20,21},... | collective-permute-start | bytes 393224 | tf_op jit(solution)/shard_map/ppermute | solution.py:37

commit v21 on v20

--- a/solution.py
+++ b/solution.py
@@ -58,7 +58,6 @@
         beside_steps.append([(h, h + stride) for h in far])
     beside_steps[-1].append((0, 1))
     beside_back = [(middle + r - 2, r) for r in range(2, middle)]
-    relieved = middle + APART
 
     def among(rows):
         found = jnp.bool_(False)
@@ -81,7 +80,6 @@
                 ((h, c), (h + stride, c))
                 for h in held[kind]
                 for c in range(3 * kind, n_col, 2)
-                if c or h + stride != relieved
             ]
             held[kind] = held[kind] + [h + stride for h in held[kind]]
         got = send(sent, pairs)
@@ -114,7 +112,7 @@
     lower, lower_far = lax.cond(working, compute, none, square, partner)
     received = lower
     far = row_here & APART != 0
-    swapped = (row_here == middle) | (row_here == relieved)
+    swapped = (row_here == middle) | (row_here == middle + APART)
 
     def route(rows, c, own):
         return [((r, 0), (r if own != (r == middle) else r + APART, c)) for r in rows]
@@ -141,11 +139,8 @@
         upper = upper_step(upper, step, upper)
     if len(beside_back) > 2:
         sent = upper
-    pairs = [((a, 1), (b, 1)) for a, b in beside_back] + [((middle + 1, 0), (relieved, 0))]
-    got = send(sent, pairs)
-    takes = (col_here == 1) & (row_here > 1) & (row_here < middle)
-    takes = takes | ((col_here == 0) & (row_here == relieved))
-    upper = jnp.where(takes, got, upper)
+    got = send(sent, [((a, 1), (b, 1)) for a, b in beside_back])
+    upper = jnp.where((col_here == 1) & (row_here > 1) & (row_here < middle), got, upper)
     got = send(
         received, [((r, c), (r, c + 1)) for r in range(1, n_row) for c in range(0, n_col, 2)]
     )

time: 29 us -> 26.5 us (0.914)
  waiting for transfers between devices: 15.6 us -> 13.1 us
    ppermute x11, waiting for transfers between devices: 15.6 us -> 13.1 us  [send(): return lax.ppermute(value, ('row', 'col'), flat)]
where the time goes in v21:
time: 26.5 us; the launch traced here: 26.1 us
  waiting for transfers between devices  13.1 us (49%)
  starting transfers between devices  10 us (38%)
  other arithmetic  1.29 us (5%)
  matrix products  1.04 us (4%)
  between operations  0.36 us (1%)
  local copies, waits for them, and re-layouts  0.3 us (1%)
    ppermute x11, waiting for transfers between devices, send(): return lax.ppermute(value, ('row', 'col'), flat)  13.1 us
    ppermute x11, starting transfers between devices, send(): return lax.ppermute(value, ('row', 'col'), flat)  10 us
    convert_element_type x1, other arithmetic, blocks(): return (matrix[:, :NB], matrix.astype(jnp.bfloat16))  1.15 us
    dot_general x1, matrix products, shards(): return matrix - jnp.dot(received, upper, preferred_element_type=jnp.float32)  1.04 us
  transfers between devices with their start and end apart: 11, of which 4 were waited for; matrix products, arithmetic and copies ran while one was open for 1% of the time, Pallas kernels for 0%

profile of v21, /device:TPU:24, one launch (start us, length us, event | category | flops | bytes accessed | tf_op | source)
XLA Modules:
  0.0 26.1 jit_solution(2849875042047854537)
XLA Ops:
  0.0 1.2 %conditional.2 = (f32[256,256]{1,0:T(8,128)S(1)}, bf16[256,512]{1,0:T(8,128)(2,1)S(1)}) conditional(s32[]{:T(128)} %convert_element_type.16, () %tuple.22, f32[256,512]{1,0:T(8,128)} %param.5), branch_computations={%region_0.0_spmd, %region_1.0_spmd} | conditional | flops 131072 | bytes 3407916 | solution.py:46
  0.0 0.0 copy-start.1
  0.0 1.1 %convert_element_type.1 = bf16[256,512]{1,0:T(8,128)(2,1)S(1)} convert(f32[256,512]{1,0:T(8,128)} %param.1) | non-fusion elementwise | flops 131072 | bytes 786432 | tf_op jit(solution)/shard_map/cond/branch_1_fun/convert_element_type | solution.py:40
  1.2 0.0 copy-done.1
  1.2 0.7 %collective-permute-start.7 = (bf16[256,512]{1,0:T(8,128)(2,1)S(1)}, bf16[256,512]{1,0:T(8,128)(2,1)S(1)}, u32[]{:S(2)}, u32[]{:S(2)}) collective-permute-start(bf16[256,512]{1,0:T(8,128)(2,1)S(1)} %get-tuple-element.22), channel_id=1, source_target_pairs={{1,17},{0,4},{2,6},{3,19}} | collective-permute-start | bytes 786440 | tf_op jit(solution)/shard_map/ppermute | solution.py:37
  1.9 1.3 %collective-permute-start = (f32[256,256]{1,0:T(8,128)S(1)}, f32[256,256]{1,0:T(8,128)S(1)}, u32[]{:S(2)}, u32[]{:S(2)}) collective-permute-start(f32[256,256]{1,0:T(8,128)S(1)} %get-tuple-element.19), channel_id=1, source_target_pairs={{0,20},{8,0},{12,4},{24,16}} | collective-permute-start | bytes 786440 | tf_op jit(solution)/shard_map/ppermute | solution.py:37
  3.2 0.7 %collective-permute-start.1 = (f32[256,256]{1,0:T(8,128)S(1)}, f32[256,256]{1,0:T(8,128)S(1)}, u32[]{:S(2)}, u32[]{:S(2)}) collective-permute-start(f32[256,256]{1,0:T(8,128)S(1)} %get-tuple-element.19), channel_id=1, source_target_pairs={{0,4},{28,20}} | collective-permute-start | bytes 786440 | tf_op jit(solution)/shard_map/ppermute | solution.py:37
  3.9 0.7 %collective-permute-start.2 = (f32[256,256]{1,0:T(8,128)S(1)}, f32[256,256]{1,0:T(8,128)S(1)}, u32[]{:S(2)}, u32[]{:S(2)}) collective-permute-start(f32[256,256]{1,0:T(8,128)S(1)} %get-tuple-element.19), channel_id=1, source_target_pairs={{0,16}} | collective-permute-start | bytes 786440 | tf_op jit(solution)/shard_map/ppermute | solution.py:37
  4.7 0.0 copy-start
  4.7 0.0 collective-permute-done.7
  4.7 0.8 %collective-permute-start.8 = (bf16[256,512]{1,0:T(8,128)(2,1)S(1)}, bf16[256,512]{1,0:T(8,128)(2,1)S(1)}, u32[]{:S(2)}, u32[]{:S(2)}) collective-permute-start(bf16[256,512]{1,0:T(8,128)(2,1)S(1)} %broadcast_select_fusion.1), channel_id=1, source_target_pairs={{17,21},{0,16},{2,18},{4,20},{6,22},{3,11},{19,27}} | collective-permute-start | bytes 786440 | tf_op jit(solution)/shard_map/ppermute | solution.py:37
  5.6 0.1 copy-done
  5.8 1.3 %collective-permute-done = f32[256,256]{1,0:T(8,128)S(1)} collective-permute-done((f32[256,256]{1,0:T(8,128)S(1)}, f32[256,256]{1,0:T(8,128)S(1)}, u32[]{:S(2)}, u32[]{:S(2)}) %collective-permute-start) | collective-permute-done | bytes 262176 | tf_op jit(solution)/shard_map/ppermute | solution.py:37
  7.1 0.0 collective-permute-done.1
  7.1 0.0 collective-permute-done.2
  7.1 0.1 conditional.3
  7.2 1.3 %collective-permute-start.5 = (bf16[256,256]{1,0:T(8,128)(2,1)S(1)}, bf16[256,256]{1,0:T(8,128)(2,1)S(1)}, u32[]{:S(2)}, u32[]{:S(2)}) collective-permute-start(bf16[256,256]{1,0:T(8,128)(2,1)S(1)} %get-tuple-element.21), channel_id=1, source_target_pairs={{0,8},{4,12},{16,24},{20,28}} | collective-permute-start | bytes 393224 | tf_op jit(solution)/shard_map/ppermute | solution.py:37
  8.5 0.7 %collective-permute-start.3 = (bf16[256,256]{1,0:T(8,128)(2,1)S(1)}, bf16[256,256]{1,0:T(8,128)(2,1)S(1)}, u32[]{:S(2)}, u32[]{:S(2)}) collective-permute-start(bf16[256,256]{1,0:T(8,128)(2,1)S(1)} %get-tuple-element.82), channel_id=1, source_target_pairs={{0,10},{4,14},{16,18},{20,30}} | collective-permute-start | bytes 393224 | tf_op jit(solution)/shard_map/ppermute | solution.py:37
  9.2 0.7 %collective-permute-start.4 = (bf16[256,256]{1,0:T(8,128)(2,1)S(1)}, bf16[256,256]{1,0:T(8,128)(2,1)S(1)}, u32[]{:S(2)}, u32[]{:S(2)}) collective-permute-start(bf16[256,256]{1,0:T(8,128)(2,1)S(1)} %get-tuple-element.81), channel_id=1, source_target_pairs={{20,22},{4,6},{16,26}} | collective-permute-start | bytes 393224 | tf_op jit(solution)/shard_map/ppermute | solution.py:37
  9.9 0.0 collective-permute-done.8
  9.9 1.3 %collective-permute-start.10 = (bf16[256,512]{1,0:T(8,128)(2,1)S(1)}, bf16[256,512]{1,0:T(8,128)(2,1)S(1)}, u32[]{:S(2)}, u32[]{:S(2)}) collective-permute-start(bf16[256,512]{1,0:T(8,128)(2,1)S(1)} %broadcast_select_fusion.2), channel_id=1, source_target_pairs={{17,25},{21,29},{1,5},{0,8},{2,10},{4,12},{6,14},{16,24},{18,26},{... | collective-permute-start | bytes 786440 | tf_op jit(solution)/shard_map/ppermute | solution.py:37
  11.2 0.7 %collective-permute-start.9 = (bf16[256,512]{1,0:T(8,128)(2,1)S(1)}, bf16[256,512]{1,0:T(8,128)(2,1)S(1)}, u32[]{:S(2)}, u32[]{:S(2)}) collective-permute-start(bf16[256,512]{1,0:T(8,128)(2,1)S(1)} %broadcast_select_fusion.2), channel_id=1, source_target_pairs={{17,9},{21,13}} | collective-permute-start | bytes 786440 | tf_op jit(solution)/shard_map/ppermute | solution.py:37
  11.9 0.0 collective-permute-done.3
  11.9 0.0 collective-permute-done.4
  11.9 7.7 %collective-permute-done.5 = bf16[256,256]{1,0:T(8,128)(2,1)S(1)} collective-permute-done((bf16[256,256]{1,0:T(8,128)(2,1)S(1)}, bf16[256,256]{1,0:T(8,128)(2,1)S(1)}, u32[]{:S(2)}, u32[]{:S(2)}) %collective-permute-start.5) | collective-permute-done | bytes 131104 | tf_op jit(solution)/shard_map/ppermute | solution.py:37
  19.7 1.3 %collective-permute-start.6 = (bf16[256,256]{1,0:T(8,128)(2,1)S(1)}, bf16[256,256]{1,0:T(8,128)(2,1)S(1)}, u32[]{:S(2)}, u32[]{:S(2)}) collective-permute-start(bf16[256,256]{1,0:T(8,128)(2,1)S(1)} %select_select_fusion.2), channel_id=1, source_target_pairs={{4,5},{6,7},{8,9},{10,11},{12,13},{14,15},{16,17},{18,19},{20,21},... | collective-permute-start | bytes 393224 | tf_op jit(solution)/shard_map/ppermute | solution.py:37
  21.1 0.9 %collective-permute-done.6 = bf16[256,256]{1,0:T(8,128)(2,1)S(1)} collective-permute-done((bf16[256,256]{1,0:T(8,128)(2,1)S(1)}, bf16[256,256]{1,0:T(8,128)(2,1)S(1)}, u32[]{:S(2)}, u32[]{:S(2)}) %collective-permute-start.6) | collective-permute-done | bytes 131104 | tf_op jit(solution)/shard_map/ppermute | solution.py:37
  22.0 3.2 %collective-permute-done.10 = bf16[256,512]{1,0:T(8,128)(2,1)S(1)} collective-permute-done((bf16[256,512]{1,0:T(8,128)(2,1)S(1)}, bf16[256,512]{1,0:T(8,128)(2,1)S(1)}, u32[]{:S(2)}, u32[]{:S(2)}) %collective-permute-start.10) | collective-permute-done | bytes 262176 | tf_op jit(solution)/shard_map/ppermute | solution.py:37
  25.1 0.0 collective-permute-done.9
  25.1 1.0 %convolution_subtract_fusion = f32[256,512]{1,0:T(8,128)} fusion(f32[256,512]{1,0:T(8,128)S(1)} %copy-done, bf16[256,512]{1,0:T(8,128)(2,1)S(1)} %collective-permute-done.9, bf16[256,512]{1,0:T(8,128)(2,1)S(1)} %collective-permute-done.10, bf16[256,512]{1,0:T(8,128)(2,1)S(1)} %broadcast_select_fusion.2, pred[]{:T(512)S(6)} %or.39, pred[]{:T(512)S(6)} %and.95, ...), kind=kOutput, calls=%fused_computation.34 | convolution fusion | flops 67764224 | bytes 2097668 | tf_op jit(solution)/shard_map/dot_general | solution.py:152
  (12 shorter events, 0.2 us)
Async XLA Ops:
  0.0 1.2 %copy-start.1 = (f32[256,512]{1,0:T(8,128)S(1)}, f32[256,512]{1,0:T(8,128)}, u32[]{:S(2)}) copy-start(f32[256,512]{1,0:T(8,128)} %param.1) | copy-start | bytes 1572868 | tf_op jit(solution)/shard_map/cond
  1.2 3.5 %collective-permute-start.7 = (bf16[256,512]{1,0:T(8,128)(2,1)S(1)}, bf16[256,512]{1,0:T(8,128)(2,1)S(1)}, u32[]{:S(2)}, u32[]{:S(2)}) collective-permute-start(bf16[256,512]{1,0:T(8,128)(2,1)S(1)} %get-tuple-element.22), channel_id=1, source_target_pairs={{1,17},{0,4},{2,6},{3,19}} | collective-permute-start | bytes 786440 | tf_op jit(solution)/shard_map/ppermute | solution.py:37
  1.9 5.2 %collective-permute-start = (f32[256,256]{1,0:T(8,128)S(1)}, f32[256,256]{1,0:T(8,128)S(1)}, u32[]{:S(2)}, u32[]{:S(2)}) collective-permute-start(f32[256,256]{1,0:T(8,128)S(1)} %get-tuple-element.19), channel_id=1, source_target_pairs={{0,20},{8,0},{12,4},{24,16}} | collective-permute-start | bytes 786440 | tf_op jit(solution)/shard_map/ppermute | solution.py:37
  3.2 3.9 %collective-permute-start.1 = (f32[256,256]{1,0:T(8,128)S(1)}, f32[256,256]{1,0:T(8,128)S(1)}, u32[]{:S(2)}, u32[]{:S(2)}) collective-permute-start(f32[256,256]{1,0:T(8,128)S(1)} %get-tuple-element.19), channel_id=1, source_target_pairs={{0,4},{28,20}} | collective-permute-start | bytes 786440 | tf_op jit(solution)/shard_map/ppermute | solution.py:37
  3.9 3.2 %collective-permute-start.2 = (f32[256,256]{1,0:T(8,128)S(1)}, f32[256,256]{1,0:T(8,128)S(1)}, u32[]{:S(2)}, u32[]{:S(2)}) collective-permute-start(f32[256,256]{1,0:T(8,128)S(1)} %get-tuple-element.19), channel_id=1, source_target_pairs={{0,16}} | collective-permute-start | bytes 786440 | tf_op jit(solution)/shard_map/ppermute | solution.py:37
  4.7 1.0 %copy-start = (f32[256,512]{1,0:T(8,128)S(1)}, f32[256,512]{1,0:T(8,128)}, u32[]{:S(2)}) copy-start(f32[256,512]{1,0:T(8,128)} %param.5) | copy-start | bytes 1572868
  4.7 5.2 %collective-permute-start.8 = (bf16[256,512]{1,0:T(8,128)(2,1)S(1)}, bf16[256,512]{1,0:T(8,128)(2,1)S(1)}, u32[]{:S(2)}, u32[]{:S(2)}) collective-permute-start(bf16[256,512]{1,0:T(8,128)(2,1)S(1)} %broadcast_select_fusion.1), channel_id=1, source_target_pairs={{17,21},{0,16},{2,18},{4,20},{6,22},{3,11},{19,27}} | collective-permute-start | bytes 786440 | tf_op jit(solution)/shard_map/ppermute | solution.py:37
  7.2 12.5 %collective-permute-start.5 = (bf16[256,256]{1,0:T(8,128)(2,1)S(1)}, bf16[256,256]{1,0:T(8,128)(2,1)S(1)}, u32[]{:S(2)}, u32[]{:S(2)}) collective-permute-start(bf16[256,256]{1,0:T(8,128)(2,1)S(1)} %get-tuple-element.21), channel_id=1, source_target_pairs={{0,8},{4,12},{16,24},{20,28}} | collective-permute-start | bytes 393224 | tf_op jit(solution)/shard_map/ppermute | solution.py:37
  8.5 3.4 %collective-permute-start.3 = (bf16[256,256]{1,0:T(8,128)(2,1)S(1)}, bf16[256,256]{1,0:T(8,128)(2,1)S(1)}, u32[]{:S(2)}, u32[]{:S(2)}) collective-permute-start(bf16[256,256]{1,0:T(8,128)(2,1)S(1)} %get-tuple-element.82), channel_id=1, source_target_pairs={{0,10},{4,14},{16,18},{20,30}} | collective-permute-start | bytes 393224 | tf_op jit(solution)/shard_map/ppermute | solution.py:37
  9.2 2.7 %collective-permute-start.4 = (bf16[256,256]{1,0:T(8,128)(2,1)S(1)}, bf16[256,256]{1,0:T(8,128)(2,1)S(1)}, u32[]{:S(2)}, u32[]{:S(2)}) collective-permute-start(bf16[256,256]{1,0:T(8,128)(2,1)S(1)} %get-tuple-element.81), channel_id=1, source_target_pairs={{20,22},{4,6},{16,26}} | collective-permute-start | bytes 393224 | tf_op jit(solution)/shard_map/ppermute | solution.py:37
  9.9 15.2 %collective-permute-start.10 = (bf16[256,512]{1,0:T(8,128)(2,1)S(1)}, bf16[256,512]{1,0:T(8,128)(2,1)S(1)}, u32[]{:S(2)}, u32[]{:S(2)}) collective-permute-start(bf16[256,512]{1,0:T(8,128)(2,1)S(1)} %broadcast_select_fusion.2), channel_id=1, source_target_pairs={{17,25},{21,29},{1,5},{0,8},{2,10},{4,12},{6,14},{16,24},{18,26},{... | collective-permute-start | bytes 786440 | tf_op jit(solution)/shard_map/ppermute | solution.py:37
  11.2 13.9 %collective-permute-start.9 = (bf16[256,512]{1,0:T(8,128)(2,1)S(1)}, bf16[256,512]{1,0:T(8,128)(2,1)S(1)}, u32[]{:S(2)}, u32[]{:S(2)}) collective-permute-start(bf16[256,512]{1,0:T(8,128)(2,1)S(1)} %broadcast_select_fusion.2), channel_id=1, source_target_pairs={{17,9},{21,13}} | collective-permute-start | bytes 786440 | tf_op jit(solution)/shard_map/ppermute | solution.py:37
  19.7 2.3 %collective-permute-start.6 = (bf16[256,256]{1,0:T(8,128)(2,1)S(1)}, bf16[256,256]{1,0:T(8,128)(2,1)S(1)}, u32[]{:S(2)}, u32[]{:S(2)}) collective-permute-start(bf16[256,256]{1,0:T(8,128)(2,1)S(1)} %select_select_fusion.2), channel_id=1, source_target_pairs={{4,5},{6,7},{8,9},{10,11},{12,13},{14,15},{16,17},{18,19},{20,21},... | collective-permute-start | bytes 393224 | tf_op jit(solution)/shard_map/ppermute | solution.py:37

commit v22 on v21

--- a/solution.py
+++ b/solution.py
@@ -86,7 +86,7 @@
         return jnp.where(takes, got, value)
 
     workers = [r for r in range(n_row) if r & APART == 0]
-    targets = workers[:1:-1]
+    targets = workers[2:]
     targets.insert(1, 1)
     square, partner = matrix[:, :NB], matrix[:, :NB]
     upper = upper_step(upper, 0, first_upper)
@@ -112,17 +112,18 @@
     lower, lower_far = lax.cond(working, compute, none, square, partner)
     received = lower
     far = row_here & APART != 0
-    swapped = (row_here == middle) | (row_here == middle + APART)
+    late = middle + 1
+    swapped = (row_here == late) | (row_here == late + APART)
 
     def route(rows, c, own):
-        return [((r, 0), (r if own != (r == middle) else r + APART, c)) for r in rows]
+        return [((r, 0), (r if own != (r == late) else r + APART, c)) for r in rows]
 
     def send_far(c):
-        sent = jnp.where(row_here == middle, lower, lower_far)
+        sent = jnp.where(row_here == late, lower, lower_far)
         return send(sent, route(workers, c, False)), (far != swapped) & (col_here == c)
 
     def send_own(c):
-        sent = jnp.where(row_here == middle, lower_far, lower)
+        sent = jnp.where(row_here == late, lower_far, lower)
         return send(sent, route(targets, c, True)), (~far != swapped) & (col_here == c)
 
     def send_near(c):

time: 26.5 us -> 28.1 us (1.060)
  the two profiles are of different devices: /device:TPU:24 before, /device:TPU:26 now
where the time goes in v22:
time: 28.1 us; the launch traced here: 27.8 us
  waiting for transfers between devices  14.7 us (52%)
  starting transfers between devices  10 us (36%)
  other arithmetic  1.29 us (5%)
  matrix products  1.03 us (4%)
  between operations  0.36 us (1%)
  local copies, waits for them, and re-layouts  0.3 us (1%)
    ppermute x11, waiting for transfers between devices, send(): return lax.ppermute(value, ('row', 'col'), flat)  14.7 us
    ppermute x11, starting transfers between devices, send(): return lax.ppermute(value, ('row', 'col'), flat)  10 us
    convert_element_type x1, other arithmetic, blocks(): return (matrix[:, :NB], matrix.astype(jnp.bfloat16))  1.15 us
    dot_general x1, matrix products, shards(): return matrix - jnp.dot(received, upper, preferred_element_type=jnp.float32)  1.03 us
  transfers between devices with their start and end apart: 11, of which 4 were waited for; matrix products, arithmetic and copies ran while one was open for 1% of the time, Pallas kernels for 0%

profile of v22, /device:TPU:26, one launch (start us, length us, event | category | flops | bytes accessed | tf_op | source)
XLA Modules:
  0.0 27.8 jit_solution(10146372735439977323)
XLA Ops:
  0.0 1.2 %conditional.2 = (f32[256,256]{1,0:T(8,128)S(1)}, bf16[256,512]{1,0:T(8,128)(2,1)S(1)}) conditional(s32[]{:T(128)} %convert_element_type.16, () %tuple.22, f32[256,512]{1,0:T(8,128)} %param.5), branch_computations={%region_0.0_spmd, %region_1.0_spmd} | conditional | flops 131072 | bytes 3407916 | solution.py:46
  0.0 0.0 copy-start.1
  0.0 1.1 %convert_element_type.1 = bf16[256,512]{1,0:T(8,128)(2,1)S(1)} convert(f32[256,512]{1,0:T(8,128)} %param.1) | non-fusion elementwise | flops 131072 | bytes 786432 | tf_op jit(solution)/shard_map/cond/branch_1_fun/convert_element_type | solution.py:40
  1.2 0.0 copy-done.1
  1.2 0.7 %collective-permute-start.7 = (bf16[256,512]{1,0:T(8,128)(2,1)S(1)}, bf16[256,512]{1,0:T(8,128)(2,1)S(1)}, u32[]{:S(2)}, u32[]{:S(2)}) collective-permute-start(bf16[256,512]{1,0:T(8,128)(2,1)S(1)} %get-tuple-element.22), channel_id=1, source_target_pairs={{1,17},{0,4},{2,6},{3,19}} | collective-permute-start | bytes 786440 | tf_op jit(solution)/shard_map/ppermute | solution.py:37
  1.9 1.3 %collective-permute-start = (f32[256,256]{1,0:T(8,128)S(1)}, f32[256,256]{1,0:T(8,128)S(1)}, u32[]{:S(2)}, u32[]{:S(2)}) collective-permute-start(f32[256,256]{1,0:T(8,128)S(1)} %get-tuple-element.19), channel_id=1, source_target_pairs={{0,16},{8,0},{12,4},{28,20}} | collective-permute-start | bytes 786440 | tf_op jit(solution)/shard_map/ppermute | solution.py:37
  3.2 0.7 %collective-permute-start.1 = (f32[256,256]{1,0:T(8,128)S(1)}, f32[256,256]{1,0:T(8,128)S(1)}, u32[]{:S(2)}, u32[]{:S(2)}) collective-permute-start(f32[256,256]{1,0:T(8,128)S(1)} %get-tuple-element.19), channel_id=1, source_target_pairs={{0,4},{24,16}} | collective-permute-start | bytes 786440 | tf_op jit(solution)/shard_map/ppermute | solution.py:37
  3.9 0.7 %collective-permute-start.2 = (f32[256,256]{1,0:T(8,128)S(1)}, f32[256,256]{1,0:T(8,128)S(1)}, u32[]{:S(2)}, u32[]{:S(2)}) collective-permute-start(f32[256,256]{1,0:T(8,128)S(1)} %get-tuple-element.19), channel_id=1, source_target_pairs={{0,20}} | collective-permute-start | bytes 786440 | tf_op jit(solution)/shard_map/ppermute | solution.py:37
  4.7 0.0 copy-start
  4.7 0.0 collective-permute-done.7
  4.7 0.8 %collective-permute-start.8 = (bf16[256,512]{1,0:T(8,128)(2,1)S(1)}, bf16[256,512]{1,0:T(8,128)(2,1)S(1)}, u32[]{:S(2)}, u32[]{:S(2)}) collective-permute-start(bf16[256,512]{1,0:T(8,128)(2,1)S(1)} %broadcast_select_fusion.1), channel_id=1, source_target_pairs={{17,21},{0,16},{2,18},{4,20},{6,22},{3,11},{19,27}} | collective-permute-start | bytes 786440 | tf_op jit(solution)/shard_map/ppermute | solution.py:37
  5.6 0.1 copy-done
  5.8 1.3 %collective-permute-done = f32[256,256]{1,0:T(8,128)S(1)} collective-permute-done((f32[256,256]{1,0:T(8,128)S(1)}, f32[256,256]{1,0:T(8,128)S(1)}, u32[]{:S(2)}, u32[]{:S(2)}) %collective-permute-start) | collective-permute-done | bytes 262176 | tf_op jit(solution)/shard_map/ppermute | solution.py:37
  7.1 0.0 collective-permute-done.1
  7.1 0.0 collective-permute-done.2
  7.1 0.1 conditional.3
  7.2 1.3 %collective-permute-start.5 = (bf16[256,256]{1,0:T(8,128)(2,1)S(1)}, bf16[256,256]{1,0:T(8,128)(2,1)S(1)}, u32[]{:S(2)}, u32[]{:S(2)}) collective-permute-start(bf16[256,256]{1,0:T(8,128)(2,1)S(1)} %get-tuple-element.21), channel_id=1, source_target_pairs={{0,8},{4,12},{16,24},{20,28}} | collective-permute-start | bytes 393224 | tf_op jit(solution)/shard_map/ppermute | solution.py:37
  8.5 0.7 %collective-permute-start.3 = (bf16[256,256]{1,0:T(8,128)(2,1)S(1)}, bf16[256,256]{1,0:T(8,128)(2,1)S(1)}, u32[]{:S(2)}, u32[]{:S(2)}) collective-permute-start(bf16[256,256]{1,0:T(8,128)(2,1)S(1)} %get-tuple-element.82), channel_id=1, source_target_pairs={{0,10},{4,14},{16,26},{20,22}} | collective-permute-start | bytes 393224 | tf_op jit(solution)/shard_map/ppermute | solution.py:37
  9.2 0.7 %collective-permute-start.4 = (bf16[256,256]{1,0:T(8,128)(2,1)S(1)}, bf16[256,256]{1,0:T(8,128)(2,1)S(1)}, u32[]{:S(2)}, u32[]{:S(2)}) collective-permute-start(bf16[256,256]{1,0:T(8,128)(2,1)S(1)} %get-tuple-element.81), channel_id=1, source_target_pairs={{16,18},{4,6},{20,30}} | collective-permute-start | bytes 393224 | tf_op jit(solution)/shard_map/ppermute | solution.py:37
  9.9 0.0 collective-permute-done.8
  9.9 1.3 %collective-permute-start.10 = (bf16[256,512]{1,0:T(8,128)(2,1)S(1)}, bf16[256,512]{1,0:T(8,128)(2,1)S(1)}, u32[]{:S(2)}, u32[]{:S(2)}) collective-permute-start(bf16[256,512]{1,0:T(8,128)(2,1)S(1)} %broadcast_select_fusion.2), channel_id=1, source_target_pairs={{17,25},{21,29},{1,5},{0,8},{2,10},{4,12},{6,14},{16,24},{18,26},{... | collective-permute-start | bytes 786440 | tf_op jit(solution)/shard_map/ppermute | solution.py:37
  11.2 0.7 %collective-permute-start.9 = (bf16[256,512]{1,0:T(8,128)(2,1)S(1)}, bf16[256,512]{1,0:T(8,128)(2,1)S(1)}, u32[]{:S(2)}, u32[]{:S(2)}) collective-permute-start(bf16[256,512]{1,0:T(8,128)(2,1)S(1)} %broadcast_select_fusion.2), channel_id=1, source_target_pairs={{17,9},{21,13}} | collective-permute-start | bytes 786440 | tf_op jit(solution)/shard_map/ppermute | solution.py:37
  11.9 0.0 collective-permute-done.3
  11.9 0.0 collective-permute-done.4
  11.9 8.7 %collective-permute-done.5 = bf16[256,256]{1,0:T(8,128)(2,1)S(1)} collective-permute-done((bf16[256,256]{1,0:T(8,128)(2,1)S(1)}, bf16[256,256]{1,0:T(8,128)(2,1)S(1)}, u32[]{:S(2)}, u32[]{:S(2)}) %collective-permute-start.5) | collective-permute-done | bytes 131104 | tf_op jit(solution)/shard_map/ppermute | solution.py:37
  20.6 1.3 %collective-permute-start.6 = (bf16[256,256]{1,0:T(8,128)(2,1)S(1)}, bf16[256,256]{1,0:T(8,128)(2,1)S(1)}, u32[]{:S(2)}, u32[]{:S(2)}) collective-permute-start(bf16[256,256]{1,0:T(8,128)(2,1)S(1)} %select_select_fusion.2), channel_id=1, source_target_pairs={{4,5},{6,7},{8,9},{10,11},{12,13},{14,15},{16,17},{18,19},{20,21},... | collective-permute-start | bytes 393224 | tf_op jit(solution)/shard_map/ppermute | solution.py:37
  22.0 0.9 %collective-permute-done.6 = bf16[256,256]{1,0:T(8,128)(2,1)S(1)} collective-permute-done((bf16[256,256]{1,0:T(8,128)(2,1)S(1)}, bf16[256,256]{1,0:T(8,128)(2,1)S(1)}, u32[]{:S(2)}, u32[]{:S(2)}) %collective-permute-start.6) | collective-permute-done | bytes 131104 | tf_op jit(solution)/shard_map/ppermute | solution.py:37
  22.9 3.8 %collective-permute-done.10 = bf16[256,512]{1,0:T(8,128)(2,1)S(1)} collective-permute-done((bf16[256,512]{1,0:T(8,128)(2,1)S(1)}, bf16[256,512]{1,0:T(8,128)(2,1)S(1)}, u32[]{:S(2)}, u32[]{:S(2)}) %collective-permute-start.10) | collective-permute-done | bytes 262176 | tf_op jit(solution)/shard_map/ppermute | solution.py:37
  26.8 0.0 collective-permute-done.9
  26.8 1.0 %convolution_subtract_fusion = f32[256,512]{1,0:T(8,128)} fusion(f32[256,512]{1,0:T(8,128)S(1)} %copy-done, bf16[256,512]{1,0:T(8,128)(2,1)S(1)} %collective-permute-done.9, bf16[256,512]{1,0:T(8,128)(2,1)S(1)} %collective-permute-done.10, bf16[256,512]{1,0:T(8,128)(2,1)S(1)} %broadcast_select_fusion.2, pred[]{:T(512)S(6)} %or.39, pred[]{:T(512)S(6)} %and.95, ...), kind=kOutput, calls=%fused_computation.34 | convolution fusion | flops 67764224 | bytes 2097668 | tf_op jit(solution)/shard_map/dot_general | solution.py:153
  (12 shorter events, 0.2 us)
Async XLA Ops:
  0.0 1.2 %copy-start.1 = (f32[256,512]{1,0:T(8,128)S(1)}, f32[256,512]{1,0:T(8,128)}, u32[]{:S(2)}) copy-start(f32[256,512]{1,0:T(8,128)} %param.1) | copy-start | bytes 1572868 | tf_op jit(solution)/shard_map/cond
  1.2 3.5 %collective-permute-start.7 = (bf16[256,512]{1,0:T(8,128)(2,1)S(1)}, bf16[256,512]{1,0:T(8,128)(2,1)S(1)}, u32[]{:S(2)}, u32[]{:S(2)}) collective-permute-start(bf16[256,512]{1,0:T(8,128)(2,1)S(1)} %get-tuple-element.22), channel_id=1, source_target_pairs={{1,17},{0,4},{2,6},{3,19}} | collective-permute-start | bytes 786440 | tf_op jit(solution)/shard_map/ppermute | solution.py:37
  1.9 5.2 %collective-permute-start = (f32[256,256]{1,0:T(8,128)S(1)}, f32[256,256]{1,0:T(8,128)S(1)}, u32[]{:S(2)}, u32[]{:S(2)}) collective-permute-start(f32[256,256]{1,0:T(8,128)S(1)} %get-tuple-element.19), channel_id=1, source_target_pairs={{0,16},{8,0},{12,4},{28,20}} | collective-permute-start | bytes 786440 | tf_op jit(solution)/shard_map/ppermute | solution.py:37
  3.2 3.9 %collective-permute-start.1 = (f32[256,256]{1,0:T(8,128)S(1)}, f32[256,256]{1,0:T(8,128)S(1)}, u32[]{:S(2)}, u32[]{:S(2)}) collective-permute-start(f32[256,256]{1,0:T(8,128)S(1)} %get-tuple-element.19), channel_id=1, source_target_pairs={{0,4},{24,16}} | collective-permute-start | bytes 786440 | tf_op jit(solution)/shard_map/ppermute | solution.py:37
  3.9 3.2 %collective-permute-start.2 = (f32[256,256]{1,0:T(8,128)S(1)}, f32[256,256]{1,0:T(8,128)S(1)}, u32[]{:S(2)}, u32[]{:S(2)}) collective-permute-start(f32[256,256]{1,0:T(8,128)S(1)} %get-tuple-element.19), channel_id=1, source_target_pairs={{0,20}} | collective-permute-start | bytes 786440 | tf_op jit(solution)/shard_map/ppermute | solution.py:37
  4.7 1.0 %copy-start = (f32[256,512]{1,0:T(8,128)S(1)}, f32[256,512]{1,0:T(8,128)}, u32[]{:S(2)}) copy-start(f32[256,512]{1,0:T(8,128)} %param.5) | copy-start | bytes 1572868
  4.7 5.2 %collective-permute-start.8 = (bf16[256,512]{1,0:T(8,128)(2,1)S(1)}, bf16[256,512]{1,0:T(8,128)(2,1)S(1)}, u32[]{:S(2)}, u32[]{:S(2)}) collective-permute-start(bf16[256,512]{1,0:T(8,128)(2,1)S(1)} %broadcast_select_fusion.1), channel_id=1, source_target_pairs={{17,21},{0,16},{2,18},{4,20},{6,22},{3,11},{19,27}} | collective-permute-start | bytes 786440 | tf_op jit(solution)/shard_map/ppermute | solution.py:37
  7.2 13.4 %collective-permute-start.5 = (bf16[256,256]{1,0:T(8,128)(2,1)S(1)}, bf16[256,256]{1,0:T(8,128)(2,1)S(1)}, u32[]{:S(2)}, u32[]{:S(2)}) collective-permute-start(bf16[256,256]{1,0:T(8,128)(2,1)S(1)} %get-tuple-element.21), channel_id=1, source_target_pairs={{0,8},{4,12},{16,24},{20,28}} | collective-permute-start | bytes 393224 | tf_op jit(solution)/shard_map/ppermute | solution.py:37
  8.5 3.4 %collective-permute-start.3 = (bf16[256,256]{1,0:T(8,128)(2,1)S(1)}, bf16[256,256]{1,0:T(8,128)(2,1)S(1)}, u32[]{:S(2)}, u32[]{:S(2)}) collective-permute-start(bf16[256,256]{1,0:T(8,128)(2,1)S(1)} %get-tuple-element.82), channel_id=1, source_target_pairs={{0,10},{4,14},{16,26},{20,22}} | collective-permute-start | bytes 393224 | tf_op jit(solution)/shard_map/ppermute | solution.py:37
  9.2 2.7 %collective-permute-start.4 = (bf16[256,256]{1,0:T(8,128)(2,1)S(1)}, bf16[256,256]{1,0:T(8,128)(2,1)S(1)}, u32[]{:S(2)}, u32[]{:S(2)}) collective-permute-start(bf16[256,256]{1,0:T(8,128)(2,1)S(1)} %get-tuple-element.81), channel_id=1, source_target_pairs={{16,18},{4,6},{20,30}} | collective-permute-start | bytes 393224 | tf_op jit(solution)/shard_map/ppermute | solution.py:37
  9.9 16.8 %collective-permute-start.10 = (bf16[256,512]{1,0:T(8,128)(2,1)S(1)}, bf16[256,512]{1,0:T(8,128)(2,1)S(1)}, u32[]{:S(2)}, u32[]{:S(2)}) collective-permute-start(bf16[256,512]{1,0:T(8,128)(2,1)S(1)} %broadcast_select_fusion.2), channel_id=1, source_target_pairs={{17,25},{21,29},{1,5},{0,8},{2,10},{4,12},{6,14},{16,24},{18,26},{... | collective-permute-start | bytes 786440 | tf_op jit(solution)/shard_map/ppermute | solution.py:37
  11.2 15.5 %collective-permute-start.9 = (bf16[256,512]{1,0:T(8,128)(2,1)S(1)}, bf16[256,512]{1,0:T(8,128)(2,1)S(1)}, u32[]{:S(2)}, u32[]{:S(2)}) collective-permute-start(bf16[256,512]{1,0:T(8,128)(2,1)S(1)} %broadcast_select_fusion.2), channel_id=1, source_target_pairs={{17,9},{21,13}} | collective-permute-start | bytes 786440 | tf_op jit(solution)/shard_map/ppermute | solution.py:37
  20.6 2.3 %collective-permute-start.6 = (bf16[256,256]{1,0:T(8,128)(2,1)S(1)}, bf16[256,256]{1,0:T(8,128)(2,1)S(1)}, u32[]{:S(2)}, u32[]{:S(2)}) collective-permute-start(bf16[256,256]{1,0:T(8,128)(2,1)S(1)} %select_select_fusion.2), channel_id=1, source_target_pairs={{4,5},{6,7},{8,9},{10,11},{12,13},{14,15},{16,17},{18,19},{20,21},... | collective-permute-start | bytes 393224 | tf_op jit(solution)/shard_map/ppermute | solution.py:37

commit v23 on v22

--- a/solution.py
+++ b/solution.py
@@ -52,7 +52,7 @@
     middle = n_row // 2
     orders = [[down[-1]] + down[:-1], down]
     held = [[0], [0]]
-    beside_steps = [[(0, middle)], [(middle, middle + 1)]]
+    beside_steps = [[(0, middle + 1)], [(middle + 1, middle)]]
     for stride in down[1:-1]:
         far = [b for step in beside_steps for _, b in step]
         beside_steps.append([(h, h + stride) for h in far])

time: 28.1 us -> 27.6 us (0.982)
  waiting for transfers between devices: 14.7 us -> 14.2 us
    ppermute x11, waiting for transfers between devices: 14.7 us -> 14.2 us  [send(): return lax.ppermute(value, ('row', 'col'), flat)]
where the time goes in v23:
time: 27.6 us; the launch traced here: 27.3 us
  waiting for transfers between devices  14.2 us (51%)
  starting transfers between devices  10 us (36%)
  other arithmetic  1.29 us (5%)
  matrix products  1.03 us (4%)
  between operations  0.36 us (1%)
  local copies, waits for them, and re-layouts  0.3 us (1%)
    ppermute x11, waiting for transfers between devices, send(): return lax.ppermute(value, ('row', 'col'), flat)  14.2 us
    ppermute x11, starting transfers between devices, send(): return lax.ppermute(value, ('row', 'col'), flat)  10 us
    convert_element_type x1, other arithmetic, blocks(): return (matrix[:, :NB], matrix.astype(jnp.bfloat16))  1.15 us
    dot_general x1, matrix products, shards(): return matrix - jnp.dot(received, upper, preferred_element_type=jnp.float32)  1.03 us
  transfers between devices with their start and end apart: 11, of which 4 were waited for; matrix products, arithmetic and copies ran while one was open for 1% of the time, Pallas kernels for 0%

profile of v23, /device:TPU:26, one launch (start us, length us, event | category | flops | bytes accessed | tf_op | source)
XLA Modules:
  0.0 27.3 jit_solution(8803303023665886670)
XLA Ops:
  0.0 1.2 %conditional.2 = (f32[256,256]{1,0:T(8,128)S(1)}, bf16[256,512]{1,0:T(8,128)(2,1)S(1)}) conditional(s32[]{:T(128)} %convert_element_type.16, () %tuple.22, f32[256,512]{1,0:T(8,128)} %param.5), branch_computations={%region_0.0_spmd, %region_1.0_spmd} | conditional | flops 131072 | bytes 3407916 | solution.py:46
  0.0 0.0 copy-start.1
  0.0 1.1 %convert_element_type.1 = bf16[256,512]{1,0:T(8,128)(2,1)S(1)} convert(f32[256,512]{1,0:T(8,128)} %param.1) | non-fusion elementwise | flops 131072 | bytes 786432 | tf_op jit(solution)/shard_map/cond/branch_1_fun/convert_element_type | solution.py:40
  1.2 0.0 copy-done.1
  1.2 0.7 %collective-permute-start.7 = (bf16[256,512]{1,0:T(8,128)(2,1)S(1)}, bf16[256,512]{1,0:T(8,128)(2,1)S(1)}, u32[]{:S(2)}, u32[]{:S(2)}) collective-permute-start(bf16[256,512]{1,0:T(8,128)(2,1)S(1)} %get-tuple-element.22), channel_id=1, source_target_pairs={{1,21},{0,4},{2,6},{3,19}} | collective-permute-start | bytes 786440 | tf_op jit(solution)/shard_map/ppermute | solution.py:37
  1.9 1.3 %collective-permute-start = (f32[256,256]{1,0:T(8,128)S(1)}, f32[256,256]{1,0:T(8,128)S(1)}, u32[]{:S(2)}, u32[]{:S(2)}) collective-permute-start(f32[256,256]{1,0:T(8,128)S(1)} %get-tuple-element.19), channel_id=1, source_target_pairs={{0,16},{8,0},{12,4},{28,20}} | collective-permute-start | bytes 786440 | tf_op jit(solution)/shard_map/ppermute | solution.py:37
  3.2 0.7 %collective-permute-start.1 = (f32[256,256]{1,0:T(8,128)S(1)}, f32[256,256]{1,0:T(8,128)S(1)}, u32[]{:S(2)}, u32[]{:S(2)}) collective-permute-start(f32[256,256]{1,0:T(8,128)S(1)} %get-tuple-element.19), channel_id=1, source_target_pairs={{0,4},{24,16}} | collective-permute-start | bytes 786440 | tf_op jit(solution)/shard_map/ppermute | solution.py:37
  3.9 0.7 %collective-permute-start.2 = (f32[256,256]{1,0:T(8,128)S(1)}, f32[256,256]{1,0:T(8,128)S(1)}, u32[]{:S(2)}, u32[]{:S(2)}) collective-permute-start(f32[256,256]{1,0:T(8,128)S(1)} %get-tuple-element.19), channel_id=1, source_target_pairs={{0,20}} | collective-permute-start | bytes 786440 | tf_op jit(solution)/shard_map/ppermute | solution.py:37
  4.7 0.0 copy-start
  4.7 0.0 collective-permute-done.7
  4.7 0.8 %collective-permute-start.8 = (bf16[256,512]{1,0:T(8,128)(2,1)S(1)}, bf16[256,512]{1,0:T(8,128)(2,1)S(1)}, u32[]{:S(2)}, u32[]{:S(2)}) collective-permute-start(bf16[256,512]{1,0:T(8,128)(2,1)S(1)} %broadcast_select_fusion.1), channel_id=1, source_target_pairs={{21,17},{0,16},{2,18},{4,20},{6,22},{3,11},{19,27}} | collective-permute-start | bytes 786440 | tf_op jit(solution)/shard_map/ppermute | solution.py:37
  5.6 0.1 copy-done
  5.8 1.3 %collective-permute-done = f32[256,256]{1,0:T(8,128)S(1)} collective-permute-done((f32[256,256]{1,0:T(8,128)S(1)}, f32[256,256]{1,0:T(8,128)S(1)}, u32[]{:S(2)}, u32[]{:S(2)}) %collective-permute-start) | collective-permute-done | bytes 262176 | tf_op jit(solution)/shard_map/ppermute | solution.py:37
  7.1 0.0 collective-permute-done.1
  7.1 0.0 collective-permute-done.2
  7.1 0.1 conditional.3
  7.2 1.3 %collective-permute-start.5 = (bf16[256,256]{1,0:T(8,128)(2,1)S(1)}, bf16[256,256]{1,0:T(8,128)(2,1)S(1)}, u32[]{:S(2)}, u32[]{:S(2)}) collective-permute-start(bf16[256,256]{1,0:T(8,128)(2,1)S(1)} %get-tuple-element.21), channel_id=1, source_target_pairs={{0,8},{4,12},{16,24},{20,28}} | collective-permute-start | bytes 393224 | tf_op jit(solution)/shard_map/ppermute | solution.py:37
  8.5 0.7 %collective-permute-start.3 = (bf16[256,256]{1,0:T(8,128)(2,1)S(1)}, bf16[256,256]{1,0:T(8,128)(2,1)S(1)}, u32[]{:S(2)}, u32[]{:S(2)}) collective-permute-start(bf16[256,256]{1,0:T(8,128)(2,1)S(1)} %get-tuple-element.82), channel_id=1, source_target_pairs={{0,10},{4,14},{16,26},{20,22}} | collective-permute-start | bytes 393224 | tf_op jit(solution)/shard_map/ppermute | solution.py:37
  9.2 0.7 %collective-permute-start.4 = (bf16[256,256]{1,0:T(8,128)(2,1)S(1)}, bf16[256,256]{1,0:T(8,128)(2,1)S(1)}, u32[]{:S(2)}, u32[]{:S(2)}) collective-permute-start(bf16[256,256]{1,0:T(8,128)(2,1)S(1)} %get-tuple-element.81), channel_id=1, source_target_pairs={{16,18},{4,6},{20,30}} | collective-permute-start | bytes 393224 | tf_op jit(solution)/shard_map/ppermute | solution.py:37
  9.9 0.0 collective-permute-done.8
  9.9 1.3 %collective-permute-start.10 = (bf16[256,512]{1,0:T(8,128)(2,1)S(1)}, bf16[256,512]{1,0:T(8,128)(2,1)S(1)}, u32[]{:S(2)}, u32[]{:S(2)}) collective-permute-start(bf16[256,512]{1,0:T(8,128)(2,1)S(1)} %broadcast_select_fusion.2), channel_id=1, source_target_pairs={{21,29},{17,25},{1,5},{0,8},{2,10},{4,12},{6,14},{16,24},{18,26},{... | collective-permute-start | bytes 786440 | tf_op jit(solution)/shard_map/ppermute | solution.py:37
  11.2 0.7 %collective-permute-start.9 = (bf16[256,512]{1,0:T(8,128)(2,1)S(1)}, bf16[256,512]{1,0:T(8,128)(2,1)S(1)}, u32[]{:S(2)}, u32[]{:S(2)}) collective-permute-start(bf16[256,512]{1,0:T(8,128)(2,1)S(1)} %broadcast_select_fusion.2), channel_id=1, source_target_pairs={{17,9},{21,13}} | collective-permute-start | bytes 786440 | tf_op jit(solution)/shard_map/ppermute | solution.py:37
  11.9 0.0 collective-permute-done.3
  11.9 0.0 collective-permute-done.4
  11.9 10.1 %collective-permute-done.5 = bf16[256,256]{1,0:T(8,128)(2,1)S(1)} collective-permute-done((bf16[256,256]{1,0:T(8,128)(2,1)S(1)}, bf16[256,256]{1,0:T(8,128)(2,1)S(1)}, u32[]{:S(2)}, u32[]{:S(2)}) %collective-permute-start.5) | collective-permute-done | bytes 131104 | tf_op jit(solution)/shard_map/ppermute | solution.py:37
  22.0 1.3 %collective-permute-start.6 = (bf16[256,256]{1,0:T(8,128)(2,1)S(1)}, bf16[256,256]{1,0:T(8,128)(2,1)S(1)}, u32[]{:S(2)}, u32[]{:S(2)}) collective-permute-start(bf16[256,256]{1,0:T(8,128)(2,1)S(1)} %select_select_fusion.2), channel_id=1, source_target_pairs={{4,5},{6,7},{8,9},{10,11},{12,13},{14,15},{16,17},{18,19},{20,21},... | collective-permute-start | bytes 393224 | tf_op jit(solution)/shard_map/ppermute | solution.py:37
  23.4 0.9 %collective-permute-done.6 = bf16[256,256]{1,0:T(8,128)(2,1)S(1)} collective-permute-done((bf16[256,256]{1,0:T(8,128)(2,1)S(1)}, bf16[256,256]{1,0:T(8,128)(2,1)S(1)}, u32[]{:S(2)}, u32[]{:S(2)}) %collective-permute-start.6) | collective-permute-done | bytes 131104 | tf_op jit(solution)/shard_map/ppermute | solution.py:37
  24.3 1.9 %collective-permute-done.10 = bf16[256,512]{1,0:T(8,128)(2,1)S(1)} collective-permute-done((bf16[256,512]{1,0:T(8,128)(2,1)S(1)}, bf16[256,512]{1,0:T(8,128)(2,1)S(1)}, u32[]{:S(2)}, u32[]{:S(2)}) %collective-permute-start.10) | collective-permute-done | bytes 262176 | tf_op jit(solution)/shard_map/ppermute | solution.py:37
  26.2 0.0 collective-permute-done.9
  26.2 1.0 %convolution_subtract_fusion = f32[256,512]{1,0:T(8,128)} fusion(f32[256,512]{1,0:T(8,128)S(1)} %copy-done, bf16[256,512]{1,0:T(8,128)(2,1)S(1)} %collective-permute-done.9, bf16[256,512]{1,0:T(8,128)(2,1)S(1)} %collective-permute-done.10, bf16[256,512]{1,0:T(8,128)(2,1)S(1)} %broadcast_select_fusion.2, pred[]{:T(512)S(6)} %or.39, pred[]{:T(512)S(6)} %and.95, ...), kind=kOutput, calls=%fused_computation.34 | convolution fusion | flops 67764224 | bytes 2097668 | tf_op jit(solution)/shard_map/dot_general | solution.py:153
  (12 shorter events, 0.2 us)
Async XLA Ops:
  0.0 1.2 %copy-start.1 = (f32[256,512]{1,0:T(8,128)S(1)}, f32[256,512]{1,0:T(8,128)}, u32[]{:S(2)}) copy-start(f32[256,512]{1,0:T(8,128)} %param.1) | copy-start | bytes 1572868 | tf_op jit(solution)/shard_map/cond
  1.2 3.5 %collective-permute-start.7 = (bf16[256,512]{1,0:T(8,128)(2,1)S(1)}, bf16[256,512]{1,0:T(8,128)(2,1)S(1)}, u32[]{:S(2)}, u32[]{:S(2)}) collective-permute-start(bf16[256,512]{1,0:T(8,128)(2,1)S(1)} %get-tuple-element.22), channel_id=1, source_target_pairs={{1,21},{0,4},{2,6},{3,19}} | collective-permute-start | bytes 786440 | tf_op jit(solution)/shard_map/ppermute | solution.py:37
  1.9 5.2 %collective-permute-start = (f32[256,256]{1,0:T(8,128)S(1)}, f32[256,256]{1,0:T(8,128)S(1)}, u32[]{:S(2)}, u32[]{:S(2)}) collective-permute-start(f32[256,256]{1,0:T(8,128)S(1)} %get-tuple-element.19), channel_id=1, source_target_pairs={{0,16},{8,0},{12,4},{28,20}} | collective-permute-start | bytes 786440 | tf_op jit(solution)/shard_map/ppermute | solution.py:37
  3.2 3.9 %collective-permute-start.1 = (f32[256,256]{1,0:T(8,128)S(1)}, f32[256,256]{1,0:T(8,128)S(1)}, u32[]{:S(2)}, u32[]{:S(2)}) collective-permute-start(f32[256,256]{1,0:T(8,128)S(1)} %get-tuple-element.19), channel_id=1, source_target_pairs={{0,4},{24,16}} | collective-permute-start | bytes 786440 | tf_op jit(solution)/shard_map/ppermute | solution.py:37
  3.9 3.2 %collective-permute-start.2 = (f32[256,256]{1,0:T(8,128)S(1)}, f32[256,256]{1,0:T(8,128)S(1)}, u32[]{:S(2)}, u32[]{:S(2)}) collective-permute-start(f32[256,256]{1,0:T(8,128)S(1)} %get-tuple-element.19), channel_id=1, source_target_pairs={{0,20}} | collective-permute-start | bytes 786440 | tf_op jit(solution)/shard_map/ppermute | solution.py:37
  4.7 1.0 %copy-start = (f32[256,512]{1,0:T(8,128)S(1)}, f32[256,512]{1,0:T(8,128)}, u32[]{:S(2)}) copy-start(f32[256,512]{1,0:T(8,128)} %param.5) | copy-start | bytes 1572868
  4.7 5.2 %collective-permute-start.8 = (bf16[256,512]{1,0:T(8,128)(2,1)S(1)}, bf16[256,512]{1,0:T(8,128)(2,1)S(1)}, u32[]{:S(2)}, u32[]{:S(2)}) collective-permute-start(bf16[256,512]{1,0:T(8,128)(2,1)S(1)} %broadcast_select_fusion.1), channel_id=1, source_target_pairs={{21,17},{0,16},{2,18},{4,20},{6,22},{3,11},{19,27}} | collective-permute-start | bytes 786440 | tf_op jit(solution)/shard_map/ppermute | solution.py:37
  7.2 14.8 %collective-permute-start.5 = (bf16[256,256]{1,0:T(8,128)(2,1)S(1)}, bf16[256,256]{1,0:T(8,128)(2,1)S(1)}, u32[]{:S(2)}, u32[]{:S(2)}) collective-permute-start(bf16[256,256]{1,0:T(8,128)(2,1)S(1)} %get-tuple-element.21), channel_id=1, source_target_pairs={{0,8},{4,12},{16,24},{20,28}} | collective-permute-start | bytes 393224 | tf_op jit(solution)/shard_map/ppermute | solution.py:37
  8.5 3.4 %collective-permute-start.3 = (bf16[256,256]{1,0:T(8,128)(2,1)S(1)}, bf16[256,256]{1,0:T(8,128)(2,1)S(1)}, u32[]{:S(2)}, u32[]{:S(2)}) collective-permute-start(bf16[256,256]{1,0:T(8,128)(2,1)S(1)} %get-tuple-element.82), channel_id=1, source_target_pairs={{0,10},{4,14},{16,26},{20,22}} | collective-permute-start | bytes 393224 | tf_op jit(solution)/shard_map/ppermute | solution.py:37
  9.2 2.7 %collective-permute-start.4 = (bf16[256,256]{1,0:T(8,128)(2,1)S(1)}, bf16[256,256]{1,0:T(8,128)(2,1)S(1)}, u32[]{:S(2)}, u32[]{:S(2)}) collective-permute-start(bf16[256,256]{1,0:T(8,128)(2,1)S(1)} %get-tuple-element.81), channel_id=1, source_target_pairs={{16,18},{4,6},{20,30}} | collective-permute-start | bytes 393224 | tf_op jit(solution)/shard_map/ppermute | solution.py:37
  9.9 16.3 %collective-permute-start.10 = (bf16[256,512]{1,0:T(8,128)(2,1)S(1)}, bf16[256,512]{1,0:T(8,128)(2,1)S(1)}, u32[]{:S(2)}, u32[]{:S(2)}) collective-permute-start(bf16[256,512]{1,0:T(8,128)(2,1)S(1)} %broadcast_select_fusion.2), channel_id=1, source_target_pairs={{21,29},{17,25},{1,5},{0,8},{2,10},{4,12},{6,14},{16,24},{18,26},{... | collective-permute-start | bytes 786440 | tf_op jit(solution)/shard_map/ppermute | solution.py:37
  11.2 15.0 %collective-permute-start.9 = (bf16[256,512]{1,0:T(8,128)(2,1)S(1)}, bf16[256,512]{1,0:T(8,128)(2,1)S(1)}, u32[]{:S(2)}, u32[]{:S(2)}) collective-permute-start(bf16[256,512]{1,0:T(8,128)(2,1)S(1)} %broadcast_select_fusion.2), channel_id=1, source_target_pairs={{17,9},{21,13}} | collective-permute-start | bytes 786440 | tf_op jit(solution)/shard_map/ppermute | solution.py:37
  22.0 2.3 %collective-permute-start.6 = (bf16[256,256]{1,0:T(8,128)(2,1)S(1)}, bf16[256,256]{1,0:T(8,128)(2,1)S(1)}, u32[]{:S(2)}, u32[]{:S(2)}) collective-permute-start(bf16[256,256]{1,0:T(8,128)(2,1)S(1)} %select_select_fusion.2), channel_id=1, source_target_pairs={{4,5},{6,7},{8,9},{10,11},{12,13},{14,15},{16,17},{18,19},{20,21},... | collective-permute-start | bytes 393224 | tf_op jit(solution)/shard_map/ppermute | solution.py:37

commit v24 on v21

--- a/solution.py
+++ b/solution.py
@@ -129,8 +129,8 @@
         pairs = [((r, 0), (r + APART, 0)) for r in workers]
         return send(lower_far, pairs), far & (col_here == 0)
 
-    even = range(2, n_col, 2)
-    for step, columns in ((send_near, [0]), (send_own, even), (send_far, even)):
+    odd = range(3, n_col, 2)
+    for step, columns in ((send_near, [0]), (send_own, odd), (send_far, odd)):
         for c in columns:
             got, takes = step(c)
             received = jnp.where(takes, got, received)
@@ -142,9 +142,11 @@
     got = send(sent, [((a, 1), (b, 1)) for a, b in beside_back])
     upper = jnp.where((col_here == 1) & (row_here > 1) & (row_here < middle), got, upper)
     got = send(
-        received, [((r, c), (r, c + 1)) for r in range(1, n_row) for c in range(0, n_col, 2)]
+        received,
+        [((r, 0), (r, 1)) for r in range(1, n_row)]
+        + [((r, c), (r, c - 1)) for r in range(1, n_row) for c in odd],
     )
-    received = jnp.where(col_here % 2 == 0, received, got)
+    received = jnp.where((col_here == 0) | (col_here > 1) & (col_here % 2 == 1), received, got)
     received = jnp.where(row_here == 0, jnp.zeros_like(received), received)
 
     col_done = col_here * cols_dev + jnp.arange(cols_dev, dtype=jnp.int32) < NB

time: 26.5 us -> 26.5 us (level)
  no operation moved by 1% of the time
where the time goes in v24:
time: 26.5 us; the launch traced here: 26.1 us
  waiting for transfers between devices  13.1 us (49%)
  starting transfers between devices  10 us (38%)
  other arithmetic  1.29 us (5%)
  matrix products  1.04 us (4%)
  between operations  0.37 us (1%)
  local copies, waits for them, and re-layouts  0.3 us (1%)
    ppermute x11, waiting for transfers between devices, send(): return lax.ppermute(value, ('row', 'col'), flat)  13.1 us
    ppermute x11, starting transfers between devices, send(): return lax.ppermute(value, ('row', 'col'), flat)  10 us
    convert_element_type x1, other arithmetic, blocks(): return (matrix[:, :NB], matrix.astype(jnp.bfloat16))  1.15 us
    dot_general x1, matrix products, shards(): return matrix - jnp.dot(received, upper, preferred_element_type=jnp.float32)  1.04 us
  transfers between devices with their start and end apart: 11, of which 4 were waited for; matrix products, arithmetic and copies ran while one was open for 1% of the time, Pallas kernels for 0%

profile of v24, /device:TPU:24, one launch (start us, length us, event | category | flops | bytes accessed | tf_op | source)
XLA Modules:
  0.0 26.1 jit_solution(6074988650916665255)
XLA Ops:
  0.0 1.2 %conditional.2 = (f32[256,256]{1,0:T(8,128)S(1)}, bf16[256,512]{1,0:T(8,128)(2,1)S(1)}) conditional(s32[]{:T(128)} %convert_element_type.16, () %tuple.22, f32[256,512]{1,0:T(8,128)} %param.5), branch_computations={%region_0.0_spmd, %region_1.0_spmd} | conditional | flops 131072 | bytes 3407916 | solution.py:46
  0.0 0.0 copy-start.1
  0.0 1.1 %convert_element_type.1 = bf16[256,512]{1,0:T(8,128)(2,1)S(1)} convert(f32[256,512]{1,0:T(8,128)} %param.1) | non-fusion elementwise | flops 131072 | bytes 786432 | tf_op jit(solution)/shard_map/cond/branch_1_fun/convert_element_type | solution.py:40
  1.2 0.0 copy-done.1
  1.2 0.7 %collective-permute-start.7 = (bf16[256,512]{1,0:T(8,128)(2,1)S(1)}, bf16[256,512]{1,0:T(8,128)(2,1)S(1)}, u32[]{:S(2)}, u32[]{:S(2)}) collective-permute-start(bf16[256,512]{1,0:T(8,128)(2,1)S(1)} %get-tuple-element.22), channel_id=1, source_target_pairs={{1,17},{0,4},{2,6},{3,19}} | collective-permute-start | bytes 786440 | tf_op jit(solution)/shard_map/ppermute | solution.py:37
  1.9 1.3 %collective-permute-start = (f32[256,256]{1,0:T(8,128)S(1)}, f32[256,256]{1,0:T(8,128)S(1)}, u32[]{:S(2)}, u32[]{:S(2)}) collective-permute-start(f32[256,256]{1,0:T(8,128)S(1)} %get-tuple-element.19), channel_id=1, source_target_pairs={{0,20},{8,0},{12,4},{24,16}} | collective-permute-start | bytes 786440 | tf_op jit(solution)/shard_map/ppermute | solution.py:37
  3.2 0.7 %collective-permute-start.1 = (f32[256,256]{1,0:T(8,128)S(1)}, f32[256,256]{1,0:T(8,128)S(1)}, u32[]{:S(2)}, u32[]{:S(2)}) collective-permute-start(f32[256,256]{1,0:T(8,128)S(1)} %get-tuple-element.19), channel_id=1, source_target_pairs={{0,4},{28,20}} | collective-permute-start | bytes 786440 | tf_op jit(solution)/shard_map/ppermute | solution.py:37
  3.9 0.7 %collective-permute-start.2 = (f32[256,256]{1,0:T(8,128)S(1)}, f32[256,256]{1,0:T(8,128)S(1)}, u32[]{:S(2)}, u32[]{:S(2)}) collective-permute-start(f32[256,256]{1,0:T(8,128)S(1)} %get-tuple-element.19), channel_id=1, source_target_pairs={{0,16}} | collective-permute-start | bytes 786440 | tf_op jit(solution)/shard_map/ppermute | solution.py:37
  4.7 0.0 copy-start
  4.7 0.0 collective-permute-done.7
  4.7 0.8 %collective-permute-start.8 = (bf16[256,512]{1,0:T(8,128)(2,1)S(1)}, bf16[256,512]{1,0:T(8,128)(2,1)S(1)}, u32[]{:S(2)}, u32[]{:S(2)}) collective-permute-start(bf16[256,512]{1,0:T(8,128)(2,1)S(1)} %broadcast_select_fusion.1), channel_id=1, source_target_pairs={{17,21},{0,16},{2,18},{4,20},{6,22},{3,11},{19,27}} | collective-permute-start | bytes 786440 | tf_op jit(solution)/shard_map/ppermute | solution.py:37
  5.6 0.1 copy-done
  5.8 1.3 %collective-permute-done = f32[256,256]{1,0:T(8,128)S(1)} collective-permute-done((f32[256,256]{1,0:T(8,128)S(1)}, f32[256,256]{1,0:T(8,128)S(1)}, u32[]{:S(2)}, u32[]{:S(2)}) %collective-permute-start) | collective-permute-done | bytes 262176 | tf_op jit(solution)/shard_map/ppermute | solution.py:37
  7.1 0.0 collective-permute-done.1
  7.1 0.0 collective-permute-done.2
  7.1 0.1 conditional.3
  7.2 1.3 %collective-permute-start.5 = (bf16[256,256]{1,0:T(8,128)(2,1)S(1)}, bf16[256,256]{1,0:T(8,128)(2,1)S(1)}, u32[]{:S(2)}, u32[]{:S(2)}) collective-permute-start(bf16[256,256]{1,0:T(8,128)(2,1)S(1)} %get-tuple-element.21), channel_id=1, source_target_pairs={{0,8},{4,12},{16,24},{20,28}} | collective-permute-start | bytes 393224 | tf_op jit(solution)/shard_map/ppermute | solution.py:37
  8.5 0.7 %collective-permute-start.3 = (bf16[256,256]{1,0:T(8,128)(2,1)S(1)}, bf16[256,256]{1,0:T(8,128)(2,1)S(1)}, u32[]{:S(2)}, u32[]{:S(2)}) collective-permute-start(bf16[256,256]{1,0:T(8,128)(2,1)S(1)} %get-tuple-element.82), channel_id=1, source_target_pairs={{0,11},{4,15},{16,19},{20,31}} | collective-permute-start | bytes 393224 | tf_op jit(solution)/shard_map/ppermute | solution.py:37
  9.2 0.7 %collective-permute-start.4 = (bf16[256,256]{1,0:T(8,128)(2,1)S(1)}, bf16[256,256]{1,0:T(8,128)(2,1)S(1)}, u32[]{:S(2)}, u32[]{:S(2)}) collective-permute-start(bf16[256,256]{1,0:T(8,128)(2,1)S(1)} %get-tuple-element.81), channel_id=1, source_target_pairs={{20,23},{4,7},{16,27}} | collective-permute-start | bytes 393224 | tf_op jit(solution)/shard_map/ppermute | solution.py:37
  9.9 0.0 collective-permute-done.8
  9.9 1.3 %collective-permute-start.10 = (bf16[256,512]{1,0:T(8,128)(2,1)S(1)}, bf16[256,512]{1,0:T(8,128)(2,1)S(1)}, u32[]{:S(2)}, u32[]{:S(2)}) collective-permute-start(bf16[256,512]{1,0:T(8,128)(2,1)S(1)} %broadcast_select_fusion.2), channel_id=1, source_target_pairs={{17,25},{21,29},{1,5},{0,8},{2,10},{4,12},{6,14},{16,24},{18,26},{... | collective-permute-start | bytes 786440 | tf_op jit(solution)/shard_map/ppermute | solution.py:37
  11.2 0.7 %collective-permute-start.9 = (bf16[256,512]{1,0:T(8,128)(2,1)S(1)}, bf16[256,512]{1,0:T(8,128)(2,1)S(1)}, u32[]{:S(2)}, u32[]{:S(2)}) collective-permute-start(bf16[256,512]{1,0:T(8,128)(2,1)S(1)} %broadcast_select_fusion.2), channel_id=1, source_target_pairs={{17,9},{21,13}} | collective-permute-start | bytes 786440 | tf_op jit(solution)/shard_map/ppermute | solution.py:37
  11.9 0.0 collective-permute-done.3
  11.9 0.0 collective-permute-done.4
  11.9 7.7 %collective-permute-done.5 = bf16[256,256]{1,0:T(8,128)(2,1)S(1)} collective-permute-done((bf16[256,256]{1,0:T(8,128)(2,1)S(1)}, bf16[256,256]{1,0:T(8,128)(2,1)S(1)}, u32[]{:S(2)}, u32[]{:S(2)}) %collective-permute-start.5) | collective-permute-done | bytes 131104 | tf_op jit(solution)/shard_map/ppermute | solution.py:37
  19.7 1.3 %collective-permute-start.6 = (bf16[256,256]{1,0:T(8,128)(2,1)S(1)}, bf16[256,256]{1,0:T(8,128)(2,1)S(1)}, u32[]{:S(2)}, u32[]{:S(2)}) collective-permute-start(bf16[256,256]{1,0:T(8,128)(2,1)S(1)} %select_select_fusion.2), channel_id=1, source_target_pairs={{4,5},{8,9},{12,13},{16,17},{20,21},{24,25},{28,29},{7,6},{11,10},... | collective-permute-start | bytes 393224 | tf_op jit(solution)/shard_map/ppermute | solution.py:37
  21.1 0.9 %collective-permute-done.6 = bf16[256,256]{1,0:T(8,128)(2,1)S(1)} collective-permute-done((bf16[256,256]{1,0:T(8,128)(2,1)S(1)}, bf16[256,256]{1,0:T(8,128)(2,1)S(1)}, u32[]{:S(2)}, u32[]{:S(2)}) %collective-permute-start.6) | collective-permute-done | bytes 131104 | tf_op jit(solution)/shard_map/ppermute | solution.py:37
  22.0 3.2 %collective-permute-done.10 = bf16[256,512]{1,0:T(8,128)(2,1)S(1)} collective-permute-done((bf16[256,512]{1,0:T(8,128)(2,1)S(1)}, bf16[256,512]{1,0:T(8,128)(2,1)S(1)}, u32[]{:S(2)}, u32[]{:S(2)}) %collective-permute-start.10) | collective-permute-done | bytes 262176 | tf_op jit(solution)/shard_map/ppermute | solution.py:37
  25.1 0.0 collective-permute-done.9
  25.1 1.0 %convolution_subtract_fusion = f32[256,512]{1,0:T(8,128)} fusion(f32[256,512]{1,0:T(8,128)S(1)} %copy-done, bf16[256,512]{1,0:T(8,128)(2,1)S(1)} %collective-permute-done.9, bf16[256,512]{1,0:T(8,128)(2,1)S(1)} %collective-permute-done.10, bf16[256,512]{1,0:T(8,128)(2,1)S(1)} %broadcast_select_fusion.2, pred[]{:T(512)S(6)} %or.43, pred[]{:T(512)S(6)} %and.99, ...), kind=kOutput, calls=%fused_computation.34 | convolution fusion | flops 67764224 | bytes 2097668 | tf_op jit(solution)/shard_map/dot_general | solution.py:154
  (12 shorter events, 0.2 us)
Async XLA Ops:
  0.0 1.2 %copy-start.1 = (f32[256,512]{1,0:T(8,128)S(1)}, f32[256,512]{1,0:T(8,128)}, u32[]{:S(2)}) copy-start(f32[256,512]{1,0:T(8,128)} %param.1) | copy-start | bytes 1572868 | tf_op jit(solution)/shard_map/cond
  1.2 3.5 %collective-permute-start.7 = (bf16[256,512]{1,0:T(8,128)(2,1)S(1)}, bf16[256,512]{1,0:T(8,128)(2,1)S(1)}, u32[]{:S(2)}, u32[]{:S(2)}) collective-permute-start(bf16[256,512]{1,0:T(8,128)(2,1)S(1)} %get-tuple-element.22), channel_id=1, source_target_pairs={{1,17},{0,4},{2,6},{3,19}} | collective-permute-start | bytes 786440 | tf_op jit(solution)/shard_map/ppermute | solution.py:37
  1.9 5.2 %collective-permute-start = (f32[256,256]{1,0:T(8,128)S(1)}, f32[256,256]{1,0:T(8,128)S(1)}, u32[]{:S(2)}, u32[]{:S(2)}) collective-permute-start(f32[256,256]{1,0:T(8,128)S(1)} %get-tuple-element.19), channel_id=1, source_target_pairs={{0,20},{8,0},{12,4},{24,16}} | collective-permute-start | bytes 786440 | tf_op jit(solution)/shard_map/ppermute | solution.py:37
  3.2 3.9 %collective-permute-start.1 = (f32[256,256]{1,0:T(8,128)S(1)}, f32[256,256]{1,0:T(8,128)S(1)}, u32[]{:S(2)}, u32[]{:S(2)}) collective-permute-start(f32[256,256]{1,0:T(8,128)S(1)} %get-tuple-element.19), channel_id=1, source_target_pairs={{0,4},{28,20}} | collective-permute-start | bytes 786440 | tf_op jit(solution)/shard_map/ppermute | solution.py:37
  3.9 3.2 %collective-permute-start.2 = (f32[256,256]{1,0:T(8,128)S(1)}, f32[256,256]{1,0:T(8,128)S(1)}, u32[]{:S(2)}, u32[]{:S(2)}) collective-permute-start(f32[256,256]{1,0:T(8,128)S(1)} %get-tuple-element.19), channel_id=1, source_target_pairs={{0,16}} | collective-permute-start | bytes 786440 | tf_op jit(solution)/shard_map/ppermute | solution.py:37
  4.7 1.0 %copy-start = (f32[256,512]{1,0:T(8,128)S(1)}, f32[256,512]{1,0:T(8,128)}, u32[]{:S(2)}) copy-start(f32[256,512]{1,0:T(8,128)} %param.5) | copy-start | bytes 1572868
  4.7 5.2 %collective-permute-start.8 = (bf16[256,512]{1,0:T(8,128)(2,1)S(1)}, bf16[256,512]{1,0:T(8,128)(2,1)S(1)}, u32[]{:S(2)}, u32[]{:S(2)}) collective-permute-start(bf16[256,512]{1,0:T(8,128)(2,1)S(1)} %broadcast_select_fusion.1), channel_id=1, source_target_pairs={{17,21},{0,16},{2,18},{4,20},{6,22},{3,11},{19,27}} | collective-permute-start | bytes 786440 | tf_op jit(solution)/shard_map/ppermute | solution.py:37
  7.2 12.5 %collective-permute-start.5 = (bf16[256,256]{1,0:T(8,128)(2,1)S(1)}, bf16[256,256]{1,0:T(8,128)(2,1)S(1)}, u32[]{:S(2)}, u32[]{:S(2)}) collective-permute-start(bf16[256,256]{1,0:T(8,128)(2,1)S(1)} %get-tuple-element.21), channel_id=1, source_target_pairs={{0,8},{4,12},{16,24},{20,28}} | collective-permute-start | bytes 393224 | tf_op jit(solution)/shard_map/ppermute | solution.py:37
  8.5 3.4 %collective-permute-start.3 = (bf16[256,256]{1,0:T(8,128)(2,1)S(1)}, bf16[256,256]{1,0:T(8,128)(2,1)S(1)}, u32[]{:S(2)}, u32[]{:S(2)}) collective-permute-start(bf16[256,256]{1,0:T(8,128)(2,1)S(1)} %get-tuple-element.82), channel_id=1, source_target_pairs={{0,11},{4,15},{16,19},{20,31}} | collective-permute-start | bytes 393224 | tf_op jit(solution)/shard_map/ppermute | solution.py:37
  9.2 2.7 %collective-permute-start.4 = (bf16[256,256]{1,0:T(8,128)(2,1)S(1)}, bf16[256,256]{1,0:T(8,128)(2,1)S(1)}, u32[]{:S(2)}, u32[]{:S(2)}) collective-permute-start(bf16[256,256]{1,0:T(8,128)(2,1)S(1)} %get-tuple-element.81), channel_id=1, source_target_pairs={{20,23},{4,7},{16,27}} | collective-permute-start | bytes 393224 | tf_op jit(solution)/shard_map/ppermute | solution.py:37
  9.9 15.2 %collective-permute-start.10 = (bf16[256,512]{1,0:T(8,128)(2,1)S(1)}, bf16[256,512]{1,0:T(8,128)(2,1)S(1)}, u32[]{:S(2)}, u32[]{:S(2)}) collective-permute-start(bf16[256,512]{1,0:T(8,128)(2,1)S(1)} %broadcast_select_fusion.2), channel_id=1, source_target_pairs={{17,25},{21,29},{1,5},{0,8},{2,10},{4,12},{6,14},{16,24},{18,26},{... | collective-permute-start | bytes 786440 | tf_op jit(solution)/shard_map/ppermute | solution.py:37
  11.2 13.9 %collective-permute-start.9 = (bf16[256,512]{1,0:T(8,128)(2,1)S(1)}, bf16[256,512]{1,0:T(8,128)(2,1)S(1)}, u32[]{:S(2)}, u32[]{:S(2)}) collective-permute-start(bf16[256,512]{1,0:T(8,128)(2,1)S(1)} %broadcast_select_fusion.2), channel_id=1, source_target_pairs={{17,9},{21,13}} | collective-permute-start | bytes 786440 | tf_op jit(solution)/shard_map/ppermute | solution.py:37
  19.7 2.3 %collective-permute-start.6 = (bf16[256,256]{1,0:T(8,128)(2,1)S(1)}, bf16[256,256]{1,0:T(8,128)(2,1)S(1)}, u32[]{:S(2)}, u32[]{:S(2)}) collective-permute-start(bf16[256,256]{1,0:T(8,128)(2,1)S(1)} %select_select_fusion.2), channel_id=1, source_target_pairs={{4,5},{8,9},{12,13},{16,17},{20,21},{24,25},{28,29},{7,6},{11,10},... | collective-permute-start | bytes 393224 | tf_op jit(solution)/shard_map/ppermute | solution.py:37

commit v25 on v24

--- a/solution.py
+++ b/solution.py
@@ -52,6 +52,8 @@
     middle = n_row // 2
     orders = [[down[-1]] + down[:-1], down]
     held = [[0], [0]]
+    fits = cols_dev == 2 * NB
+    row_upper = upper[:, NB:]
     beside_steps = [[(0, middle)], [(middle, middle + 1)]]
     for stride in down[1:-1]:
         far = [b for step in beside_steps for _, b in step]
@@ -76,11 +78,13 @@
                 & (col_here % 2 == kind)
                 & ((row_here & (stride | missing)) == stride)
             )
-            pairs += [
-                ((h, c), (h + stride, c))
-                for h in held[kind]
-                for c in range(3 * kind, n_col, 2)
-            ]
+            hops = [(h, h + stride) for h in held[kind]]
+            pairs += [((a, c), (b, c)) for a, b in hops for c in range(2 + kind, n_col, 2)]
+            if kind == 0:
+                if step == len(down) - 1:
+                    crossed = {middle: middle + APART + 1, middle + 1: middle + APART}
+                    hops = [(a, crossed.get(a, b)) for a, b in hops if a or not fits]
+                pairs += [((a, 0), (b, 0)) for a, b in hops]
             held[kind] = held[kind] + [h + stride for h in held[kind]]
         got = send(sent, pairs)
         return jnp.where(takes, got, value)
@@ -123,7 +127,11 @@
 
     def send_own(c):
         sent = jnp.where(row_here == middle, lower_far, lower)
-        return send(sent, route(targets, c, True)), (~far != swapped) & (col_here == c)
+        pairs = route(targets, c, True)
+        if fits and c == 3:
+            sent = jnp.where(row_here == 0, row_upper, sent)
+            pairs += [((0, 0), (APART, 0))]
+        return send(sent, pairs), (~far != swapped) & (col_here == c)
 
     def send_near(c):
         pairs = [((r, 0), (r + APART, 0)) for r in workers]
@@ -134,6 +142,8 @@
         for c in columns:
             got, takes = step(c)
             received = jnp.where(takes, got, received)
+            if step is send_own and c == 3:
+                third_got = got
     sent = upper
     for step in range(2, len(down)):
         upper = upper_step(upper, step, upper)
@@ -149,6 +159,9 @@
     received = jnp.where((col_here == 0) | (col_here > 1) & (col_here % 2 == 1), received, got)
     received = jnp.where(row_here == 0, jnp.zeros_like(received), received)
 
+    if fits:
+        relayed = jnp.pad(third_got, ((0, 0), (NB, 0)))
+        upper = jnp.where((row_here == APART) & (col_here == 0), relayed, upper)
     col_done = col_here * cols_dev + jnp.arange(cols_dev, dtype=jnp.int32) < NB
     upper = jnp.where(col_done[None, :], jnp.zeros_like(upper), upper)
     return matrix - jnp.dot(received, upper, preferred_element_type=jnp.float32)

time: 26.5 us -> 26.5 us (level)
  the two profiles are of different devices: /device:TPU:24 before, /device:TPU:26 now
where the time goes in v25:
time: 26.5 us; the launch traced here: 26.2 us
  waiting for transfers between devices  12.5 us (47%)
  starting transfers between devices  10.6 us (40%)
  other arithmetic  1.29 us (5%)
  matrix products  1.11 us (4%)
  between operations  0.39 us (1%)
  local copies, waits for them, and re-layouts  0.29 us (1%)
    ppermute x11, waiting for transfers between devices, send(): return lax.ppermute(value, ('row', 'col'), flat)  12.5 us
    ppermute x11, starting transfers between devices, send(): return lax.ppermute(value, ('row', 'col'), flat)  10.6 us
    convert_element_type x1, other arithmetic, blocks(): return (matrix[:, :NB], matrix.astype(jnp.bfloat16))  1.15 us
    dot_general x1, matrix products, shards(): return matrix - jnp.dot(received, upper, preferred_element_type=jnp.float32)  1.11 us
  transfers between devices with their start and end apart: 11, of which 4 were waited for; matrix products, arithmetic and copies ran while one was open for 1% of the time, Pallas kernels for 0%

profile of v25, /device:TPU:26, one launch (start us, length us, event | category | flops | bytes accessed | tf_op | source)
XLA Modules:
  0.0 26.2 jit_solution(17607729608381876842)
XLA Ops:
  0.0 1.2 %conditional.2 = (f32[256,256]{1,0:T(8,128)S(1)}, bf16[256,512]{1,0:T(8,128)(2,1)S(1)}) conditional(s32[]{:T(128)} %convert_element_type.18, () %tuple.22, f32[256,512]{1,0:T(8,128)} %param.5), branch_computations={%region_0.0_spmd, %region_1.0_spmd} | conditional | flops 131072 | bytes 3407916 | solution.py:46
  0.0 0.0 copy-start.1
  0.0 1.1 %convert_element_type.10 = bf16[256,512]{1,0:T(8,128)(2,1)S(1)} convert(f32[256,512]{1,0:T(8,128)} %param.1) | non-fusion elementwise | flops 131072 | bytes 786432 | tf_op jit(solution)/shard_map/cond/branch_1_fun/convert_element_type | solution.py:40
  1.2 0.0 copy-done.1
  1.2 0.7 %collective-permute-start.7 = (bf16[256,512]{1,0:T(8,128)(2,1)S(1)}, bf16[256,512]{1,0:T(8,128)(2,1)S(1)}, u32[]{:S(2)}, u32[]{:S(2)}) collective-permute-start(bf16[256,512]{1,0:T(8,128)(2,1)S(1)} %get-tuple-element.22), channel_id=1, source_target_pairs={{1,17},{2,6},{0,4},{3,19}} | collective-permute-start | bytes 786440 | tf_op jit(solution)/shard_map/ppermute | solution.py:37
  1.9 0.7 %collective-permute-start = (f32[256,256]{1,0:T(8,128)S(1)}, f32[256,256]{1,0:T(8,128)S(1)}, u32[]{:S(2)}, u32[]{:S(2)}) collective-permute-start(f32[256,256]{1,0:T(8,128)S(1)} %get-tuple-element.19), channel_id=1, source_target_pairs={{0,20},{8,0},{12,4},{24,16}} | collective-permute-start | bytes 786440 | tf_op jit(solution)/shard_map/ppermute | solution.py:37
  2.6 1.8 %collective-permute-start.1 = (f32[256,256]{1,0:T(8,128)S(1)}, f32[256,256]{1,0:T(8,128)S(1)}, u32[]{:S(2)}, u32[]{:S(2)}) collective-permute-start(f32[256,256]{1,0:T(8,128)S(1)} %get-tuple-element.19), channel_id=1, source_target_pairs={{0,4},{28,20}} | collective-permute-start | bytes 786440 | tf_op jit(solution)/shard_map/ppermute | solution.py:37
  4.4 0.7 %collective-permute-start.2 = (f32[256,256]{1,0:T(8,128)S(1)}, f32[256,256]{1,0:T(8,128)S(1)}, u32[]{:S(2)}, u32[]{:S(2)}) collective-permute-start(f32[256,256]{1,0:T(8,128)S(1)} %get-tuple-element.19), channel_id=1, source_target_pairs={{0,16}} | collective-permute-start | bytes 786440 | tf_op jit(solution)/shard_map/ppermute | solution.py:37
  5.2 0.0 copy-start
  5.2 0.0 collective-permute-done.7
  5.3 0.8 %collective-permute-start.8 = (bf16[256,512]{1,0:T(8,128)(2,1)S(1)}, bf16[256,512]{1,0:T(8,128)(2,1)S(1)}, u32[]{:S(2)}, u32[]{:S(2)}) collective-permute-start(bf16[256,512]{1,0:T(8,128)(2,1)S(1)} %broadcast_select_fusion), channel_id=1, source_target_pairs={{17,21},{2,18},{6,22},{0,16},{4,20},{3,11},{19,27}} | collective-permute-start | bytes 786440 | tf_op jit(solution)/shard_map/ppermute | solution.py:37
  6.1 0.1 copy-done
  6.3 0.0 collective-permute-done
  6.3 2.0 %collective-permute-done.1 = f32[256,256]{1,0:T(8,128)S(1)} collective-permute-done((f32[256,256]{1,0:T(8,128)S(1)}, f32[256,256]{1,0:T(8,128)S(1)}, u32[]{:S(2)}, u32[]{:S(2)}) %collective-permute-start.1) | collective-permute-done | bytes 262176 | tf_op jit(solution)/shard_map/ppermute | solution.py:37
  8.3 0.0 collective-permute-done.2
  8.3 0.1 conditional.3
  8.4 1.3 %collective-permute-start.5 = (bf16[256,256]{1,0:T(8,128)(2,1)S(1)}, bf16[256,256]{1,0:T(8,128)(2,1)S(1)}, u32[]{:S(2)}, u32[]{:S(2)}) collective-permute-start(bf16[256,256]{1,0:T(8,128)(2,1)S(1)} %get-tuple-element.21), channel_id=1, source_target_pairs={{0,8},{4,12},{16,24},{20,28}} | collective-permute-start | bytes 393224 | tf_op jit(solution)/shard_map/ppermute | solution.py:37
  9.7 0.7 %collective-permute-start.3 = (bf16[256,256]{1,0:T(8,128)(2,1)S(1)}, bf16[256,256]{1,0:T(8,128)(2,1)S(1)}, u32[]{:S(2)}, u32[]{:S(2)}) collective-permute-start(bf16[256,256]{1,0:T(8,128)(2,1)S(1)} %get-tuple-element.81), channel_id=1, source_target_pairs={{0,11},{4,15},{16,19},{20,31}} | collective-permute-start | bytes 393224 | tf_op jit(solution)/shard_map/ppermute | solution.py:37
  10.4 0.7 %collective-permute-start.4 = (bf16[256,256]{1,0:T(8,128)(2,1)S(1)}, bf16[256,256]{1,0:T(8,128)(2,1)S(1)}, u32[]{:S(2)}, u32[]{:S(2)}) collective-permute-start(bf16[256,256]{1,0:T(8,128)(2,1)S(1)} %get-tuple-element.82), channel_id=1, source_target_pairs={{20,23},{4,7},{16,27},{0,8}} | collective-permute-start | bytes 393224 | tf_op jit(solution)/shard_map/ppermute | solution.py:37
  11.1 0.0 collective-permute-done.8
  11.1 1.3 %collective-permute-start.10 = (bf16[256,512]{1,0:T(8,128)(2,1)S(1)}, bf16[256,512]{1,0:T(8,128)(2,1)S(1)}, u32[]{:S(2)}, u32[]{:S(2)}) collective-permute-start(bf16[256,512]{1,0:T(8,128)(2,1)S(1)} %broadcast_select_fusion.1), channel_id=1, source_target_pairs={{17,25},{21,29},{1,5},{2,10},{6,14},{18,26},{22,30},{4,12},{16,28}... | collective-permute-start | bytes 786440 | tf_op jit(solution)/shard_map/ppermute | solution.py:37
  12.4 0.7 %collective-permute-start.9 = (bf16[256,512]{1,0:T(8,128)(2,1)S(1)}, bf16[256,512]{1,0:T(8,128)(2,1)S(1)}, u32[]{:S(2)}, u32[]{:S(2)}) collective-permute-start(bf16[256,512]{1,0:T(8,128)(2,1)S(1)} %broadcast_select_fusion.1), channel_id=1, source_target_pairs={{17,9},{21,13}} | collective-permute-start | bytes 786440 | tf_op jit(solution)/shard_map/ppermute | solution.py:37
  13.1 0.0 collective-permute-done.3
  13.1 0.0 collective-permute-done.4
  13.1 4.2 %collective-permute-done.5 = bf16[256,256]{1,0:T(8,128)(2,1)S(1)} collective-permute-done((bf16[256,256]{1,0:T(8,128)(2,1)S(1)}, bf16[256,256]{1,0:T(8,128)(2,1)S(1)}, u32[]{:S(2)}, u32[]{:S(2)}) %collective-permute-start.5) | collective-permute-done | bytes 131104 | tf_op jit(solution)/shard_map/ppermute | solution.py:37
  17.4 1.3 %collective-permute-start.6 = (bf16[256,256]{1,0:T(8,128)(2,1)S(1)}, bf16[256,256]{1,0:T(8,128)(2,1)S(1)}, u32[]{:S(2)}, u32[]{:S(2)}) collective-permute-start(bf16[256,256]{1,0:T(8,128)(2,1)S(1)} %select_select_fusion.2), channel_id=1, source_target_pairs={{4,5},{8,9},{12,13},{16,17},{20,21},{24,25},{28,29},{7,6},{11,10},... | collective-permute-start | bytes 393224 | tf_op jit(solution)/shard_map/ppermute | solution.py:37
  18.7 0.9 %collective-permute-done.6 = bf16[256,256]{1,0:T(8,128)(2,1)S(1)} collective-permute-done((bf16[256,256]{1,0:T(8,128)(2,1)S(1)}, bf16[256,256]{1,0:T(8,128)(2,1)S(1)}, u32[]{:S(2)}, u32[]{:S(2)}) %collective-permute-start.6) | collective-permute-done | bytes 131104 | tf_op jit(solution)/shard_map/ppermute | solution.py:37
  19.6 5.5 %collective-permute-done.10 = bf16[256,512]{1,0:T(8,128)(2,1)S(1)} collective-permute-done((bf16[256,512]{1,0:T(8,128)(2,1)S(1)}, bf16[256,512]{1,0:T(8,128)(2,1)S(1)}, u32[]{:S(2)}, u32[]{:S(2)}) %collective-permute-start.10) | collective-permute-done | bytes 262176 | tf_op jit(solution)/shard_map/ppermute | solution.py:37
  25.1 0.0 collective-permute-done.9
  25.1 1.1 %convolution_subtract_fusion = f32[256,512]{1,0:T(8,128)} fusion(f32[256,512]{1,0:T(8,128)S(1)} %copy-done, bf16[256,512]{1,0:T(8,128)(2,1)S(1)} %collective-permute-done.9, bf16[256,512]{1,0:T(8,128)(2,1)S(1)} %collective-permute-done.10, bf16[256,512]{1,0:T(8,128)(2,1)S(1)} %broadcast_select_fusion.1, bf16[256,256]{1,0:T(8,128)(2,1)S(1)} %collective-permute-done.4, ...), kind=kOutput, calls=%fused_computation.34 | convolution fusion | flops 67895296 | bytes 2228741 | tf_op jit(solution)/shard_map/dot_general | solution.py:167
  (12 shorter events, 0.3 us)
Async XLA Ops:
  0.0 1.2 %copy-start.1 = (f32[256,512]{1,0:T(8,128)S(1)}, f32[256,512]{1,0:T(8,128)}, u32[]{:S(2)}) copy-start(f32[256,512]{1,0:T(8,128)} %param.1) | copy-start | bytes 1572868 | tf_op jit(solution)/shard_map/cond
  1.2 4.0 %collective-permute-start.7 = (bf16[256,512]{1,0:T(8,128)(2,1)S(1)}, bf16[256,512]{1,0:T(8,128)(2,1)S(1)}, u32[]{:S(2)}, u32[]{:S(2)}) collective-permute-start(bf16[256,512]{1,0:T(8,128)(2,1)S(1)} %get-tuple-element.22), channel_id=1, source_target_pairs={{1,17},{2,6},{0,4},{3,19}} | collective-permute-start | bytes 786440 | tf_op jit(solution)/shard_map/ppermute | solution.py:37
  1.9 4.4 %collective-permute-start = (f32[256,256]{1,0:T(8,128)S(1)}, f32[256,256]{1,0:T(8,128)S(1)}, u32[]{:S(2)}, u32[]{:S(2)}) collective-permute-start(f32[256,256]{1,0:T(8,128)S(1)} %get-tuple-element.19), channel_id=1, source_target_pairs={{0,20},{8,0},{12,4},{24,16}} | collective-permute-start | bytes 786440 | tf_op jit(solution)/shard_map/ppermute | solution.py:37
  2.6 5.7 %collective-permute-start.1 = (f32[256,256]{1,0:T(8,128)S(1)}, f32[256,256]{1,0:T(8,128)S(1)}, u32[]{:S(2)}, u32[]{:S(2)}) collective-permute-start(f32[256,256]{1,0:T(8,128)S(1)} %get-tuple-element.19), channel_id=1, source_target_pairs={{0,4},{28,20}} | collective-permute-start | bytes 786440 | tf_op jit(solution)/shard_map/ppermute | solution.py:37
  4.4 3.9 %collective-permute-start.2 = (f32[256,256]{1,0:T(8,128)S(1)}, f32[256,256]{1,0:T(8,128)S(1)}, u32[]{:S(2)}, u32[]{:S(2)}) collective-permute-start(f32[256,256]{1,0:T(8,128)S(1)} %get-tuple-element.19), channel_id=1, source_target_pairs={{0,16}} | collective-permute-start | bytes 786440 | tf_op jit(solution)/shard_map/ppermute | solution.py:37
  5.2 1.0 %copy-start = (f32[256,512]{1,0:T(8,128)S(1)}, f32[256,512]{1,0:T(8,128)}, u32[]{:S(2)}) copy-start(f32[256,512]{1,0:T(8,128)} %param.5) | copy-start | bytes 1572868
  5.3 5.8 %collective-permute-start.8 = (bf16[256,512]{1,0:T(8,128)(2,1)S(1)}, bf16[256,512]{1,0:T(8,128)(2,1)S(1)}, u32[]{:S(2)}, u32[]{:S(2)}) collective-permute-start(bf16[256,512]{1,0:T(8,128)(2,1)S(1)} %broadcast_select_fusion), channel_id=1, source_target_pairs={{17,21},{2,18},{6,22},{0,16},{4,20},{3,11},{19,27}} | collective-permute-start | bytes 786440 | tf_op jit(solution)/shard_map/ppermute | solution.py:37
  8.4 8.9 %collective-permute-start.5 = (bf16[256,256]{1,0:T(8,128)(2,1)S(1)}, bf16[256,256]{1,0:T(8,128)(2,1)S(1)}, u32[]{:S(2)}, u32[]{:S(2)}) collective-permute-start(bf16[256,256]{1,0:T(8,128)(2,1)S(1)} %get-tuple-element.21), channel_id=1, source_target_pairs={{0,8},{4,12},{16,24},{20,28}} | collective-permute-start | bytes 393224 | tf_op jit(solution)/shard_map/ppermute | solution.py:37
  9.7 3.4 %collective-permute-start.3 = (bf16[256,256]{1,0:T(8,128)(2,1)S(1)}, bf16[256,256]{1,0:T(8,128)(2,1)S(1)}, u32[]{:S(2)}, u32[]{:S(2)}) collective-permute-start(bf16[256,256]{1,0:T(8,128)(2,1)S(1)} %get-tuple-element.81), channel_id=1, source_target_pairs={{0,11},{4,15},{16,19},{20,31}} | collective-permute-start | bytes 393224 | tf_op jit(solution)/shard_map/ppermute | solution.py:37
  10.4 2.7 %collective-permute-start.4 = (bf16[256,256]{1,0:T(8,128)(2,1)S(1)}, bf16[256,256]{1,0:T(8,128)(2,1)S(1)}, u32[]{:S(2)}, u32[]{:S(2)}) collective-permute-start(bf16[256,256]{1,0:T(8,128)(2,1)S(1)} %get-tuple-element.82), channel_id=1, source_target_pairs={{20,23},{4,7},{16,27},{0,8}} | collective-permute-start | bytes 393224 | tf_op jit(solution)/shard_map/ppermute | solution.py:37
  11.1 13.9 %collective-permute-start.10 = (bf16[256,512]{1,0:T(8,128)(2,1)S(1)}, bf16[256,512]{1,0:T(8,128)(2,1)S(1)}, u32[]{:S(2)}, u32[]{:S(2)}) collective-permute-start(bf16[256,512]{1,0:T(8,128)(2,1)S(1)} %broadcast_select_fusion.1), channel_id=1, source_target_pairs={{17,25},{21,29},{1,5},{2,10},{6,14},{18,26},{22,30},{4,12},{16,28}... | collective-permute-start | bytes 786440 | tf_op jit(solution)/shard_map/ppermute | solution.py:37
  12.4 12.7 %collective-permute-start.9 = (bf16[256,512]{1,0:T(8,128)(2,1)S(1)}, bf16[256,512]{1,0:T(8,128)(2,1)S(1)}, u32[]{:S(2)}, u32[]{:S(2)}) collective-permute-start(bf16[256,512]{1,0:T(8,128)(2,1)S(1)} %broadcast_select_fusion.1), channel_id=1, source_target_pairs={{17,9},{21,13}} | collective-permute-start | bytes 786440 | tf_op jit(solution)/shard_map/ppermute | solution.py:37
  17.4 2.3 %collective-permute-start.6 = (bf16[256,256]{1,0:T(8,128)(2,1)S(1)}, bf16[256,256]{1,0:T(8,128)(2,1)S(1)}, u32[]{:S(2)}, u32[]{:S(2)}) collective-permute-start(bf16[256,256]{1,0:T(8,128)(2,1)S(1)} %select_select_fusion.2), channel_id=1, source_target_pairs={{4,5},{8,9},{12,13},{16,17},{20,21},{24,25},{28,29},{7,6},{11,10},... | collective-permute-start | bytes 393224 | tf_op jit(solution)/shard_map/ppermute | solution.py:37

commit v26 on v25

--- a/solution.py
+++ b/solution.py
@@ -81,9 +81,8 @@
             hops = [(h, h + stride) for h in held[kind]]
             pairs += [((a, c), (b, c)) for a, b in hops for c in range(2 + kind, n_col, 2)]
             if kind == 0:
-                if step == len(down) - 1:
-                    crossed = {middle: middle + APART + 1, middle + 1: middle + APART}
-                    hops = [(a, crossed.get(a, b)) for a, b in hops if a or not fits]
+                if step == len(down) - 1 and fits:
+                    hops = [(a, b if a else middle + APART) for a, b in hops if a != middle]
                 pairs += [((a, 0), (b, 0)) for a, b in hops]
             held[kind] = held[kind] + [h + stride for h in held[kind]]
         got = send(sent, pairs)

time: 26.5 us -> 28.8 us (1.087)
  the two profiles are of different devices: /device:TPU:26 before, /device:TPU:29 now
where the time goes in v26:
time: 28.8 us; the launch traced here: 28.5 us
  waiting for transfers between devices  16.6 us (58%)
  starting transfers between devices  10 us (35%)
  matrix products  1.12 us (4%)
  between operations  0.4 us (1%)
    ppermute x11, waiting for transfers between devices, send(): return lax.ppermute(value, ('row', 'col'), flat)  16.6 us
    ppermute x11, starting transfers between devices, send(): return lax.ppermute(value, ('row', 'col'), flat)  10 us
    dot_general x1, matrix products, shards(): return matrix - jnp.dot(received, upper, preferred_element_type=jnp.float32)  1.12 us
  transfers between devices with their start and end apart: 11, of which 3 were waited for; matrix products, arithmetic and copies ran while one was open for 1% of the time, Pallas kernels for 0%

profile of v26, /device:TPU:29, one launch (start us, length us, event | category | flops | bytes accessed | tf_op | source)
XLA Modules:
  0.0 28.5 jit_solution(2143606348963298594)
XLA Ops:
  0.0 0.1 conditional.2
  0.1 0.7 %collective-permute-start.7 = (bf16[256,512]{1,0:T(8,128)(2,1)S(1)}, bf16[256,512]{1,0:T(8,128)(2,1)S(1)}, u32[]{:S(2)}, u32[]{:S(2)}) collective-permute-start(bf16[256,512]{1,0:T(8,128)(2,1)S(1)} %get-tuple-element.22), channel_id=1, source_target_pairs={{1,17},{2,6},{0,4},{3,19}} | collective-permute-start | bytes 786440 | tf_op jit(solution)/shard_map/ppermute | solution.py:37
  0.7 0.7 %collective-permute-start = (f32[256,256]{1,0:T(8,128)S(1)}, f32[256,256]{1,0:T(8,128)S(1)}, u32[]{:S(2)}, u32[]{:S(2)}) collective-permute-start(f32[256,256]{1,0:T(8,128)S(1)} %get-tuple-element.19), channel_id=1, source_target_pairs={{0,20},{8,0},{12,4},{24,16}} | collective-permute-start | bytes 786440 | tf_op jit(solution)/shard_map/ppermute | solution.py:37
  1.4 0.7 %collective-permute-start.1 = (f32[256,256]{1,0:T(8,128)S(1)}, f32[256,256]{1,0:T(8,128)S(1)}, u32[]{:S(2)}, u32[]{:S(2)}) collective-permute-start(f32[256,256]{1,0:T(8,128)S(1)} %get-tuple-element.19), channel_id=1, source_target_pairs={{0,4},{28,20}} | collective-permute-start | bytes 786440 | tf_op jit(solution)/shard_map/ppermute | solution.py:37
  2.1 0.7 %collective-permute-start.2 = (f32[256,256]{1,0:T(8,128)S(1)}, f32[256,256]{1,0:T(8,128)S(1)}, u32[]{:S(2)}, u32[]{:S(2)}) collective-permute-start(f32[256,256]{1,0:T(8,128)S(1)} %get-tuple-element.19), channel_id=1, source_target_pairs={{0,16}} | collective-permute-start | bytes 786440 | tf_op jit(solution)/shard_map/ppermute | solution.py:37
  2.9 0.0 copy-start
  2.9 0.0 collective-permute-done.7
  2.9 1.4 %collective-permute-start.8 = (bf16[256,512]{1,0:T(8,128)(2,1)S(1)}, bf16[256,512]{1,0:T(8,128)(2,1)S(1)}, u32[]{:S(2)}, u32[]{:S(2)}) collective-permute-start(bf16[256,512]{1,0:T(8,128)(2,1)S(1)} %broadcast_select_fusion), channel_id=1, source_target_pairs={{17,21},{2,18},{6,22},{0,16},{4,20},{3,11},{19,27}} | collective-permute-start | bytes 786440 | tf_op jit(solution)/shard_map/ppermute | solution.py:37
  4.4 0.0 copy-done
  4.5 0.0 collective-permute-done
  4.5 0.0 collective-permute-done.1
  4.5 0.0 collective-permute-done.2
  4.6 0.1 conditional.3
  4.6 0.7 %collective-permute-start.5 = (bf16[256,256]{1,0:T(8,128)(2,1)S(1)}, bf16[256,256]{1,0:T(8,128)(2,1)S(1)}, u32[]{:S(2)}, u32[]{:S(2)}) collective-permute-start(bf16[256,256]{1,0:T(8,128)(2,1)S(1)} %get-tuple-element.21), channel_id=1, source_target_pairs={{0,8},{4,12},{16,24},{20,28}} | collective-permute-start | bytes 393224 | tf_op jit(solution)/shard_map/ppermute | solution.py:37
  5.3 0.7 %collective-permute-start.3 = (bf16[256,256]{1,0:T(8,128)(2,1)S(1)}, bf16[256,256]{1,0:T(8,128)(2,1)S(1)}, u32[]{:S(2)}, u32[]{:S(2)}) collective-permute-start(bf16[256,256]{1,0:T(8,128)(2,1)S(1)} %get-tuple-element.81), channel_id=1, source_target_pairs={{0,11},{4,15},{16,19},{20,31}} | collective-permute-start | bytes 393224 | tf_op jit(solution)/shard_map/ppermute | solution.py:37
  6.0 1.3 %collective-permute-start.4 = (bf16[256,256]{1,0:T(8,128)(2,1)S(1)}, bf16[256,256]{1,0:T(8,128)(2,1)S(1)}, u32[]{:S(2)}, u32[]{:S(2)}) collective-permute-start(bf16[256,256]{1,0:T(8,128)(2,1)S(1)} %get-tuple-element.82), channel_id=1, source_target_pairs={{20,23},{4,7},{16,27},{0,8}} | collective-permute-start | bytes 393224 | tf_op jit(solution)/shard_map/ppermute | solution.py:37
  7.3 6.0 %collective-permute-done.8 = bf16[256,512]{1,0:T(8,128)(2,1)S(1)} collective-permute-done((bf16[256,512]{1,0:T(8,128)(2,1)S(1)}, bf16[256,512]{1,0:T(8,128)(2,1)S(1)}, u32[]{:S(2)}, u32[]{:S(2)}) %collective-permute-start.8) | collective-permute-done | bytes 262176 | tf_op jit(solution)/shard_map/ppermute | solution.py:37
  13.3 1.3 %collective-permute-start.10 = (bf16[256,512]{1,0:T(8,128)(2,1)S(1)}, bf16[256,512]{1,0:T(8,128)(2,1)S(1)}, u32[]{:S(2)}, u32[]{:S(2)}) collective-permute-start(bf16[256,512]{1,0:T(8,128)(2,1)S(1)} %broadcast_select_fusion.1), channel_id=1, source_target_pairs={{17,25},{21,29},{1,5},{2,10},{6,14},{18,26},{22,30},{0,24},{4,12},... | collective-permute-start | bytes 786440 | tf_op jit(solution)/shard_map/ppermute | solution.py:37
  14.7 0.7 %collective-permute-start.9 = (bf16[256,512]{1,0:T(8,128)(2,1)S(1)}, bf16[256,512]{1,0:T(8,128)(2,1)S(1)}, u32[]{:S(2)}, u32[]{:S(2)}) collective-permute-start(bf16[256,512]{1,0:T(8,128)(2,1)S(1)} %broadcast_select_fusion.1), channel_id=1, source_target_pairs={{17,9},{21,13}} | collective-permute-start | bytes 786440 | tf_op jit(solution)/shard_map/ppermute | solution.py:37
  15.3 0.0 collective-permute-done.3
  15.4 9.7 %collective-permute-done.4 = bf16[256,256]{1,0:T(8,128)(2,1)S(1)} collective-permute-done((bf16[256,256]{1,0:T(8,128)(2,1)S(1)}, bf16[256,256]{1,0:T(8,128)(2,1)S(1)}, u32[]{:S(2)}, u32[]{:S(2)}) %collective-permute-start.4) | collective-permute-done | bytes 131104 | tf_op jit(solution)/shard_map/ppermute | solution.py:37
  25.0 0.0 collective-permute-done.5
  25.1 1.3 %collective-permute-start.6 = (bf16[256,256]{1,0:T(8,128)(2,1)S(1)}, bf16[256,256]{1,0:T(8,128)(2,1)S(1)}, u32[]{:S(2)}, u32[]{:S(2)}) collective-permute-start(bf16[256,256]{1,0:T(8,128)(2,1)S(1)} %select_select_fusion.2), channel_id=1, source_target_pairs={{4,5},{8,9},{12,13},{16,17},{20,21},{24,25},{28,29},{7,6},{11,10},... | collective-permute-start | bytes 393224 | tf_op jit(solution)/shard_map/ppermute | solution.py:37
  26.5 0.9 %collective-permute-done.6 = bf16[256,256]{1,0:T(8,128)(2,1)S(1)} collective-permute-done((bf16[256,256]{1,0:T(8,128)(2,1)S(1)}, bf16[256,256]{1,0:T(8,128)(2,1)S(1)}, u32[]{:S(2)}, u32[]{:S(2)}) %collective-permute-start.6) | collective-permute-done | bytes 131104 | tf_op jit(solution)/shard_map/ppermute | solution.py:37
  27.3 0.0 collective-permute-done.10
  27.3 0.0 collective-permute-done.9
  27.3 1.1 %convolution_subtract_fusion = f32[256,512]{1,0:T(8,128)} fusion(f32[256,512]{1,0:T(8,128)S(1)} %copy-done, bf16[256,512]{1,0:T(8,128)(2,1)S(1)} %collective-permute-done.9, bf16[256,512]{1,0:T(8,128)(2,1)S(1)} %collective-permute-done.10, bf16[256,512]{1,0:T(8,128)(2,1)S(1)} %broadcast_select_fusion.1, bf16[256,256]{1,0:T(8,128)(2,1)S(1)} %collective-permute-done.4, ...), kind=kOutput, calls=%fused_computation.34 | convolution fusion | flops 67895296 | bytes 2228741 | tf_op jit(solution)/shard_map/dot_general | solution.py:166
  (13 shorter events, 0.3 us)
Async XLA Ops:
  0.1 2.8 %collective-permute-start.7 = (bf16[256,512]{1,0:T(8,128)(2,1)S(1)}, bf16[256,512]{1,0:T(8,128)(2,1)S(1)}, u32[]{:S(2)}, u32[]{:S(2)}) collective-permute-start(bf16[256,512]{1,0:T(8,128)(2,1)S(1)} %get-tuple-element.22), channel_id=1, source_target_pairs={{1,17},{2,6},{0,4},{3,19}} | collective-permute-start | bytes 786440 | tf_op jit(solution)/shard_map/ppermute | solution.py:37
  0.7 3.7 %collective-permute-start = (f32[256,256]{1,0:T(8,128)S(1)}, f32[256,256]{1,0:T(8,128)S(1)}, u32[]{:S(2)}, u32[]{:S(2)}) collective-permute-start(f32[256,256]{1,0:T(8,128)S(1)} %get-tuple-element.19), channel_id=1, source_target_pairs={{0,20},{8,0},{12,4},{24,16}} | collective-permute-start | bytes 786440 | tf_op jit(solution)/shard_map/ppermute | solution.py:37
  1.4 3.1 %collective-permute-start.1 = (f32[256,256]{1,0:T(8,128)S(1)}, f32[256,256]{1,0:T(8,128)S(1)}, u32[]{:S(2)}, u32[]{:S(2)}) collective-permute-start(f32[256,256]{1,0:T(8,128)S(1)} %get-tuple-element.19), channel_id=1, source_target_pairs={{0,4},{28,20}} | collective-permute-start | bytes 786440 | tf_op jit(solution)/shard_map/ppermute | solution.py:37
  2.1 2.4 %collective-permute-start.2 = (f32[256,256]{1,0:T(8,128)S(1)}, f32[256,256]{1,0:T(8,128)S(1)}, u32[]{:S(2)}, u32[]{:S(2)}) collective-permute-start(f32[256,256]{1,0:T(8,128)S(1)} %get-tuple-element.19), channel_id=1, source_target_pairs={{0,16}} | collective-permute-start | bytes 786440 | tf_op jit(solution)/shard_map/ppermute | solution.py:37
  2.9 1.5 %copy-start = (f32[256,512]{1,0:T(8,128)S(1)}, f32[256,512]{1,0:T(8,128)}, u32[]{:S(2)}) copy-start(f32[256,512]{1,0:T(8,128)} %param.5) | copy-start | bytes 1572868
  2.9 10.4 %collective-permute-start.8 = (bf16[256,512]{1,0:T(8,128)(2,1)S(1)}, bf16[256,512]{1,0:T(8,128)(2,1)S(1)}, u32[]{:S(2)}, u32[]{:S(2)}) collective-permute-start(bf16[256,512]{1,0:T(8,128)(2,1)S(1)} %broadcast_select_fusion), channel_id=1, source_target_pairs={{17,21},{2,18},{6,22},{0,16},{4,20},{3,11},{19,27}} | collective-permute-start | bytes 786440 | tf_op jit(solution)/shard_map/ppermute | solution.py:37
  4.6 20.4 %collective-permute-start.5 = (bf16[256,256]{1,0:T(8,128)(2,1)S(1)}, bf16[256,256]{1,0:T(8,128)(2,1)S(1)}, u32[]{:S(2)}, u32[]{:S(2)}) collective-permute-start(bf16[256,256]{1,0:T(8,128)(2,1)S(1)} %get-tuple-element.21), channel_id=1, source_target_pairs={{0,8},{4,12},{16,24},{20,28}} | collective-permute-start | bytes 393224 | tf_op jit(solution)/shard_map/ppermute | solution.py:37
  5.3 10.0 %collective-permute-start.3 = (bf16[256,256]{1,0:T(8,128)(2,1)S(1)}, bf16[256,256]{1,0:T(8,128)(2,1)S(1)}, u32[]{:S(2)}, u32[]{:S(2)}) collective-permute-start(bf16[256,256]{1,0:T(8,128)(2,1)S(1)} %get-tuple-element.81), channel_id=1, source_target_pairs={{0,11},{4,15},{16,19},{20,31}} | collective-permute-start | bytes 393224 | tf_op jit(solution)/shard_map/ppermute | solution.py:37
  6.0 19.0 %collective-permute-start.4 = (bf16[256,256]{1,0:T(8,128)(2,1)S(1)}, bf16[256,256]{1,0:T(8,128)(2,1)S(1)}, u32[]{:S(2)}, u32[]{:S(2)}) collective-permute-start(bf16[256,256]{1,0:T(8,128)(2,1)S(1)} %get-tuple-element.82), channel_id=1, source_target_pairs={{20,23},{4,7},{16,27},{0,8}} | collective-permute-start | bytes 393224 | tf_op jit(solution)/shard_map/ppermute | solution.py:37
  13.3 14.0 %collective-permute-start.10 = (bf16[256,512]{1,0:T(8,128)(2,1)S(1)}, bf16[256,512]{1,0:T(8,128)(2,1)S(1)}, u32[]{:S(2)}, u32[]{:S(2)}) collective-permute-start(bf16[256,512]{1,0:T(8,128)(2,1)S(1)} %broadcast_select_fusion.1), channel_id=1, source_target_pairs={{17,25},{21,29},{1,5},{2,10},{6,14},{18,26},{22,30},{0,24},{4,12},... | collective-permute-start | bytes 786440 | tf_op jit(solution)/shard_map/ppermute | solution.py:37
  14.7 12.7 %collective-permute-start.9 = (bf16[256,512]{1,0:T(8,128)(2,1)S(1)}, bf16[256,512]{1,0:T(8,128)(2,1)S(1)}, u32[]{:S(2)}, u32[]{:S(2)}) collective-permute-start(bf16[256,512]{1,0:T(8,128)(2,1)S(1)} %broadcast_select_fusion.1), channel_id=1, source_target_pairs={{17,9},{21,13}} | collective-permute-start | bytes 786440 | tf_op jit(solution)/shard_map/ppermute | solution.py:37
  25.1 2.3 %collective-permute-start.6 = (bf16[256,256]{1,0:T(8,128)(2,1)S(1)}, bf16[256,256]{1,0:T(8,128)(2,1)S(1)}, u32[]{:S(2)}, u32[]{:S(2)}) collective-permute-start(bf16[256,256]{1,0:T(8,128)(2,1)S(1)} %select_select_fusion.2), channel_id=1, source_target_pairs={{4,5},{8,9},{12,13},{16,17},{20,21},{24,25},{28,29},{7,6},{11,10},... | collective-permute-start | bytes 393224 | tf_op jit(solution)/shard_map/ppermute | solution.py:37

commit v27 on v25

--- a/solution.py
+++ b/solution.py
@@ -106,7 +106,7 @@
     def compute(square, partner):
         both = multipliers(square, jnp.concatenate([matrix[:, :NB], partner], axis=0))
         both = both.astype(jnp.bfloat16)
-        return both[:NB], both[NB:]
+        return jnp.where(row_here == 0, jnp.zeros_like(both[:NB]), both[:NB]), both[NB:]
 
     def none(square, partner):
         zero = jnp.zeros((NB, NB), jnp.bfloat16)
@@ -157,7 +157,6 @@
         + [((r, c), (r, c - 1)) for r in range(1, n_row) for c in odd],
     )
     received = jnp.where((col_here == 0) | (col_here > 1) & (col_here % 2 == 1), received, got)
-    received = jnp.where(row_here == 0, jnp.zeros_like(received), received)
 
     if fits:
         relayed = jnp.pad(third_got, ((0, 0), (NB, 0)))

time: 26.5 us -> 26.5 us (level)
  no operation moved by 1% of the time
where the time goes in v27:
time: 26.5 us; the launch traced here: 26.2 us
  waiting for transfers between devices  12.7 us (48%)
  starting transfers between devices  10.6 us (40%)
  other arithmetic  1.29 us (5%)
  matrix products  1.11 us (4%)
  between operations  0.38 us (1%)
    ppermute x11, waiting for transfers between devices, send(): return lax.ppermute(value, ('row', 'col'), flat)  12.7 us
    ppermute x11, starting transfers between devices, send(): return lax.ppermute(value, ('row', 'col'), flat)  10.6 us
    convert_element_type x1, other arithmetic, blocks(): return (matrix[:, :NB], matrix.astype(jnp.bfloat16))  1.15 us
    dot_general x1, matrix products, shards(): return matrix - jnp.dot(received, upper, preferred_element_type=jnp.float32)  1.11 us
  transfers between devices with their start and end apart: 11, of which 4 were waited for; matrix products, arithmetic and copies ran while one was open for 1% of the time, Pallas kernels for 0%

profile of v27, /device:TPU:26, one launch (start us, length us, event | category | flops | bytes accessed | tf_op | source)
XLA Modules:
  0.0 26.2 jit_solution(6058776954030921128)
XLA Ops:
  0.0 1.2 %conditional.2 = (f32[256,256]{1,0:T(8,128)S(1)}, bf16[256,512]{1,0:T(8,128)(2,1)S(1)}) conditional(s32[]{:T(128)} %convert_element_type.18, () %tuple.22, f32[256,512]{1,0:T(8,128)} %param.5), branch_computations={%region_0.0_spmd, %region_1.0_spmd} | conditional | flops 131072 | bytes 3407916 | solution.py:46
  0.0 0.0 copy-start.1
  0.0 1.1 %convert_element_type.10 = bf16[256,512]{1,0:T(8,128)(2,1)S(1)} convert(f32[256,512]{1,0:T(8,128)} %param.1) | non-fusion elementwise | flops 131072 | bytes 786432 | tf_op jit(solution)/shard_map/cond/branch_1_fun/convert_element_type | solution.py:40
  1.2 0.0 copy-done.1
  1.2 0.7 %collective-permute-start.7 = (bf16[256,512]{1,0:T(8,128)(2,1)S(1)}, bf16[256,512]{1,0:T(8,128)(2,1)S(1)}, u32[]{:S(2)}, u32[]{:S(2)}) collective-permute-start(bf16[256,512]{1,0:T(8,128)(2,1)S(1)} %get-tuple-element.25), channel_id=1, source_target_pairs={{1,17},{2,6},{0,4},{3,19}} | collective-permute-start | bytes 786440 | tf_op jit(solution)/shard_map/ppermute | solution.py:37
  1.9 0.7 %collective-permute-start = (f32[256,256]{1,0:T(8,128)S(1)}, f32[256,256]{1,0:T(8,128)S(1)}, u32[]{:S(2)}, u32[]{:S(2)}) collective-permute-start(f32[256,256]{1,0:T(8,128)S(1)} %get-tuple-element.22), channel_id=1, source_target_pairs={{0,20},{8,0},{12,4},{24,16}} | collective-permute-start | bytes 786440 | tf_op jit(solution)/shard_map/ppermute | solution.py:37
  2.6 1.8 %collective-permute-start.1 = (f32[256,256]{1,0:T(8,128)S(1)}, f32[256,256]{1,0:T(8,128)S(1)}, u32[]{:S(2)}, u32[]{:S(2)}) collective-permute-start(f32[256,256]{1,0:T(8,128)S(1)} %get-tuple-element.22), channel_id=1, source_target_pairs={{0,4},{28,20}} | collective-permute-start | bytes 786440 | tf_op jit(solution)/shard_map/ppermute | solution.py:37
  4.4 0.7 %collective-permute-start.2 = (f32[256,256]{1,0:T(8,128)S(1)}, f32[256,256]{1,0:T(8,128)S(1)}, u32[]{:S(2)}, u32[]{:S(2)}) collective-permute-start(f32[256,256]{1,0:T(8,128)S(1)} %get-tuple-element.22), channel_id=1, source_target_pairs={{0,16}} | collective-permute-start | bytes 786440 | tf_op jit(solution)/shard_map/ppermute | solution.py:37
  5.2 0.0 copy-start
  5.2 0.0 collective-permute-done.7
  5.3 0.8 %collective-permute-start.8 = (bf16[256,512]{1,0:T(8,128)(2,1)S(1)}, bf16[256,512]{1,0:T(8,128)(2,1)S(1)}, u32[]{:S(2)}, u32[]{:S(2)}) collective-permute-start(bf16[256,512]{1,0:T(8,128)(2,1)S(1)} %broadcast_select_fusion), channel_id=1, source_target_pairs={{17,21},{2,18},{6,22},{0,16},{4,20},{3,11},{19,27}} | collective-permute-start | bytes 786440 | tf_op jit(solution)/shard_map/ppermute | solution.py:37
  6.1 0.0 collective-permute-done
  6.1 2.1 %collective-permute-done.1 = f32[256,256]{1,0:T(8,128)S(1)} collective-permute-done((f32[256,256]{1,0:T(8,128)S(1)}, f32[256,256]{1,0:T(8,128)S(1)}, u32[]{:S(2)}, u32[]{:S(2)}) %collective-permute-start.1) | collective-permute-done | bytes 262176 | tf_op jit(solution)/shard_map/ppermute | solution.py:37
  8.3 0.0 collective-permute-done.2
  8.3 0.0 copy-done
  8.3 0.1 conditional.3
  8.4 1.3 %collective-permute-start.5 = (bf16[256,256]{1,0:T(8,128)(2,1)S(1)}, bf16[256,256]{1,0:T(8,128)(2,1)S(1)}, u32[]{:S(2)}, u32[]{:S(2)}) collective-permute-start(bf16[256,256]{1,0:T(8,128)(2,1)S(1)} %get-tuple-element.24), channel_id=1, source_target_pairs={{0,8},{4,12},{16,24},{20,28}} | collective-permute-start | bytes 393224 | tf_op jit(solution)/shard_map/ppermute | solution.py:37
  9.7 0.7 %collective-permute-start.3 = (bf16[256,256]{1,0:T(8,128)(2,1)S(1)}, bf16[256,256]{1,0:T(8,128)(2,1)S(1)}, u32[]{:S(2)}, u32[]{:S(2)}) collective-permute-start(bf16[256,256]{1,0:T(8,128)(2,1)S(1)} %get-tuple-element.110), channel_id=1, source_target_pairs={{0,11},{4,15},{16,19},{20,31}} | collective-permute-start | bytes 393224 | tf_op jit(solution)/shard_map/ppermute | solution.py:37
  10.4 0.7 %collective-permute-start.4 = (bf16[256,256]{1,0:T(8,128)(2,1)S(1)}, bf16[256,256]{1,0:T(8,128)(2,1)S(1)}, u32[]{:S(2)}, u32[]{:S(2)}) collective-permute-start(bf16[256,256]{1,0:T(8,128)(2,1)S(1)} %get-tuple-element.111), channel_id=1, source_target_pairs={{20,23},{4,7},{16,27},{0,8}} | collective-permute-start | bytes 393224 | tf_op jit(solution)/shard_map/ppermute | solution.py:37
  11.1 0.0 collective-permute-done.8
  11.1 1.3 %collective-permute-start.10 = (bf16[256,512]{1,0:T(8,128)(2,1)S(1)}, bf16[256,512]{1,0:T(8,128)(2,1)S(1)}, u32[]{:S(2)}, u32[]{:S(2)}) collective-permute-start(bf16[256,512]{1,0:T(8,128)(2,1)S(1)} %broadcast_select_fusion.1), channel_id=1, source_target_pairs={{17,25},{21,29},{1,5},{2,10},{6,14},{18,26},{22,30},{4,12},{16,28}... | collective-permute-start | bytes 786440 | tf_op jit(solution)/shard_map/ppermute | solution.py:37
  12.4 0.7 %collective-permute-start.9 = (bf16[256,512]{1,0:T(8,128)(2,1)S(1)}, bf16[256,512]{1,0:T(8,128)(2,1)S(1)}, u32[]{:S(2)}, u32[]{:S(2)}) collective-permute-start(bf16[256,512]{1,0:T(8,128)(2,1)S(1)} %broadcast_select_fusion.1), channel_id=1, source_target_pairs={{17,9},{21,13}} | collective-permute-start | bytes 786440 | tf_op jit(solution)/shard_map/ppermute | solution.py:37
  13.1 0.0 collective-permute-done.3
  13.1 0.0 collective-permute-done.4
  13.1 4.1 %collective-permute-done.5 = bf16[256,256]{1,0:T(8,128)(2,1)S(1)} collective-permute-done((bf16[256,256]{1,0:T(8,128)(2,1)S(1)}, bf16[256,256]{1,0:T(8,128)(2,1)S(1)}, u32[]{:S(2)}, u32[]{:S(2)}) %collective-permute-start.5) | collective-permute-done | bytes 131104 | tf_op jit(solution)/shard_map/ppermute | solution.py:37
  17.3 1.3 %collective-permute-start.6 = (bf16[256,256]{1,0:T(8,128)(2,1)S(1)}, bf16[256,256]{1,0:T(8,128)(2,1)S(1)}, u32[]{:S(2)}, u32[]{:S(2)}) collective-permute-start(bf16[256,256]{1,0:T(8,128)(2,1)S(1)} %select_select_fusion.2), channel_id=1, source_target_pairs={{4,5},{8,9},{12,13},{16,17},{20,21},{24,25},{28,29},{7,6},{11,10},... | collective-permute-start | bytes 393224 | tf_op jit(solution)/shard_map/ppermute | solution.py:37
  18.7 0.9 %collective-permute-done.6 = bf16[256,256]{1,0:T(8,128)(2,1)S(1)} collective-permute-done((bf16[256,256]{1,0:T(8,128)(2,1)S(1)}, bf16[256,256]{1,0:T(8,128)(2,1)S(1)}, u32[]{:S(2)}, u32[]{:S(2)}) %collective-permute-start.6) | collective-permute-done | bytes 131104 | tf_op jit(solution)/shard_map/ppermute | solution.py:37
  19.6 5.5 %collective-permute-done.10 = bf16[256,512]{1,0:T(8,128)(2,1)S(1)} collective-permute-done((bf16[256,512]{1,0:T(8,128)(2,1)S(1)}, bf16[256,512]{1,0:T(8,128)(2,1)S(1)}, u32[]{:S(2)}, u32[]{:S(2)}) %collective-permute-start.10) | collective-permute-done | bytes 262176 | tf_op jit(solution)/shard_map/ppermute | solution.py:37
  25.1 0.0 collective-permute-done.9
  25.1 1.1 %convolution_subtract_fusion = f32[256,512]{1,0:T(8,128)} fusion(f32[256,512]{1,0:T(8,128)S(1)} %copy-done, bf16[256,512]{1,0:T(8,128)(2,1)S(1)} %collective-permute-done.9, bf16[256,512]{1,0:T(8,128)(2,1)S(1)} %collective-permute-done.10, bf16[256,512]{1,0:T(8,128)(2,1)S(1)} %broadcast_select_fusion.1, bf16[256,256]{1,0:T(8,128)(2,1)S(1)} %collective-permute-done.4, ...), kind=kOutput, calls=%fused_computation.35 | convolution fusion | flops 67829760 | bytes 2228740 | tf_op jit(solution)/shard_map/dot_general | solution.py:166
  (10 shorter events, 0.2 us)
Async XLA Ops:
  0.0 1.2 %copy-start.1 = (f32[256,512]{1,0:T(8,128)S(1)}, f32[256,512]{1,0:T(8,128)}, u32[]{:S(2)}) copy-start(f32[256,512]{1,0:T(8,128)} %param.1) | copy-start | bytes 1572868 | tf_op jit(solution)/shard_map/cond
  1.2 4.0 %collective-permute-start.7 = (bf16[256,512]{1,0:T(8,128)(2,1)S(1)}, bf16[256,512]{1,0:T(8,128)(2,1)S(1)}, u32[]{:S(2)}, u32[]{:S(2)}) collective-permute-start(bf16[256,512]{1,0:T(8,128)(2,1)S(1)} %get-tuple-element.25), channel_id=1, source_target_pairs={{1,17},{2,6},{0,4},{3,19}} | collective-permute-start | bytes 786440 | tf_op jit(solution)/shard_map/ppermute | solution.py:37
  1.9 4.2 %collective-permute-start = (f32[256,256]{1,0:T(8,128)S(1)}, f32[256,256]{1,0:T(8,128)S(1)}, u32[]{:S(2)}, u32[]{:S(2)}) collective-permute-start(f32[256,256]{1,0:T(8,128)S(1)} %get-tuple-element.22), channel_id=1, source_target_pairs={{0,20},{8,0},{12,4},{24,16}} | collective-permute-start | bytes 786440 | tf_op jit(solution)/shard_map/ppermute | solution.py:37
  2.6 5.7 %collective-permute-start.1 = (f32[256,256]{1,0:T(8,128)S(1)}, f32[256,256]{1,0:T(8,128)S(1)}, u32[]{:S(2)}, u32[]{:S(2)}) collective-permute-start(f32[256,256]{1,0:T(8,128)S(1)} %get-tuple-element.22), channel_id=1, source_target_pairs={{0,4},{28,20}} | collective-permute-start | bytes 786440 | tf_op jit(solution)/shard_map/ppermute | solution.py:37
  4.4 3.9 %collective-permute-start.2 = (f32[256,256]{1,0:T(8,128)S(1)}, f32[256,256]{1,0:T(8,128)S(1)}, u32[]{:S(2)}, u32[]{:S(2)}) collective-permute-start(f32[256,256]{1,0:T(8,128)S(1)} %get-tuple-element.22), channel_id=1, source_target_pairs={{0,16}} | collective-permute-start | bytes 786440 | tf_op jit(solution)/shard_map/ppermute | solution.py:37
  5.2 3.1 %copy-start = (f32[256,512]{1,0:T(8,128)S(1)}, f32[256,512]{1,0:T(8,128)}, u32[]{:S(2)}) copy-start(f32[256,512]{1,0:T(8,128)} %param.5) | copy-start | bytes 1572868
  5.3 5.8 %collective-permute-start.8 = (bf16[256,512]{1,0:T(8,128)(2,1)S(1)}, bf16[256,512]{1,0:T(8,128)(2,1)S(1)}, u32[]{:S(2)}, u32[]{:S(2)}) collective-permute-start(bf16[256,512]{1,0:T(8,128)(2,1)S(1)} %broadcast_select_fusion), channel_id=1, source_target_pairs={{17,21},{2,18},{6,22},{0,16},{4,20},{3,11},{19,27}} | collective-permute-start | bytes 786440 | tf_op jit(solution)/shard_map/ppermute | solution.py:37
  8.4 8.9 %collective-permute-start.5 = (bf16[256,256]{1,0:T(8,128)(2,1)S(1)}, bf16[256,256]{1,0:T(8,128)(2,1)S(1)}, u32[]{:S(2)}, u32[]{:S(2)}) collective-permute-start(bf16[256,256]{1,0:T(8,128)(2,1)S(1)} %get-tuple-element.24), channel_id=1, source_target_pairs={{0,8},{4,12},{16,24},{20,28}} | collective-permute-start | bytes 393224 | tf_op jit(solution)/shard_map/ppermute | solution.py:37
  9.7 3.4 %collective-permute-start.3 = (bf16[256,256]{1,0:T(8,128)(2,1)S(1)}, bf16[256,256]{1,0:T(8,128)(2,1)S(1)}, u32[]{:S(2)}, u32[]{:S(2)}) collective-permute-start(bf16[256,256]{1,0:T(8,128)(2,1)S(1)} %get-tuple-element.110), channel_id=1, source_target_pairs={{0,11},{4,15},{16,19},{20,31}} | collective-permute-start | bytes 393224 | tf_op jit(solution)/shard_map/ppermute | solution.py:37
  10.4 2.7 %collective-permute-start.4 = (bf16[256,256]{1,0:T(8,128)(2,1)S(1)}, bf16[256,256]{1,0:T(8,128)(2,1)S(1)}, u32[]{:S(2)}, u32[]{:S(2)}) collective-permute-start(bf16[256,256]{1,0:T(8,128)(2,1)S(1)} %get-tuple-element.111), channel_id=1, source_target_pairs={{20,23},{4,7},{16,27},{0,8}} | collective-permute-start | bytes 393224 | tf_op jit(solution)/shard_map/ppermute | solution.py:37
  11.1 13.9 %collective-permute-start.10 = (bf16[256,512]{1,0:T(8,128)(2,1)S(1)}, bf16[256,512]{1,0:T(8,128)(2,1)S(1)}, u32[]{:S(2)}, u32[]{:S(2)}) collective-permute-start(bf16[256,512]{1,0:T(8,128)(2,1)S(1)} %broadcast_select_fusion.1), channel_id=1, source_target_pairs={{17,25},{21,29},{1,5},{2,10},{6,14},{18,26},{22,30},{4,12},{16,28}... | collective-permute-start | bytes 786440 | tf_op jit(solution)/shard_map/ppermute | solution.py:37
  12.4 12.6 %collective-permute-start.9 = (bf16[256,512]{1,0:T(8,128)(2,1)S(1)}, bf16[256,512]{1,0:T(8,128)(2,1)S(1)}, u32[]{:S(2)}, u32[]{:S(2)}) collective-permute-start(bf16[256,512]{1,0:T(8,128)(2,1)S(1)} %broadcast_select_fusion.1), channel_id=1, source_target_pairs={{17,9},{21,13}} | collective-permute-start | bytes 786440 | tf_op jit(solution)/shard_map/ppermute | solution.py:37
  17.3 2.3 %collective-permute-start.6 = (bf16[256,256]{1,0:T(8,128)(2,1)S(1)}, bf16[256,256]{1,0:T(8,128)(2,1)S(1)}, u32[]{:S(2)}, u32[]{:S(2)}) collective-permute-start(bf16[256,256]{1,0:T(8,128)(2,1)S(1)} %select_select_fusion.2), channel_id=1, source_target_pairs={{4,5},{8,9},{12,13},{16,17},{20,21},{24,25},{28,29},{7,6},{11,10},... | collective-permute-start | bytes 393224 | tf_op jit(solution)/shard_map/ppermute | solution.py:37

commit v28 on v27

--- a/solution.py
+++ b/solution.py
@@ -52,8 +52,6 @@
     middle = n_row // 2
     orders = [[down[-1]] + down[:-1], down]
     held = [[0], [0]]
-    fits = cols_dev == 2 * NB
-    row_upper = upper[:, NB:]
     beside_steps = [[(0, middle)], [(middle, middle + 1)]]
     for stride in down[1:-1]:
         far = [b for step in beside_steps for _, b in step]
@@ -83,7 +81,7 @@
             if kind == 0:
                 if step == len(down) - 1:
                     crossed = {middle: middle + APART + 1, middle + 1: middle + APART}
-                    hops = [(a, crossed.get(a, b)) for a, b in hops if a or not fits]
+                    hops = [(a, crossed.get(a, b)) for a, b in hops]
                 pairs += [((a, 0), (b, 0)) for a, b in hops]
             held[kind] = held[kind] + [h + stride for h in held[kind]]
         got = send(sent, pairs)
@@ -127,11 +125,7 @@
 
     def send_own(c):
         sent = jnp.where(row_here == middle, lower_far, lower)
-        pairs = route(targets, c, True)
-        if fits and c == 3:
-            sent = jnp.where(row_here == 0, row_upper, sent)
-            pairs += [((0, 0), (APART, 0))]
-        return send(sent, pairs), (~far != swapped) & (col_here == c)
+        return send(sent, route(targets, c, True)), (~far != swapped) & (col_here == c)
 
     def send_near(c):
         pairs = [((r, 0), (r + APART, 0)) for r in workers]
@@ -142,8 +136,6 @@
         for c in columns:
             got, takes = step(c)
             received = jnp.where(takes, got, received)
-            if step is send_own and c == 3:
-                third_got = got
     sent = upper
     for step in range(2, len(down)):
         upper = upper_step(upper, step, upper)
@@ -158,9 +150,6 @@
     )
     received = jnp.where((col_here == 0) | (col_here > 1) & (col_here % 2 == 1), received, got)
 
-    if fits:
-        relayed = jnp.pad(third_got, ((0, 0), (NB, 0)))
-        upper = jnp.where((row_here == APART) & (col_here == 0), relayed, upper)
     col_done = col_here * cols_dev + jnp.arange(cols_dev, dtype=jnp.int32) < NB
     upper = jnp.where(col_done[None, :], jnp.zeros_like(upper), upper)
     return matrix - jnp.dot(received, upper, preferred_element_type=jnp.float32)

time: 26.5 us -> 26.4 us (level)
  no operation moved by 1% of the time
where the time goes in v28:
time: 26.4 us; the launch traced here: 26.1 us
  waiting for transfers between devices  12.7 us (48%)
  starting transfers between devices  10.6 us (40%)
  other arithmetic  1.31 us (5%)
  matrix products  1.03 us (4%)
  between operations  0.37 us (1%)
    ppermute x11, waiting for transfers between devices, send(): return lax.ppermute(value, ('row', 'col'), flat)  12.7 us
    ppermute x11, starting transfers between devices, send(): return lax.ppermute(value, ('row', 'col'), flat)  10.6 us
    convert_element_type x1, other arithmetic, blocks(): return (matrix[:, :NB], matrix.astype(jnp.bfloat16))  1.15 us
    dot_general x1, matrix products, shards(): return matrix - jnp.dot(received, upper, preferred_element_type=jnp.float32)  1.03 us
  transfers between devices with their start and end apart: 11, of which 4 were waited for; matrix products, arithmetic and copies ran while one was open for 1% of the time, Pallas kernels for 0%

profile of v28, /device:TPU:26, one launch (start us, length us, event | category | flops | bytes accessed | tf_op | source)
XLA Modules:
  0.0 26.1 jit_solution(3631174413897633219)
XLA Ops:
  0.0 1.2 %conditional.2 = (f32[256,256]{1,0:T(8,128)S(1)}, bf16[256,512]{1,0:T(8,128)(2,1)S(1)}) conditional(s32[]{:T(128)} %convert_element_type.16, () %tuple.22, f32[256,512]{1,0:T(8,128)} %param.5), branch_computations={%region_0.0_spmd, %region_1.0_spmd} | conditional | flops 131072 | bytes 3407916 | solution.py:46
  0.0 0.0 copy-start.1
  0.0 1.1 %convert_element_type.1 = bf16[256,512]{1,0:T(8,128)(2,1)S(1)} convert(f32[256,512]{1,0:T(8,128)} %param.1) | non-fusion elementwise | flops 131072 | bytes 786432 | tf_op jit(solution)/shard_map/cond/branch_1_fun/convert_element_type | solution.py:40
  1.2 0.0 copy-done.1
  1.2 0.7 %collective-permute-start.7 = (bf16[256,512]{1,0:T(8,128)(2,1)S(1)}, bf16[256,512]{1,0:T(8,128)(2,1)S(1)}, u32[]{:S(2)}, u32[]{:S(2)}) collective-permute-start(bf16[256,512]{1,0:T(8,128)(2,1)S(1)} %get-tuple-element.25), channel_id=1, source_target_pairs={{1,17},{2,6},{0,4},{3,19}} | collective-permute-start | bytes 786440 | tf_op jit(solution)/shard_map/ppermute | solution.py:37
  1.9 0.7 %collective-permute-start = (f32[256,256]{1,0:T(8,128)S(1)}, f32[256,256]{1,0:T(8,128)S(1)}, u32[]{:S(2)}, u32[]{:S(2)}) collective-permute-start(f32[256,256]{1,0:T(8,128)S(1)} %get-tuple-element.22), channel_id=1, source_target_pairs={{0,20},{8,0},{12,4},{24,16}} | collective-permute-start | bytes 786440 | tf_op jit(solution)/shard_map/ppermute | solution.py:37
  2.6 1.8 %collective-permute-start.1 = (f32[256,256]{1,0:T(8,128)S(1)}, f32[256,256]{1,0:T(8,128)S(1)}, u32[]{:S(2)}, u32[]{:S(2)}) collective-permute-start(f32[256,256]{1,0:T(8,128)S(1)} %get-tuple-element.22), channel_id=1, source_target_pairs={{0,4},{28,20}} | collective-permute-start | bytes 786440 | tf_op jit(solution)/shard_map/ppermute | solution.py:37
  4.4 0.7 %collective-permute-start.2 = (f32[256,256]{1,0:T(8,128)S(1)}, f32[256,256]{1,0:T(8,128)S(1)}, u32[]{:S(2)}, u32[]{:S(2)}) collective-permute-start(f32[256,256]{1,0:T(8,128)S(1)} %get-tuple-element.22), channel_id=1, source_target_pairs={{0,16}} | collective-permute-start | bytes 786440 | tf_op jit(solution)/shard_map/ppermute | solution.py:37
  5.2 0.0 copy-start
  5.2 0.0 collective-permute-done.7
  5.2 0.8 %collective-permute-start.8 = (bf16[256,512]{1,0:T(8,128)(2,1)S(1)}, bf16[256,512]{1,0:T(8,128)(2,1)S(1)}, u32[]{:S(2)}, u32[]{:S(2)}) collective-permute-start(bf16[256,512]{1,0:T(8,128)(2,1)S(1)} %broadcast_select_fusion.1), channel_id=1, source_target_pairs={{17,21},{2,18},{6,22},{0,16},{4,20},{3,11},{19,27}} | collective-permute-start | bytes 786440 | tf_op jit(solution)/shard_map/ppermute | solution.py:37
  6.1 0.0 collective-permute-done
  6.1 2.1 %collective-permute-done.1 = f32[256,256]{1,0:T(8,128)S(1)} collective-permute-done((f32[256,256]{1,0:T(8,128)S(1)}, f32[256,256]{1,0:T(8,128)S(1)}, u32[]{:S(2)}, u32[]{:S(2)}) %collective-permute-start.1) | collective-permute-done | bytes 262176 | tf_op jit(solution)/shard_map/ppermute | solution.py:37
  8.3 0.0 collective-permute-done.2
  8.3 0.0 copy-done
  8.3 0.1 conditional.3
  8.4 1.3 %collective-permute-start.5 = (bf16[256,256]{1,0:T(8,128)(2,1)S(1)}, bf16[256,256]{1,0:T(8,128)(2,1)S(1)}, u32[]{:S(2)}, u32[]{:S(2)}) collective-permute-start(bf16[256,256]{1,0:T(8,128)(2,1)S(1)} %get-tuple-element.24), channel_id=1, source_target_pairs={{0,8},{4,12},{16,24},{20,28}} | collective-permute-start | bytes 393224 | tf_op jit(solution)/shard_map/ppermute | solution.py:37
  9.7 0.7 %collective-permute-start.3 = (bf16[256,256]{1,0:T(8,128)(2,1)S(1)}, bf16[256,256]{1,0:T(8,128)(2,1)S(1)}, u32[]{:S(2)}, u32[]{:S(2)}) collective-permute-start(bf16[256,256]{1,0:T(8,128)(2,1)S(1)} %get-tuple-element.111), channel_id=1, source_target_pairs={{0,11},{4,15},{16,19},{20,31}} | collective-permute-start | bytes 393224 | tf_op jit(solution)/shard_map/ppermute | solution.py:37
  10.4 0.7 %collective-permute-start.4 = (bf16[256,256]{1,0:T(8,128)(2,1)S(1)}, bf16[256,256]{1,0:T(8,128)(2,1)S(1)}, u32[]{:S(2)}, u32[]{:S(2)}) collective-permute-start(bf16[256,256]{1,0:T(8,128)(2,1)S(1)} %get-tuple-element.110), channel_id=1, source_target_pairs={{20,23},{4,7},{16,27}} | collective-permute-start | bytes 393224 | tf_op jit(solution)/shard_map/ppermute | solution.py:37
  11.1 0.0 collective-permute-done.8
  11.1 1.3 %collective-permute-start.10 = (bf16[256,512]{1,0:T(8,128)(2,1)S(1)}, bf16[256,512]{1,0:T(8,128)(2,1)S(1)}, u32[]{:S(2)}, u32[]{:S(2)}) collective-permute-start(bf16[256,512]{1,0:T(8,128)(2,1)S(1)} %broadcast_select_fusion.2), channel_id=1, source_target_pairs={{17,25},{21,29},{1,5},{2,10},{6,14},{18,26},{22,30},{0,8},{4,12},{... | collective-permute-start | bytes 786440 | tf_op jit(solution)/shard_map/ppermute | solution.py:37
  12.4 0.7 %collective-permute-start.9 = (bf16[256,512]{1,0:T(8,128)(2,1)S(1)}, bf16[256,512]{1,0:T(8,128)(2,1)S(1)}, u32[]{:S(2)}, u32[]{:S(2)}) collective-permute-start(bf16[256,512]{1,0:T(8,128)(2,1)S(1)} %broadcast_select_fusion.2), channel_id=1, source_target_pairs={{17,9},{21,13}} | collective-permute-start | bytes 786440 | tf_op jit(solution)/shard_map/ppermute | solution.py:37
  13.1 0.0 collective-permute-done.3
  13.1 0.0 collective-permute-done.4
  13.1 4.1 %collective-permute-done.5 = bf16[256,256]{1,0:T(8,128)(2,1)S(1)} collective-permute-done((bf16[256,256]{1,0:T(8,128)(2,1)S(1)}, bf16[256,256]{1,0:T(8,128)(2,1)S(1)}, u32[]{:S(2)}, u32[]{:S(2)}) %collective-permute-start.5) | collective-permute-done | bytes 131104 | tf_op jit(solution)/shard_map/ppermute | solution.py:37
  17.3 1.3 %collective-permute-start.6 = (bf16[256,256]{1,0:T(8,128)(2,1)S(1)}, bf16[256,256]{1,0:T(8,128)(2,1)S(1)}, u32[]{:S(2)}, u32[]{:S(2)}) collective-permute-start(bf16[256,256]{1,0:T(8,128)(2,1)S(1)} %select_select_fusion.2), channel_id=1, source_target_pairs={{4,5},{8,9},{12,13},{16,17},{20,21},{24,25},{28,29},{7,6},{11,10},... | collective-permute-start | bytes 393224 | tf_op jit(solution)/shard_map/ppermute | solution.py:37
  18.7 0.9 %collective-permute-done.6 = bf16[256,256]{1,0:T(8,128)(2,1)S(1)} collective-permute-done((bf16[256,256]{1,0:T(8,128)(2,1)S(1)}, bf16[256,256]{1,0:T(8,128)(2,1)S(1)}, u32[]{:S(2)}, u32[]{:S(2)}) %collective-permute-start.6) | collective-permute-done | bytes 131104 | tf_op jit(solution)/shard_map/ppermute | solution.py:37
  19.6 5.5 %collective-permute-done.10 = bf16[256,512]{1,0:T(8,128)(2,1)S(1)} collective-permute-done((bf16[256,512]{1,0:T(8,128)(2,1)S(1)}, bf16[256,512]{1,0:T(8,128)(2,1)S(1)}, u32[]{:S(2)}, u32[]{:S(2)}) %collective-permute-start.10) | collective-permute-done | bytes 262176 | tf_op jit(solution)/shard_map/ppermute | solution.py:37
  25.1 0.0 collective-permute-done.9
  25.1 1.0 %convolution_subtract_fusion = f32[256,512]{1,0:T(8,128)} fusion(f32[256,512]{1,0:T(8,128)S(1)} %copy-done, bf16[256,512]{1,0:T(8,128)(2,1)S(1)} %collective-permute-done.9, bf16[256,512]{1,0:T(8,128)(2,1)S(1)} %collective-permute-done.10, bf16[256,512]{1,0:T(8,128)(2,1)S(1)} %broadcast_select_fusion.2, pred[]{:T(512)S(6)} %or.43, pred[]{:T(512)S(6)} %and.99, ...), kind=kOutput, calls=%fused_computation.35 | convolution fusion | flops 67698688 | bytes 2097667 | tf_op jit(solution)/shard_map/dot_general | solution.py:155
  (10 shorter events, 0.2 us)
Async XLA Ops:
  0.0 1.2 %copy-start.1 = (f32[256,512]{1,0:T(8,128)S(1)}, f32[256,512]{1,0:T(8,128)}, u32[]{:S(2)}) copy-start(f32[256,512]{1,0:T(8,128)} %param.1) | copy-start | bytes 1572868 | tf_op jit(solution)/shard_map/cond
  1.2 4.0 %collective-permute-start.7 = (bf16[256,512]{1,0:T(8,128)(2,1)S(1)}, bf16[256,512]{1,0:T(8,128)(2,1)S(1)}, u32[]{:S(2)}, u32[]{:S(2)}) collective-permute-start(bf16[256,512]{1,0:T(8,128)(2,1)S(1)} %get-tuple-element.25), channel_id=1, source_target_pairs={{1,17},{2,6},{0,4},{3,19}} | collective-permute-start | bytes 786440 | tf_op jit(solution)/shard_map/ppermute | solution.py:37
  1.9 4.2 %collective-permute-start = (f32[256,256]{1,0:T(8,128)S(1)}, f32[256,256]{1,0:T(8,128)S(1)}, u32[]{:S(2)}, u32[]{:S(2)}) collective-permute-start(f32[256,256]{1,0:T(8,128)S(1)} %get-tuple-element.22), channel_id=1, source_target_pairs={{0,20},{8,0},{12,4},{24,16}} | collective-permute-start | bytes 786440 | tf_op jit(solution)/shard_map/ppermute | solution.py:37
  2.6 5.7 %collective-permute-start.1 = (f32[256,256]{1,0:T(8,128)S(1)}, f32[256,256]{1,0:T(8,128)S(1)}, u32[]{:S(2)}, u32[]{:S(2)}) collective-permute-start(f32[256,256]{1,0:T(8,128)S(1)} %get-tuple-element.22), channel_id=1, source_target_pairs={{0,4},{28,20}} | collective-permute-start | bytes 786440 | tf_op jit(solution)/shard_map/ppermute | solution.py:37
  4.4 3.9 %collective-permute-start.2 = (f32[256,256]{1,0:T(8,128)S(1)}, f32[256,256]{1,0:T(8,128)S(1)}, u32[]{:S(2)}, u32[]{:S(2)}) collective-permute-start(f32[256,256]{1,0:T(8,128)S(1)} %get-tuple-element.22), channel_id=1, source_target_pairs={{0,16}} | collective-permute-start | bytes 786440 | tf_op jit(solution)/shard_map/ppermute | solution.py:37
  5.2 3.1 %copy-start = (f32[256,512]{1,0:T(8,128)S(1)}, f32[256,512]{1,0:T(8,128)}, u32[]{:S(2)}) copy-start(f32[256,512]{1,0:T(8,128)} %param.5) | copy-start | bytes 1572868
  5.2 5.8 %collective-permute-start.8 = (bf16[256,512]{1,0:T(8,128)(2,1)S(1)}, bf16[256,512]{1,0:T(8,128)(2,1)S(1)}, u32[]{:S(2)}, u32[]{:S(2)}) collective-permute-start(bf16[256,512]{1,0:T(8,128)(2,1)S(1)} %broadcast_select_fusion.1), channel_id=1, source_target_pairs={{17,21},{2,18},{6,22},{0,16},{4,20},{3,11},{19,27}} | collective-permute-start | bytes 786440 | tf_op jit(solution)/shard_map/ppermute | solution.py:37
  8.4 8.9 %collective-permute-start.5 = (bf16[256,256]{1,0:T(8,128)(2,1)S(1)}, bf16[256,256]{1,0:T(8,128)(2,1)S(1)}, u32[]{:S(2)}, u32[]{:S(2)}) collective-permute-start(bf16[256,256]{1,0:T(8,128)(2,1)S(1)} %get-tuple-element.24), channel_id=1, source_target_pairs={{0,8},{4,12},{16,24},{20,28}} | collective-permute-start | bytes 393224 | tf_op jit(solution)/shard_map/ppermute | solution.py:37
  9.7 3.4 %collective-permute-start.3 = (bf16[256,256]{1,0:T(8,128)(2,1)S(1)}, bf16[256,256]{1,0:T(8,128)(2,1)S(1)}, u32[]{:S(2)}, u32[]{:S(2)}) collective-permute-start(bf16[256,256]{1,0:T(8,128)(2,1)S(1)} %get-tuple-element.111), channel_id=1, source_target_pairs={{0,11},{4,15},{16,19},{20,31}} | collective-permute-start | bytes 393224 | tf_op jit(solution)/shard_map/ppermute | solution.py:37
  10.4 2.7 %collective-permute-start.4 = (bf16[256,256]{1,0:T(8,128)(2,1)S(1)}, bf16[256,256]{1,0:T(8,128)(2,1)S(1)}, u32[]{:S(2)}, u32[]{:S(2)}) collective-permute-start(bf16[256,256]{1,0:T(8,128)(2,1)S(1)} %get-tuple-element.110), channel_id=1, source_target_pairs={{20,23},{4,7},{16,27}} | collective-permute-start | bytes 393224 | tf_op jit(solution)/shard_map/ppermute | solution.py:37
  11.1 13.9 %collective-permute-start.10 = (bf16[256,512]{1,0:T(8,128)(2,1)S(1)}, bf16[256,512]{1,0:T(8,128)(2,1)S(1)}, u32[]{:S(2)}, u32[]{:S(2)}) collective-permute-start(bf16[256,512]{1,0:T(8,128)(2,1)S(1)} %broadcast_select_fusion.2), channel_id=1, source_target_pairs={{17,25},{21,29},{1,5},{2,10},{6,14},{18,26},{22,30},{0,8},{4,12},{... | collective-permute-start | bytes 786440 | tf_op jit(solution)/shard_map/ppermute | solution.py:37
  12.4 12.6 %collective-permute-start.9 = (bf16[256,512]{1,0:T(8,128)(2,1)S(1)}, bf16[256,512]{1,0:T(8,128)(2,1)S(1)}, u32[]{:S(2)}, u32[]{:S(2)}) collective-permute-start(bf16[256,512]{1,0:T(8,128)(2,1)S(1)} %broadcast_select_fusion.2), channel_id=1, source_target_pairs={{17,9},{21,13}} | collective-permute-start | bytes 786440 | tf_op jit(solution)/shard_map/ppermute | solution.py:37
  17.3 2.3 %collective-permute-start.6 = (bf16[256,256]{1,0:T(8,128)(2,1)S(1)}, bf16[256,256]{1,0:T(8,128)(2,1)S(1)}, u32[]{:S(2)}, u32[]{:S(2)}) collective-permute-start(bf16[256,256]{1,0:T(8,128)(2,1)S(1)} %select_select_fusion.2), channel_id=1, source_target_pairs={{4,5},{8,9},{12,13},{16,17},{20,21},{24,25},{28,29},{7,6},{11,10},... | collective-permute-start | bytes 393224 | tf_op jit(solution)/shard_map/ppermute | solution.py:37

commit v29 on v28

--- a/solution.py
+++ b/solution.py
@@ -88,8 +88,7 @@
         return jnp.where(takes, got, value)
 
     workers = [r for r in range(n_row) if r & APART == 0]
-    targets = workers[:1:-1]
-    targets.insert(1, 1)
+    targets = workers[:0:-1]
     square, partner = matrix[:, :NB], matrix[:, :NB]
     upper = upper_step(upper, 0, first_upper)
     for index, target in reversed(list(enumerate(targets))):

time: 26.4 us -> 26.8 us (1.015)
  the two profiles are of different devices: /device:TPU:26 before, /device:TPU:10 now
where the time goes in v29:
time: 26.8 us; the launch traced here: 26.5 us
  waiting for transfers between devices  13.1 us (49%)
  starting transfers between devices  10.6 us (40%)
  other arithmetic  1.3 us (5%)
  matrix products  1.03 us (4%)
  between operations  0.35 us (1%)
    ppermute x11, waiting for transfers between devices, send(): return lax.ppermute(value, ('row', 'col'), flat)  13.1 us
    ppermute x11, starting transfers between devices, send(): return lax.ppermute(value, ('row', 'col'), flat)  10.6 us
    convert_element_type x1, other arithmetic, blocks(): return (matrix[:, :NB], matrix.astype(jnp.bfloat16))  1.15 us
    dot_general x1, matrix products, shards(): return matrix - jnp.dot(received, upper, preferred_element_type=jnp.float32)  1.03 us
  transfers between devices with their start and end apart: 11, of which 4 were waited for; matrix products, arithmetic and copies ran while one was open for 1% of the time, Pallas kernels for 0%

profile of v29, /device:TPU:10, one launch (start us, length us, event | category | flops | bytes accessed | tf_op | source)
XLA Modules:
  0.0 26.5 jit_solution(4620229577100661868)
XLA Ops:
  0.0 1.2 %conditional.2 = (f32[256,256]{1,0:T(8,128)S(1)}, bf16[256,512]{1,0:T(8,128)(2,1)S(1)}) conditional(s32[]{:T(128)} %convert_element_type.16, () %tuple.22, f32[256,512]{1,0:T(8,128)} %param.5), branch_computations={%region_0.0_spmd, %region_1.0_spmd} | conditional | flops 131072 | bytes 3407916 | solution.py:46
  0.0 0.0 copy-start.1
  0.0 1.1 %convert_element_type.1 = bf16[256,512]{1,0:T(8,128)(2,1)S(1)} convert(f32[256,512]{1,0:T(8,128)} %param.1) | non-fusion elementwise | flops 131072 | bytes 786432 | tf_op jit(solution)/shard_map/cond/branch_1_fun/convert_element_type | solution.py:40
  1.2 0.0 copy-done.1
  1.2 0.7 %collective-permute-start.7 = (bf16[256,512]{1,0:T(8,128)(2,1)S(1)}, bf16[256,512]{1,0:T(8,128)(2,1)S(1)}, u32[]{:S(2)}, u32[]{:S(2)}) collective-permute-start(bf16[256,512]{1,0:T(8,128)(2,1)S(1)} %get-tuple-element.25), channel_id=1, source_target_pairs={{1,17},{2,6},{0,4},{3,19}} | collective-permute-start | bytes 786440 | tf_op jit(solution)/shard_map/ppermute | solution.py:37
  1.9 1.8 %collective-permute-start = (f32[256,256]{1,0:T(8,128)S(1)}, f32[256,256]{1,0:T(8,128)S(1)}, u32[]{:S(2)}, u32[]{:S(2)}) collective-permute-start(f32[256,256]{1,0:T(8,128)S(1)} %get-tuple-element.22), channel_id=1, source_target_pairs={{0,20},{8,0},{24,16},{12,4}} | collective-permute-start | bytes 786440 | tf_op jit(solution)/shard_map/ppermute | solution.py:37
  3.7 0.7 %collective-permute-start.1 = (f32[256,256]{1,0:T(8,128)S(1)}, f32[256,256]{1,0:T(8,128)S(1)}, u32[]{:S(2)}, u32[]{:S(2)}) collective-permute-start(f32[256,256]{1,0:T(8,128)S(1)} %get-tuple-element.22), channel_id=1, source_target_pairs={{0,16},{28,20}} | collective-permute-start | bytes 786440 | tf_op jit(solution)/shard_map/ppermute | solution.py:37
  4.4 0.7 %collective-permute-start.2 = (f32[256,256]{1,0:T(8,128)S(1)}, f32[256,256]{1,0:T(8,128)S(1)}, u32[]{:S(2)}, u32[]{:S(2)}) collective-permute-start(f32[256,256]{1,0:T(8,128)S(1)} %get-tuple-element.22), channel_id=1, source_target_pairs={{0,4}} | collective-permute-start | bytes 786440 | tf_op jit(solution)/shard_map/ppermute | solution.py:37
  5.2 0.0 copy-start
  5.2 0.0 collective-permute-done.7
  5.2 0.8 %collective-permute-start.8 = (bf16[256,512]{1,0:T(8,128)(2,1)S(1)}, bf16[256,512]{1,0:T(8,128)(2,1)S(1)}, u32[]{:S(2)}, u32[]{:S(2)}) collective-permute-start(bf16[256,512]{1,0:T(8,128)(2,1)S(1)} %broadcast_select_fusion.1), channel_id=1, source_target_pairs={{17,21},{2,18},{6,22},{0,16},{4,20},{3,11},{19,27}} | collective-permute-start | bytes 786440 | tf_op jit(solution)/shard_map/ppermute | solution.py:37
  6.1 1.5 %collective-permute-done = f32[256,256]{1,0:T(8,128)S(1)} collective-permute-done((f32[256,256]{1,0:T(8,128)S(1)}, f32[256,256]{1,0:T(8,128)S(1)}, u32[]{:S(2)}, u32[]{:S(2)}) %collective-permute-start) | collective-permute-done | bytes 262176 | tf_op jit(solution)/shard_map/ppermute | solution.py:37
  7.6 0.0 collective-permute-done.1
  7.6 0.0 collective-permute-done.2
  7.6 0.0 copy-done
  7.6 0.1 conditional.3
  7.7 1.3 %collective-permute-start.5 = (bf16[256,256]{1,0:T(8,128)(2,1)S(1)}, bf16[256,256]{1,0:T(8,128)(2,1)S(1)}, u32[]{:S(2)}, u32[]{:S(2)}) collective-permute-start(bf16[256,256]{1,0:T(8,128)(2,1)S(1)} %get-tuple-element.24), channel_id=1, source_target_pairs={{0,8},{4,12},{16,24},{20,28}} | collective-permute-start | bytes 393224 | tf_op jit(solution)/shard_map/ppermute | solution.py:37
  9.0 0.7 %collective-permute-start.3 = (bf16[256,256]{1,0:T(8,128)(2,1)S(1)}, bf16[256,256]{1,0:T(8,128)(2,1)S(1)}, u32[]{:S(2)}, u32[]{:S(2)}) collective-permute-start(bf16[256,256]{1,0:T(8,128)(2,1)S(1)} %get-tuple-element.110), channel_id=1, source_target_pairs={{0,11},{4,15},{16,19},{20,31}} | collective-permute-start | bytes 393224 | tf_op jit(solution)/shard_map/ppermute | solution.py:37
  9.7 0.7 %collective-permute-start.4 = (bf16[256,256]{1,0:T(8,128)(2,1)S(1)}, bf16[256,256]{1,0:T(8,128)(2,1)S(1)}, u32[]{:S(2)}, u32[]{:S(2)}) collective-permute-start(bf16[256,256]{1,0:T(8,128)(2,1)S(1)} %get-tuple-element.109), channel_id=1, source_target_pairs={{20,23},{16,27},{4,7}} | collective-permute-start | bytes 393224 | tf_op jit(solution)/shard_map/ppermute | solution.py:37
  10.4 0.0 collective-permute-done.8
  10.4 1.3 %collective-permute-start.10 = (bf16[256,512]{1,0:T(8,128)(2,1)S(1)}, bf16[256,512]{1,0:T(8,128)(2,1)S(1)}, u32[]{:S(2)}, u32[]{:S(2)}) collective-permute-start(bf16[256,512]{1,0:T(8,128)(2,1)S(1)} %broadcast_select_fusion.2), channel_id=1, source_target_pairs={{17,25},{21,29},{1,5},{2,10},{6,14},{18,26},{22,30},{0,8},{4,12},{... | collective-permute-start | bytes 786440 | tf_op jit(solution)/shard_map/ppermute | solution.py:37
  11.7 0.7 %collective-permute-start.9 = (bf16[256,512]{1,0:T(8,128)(2,1)S(1)}, bf16[256,512]{1,0:T(8,128)(2,1)S(1)}, u32[]{:S(2)}, u32[]{:S(2)}) collective-permute-start(bf16[256,512]{1,0:T(8,128)(2,1)S(1)} %broadcast_select_fusion.2), channel_id=1, source_target_pairs={{17,9},{21,13}} | collective-permute-start | bytes 786440 | tf_op jit(solution)/shard_map/ppermute | solution.py:37
  12.4 0.0 collective-permute-done.3
  12.4 0.0 collective-permute-done.4
  12.4 7.6 %collective-permute-done.5 = bf16[256,256]{1,0:T(8,128)(2,1)S(1)} collective-permute-done((bf16[256,256]{1,0:T(8,128)(2,1)S(1)}, bf16[256,256]{1,0:T(8,128)(2,1)S(1)}, u32[]{:S(2)}, u32[]{:S(2)}) %collective-permute-start.5) | collective-permute-done | bytes 131104 | tf_op jit(solution)/shard_map/ppermute | solution.py:37
  20.1 1.3 %collective-permute-start.6 = (bf16[256,256]{1,0:T(8,128)(2,1)S(1)}, bf16[256,256]{1,0:T(8,128)(2,1)S(1)}, u32[]{:S(2)}, u32[]{:S(2)}) collective-permute-start(bf16[256,256]{1,0:T(8,128)(2,1)S(1)} %select_select_fusion.2), channel_id=1, source_target_pairs={{4,5},{8,9},{12,13},{16,17},{20,21},{24,25},{28,29},{7,6},{11,10},... | collective-permute-start | bytes 393224 | tf_op jit(solution)/shard_map/ppermute | solution.py:37
  21.4 0.9 %collective-permute-done.6 = bf16[256,256]{1,0:T(8,128)(2,1)S(1)} collective-permute-done((bf16[256,256]{1,0:T(8,128)(2,1)S(1)}, bf16[256,256]{1,0:T(8,128)(2,1)S(1)}, u32[]{:S(2)}, u32[]{:S(2)}) %collective-permute-start.6) | collective-permute-done | bytes 131104 | tf_op jit(solution)/shard_map/ppermute | solution.py:37
  22.3 3.1 %collective-permute-done.10 = bf16[256,512]{1,0:T(8,128)(2,1)S(1)} collective-permute-done((bf16[256,512]{1,0:T(8,128)(2,1)S(1)}, bf16[256,512]{1,0:T(8,128)(2,1)S(1)}, u32[]{:S(2)}, u32[]{:S(2)}) %collective-permute-start.10) | collective-permute-done | bytes 262176 | tf_op jit(solution)/shard_map/ppermute | solution.py:37
  25.4 0.0 collective-permute-done.9
  25.4 1.0 %convolution_subtract_fusion = f32[256,512]{1,0:T(8,128)} fusion(f32[256,512]{1,0:T(8,128)S(1)} %copy-done, bf16[256,512]{1,0:T(8,128)(2,1)S(1)} %collective-permute-done.9, bf16[256,512]{1,0:T(8,128)(2,1)S(1)} %collective-permute-done.10, bf16[256,512]{1,0:T(8,128)(2,1)S(1)} %broadcast_select_fusion.2, pred[]{:T(512)S(6)} %or.43, pred[]{:T(512)S(6)} %and.99, ...), kind=kOutput, calls=%fused_computation.35 | convolution fusion | flops 67698688 | bytes 2097667 | tf_op jit(solution)/shard_map/dot_general | solution.py:154
  (9 shorter events, 0.2 us)
Async XLA Ops:
  0.0 1.2 %copy-start.1 = (f32[256,512]{1,0:T(8,128)S(1)}, f32[256,512]{1,0:T(8,128)}, u32[]{:S(2)}) copy-start(f32[256,512]{1,0:T(8,128)} %param.1) | copy-start | bytes 1572868 | tf_op jit(solution)/shard_map/cond
  1.2 4.0 %collective-permute-start.7 = (bf16[256,512]{1,0:T(8,128)(2,1)S(1)}, bf16[256,512]{1,0:T(8,128)(2,1)S(1)}, u32[]{:S(2)}, u32[]{:S(2)}) collective-permute-start(bf16[256,512]{1,0:T(8,128)(2,1)S(1)} %get-tuple-element.25), channel_id=1, source_target_pairs={{1,17},{2,6},{0,4},{3,19}} | collective-permute-start | bytes 786440 | tf_op jit(solution)/shard_map/ppermute | solution.py:37
  1.9 5.7 %collective-permute-start = (f32[256,256]{1,0:T(8,128)S(1)}, f32[256,256]{1,0:T(8,128)S(1)}, u32[]{:S(2)}, u32[]{:S(2)}) collective-permute-start(f32[256,256]{1,0:T(8,128)S(1)} %get-tuple-element.22), channel_id=1, source_target_pairs={{0,20},{8,0},{24,16},{12,4}} | collective-permute-start | bytes 786440 | tf_op jit(solution)/shard_map/ppermute | solution.py:37
  3.7 3.9 %collective-permute-start.1 = (f32[256,256]{1,0:T(8,128)S(1)}, f32[256,256]{1,0:T(8,128)S(1)}, u32[]{:S(2)}, u32[]{:S(2)}) collective-permute-start(f32[256,256]{1,0:T(8,128)S(1)} %get-tuple-element.22), channel_id=1, source_target_pairs={{0,16},{28,20}} | collective-permute-start | bytes 786440 | tf_op jit(solution)/shard_map/ppermute | solution.py:37
  4.4 3.2 %collective-permute-start.2 = (f32[256,256]{1,0:T(8,128)S(1)}, f32[256,256]{1,0:T(8,128)S(1)}, u32[]{:S(2)}, u32[]{:S(2)}) collective-permute-start(f32[256,256]{1,0:T(8,128)S(1)} %get-tuple-element.22), channel_id=1, source_target_pairs={{0,4}} | collective-permute-start | bytes 786440 | tf_op jit(solution)/shard_map/ppermute | solution.py:37
  5.2 2.4 %copy-start = (f32[256,512]{1,0:T(8,128)S(1)}, f32[256,512]{1,0:T(8,128)}, u32[]{:S(2)}) copy-start(f32[256,512]{1,0:T(8,128)} %param.5) | copy-start | bytes 1572868
  5.2 5.1 %collective-permute-start.8 = (bf16[256,512]{1,0:T(8,128)(2,1)S(1)}, bf16[256,512]{1,0:T(8,128)(2,1)S(1)}, u32[]{:S(2)}, u32[]{:S(2)}) collective-permute-start(bf16[256,512]{1,0:T(8,128)(2,1)S(1)} %broadcast_select_fusion.1), channel_id=1, source_target_pairs={{17,21},{2,18},{6,22},{0,16},{4,20},{3,11},{19,27}} | collective-permute-start | bytes 786440 | tf_op jit(solution)/shard_map/ppermute | solution.py:37
  7.7 12.3 %collective-permute-start.5 = (bf16[256,256]{1,0:T(8,128)(2,1)S(1)}, bf16[256,256]{1,0:T(8,128)(2,1)S(1)}, u32[]{:S(2)}, u32[]{:S(2)}) collective-permute-start(bf16[256,256]{1,0:T(8,128)(2,1)S(1)} %get-tuple-element.24), channel_id=1, source_target_pairs={{0,8},{4,12},{16,24},{20,28}} | collective-permute-start | bytes 393224 | tf_op jit(solution)/shard_map/ppermute | solution.py:37
  9.0 3.4 %collective-permute-start.3 = (bf16[256,256]{1,0:T(8,128)(2,1)S(1)}, bf16[256,256]{1,0:T(8,128)(2,1)S(1)}, u32[]{:S(2)}, u32[]{:S(2)}) collective-permute-start(bf16[256,256]{1,0:T(8,128)(2,1)S(1)} %get-tuple-element.110), channel_id=1, source_target_pairs={{0,11},{4,15},{16,19},{20,31}} | collective-permute-start | bytes 393224 | tf_op jit(solution)/shard_map/ppermute | solution.py:37
  9.7 2.7 %collective-permute-start.4 = (bf16[256,256]{1,0:T(8,128)(2,1)S(1)}, bf16[256,256]{1,0:T(8,128)(2,1)S(1)}, u32[]{:S(2)}, u32[]{:S(2)}) collective-permute-start(bf16[256,256]{1,0:T(8,128)(2,1)S(1)} %get-tuple-element.109), channel_id=1, source_target_pairs={{20,23},{16,27},{4,7}} | collective-permute-start | bytes 393224 | tf_op jit(solution)/shard_map/ppermute | solution.py:37
  10.4 15.0 %collective-permute-start.10 = (bf16[256,512]{1,0:T(8,128)(2,1)S(1)}, bf16[256,512]{1,0:T(8,128)(2,1)S(1)}, u32[]{:S(2)}, u32[]{:S(2)}) collective-permute-start(bf16[256,512]{1,0:T(8,128)(2,1)S(1)} %broadcast_select_fusion.2), channel_id=1, source_target_pairs={{17,25},{21,29},{1,5},{2,10},{6,14},{18,26},{22,30},{0,8},{4,12},{... | collective-permute-start | bytes 786440 | tf_op jit(solution)/shard_map/ppermute | solution.py:37
  11.7 13.7 %collective-permute-start.9 = (bf16[256,512]{1,0:T(8,128)(2,1)S(1)}, bf16[256,512]{1,0:T(8,128)(2,1)S(1)}, u32[]{:S(2)}, u32[]{:S(2)}) collective-permute-start(bf16[256,512]{1,0:T(8,128)(2,1)S(1)} %broadcast_select_fusion.2), channel_id=1, source_target_pairs={{17,9},{21,13}} | collective-permute-start | bytes 786440 | tf_op jit(solution)/shard_map/ppermute | solution.py:37
  20.1 2.3 %collective-permute-start.6 = (bf16[256,256]{1,0:T(8,128)(2,1)S(1)}, bf16[256,256]{1,0:T(8,128)(2,1)S(1)}, u32[]{:S(2)}, u32[]{:S(2)}) collective-permute-start(bf16[256,256]{1,0:T(8,128)(2,1)S(1)} %select_select_fusion.2), channel_id=1, source_target_pairs={{4,5},{8,9},{12,13},{16,17},{20,21},{24,25},{28,29},{7,6},{11,10},... | collective-permute-start | bytes 393224 | tf_op jit(solution)/shard_map/ppermute | solution.py:37

commit v30 on v28

--- a/solution.py
+++ b/solution.py
@@ -58,6 +58,9 @@
         beside_steps.append([(h, h + stride) for h in far])
     beside_steps[-1].append((0, 1))
     beside_back = [(middle + r - 2, r) for r in range(2, middle)]
+    if n_row == 4 * APART:
+        beside_steps[-1] = [(middle, n_row - 1), (middle + 1, APART + 1), (0, 1)]
+        beside_back = [(middle, middle + APART), (middle + 1, APART)]
 
     def among(rows):
         found = jnp.bool_(False)
@@ -142,7 +145,7 @@
     if len(beside_back) > 2:
         sent = upper
     got = send(sent, [((a, 1), (b, 1)) for a, b in beside_back])
-    upper = jnp.where((col_here == 1) & (row_here > 1) & (row_here < middle), got, upper)
+    upper = jnp.where((col_here == 1) & among([b for _, b in beside_back]), got, upper)
     got = send(
         received,
         [((r, 0), (r, 1)) for r in range(1, n_row)]

time: 26.4 us -> 28 us (1.061)
  waiting for transfers between devices: 12.7 us -> 14.2 us
    ppermute x11, waiting for transfers between devices: 12.7 us -> 14.2 us  [send(): return lax.ppermute(value, ('row', 'col'), flat)]
where the time goes in v30:
time: 28 us; the launch traced here: 27.7 us
  waiting for transfers between devices  14.2 us (51%)
  starting transfers between devices  10.6 us (38%)
  other arithmetic  1.31 us (5%)
  matrix products  1.03 us (4%)
  between operations  0.37 us (1%)
    ppermute x11, waiting for transfers between devices, send(): return lax.ppermute(value, ('row', 'col'), flat)  14.2 us
    ppermute x11, starting transfers between devices, send(): return lax.ppermute(value, ('row', 'col'), flat)  10.6 us
    convert_element_type x1, other arithmetic, blocks(): return (matrix[:, :NB], matrix.astype(jnp.bfloat16))  1.15 us
    dot_general x1, matrix products, shards(): return matrix - jnp.dot(received, upper, preferred_element_type=jnp.float32)  1.03 us
  transfers between devices with their start and end apart: 11, of which 4 were waited for; matrix products, arithmetic and copies ran while one was open for 1% of the time, Pallas kernels for 0%

profile of v30, /device:TPU:26, one launch (start us, length us, event | category | flops | bytes accessed | tf_op | source)
XLA Modules:
  0.0 27.7 jit_solution(11364334031291180752)
XLA Ops:
  0.0 1.2 %conditional.2 = (f32[256,256]{1,0:T(8,128)S(1)}, bf16[256,512]{1,0:T(8,128)(2,1)S(1)}) conditional(s32[]{:T(128)} %convert_element_type.16, () %tuple.22, f32[256,512]{1,0:T(8,128)} %param.5), branch_computations={%region_0.0_spmd, %region_1.0_spmd} | conditional | flops 131072 | bytes 3407916 | solution.py:46
  0.0 0.0 copy-start.1
  0.0 1.1 %convert_element_type.1 = bf16[256,512]{1,0:T(8,128)(2,1)S(1)} convert(f32[256,512]{1,0:T(8,128)} %param.1) | non-fusion elementwise | flops 131072 | bytes 786432 | tf_op jit(solution)/shard_map/cond/branch_1_fun/convert_element_type | solution.py:40
  1.2 0.0 copy-done.1
  1.2 0.7 %collective-permute-start.7 = (bf16[256,512]{1,0:T(8,128)(2,1)S(1)}, bf16[256,512]{1,0:T(8,128)(2,1)S(1)}, u32[]{:S(2)}, u32[]{:S(2)}) collective-permute-start(bf16[256,512]{1,0:T(8,128)(2,1)S(1)} %get-tuple-element.25), channel_id=1, source_target_pairs={{1,17},{2,6},{0,4},{3,19}} | collective-permute-start | bytes 786440 | tf_op jit(solution)/shard_map/ppermute | solution.py:37
  1.9 0.7 %collective-permute-start = (f32[256,256]{1,0:T(8,128)S(1)}, f32[256,256]{1,0:T(8,128)S(1)}, u32[]{:S(2)}, u32[]{:S(2)}) collective-permute-start(f32[256,256]{1,0:T(8,128)S(1)} %get-tuple-element.22), channel_id=1, source_target_pairs={{0,20},{8,0},{12,4},{24,16}} | collective-permute-start | bytes 786440 | tf_op jit(solution)/shard_map/ppermute | solution.py:37
  2.6 1.8 %collective-permute-start.1 = (f32[256,256]{1,0:T(8,128)S(1)}, f32[256,256]{1,0:T(8,128)S(1)}, u32[]{:S(2)}, u32[]{:S(2)}) collective-permute-start(f32[256,256]{1,0:T(8,128)S(1)} %get-tuple-element.22), channel_id=1, source_target_pairs={{0,4},{28,20}} | collective-permute-start | bytes 786440 | tf_op jit(solution)/shard_map/ppermute | solution.py:37
  4.4 0.7 %collective-permute-start.2 = (f32[256,256]{1,0:T(8,128)S(1)}, f32[256,256]{1,0:T(8,128)S(1)}, u32[]{:S(2)}, u32[]{:S(2)}) collective-permute-start(f32[256,256]{1,0:T(8,128)S(1)} %get-tuple-element.22), channel_id=1, source_target_pairs={{0,16}} | collective-permute-start | bytes 786440 | tf_op jit(solution)/shard_map/ppermute | solution.py:37
  5.2 0.0 copy-start
  5.2 0.0 collective-permute-done.7
  5.2 0.8 %collective-permute-start.8 = (bf16[256,512]{1,0:T(8,128)(2,1)S(1)}, bf16[256,512]{1,0:T(8,128)(2,1)S(1)}, u32[]{:S(2)}, u32[]{:S(2)}) collective-permute-start(bf16[256,512]{1,0:T(8,128)(2,1)S(1)} %broadcast_select_fusion.1), channel_id=1, source_target_pairs={{17,21},{2,18},{6,22},{0,16},{4,20},{3,11},{19,27}} | collective-permute-start | bytes 786440 | tf_op jit(solution)/shard_map/ppermute | solution.py:37
  6.1 0.0 collective-permute-done
  6.1 2.1 %collective-permute-done.1 = f32[256,256]{1,0:T(8,128)S(1)} collective-permute-done((f32[256,256]{1,0:T(8,128)S(1)}, f32[256,256]{1,0:T(8,128)S(1)}, u32[]{:S(2)}, u32[]{:S(2)}) %collective-permute-start.1) | collective-permute-done | bytes 262176 | tf_op jit(solution)/shard_map/ppermute | solution.py:37
  8.3 0.0 collective-permute-done.2
  8.3 0.0 copy-done
  8.3 0.1 conditional.3
  8.4 1.3 %collective-permute-start.5 = (bf16[256,256]{1,0:T(8,128)(2,1)S(1)}, bf16[256,256]{1,0:T(8,128)(2,1)S(1)}, u32[]{:S(2)}, u32[]{:S(2)}) collective-permute-start(bf16[256,256]{1,0:T(8,128)(2,1)S(1)} %get-tuple-element.24), channel_id=1, source_target_pairs={{0,8},{4,12},{16,24},{20,28}} | collective-permute-start | bytes 393224 | tf_op jit(solution)/shard_map/ppermute | solution.py:37
  9.7 0.7 %collective-permute-start.3 = (bf16[256,256]{1,0:T(8,128)(2,1)S(1)}, bf16[256,256]{1,0:T(8,128)(2,1)S(1)}, u32[]{:S(2)}, u32[]{:S(2)}) collective-permute-start(bf16[256,256]{1,0:T(8,128)(2,1)S(1)} %get-tuple-element.111), channel_id=1, source_target_pairs={{0,11},{4,15},{16,19},{20,31}} | collective-permute-start | bytes 393224 | tf_op jit(solution)/shard_map/ppermute | solution.py:37
  10.4 0.7 %collective-permute-start.4 = (bf16[256,256]{1,0:T(8,128)(2,1)S(1)}, bf16[256,256]{1,0:T(8,128)(2,1)S(1)}, u32[]{:S(2)}, u32[]{:S(2)}) collective-permute-start(bf16[256,256]{1,0:T(8,128)(2,1)S(1)} %get-tuple-element.110), channel_id=1, source_target_pairs={{20,23},{4,7},{16,27}} | collective-permute-start | bytes 393224 | tf_op jit(solution)/shard_map/ppermute | solution.py:37
  11.1 0.0 collective-permute-done.8
  11.1 1.3 %collective-permute-start.10 = (bf16[256,512]{1,0:T(8,128)(2,1)S(1)}, bf16[256,512]{1,0:T(8,128)(2,1)S(1)}, u32[]{:S(2)}, u32[]{:S(2)}) collective-permute-start(bf16[256,512]{1,0:T(8,128)(2,1)S(1)} %broadcast_select_fusion.2), channel_id=1, source_target_pairs={{17,29},{21,13},{1,5},{2,10},{6,14},{18,26},{22,30},{0,8},{4,12},{... | collective-permute-start | bytes 786440 | tf_op jit(solution)/shard_map/ppermute | solution.py:37
  12.4 0.7 %collective-permute-start.9 = (bf16[256,512]{1,0:T(8,128)(2,1)S(1)}, bf16[256,512]{1,0:T(8,128)(2,1)S(1)}, u32[]{:S(2)}, u32[]{:S(2)}) collective-permute-start(bf16[256,512]{1,0:T(8,128)(2,1)S(1)} %broadcast_select_fusion.2), channel_id=1, source_target_pairs={{17,25},{21,9}} | collective-permute-start | bytes 786440 | tf_op jit(solution)/shard_map/ppermute | solution.py:37
  13.1 0.0 collective-permute-done.3
  13.1 0.0 collective-permute-done.4
  13.1 3.7 %collective-permute-done.5 = bf16[256,256]{1,0:T(8,128)(2,1)S(1)} collective-permute-done((bf16[256,256]{1,0:T(8,128)(2,1)S(1)}, bf16[256,256]{1,0:T(8,128)(2,1)S(1)}, u32[]{:S(2)}, u32[]{:S(2)}) %collective-permute-start.5) | collective-permute-done | bytes 131104 | tf_op jit(solution)/shard_map/ppermute | solution.py:37
  16.9 1.3 %collective-permute-start.6 = (bf16[256,256]{1,0:T(8,128)(2,1)S(1)}, bf16[256,256]{1,0:T(8,128)(2,1)S(1)}, u32[]{:S(2)}, u32[]{:S(2)}) collective-permute-start(bf16[256,256]{1,0:T(8,128)(2,1)S(1)} %select_select_fusion.2), channel_id=1, source_target_pairs={{4,5},{8,9},{12,13},{16,17},{20,21},{24,25},{28,29},{7,6},{11,10},... | collective-permute-start | bytes 393224 | tf_op jit(solution)/shard_map/ppermute | solution.py:37
  18.2 0.9 %collective-permute-done.6 = bf16[256,256]{1,0:T(8,128)(2,1)S(1)} collective-permute-done((bf16[256,256]{1,0:T(8,128)(2,1)S(1)}, bf16[256,256]{1,0:T(8,128)(2,1)S(1)}, u32[]{:S(2)}, u32[]{:S(2)}) %collective-permute-start.6) | collective-permute-done | bytes 131104 | tf_op jit(solution)/shard_map/ppermute | solution.py:37
  19.1 7.5 %collective-permute-done.10 = bf16[256,512]{1,0:T(8,128)(2,1)S(1)} collective-permute-done((bf16[256,512]{1,0:T(8,128)(2,1)S(1)}, bf16[256,512]{1,0:T(8,128)(2,1)S(1)}, u32[]{:S(2)}, u32[]{:S(2)}) %collective-permute-start.10) | collective-permute-done | bytes 262176 | tf_op jit(solution)/shard_map/ppermute | solution.py:37
  26.6 0.0 collective-permute-done.9
  26.6 1.0 %convolution_subtract_fusion = f32[256,512]{1,0:T(8,128)} fusion(f32[256,512]{1,0:T(8,128)S(1)} %copy-done, bf16[256,512]{1,0:T(8,128)(2,1)S(1)} %collective-permute-done.9, bf16[256,512]{1,0:T(8,128)(2,1)S(1)} %collective-permute-done.10, bf16[256,512]{1,0:T(8,128)(2,1)S(1)} %broadcast_select_fusion.2, pred[]{:T(512)S(6)} %or.47, pred[]{:T(512)S(6)} %and.95, ...), kind=kOutput, calls=%fused_computation.35 | convolution fusion | flops 67698688 | bytes 2097667 | tf_op jit(solution)/shard_map/dot_general | solution.py:158
  (10 shorter events, 0.2 us)
Async XLA Ops:
  0.0 1.2 %copy-start.1 = (f32[256,512]{1,0:T(8,128)S(1)}, f32[256,512]{1,0:T(8,128)}, u32[]{:S(2)}) copy-start(f32[256,512]{1,0:T(8,128)} %param.1) | copy-start | bytes 1572868 | tf_op jit(solution)/shard_map/cond
  1.2 4.0 %collective-permute-start.7 = (bf16[256,512]{1,0:T(8,128)(2,1)S(1)}, bf16[256,512]{1,0:T(8,128)(2,1)S(1)}, u32[]{:S(2)}, u32[]{:S(2)}) collective-permute-start(bf16[256,512]{1,0:T(8,128)(2,1)S(1)} %get-tuple-element.25), channel_id=1, source_target_pairs={{1,17},{2,6},{0,4},{3,19}} | collective-permute-start | bytes 786440 | tf_op jit(solution)/shard_map/ppermute | solution.py:37
  1.9 4.2 %collective-permute-start = (f32[256,256]{1,0:T(8,128)S(1)}, f32[256,256]{1,0:T(8,128)S(1)}, u32[]{:S(2)}, u32[]{:S(2)}) collective-permute-start(f32[256,256]{1,0:T(8,128)S(1)} %get-tuple-element.22), channel_id=1, source_target_pairs={{0,20},{8,0},{12,4},{24,16}} | collective-permute-start | bytes 786440 | tf_op jit(solution)/shard_map/ppermute | solution.py:37
  2.6 5.7 %collective-permute-start.1 = (f32[256,256]{1,0:T(8,128)S(1)}, f32[256,256]{1,0:T(8,128)S(1)}, u32[]{:S(2)}, u32[]{:S(2)}) collective-permute-start(f32[256,256]{1,0:T(8,128)S(1)} %get-tuple-element.22), channel_id=1, source_target_pairs={{0,4},{28,20}} | collective-permute-start | bytes 786440 | tf_op jit(solution)/shard_map/ppermute | solution.py:37
  4.4 3.9 %collective-permute-start.2 = (f32[256,256]{1,0:T(8,128)S(1)}, f32[256,256]{1,0:T(8,128)S(1)}, u32[]{:S(2)}, u32[]{:S(2)}) collective-permute-start(f32[256,256]{1,0:T(8,128)S(1)} %get-tuple-element.22), channel_id=1, source_target_pairs={{0,16}} | collective-permute-start | bytes 786440 | tf_op jit(solution)/shard_map/ppermute | solution.py:37
  5.2 3.1 %copy-start = (f32[256,512]{1,0:T(8,128)S(1)}, f32[256,512]{1,0:T(8,128)}, u32[]{:S(2)}) copy-start(f32[256,512]{1,0:T(8,128)} %param.5) | copy-start | bytes 1572868
  5.2 5.8 %collective-permute-start.8 = (bf16[256,512]{1,0:T(8,128)(2,1)S(1)}, bf16[256,512]{1,0:T(8,128)(2,1)S(1)}, u32[]{:S(2)}, u32[]{:S(2)}) collective-permute-start(bf16[256,512]{1,0:T(8,128)(2,1)S(1)} %broadcast_select_fusion.1), channel_id=1, source_target_pairs={{17,21},{2,18},{6,22},{0,16},{4,20},{3,11},{19,27}} | collective-permute-start | bytes 786440 | tf_op jit(solution)/shard_map/ppermute | solution.py:37
  8.4 8.5 %collective-permute-start.5 = (bf16[256,256]{1,0:T(8,128)(2,1)S(1)}, bf16[256,256]{1,0:T(8,128)(2,1)S(1)}, u32[]{:S(2)}, u32[]{:S(2)}) collective-permute-start(bf16[256,256]{1,0:T(8,128)(2,1)S(1)} %get-tuple-element.24), channel_id=1, source_target_pairs={{0,8},{4,12},{16,24},{20,28}} | collective-permute-start | bytes 393224 | tf_op jit(solution)/shard_map/ppermute | solution.py:37
  9.7 3.4 %collective-permute-start.3 = (bf16[256,256]{1,0:T(8,128)(2,1)S(1)}, bf16[256,256]{1,0:T(8,128)(2,1)S(1)}, u32[]{:S(2)}, u32[]{:S(2)}) collective-permute-start(bf16[256,256]{1,0:T(8,128)(2,1)S(1)} %get-tuple-element.111), channel_id=1, source_target_pairs={{0,11},{4,15},{16,19},{20,31}} | collective-permute-start | bytes 393224 | tf_op jit(solution)/shard_map/ppermute | solution.py:37
  10.4 2.7 %collective-permute-start.4 = (bf16[256,256]{1,0:T(8,128)(2,1)S(1)}, bf16[256,256]{1,0:T(8,128)(2,1)S(1)}, u32[]{:S(2)}, u32[]{:S(2)}) collective-permute-start(bf16[256,256]{1,0:T(8,128)(2,1)S(1)} %get-tuple-element.110), channel_id=1, source_target_pairs={{20,23},{4,7},{16,27}} | collective-permute-start | bytes 393224 | tf_op jit(solution)/shard_map/ppermute | solution.py:37
  11.1 15.5 %collective-permute-start.10 = (bf16[256,512]{1,0:T(8,128)(2,1)S(1)}, bf16[256,512]{1,0:T(8,128)(2,1)S(1)}, u32[]{:S(2)}, u32[]{:S(2)}) collective-permute-start(bf16[256,512]{1,0:T(8,128)(2,1)S(1)} %broadcast_select_fusion.2), channel_id=1, source_target_pairs={{17,29},{21,13},{1,5},{2,10},{6,14},{18,26},{22,30},{0,8},{4,12},{... | collective-permute-start | bytes 786440 | tf_op jit(solution)/shard_map/ppermute | solution.py:37
  12.4 14.2 %collective-permute-start.9 = (bf16[256,512]{1,0:T(8,128)(2,1)S(1)}, bf16[256,512]{1,0:T(8,128)(2,1)S(1)}, u32[]{:S(2)}, u32[]{:S(2)}) collective-permute-start(bf16[256,512]{1,0:T(8,128)(2,1)S(1)} %broadcast_select_fusion.2), channel_id=1, source_target_pairs={{17,25},{21,9}} | collective-permute-start | bytes 786440 | tf_op jit(solution)/shard_map/ppermute | solution.py:37
  16.9 2.3 %collective-permute-start.6 = (bf16[256,256]{1,0:T(8,128)(2,1)S(1)}, bf16[256,256]{1,0:T(8,128)(2,1)S(1)}, u32[]{:S(2)}, u32[]{:S(2)}) collective-permute-start(bf16[256,256]{1,0:T(8,128)(2,1)S(1)} %select_select_fusion.2), channel_id=1, source_target_pairs={{4,5},{8,9},{12,13},{16,17},{20,21},{24,25},{28,29},{7,6},{11,10},... | collective-permute-start | bytes 393224 | tf_op jit(solution)/shard_map/ppermute | solution.py:37

commit v31 on v28

--- a/solution.py
+++ b/solution.py
@@ -22,8 +22,8 @@
     across = 1.0 / jnp.sum(diagonal, axis=0, keepdims=True)
     down = 1.0 / jnp.sum(diagonal, axis=1, keepdims=True)
     approx = down * (2.0 * identity - square * across)
-    product = jnp.dot(jnp.concatenate([square, columns], axis=0), approx, precision=HIGH)
-    return jnp.dot(product[NB:], 2.0 * identity - product[:NB], precision=HIGH)
+    rest = 2.0 * identity - jnp.dot(square, approx, precision=HIGH)
+    return jnp.dot(jnp.dot(columns, approx, precision=HIGH), rest, precision=HIGH)
 
 
 def shards(matrix):

time: 26.4 us -> 26.6 us (level)
  no operation moved by 1% of the time
where the time goes in v31:
time: 26.6 us; the launch traced here: 26.3 us
  waiting for transfers between devices  12.9 us (48%)
  starting transfers between devices  10.6 us (40%)
  other arithmetic  1.31 us (5%)
  matrix products  1.03 us (4%)
  between operations  0.37 us (1%)
    ppermute x11, waiting for transfers between devices, send(): return lax.ppermute(value, ('row', 'col'), flat)  12.9 us
    ppermute x11, starting transfers between devices, send(): return lax.ppermute(value, ('row', 'col'), flat)  10.6 us
    convert_element_type x1, other arithmetic, blocks(): return (matrix[:, :NB], matrix.astype(jnp.bfloat16))  1.15 us
    dot_general x1, matrix products, shards(): return matrix - jnp.dot(received, upper, preferred_element_type=jnp.float32)  1.03 us
  transfers between devices with their start and end apart: 11, of which 4 were waited for; matrix products, arithmetic and copies ran while one was open for 1% of the time, Pallas kernels for 0%

profile of v31, /device:TPU:26, one launch (start us, length us, event | category | flops | bytes accessed | tf_op | source)
XLA Modules:
  0.0 26.3 jit_solution(16029157930686923104)
XLA Ops:
  0.0 1.2 %conditional.2 = (f32[256,256]{1,0:T(8,128)S(1)}, bf16[256,512]{1,0:T(8,128)(2,1)S(1)}) conditional(s32[]{:T(128)} %convert_element_type.16, () %tuple.22, f32[256,512]{1,0:T(8,128)} %param.5), branch_computations={%region_0.0_spmd, %region_1.0_spmd} | conditional | flops 131072 | bytes 3407916 | solution.py:46
  0.0 0.0 copy-start.1
  0.0 1.1 %convert_element_type.1 = bf16[256,512]{1,0:T(8,128)(2,1)S(1)} convert(f32[256,512]{1,0:T(8,128)} %param.1) | non-fusion elementwise | flops 131072 | bytes 786432 | tf_op jit(solution)/shard_map/cond/branch_1_fun/convert_element_type | solution.py:40
  1.2 0.0 copy-done.1
  1.2 0.7 %collective-permute-start.7 = (bf16[256,512]{1,0:T(8,128)(2,1)S(1)}, bf16[256,512]{1,0:T(8,128)(2,1)S(1)}, u32[]{:S(2)}, u32[]{:S(2)}) collective-permute-start(bf16[256,512]{1,0:T(8,128)(2,1)S(1)} %get-tuple-element.25), channel_id=1, source_target_pairs={{1,17},{2,6},{0,4},{3,19}} | collective-permute-start | bytes 786440 | tf_op jit(solution)/shard_map/ppermute | solution.py:37
  1.9 0.7 %collective-permute-start = (f32[256,256]{1,0:T(8,128)S(1)}, f32[256,256]{1,0:T(8,128)S(1)}, u32[]{:S(2)}, u32[]{:S(2)}) collective-permute-start(f32[256,256]{1,0:T(8,128)S(1)} %get-tuple-element.22), channel_id=1, source_target_pairs={{0,20},{8,0},{12,4},{24,16}} | collective-permute-start | bytes 786440 | tf_op jit(solution)/shard_map/ppermute | solution.py:37
  2.6 1.8 %collective-permute-start.1 = (f32[256,256]{1,0:T(8,128)S(1)}, f32[256,256]{1,0:T(8,128)S(1)}, u32[]{:S(2)}, u32[]{:S(2)}) collective-permute-start(f32[256,256]{1,0:T(8,128)S(1)} %get-tuple-element.22), channel_id=1, source_target_pairs={{0,4},{28,20}} | collective-permute-start | bytes 786440 | tf_op jit(solution)/shard_map/ppermute | solution.py:37
  4.4 0.7 %collective-permute-start.2 = (f32[256,256]{1,0:T(8,128)S(1)}, f32[256,256]{1,0:T(8,128)S(1)}, u32[]{:S(2)}, u32[]{:S(2)}) collective-permute-start(f32[256,256]{1,0:T(8,128)S(1)} %get-tuple-element.22), channel_id=1, source_target_pairs={{0,16}} | collective-permute-start | bytes 786440 | tf_op jit(solution)/shard_map/ppermute | solution.py:37
  5.2 0.0 copy-start
  5.2 0.0 collective-permute-done.7
  5.2 0.8 %collective-permute-start.8 = (bf16[256,512]{1,0:T(8,128)(2,1)S(1)}, bf16[256,512]{1,0:T(8,128)(2,1)S(1)}, u32[]{:S(2)}, u32[]{:S(2)}) collective-permute-start(bf16[256,512]{1,0:T(8,128)(2,1)S(1)} %broadcast_select_fusion.1), channel_id=1, source_target_pairs={{17,21},{2,18},{6,22},{0,16},{4,20},{3,11},{19,27}} | collective-permute-start | bytes 786440 | tf_op jit(solution)/shard_map/ppermute | solution.py:37
  6.1 0.0 collective-permute-done
  6.1 2.1 %collective-permute-done.1 = f32[256,256]{1,0:T(8,128)S(1)} collective-permute-done((f32[256,256]{1,0:T(8,128)S(1)}, f32[256,256]{1,0:T(8,128)S(1)}, u32[]{:S(2)}, u32[]{:S(2)}) %collective-permute-start.1) | collective-permute-done | bytes 262176 | tf_op jit(solution)/shard_map/ppermute | solution.py:37
  8.3 0.0 collective-permute-done.2
  8.3 0.0 copy-done
  8.3 0.1 conditional.3
  8.4 1.3 %collective-permute-start.5 = (bf16[256,256]{1,0:T(8,128)(2,1)S(1)}, bf16[256,256]{1,0:T(8,128)(2,1)S(1)}, u32[]{:S(2)}, u32[]{:S(2)}) collective-permute-start(bf16[256,256]{1,0:T(8,128)(2,1)S(1)} %get-tuple-element.24), channel_id=1, source_target_pairs={{0,8},{4,12},{16,24},{20,28}} | collective-permute-start | bytes 393224 | tf_op jit(solution)/shard_map/ppermute | solution.py:37
  9.7 0.7 %collective-permute-start.3 = (bf16[256,256]{1,0:T(8,128)(2,1)S(1)}, bf16[256,256]{1,0:T(8,128)(2,1)S(1)}, u32[]{:S(2)}, u32[]{:S(2)}) collective-permute-start(bf16[256,256]{1,0:T(8,128)(2,1)S(1)} %get-tuple-element.111), channel_id=1, source_target_pairs={{0,11},{4,15},{16,19},{20,31}} | collective-permute-start | bytes 393224 | tf_op jit(solution)/shard_map/ppermute | solution.py:37
  10.4 0.7 %collective-permute-start.4 = (bf16[256,256]{1,0:T(8,128)(2,1)S(1)}, bf16[256,256]{1,0:T(8,128)(2,1)S(1)}, u32[]{:S(2)}, u32[]{:S(2)}) collective-permute-start(bf16[256,256]{1,0:T(8,128)(2,1)S(1)} %get-tuple-element.110), channel_id=1, source_target_pairs={{20,23},{4,7},{16,27}} | collective-permute-start | bytes 393224 | tf_op jit(solution)/shard_map/ppermute | solution.py:37
  11.1 0.0 collective-permute-done.8
  11.1 1.3 %collective-permute-start.10 = (bf16[256,512]{1,0:T(8,128)(2,1)S(1)}, bf16[256,512]{1,0:T(8,128)(2,1)S(1)}, u32[]{:S(2)}, u32[]{:S(2)}) collective-permute-start(bf16[256,512]{1,0:T(8,128)(2,1)S(1)} %broadcast_select_fusion.2), channel_id=1, source_target_pairs={{17,25},{21,29},{1,5},{2,10},{6,14},{18,26},{22,30},{0,8},{4,12},{... | collective-permute-start | bytes 786440 | tf_op jit(solution)/shard_map/ppermute | solution.py:37
  12.4 0.7 %collective-permute-start.9 = (bf16[256,512]{1,0:T(8,128)(2,1)S(1)}, bf16[256,512]{1,0:T(8,128)(2,1)S(1)}, u32[]{:S(2)}, u32[]{:S(2)}) collective-permute-start(bf16[256,512]{1,0:T(8,128)(2,1)S(1)} %broadcast_select_fusion.2), channel_id=1, source_target_pairs={{17,9},{21,13}} | collective-permute-start | bytes 786440 | tf_op jit(solution)/shard_map/ppermute | solution.py:37
  13.1 0.0 collective-permute-done.3
  13.1 0.0 collective-permute-done.4
  13.1 4.6 %collective-permute-done.5 = bf16[256,256]{1,0:T(8,128)(2,1)S(1)} collective-permute-done((bf16[256,256]{1,0:T(8,128)(2,1)S(1)}, bf16[256,256]{1,0:T(8,128)(2,1)S(1)}, u32[]{:S(2)}, u32[]{:S(2)}) %collective-permute-start.5) | collective-permute-done | bytes 131104 | tf_op jit(solution)/shard_map/ppermute | solution.py:37
  17.8 1.3 %collective-permute-start.6 = (bf16[256,256]{1,0:T(8,128)(2,1)S(1)}, bf16[256,256]{1,0:T(8,128)(2,1)S(1)}, u32[]{:S(2)}, u32[]{:S(2)}) collective-permute-start(bf16[256,256]{1,0:T(8,128)(2,1)S(1)} %select_select_fusion.2), channel_id=1, source_target_pairs={{4,5},{8,9},{12,13},{16,17},{20,21},{24,25},{28,29},{7,6},{11,10},... | collective-permute-start | bytes 393224 | tf_op jit(solution)/shard_map/ppermute | solution.py:37
  19.2 0.9 %collective-permute-done.6 = bf16[256,256]{1,0:T(8,128)(2,1)S(1)} collective-permute-done((bf16[256,256]{1,0:T(8,128)(2,1)S(1)}, bf16[256,256]{1,0:T(8,128)(2,1)S(1)}, u32[]{:S(2)}, u32[]{:S(2)}) %collective-permute-start.6) | collective-permute-done | bytes 131104 | tf_op jit(solution)/shard_map/ppermute | solution.py:37
  20.1 5.2 %collective-permute-done.10 = bf16[256,512]{1,0:T(8,128)(2,1)S(1)} collective-permute-done((bf16[256,512]{1,0:T(8,128)(2,1)S(1)}, bf16[256,512]{1,0:T(8,128)(2,1)S(1)}, u32[]{:S(2)}, u32[]{:S(2)}) %collective-permute-start.10) | collective-permute-done | bytes 262176 | tf_op jit(solution)/shard_map/ppermute | solution.py:37
  25.3 0.0 collective-permute-done.9
  25.3 1.0 %convolution_subtract_fusion.1 = f32[256,512]{1,0:T(8,128)} fusion(f32[256,512]{1,0:T(8,128)S(1)} %copy-done, bf16[256,512]{1,0:T(8,128)(2,1)S(1)} %collective-permute-done.9, bf16[256,512]{1,0:T(8,128)(2,1)S(1)} %collective-permute-done.10, bf16[256,512]{1,0:T(8,128)(2,1)S(1)} %broadcast_select_fusion.2, pred[]{:T(512)S(6)} %or.43, pred[]{:T(512)S(6)} %and.99, ...), kind=kOutput, calls=%fused_computation.32 | convolution fusion | flops 67698688 | bytes 2097667 | tf_op jit(solution)/shard_map/dot_general | solution.py:155
  (10 shorter events, 0.2 us)
Async XLA Ops:
  0.0 1.2 %copy-start.1 = (f32[256,512]{1,0:T(8,128)S(1)}, f32[256,512]{1,0:T(8,128)}, u32[]{:S(2)}) copy-start(f32[256,512]{1,0:T(8,128)} %param.1) | copy-start | bytes 1572868 | tf_op jit(solution)/shard_map/cond
  1.2 4.0 %collective-permute-start.7 = (bf16[256,512]{1,0:T(8,128)(2,1)S(1)}, bf16[256,512]{1,0:T(8,128)(2,1)S(1)}, u32[]{:S(2)}, u32[]{:S(2)}) collective-permute-start(bf16[256,512]{1,0:T(8,128)(2,1)S(1)} %get-tuple-element.25), channel_id=1, source_target_pairs={{1,17},{2,6},{0,4},{3,19}} | collective-permute-start | bytes 786440 | tf_op jit(solution)/shard_map/ppermute | solution.py:37
  1.9 4.2 %collective-permute-start = (f32[256,256]{1,0:T(8,128)S(1)}, f32[256,256]{1,0:T(8,128)S(1)}, u32[]{:S(2)}, u32[]{:S(2)}) collective-permute-start(f32[256,256]{1,0:T(8,128)S(1)} %get-tuple-element.22), channel_id=1, source_target_pairs={{0,20},{8,0},{12,4},{24,16}} | collective-permute-start | bytes 786440 | tf_op jit(solution)/shard_map/ppermute | solution.py:37
  2.6 5.7 %collective-permute-start.1 = (f32[256,256]{1,0:T(8,128)S(1)}, f32[256,256]{1,0:T(8,128)S(1)}, u32[]{:S(2)}, u32[]{:S(2)}) collective-permute-start(f32[256,256]{1,0:T(8,128)S(1)} %get-tuple-element.22), channel_id=1, source_target_pairs={{0,4},{28,20}} | collective-permute-start | bytes 786440 | tf_op jit(solution)/shard_map/ppermute | solution.py:37
  4.4 3.9 %collective-permute-start.2 = (f32[256,256]{1,0:T(8,128)S(1)}, f32[256,256]{1,0:T(8,128)S(1)}, u32[]{:S(2)}, u32[]{:S(2)}) collective-permute-start(f32[256,256]{1,0:T(8,128)S(1)} %get-tuple-element.22), channel_id=1, source_target_pairs={{0,16}} | collective-permute-start | bytes 786440 | tf_op jit(solution)/shard_map/ppermute | solution.py:37
  5.2 3.1 %copy-start = (f32[256,512]{1,0:T(8,128)S(1)}, f32[256,512]{1,0:T(8,128)}, u32[]{:S(2)}) copy-start(f32[256,512]{1,0:T(8,128)} %param.5) | copy-start | bytes 1572868
  5.2 5.8 %collective-permute-start.8 = (bf16[256,512]{1,0:T(8,128)(2,1)S(1)}, bf16[256,512]{1,0:T(8,128)(2,1)S(1)}, u32[]{:S(2)}, u32[]{:S(2)}) collective-permute-start(bf16[256,512]{1,0:T(8,128)(2,1)S(1)} %broadcast_select_fusion.1), channel_id=1, source_target_pairs={{17,21},{2,18},{6,22},{0,16},{4,20},{3,11},{19,27}} | collective-permute-start | bytes 786440 | tf_op jit(solution)/shard_map/ppermute | solution.py:37
  8.4 9.4 %collective-permute-start.5 = (bf16[256,256]{1,0:T(8,128)(2,1)S(1)}, bf16[256,256]{1,0:T(8,128)(2,1)S(1)}, u32[]{:S(2)}, u32[]{:S(2)}) collective-permute-start(bf16[256,256]{1,0:T(8,128)(2,1)S(1)} %get-tuple-element.24), channel_id=1, source_target_pairs={{0,8},{4,12},{16,24},{20,28}} | collective-permute-start | bytes 393224 | tf_op jit(solution)/shard_map/ppermute | solution.py:37
  9.7 3.4 %collective-permute-start.3 = (bf16[256,256]{1,0:T(8,128)(2,1)S(1)}, bf16[256,256]{1,0:T(8,128)(2,1)S(1)}, u32[]{:S(2)}, u32[]{:S(2)}) collective-permute-start(bf16[256,256]{1,0:T(8,128)(2,1)S(1)} %get-tuple-element.111), channel_id=1, source_target_pairs={{0,11},{4,15},{16,19},{20,31}} | collective-permute-start | bytes 393224 | tf_op jit(solution)/shard_map/ppermute | solution.py:37
  10.4 2.7 %collective-permute-start.4 = (bf16[256,256]{1,0:T(8,128)(2,1)S(1)}, bf16[256,256]{1,0:T(8,128)(2,1)S(1)}, u32[]{:S(2)}, u32[]{:S(2)}) collective-permute-start(bf16[256,256]{1,0:T(8,128)(2,1)S(1)} %get-tuple-element.110), channel_id=1, source_target_pairs={{20,23},{4,7},{16,27}} | collective-permute-start | bytes 393224 | tf_op jit(solution)/shard_map/ppermute | solution.py:37
  11.1 14.2 %collective-permute-start.10 = (bf16[256,512]{1,0:T(8,128)(2,1)S(1)}, bf16[256,512]{1,0:T(8,128)(2,1)S(1)}, u32[]{:S(2)}, u32[]{:S(2)}) collective-permute-start(bf16[256,512]{1,0:T(8,128)(2,1)S(1)} %broadcast_select_fusion.2), channel_id=1, source_target_pairs={{17,25},{21,29},{1,5},{2,10},{6,14},{18,26},{22,30},{0,8},{4,12},{... | collective-permute-start | bytes 786440 | tf_op jit(solution)/shard_map/ppermute | solution.py:37
  12.4 12.9 %collective-permute-start.9 = (bf16[256,512]{1,0:T(8,128)(2,1)S(1)}, bf16[256,512]{1,0:T(8,128)(2,1)S(1)}, u32[]{:S(2)}, u32[]{:S(2)}) collective-permute-start(bf16[256,512]{1,0:T(8,128)(2,1)S(1)} %broadcast_select_fusion.2), channel_id=1, source_target_pairs={{17,9},{21,13}} | collective-permute-start | bytes 786440 | tf_op jit(solution)/shard_map/ppermute | solution.py:37
  17.8 2.3 %collective-permute-start.6 = (bf16[256,256]{1,0:T(8,128)(2,1)S(1)}, bf16[256,256]{1,0:T(8,128)(2,1)S(1)}, u32[]{:S(2)}, u32[]{:S(2)}) collective-permute-start(bf16[256,256]{1,0:T(8,128)(2,1)S(1)} %select_select_fusion.2), channel_id=1, source_target_pairs={{4,5},{8,9},{12,13},{16,17},{20,21},{24,25},{28,29},{7,6},{11,10},... | collective-permute-start | bytes 393224 | tf_op jit(solution)/shard_map/ppermute | solution.py:37
